TPU v7x, 256 devices: a whole 4x4x8 slice. The times are simulated.
256 devices in a mesh: batch: 32 (over y, z), hist: 4 (over x), rep: 2 (over core).
Axes of the slice: x: 4, y: 4, z: 8, core: 2. Of those that a mesh axis runs over, the one named last changes fastest.
Arguments:
- node_input: float32 [131072, 512], P(('batch', 'hist', 'rep')), may hold values from -6 to 6
- initial: float32 [131072, 512], P(('batch', 'hist', 'rep')), may hold values from -12 to 12
- cotangent: float32 [131072, 512], P(('batch', 'hist', 'rep')), may hold values from -6 to 6
- weight: float32 [512, 512], replicated, may hold values from -0.25 to 0.25
- edge_weight: float32 [131072, 8], P(('batch', 'hist', 'rep')), may hold values from 0.05 to 0.3
- neighbors: int32 [131072, 8], P(('batch', 'hist', 'rep')), may hold values from 0 to 2815, as said below
- halo_rows: int32 [256, 128, 2], P(('batch', 'hist', 'rep')), may hold values from 0 to 1279
- cold_history: float32 [163840, 512], P(('batch', 'hist')), may hold values from -6 to 6
- hot_history: float32 [2048, 512], P('rep'), may hold values from -6 to 6
- dest_rows: int32 [128, 1024], P(('batch', 'hist')), may hold values from 0 to 1279, as said below
Outputs:
- grad_weight: float32 [512, 512], replicated
- grad_input: float32 [131072, 512], P(('batch', 'hist', 'rep'))
- new_history: float32 [163840, 512], P(('batch', 'hist'))
Inputs may be any that keep to these rules, and one draw needn't show every extreme that they name: `neighbors`: column 0 of each node lies in the halo range [512, 768), column 1 in the hot range from 768, the others name nodes of the same device below 512. `dest_rows`: each row of an owner names 1024 distinct rows.
All inputs are finite; a program needn't handle non-finite values.
Results may differ from a plain program's by a relative error of at most 0.0003.
Values sent between devices are 32-bit elements; how exact they have to be, the bound alone decides.
No kernel may reach another device: no remote copies, remote signals or barrier semaphores. Data moves between devices by JAX's collectives and lax.ppermute only.
A program may use at most 128 MiB of HBM per device.

v0:
```python
import math

import jax
import jax.numpy as jnp
from jax import lax
from jax.sharding import PartitionSpec as P

ALPHA = 0.1
BETA = math.log(1.5)
HIGH = lax.Precision.HIGHEST


def body(
    node_input,
    initial,
    cotangent,
    weight,
    edge_weight,
    neighbors,
    halo_rows,
    cold_history,
    hot_history,
    dest_rows,
):
    local_rows = node_input.shape[0]
    width = node_input.shape[1]
    owners = lax.axis_size(("batch", "hist"))
    replicas = lax.axis_size("rep")
    per_owner = halo_rows.shape[2]
    halo_count = owners * per_owner
    hot_count = hot_history.shape[0] * replicas
    columns = local_rows + halo_count + hot_count
    column_ids = lax.broadcasted_iota(jnp.int32, (1, columns), 1)
    tile = jnp.zeros((local_rows, columns), jnp.float32)
    for slot in range(neighbors.shape[1]):
        tile = tile + jnp.where(
            neighbors[:, slot : slot + 1] == column_ids, edge_weight[:, slot : slot + 1], 0.0
        )
    found = cold_history[
        lax.all_to_all(halo_rows[0], ("batch", "hist"), split_axis=0, concat_axis=0, tiled=True)
    ]
    halo = lax.all_to_all(found, ("batch", "hist"), split_axis=0, concat_axis=0, tiled=True)
    halo = halo.reshape(halo_count, width)
    agg = jnp.dot(
        tile[:, :local_rows], node_input, precision=HIGH, preferred_element_type=jnp.float32
    )
    agg = agg + jnp.dot(
        tile[:, local_rows : local_rows + halo_count],
        halo,
        precision=HIGH,
        preferred_element_type=jnp.float32,
    )
    hot_tile = tile[:, local_rows + halo_count :]
    agg = agg + jnp.dot(
        hot_tile,
        lax.all_gather(hot_history, "rep", axis=0, tiled=True),
        precision=HIGH,
        preferred_element_type=jnp.float32,
    )
    z = (1.0 - ALPHA) * agg + ALPHA * initial
    u = (1.0 - BETA) * z + BETA * jnp.dot(
        z, weight, precision=HIGH, preferred_element_type=jnp.float32
    )
    embed, pull = jax.vjp(lambda v: jax.nn.gelu(v, approximate=True), u)
    du = pull(cotangent)[0]
    dz = (1.0 - BETA) * du + BETA * lax.dot_general(
        du, weight, (((1,), (1,)), ((), ())), precision=HIGH, preferred_element_type=jnp.float32
    )
    all_nodes = local_rows * lax.axis_size(("batch", "hist", "rep"))
    term = lax.dot_general(
        z, du, (((0,), (0,)), ((), ())), precision=HIGH, preferred_element_type=jnp.float32
    )
    grad_weight = lax.psum(term * (BETA / math.sqrt(all_nodes)), ("batch", "hist", "rep"))
    grad_input = (1.0 - ALPHA) * lax.dot_general(
        tile[:, :local_rows],
        dz,
        (((0,), (0,)), ((), ())),
        precision=HIGH,
        preferred_element_type=jnp.float32,
    )
    per_q = local_rows // owners
    outgoing = embed.reshape(owners, per_q, width)
    arrived = lax.all_to_all(outgoing, ("batch", "hist"), split_axis=0, concat_axis=0, tiled=True)
    received = lax.all_gather(arrived[None], "rep", axis=0, tiled=True)
    received = received.reshape(replicas * local_rows, width)
    new_history = cold_history.at[dest_rows[0]].set(received)
    return (grad_weight, grad_input, new_history)


def solution(mesh):
    return jax.shard_map(
        body,
        mesh=mesh,
        in_specs=(
            P(("batch", "hist", "rep"), None),
            P(("batch", "hist", "rep"), None),
            P(("batch", "hist", "rep"), None),
            P(),
            P(("batch", "hist", "rep"), None),
            P(("batch", "hist", "rep"), None),
            P(("batch", "hist", "rep"), None, None),
            P(("batch", "hist"), None),
            P("rep", None),
            P(("batch", "hist"), None),
        ),
        out_specs=(P(), P(("batch", "hist", "rep"), None), P(("batch", "hist"), None)),
        check_vma=False,
    )
```

profile of v0, /device:TPU:1, one launch (start us, length us, event | category | flops | bytes accessed | tf_op | source)
XLA Modules:
  0.0 407.5 jit_solution(2221548605867174468)
XLA Ops:
  7.2 0.0 copy-start
  7.2 0.0 copy-start.5
  7.2 0.0 copy-start.6
  7.2 0.0 copy-start.8
  7.2 0.0 all-gather.4.cloned.1.call-start
  7.3 3.5 copy.18
  10.8 0.0 all-gather.4.cloned.1.call-update
  10.8 0.0 copy-done.8
  10.8 0.7 copy.14
  11.6 16.3 %all-to-all-start = ((s32[128,1,2]{2,1,0:T(1,128)}), s32[128,1,2]{2,1,0:T(1,128)S(1)}, u32[]{:S(2)}, u32[]{:S(2)}) async-start(s32[128,1,2]{2,1,0:T(1,128)} %bitcast.16), calls=%async_computation | async-start | bytes 131072 | tf_op jit(solution)/shard_map/all_to_all | solution.py:40
  27.9 0.0 copy-done.5
  28.0 0.0 copy-done.6
  28.0 10.4 %all-to-all-done = s32[128,1,2]{2,1,0:T(1,128)S(1)} async-done(((s32[128,1,2]{2,1,0:T(1,128)}), s32[128,1,2]{2,1,0:T(1,128)S(1)}, u32[]{:S(2)}, u32[]{:S(2)}) %all-to-all-start) | async-done | bytes 1056 | tf_op jit(solution)/shard_map/all_to_all | solution.py:40
  38.4 0.1 reshape.79
  38.6 3.0 gather_fusion
  41.5 1.1 reshape.78
  42.6 6.2 %all-to-all-start.1 = ((f32[128,2,512]{2,1,0:T(2,128)}), f32[128,2,512]{2,1,0:T(2,128)S(1)}, u32[]{:S(2)}, u32[]{:S(2)}) async-start(f32[128,2,512]{2,1,0:T(2,128)} %reshape.78), calls=%async_computation.1 | async-start | bytes 1048576 | tf_op jit(solution)/shard_map/all_to_all | solution.py:42
  48.8 0.2 all-gather.6.cloned.1.call-start
  49.1 10.7 %select_add_fusion = f32[512,2816]{1,0:T(8,128)S(1)} fusion(f32[512]{0:T(512)S(1)} %bitcast.39, s32[512]{0:T(512)S(1)} %bitcast.47, f32[512]{0:T(512)S(1)} %bitcast.40, s32[512]{0:T(512)S(1)} %bitcast.48, f32[512]{0:T(512)S(1)} %bitcast.34, s32[512]{0:T(512)S(1)} %bitcast.42, f32[512]{0:T(512)S(1)} %bitcast.35, s32[512]{0:T(512)S(1)} %bitcast.43, ...), kind=kLoop, calls=%fused_computation.2 | loop fusion | flops 33161216 | bytes 5799936 | tf_op jit(solution)/shard_map/add | solution.py:36
  59.8 0.0 copy-start.1
  59.8 2.5 copy-done.1
  62.3 3.1 fusion.14
  65.3 0.0 all-to-all-done.1
  65.4 1.2 reshape.74
  66.5 0.0 all-gather.4.cloned.1.call-done
  66.5 0.0 copy-start.2
  66.5 0.0 copy-start.3
  66.5 9.6 %fusion = f32[512,512]{1,0:T(8,128)S(1)} fusion(f32[2048,512]{1,0:T(8,128)} %all-gather.4.cloned.1.call-done, f32[512,2816]{1,0:T(8,128)} %copy-done.1), kind=kOutput, calls=%fused_computation.11 | convolution fusion | flops 6442450944 | bytes 9437184 | tf_op jit(solution)/shard_map/dot_general | solution.py:54
  76.2 0.0 copy-done.2
  76.2 0.0 copy-done.3
  76.2 2.3 fusion.6
  78.4 0.0 copy-done
  78.5 0.0 copy-start.7
  78.5 3.5 multiply_multiply_fusion.2
  81.9 1.5 reshape.75
  83.5 38.6 %all_to_all.22 = f32[128,4,512]{2,1,0:T(4,128)} all-to-all(f32[128,4,512]{2,1,0:T(4,128)S(1)} %reshape.75), channel_id=1, replica_groups=mesh['batch'=32,'hist'=4,'rep'=2] {'batch','hist'}, dimensions={0} | all-to-all | bytes 2097152 | tf_op jit(solution)/shard_map/all_to_all | solution.py:83
  122.1 0.0 copy-start.4
  122.1 0.0 all-gather.6.cloned.1.call-update
  122.1 0.0 all-reduce.2.cloned.1.call-start
  122.1 0.0 copy-done.7
  122.2 5.1 %convolution_multiply_fusion.2 = f32[512,512]{1,0:T(8,128)} fusion(f32[512,512]{1,0:T(8,128)S(1)} %fusion.6, f32[512,512]{1,0:T(8,128)} %get-tuple-element.20, f32[512,512]{1,0:T(8,128)} %param.12), kind=kOutput, calls=%fused_computation.18 | convolution fusion | flops 1615855616 | bytes 4194304 | tf_op jit(solution)/shard_map/dot_general | solution.py:70
  127.2 0.0 all-reduce.2.cloned.1.call-update
  127.3 0.0 copy-done.4
  127.3 4.9 %fusion.2 = f32[512,512]{1,0:T(8,128)S(1)} fusion(f32[512,512]{1,0:T(8,128)S(1)} %copy-done, f32[512,512]{1,0:T(8,128)S(1)} %copy-done.4, f32[512,512]{1,0:T(8,128)} %param.12), kind=kOutput, calls=%fused_computation.17 | convolution fusion | flops 1621360640 | bytes 4194304 | tf_op jit(solution)/shard_map/dot_general | solution.py:66
  132.2 4.2 %convolution_multiply_fusion = f32[512,512]{1,0:T(8,128)} fusion(f32[512,512]{1,0:T(8,128)S(1)} %fusion.2, f32[512,2816]{1,0:T(8,128)} %copy-done.1), kind=kOutput, calls=%fused_computation.15 | convolution fusion | flops 1610874880 | bytes 3145728 | tf_op jit(solution)/shard_map/dot_general | solution.py:74
  136.4 1.7 all-gather.6.cloned.1.call-done
  138.1 2.0 reshape.89
  140.1 8.0 %scatter_fusion = f32[1280,512]{1,0:T(8,128)} fusion(f32[1280,512]{1,0:T(8,128)} %copy.18, s32[1024]{0:T(1024)S(1)} %bitcast.32, f32[1024,512]{1,0:T(8,128)S(1)} %reshape.89), kind=kCustom, calls=%fused_computation.1 | custom fusion | bytes 6295552 | tf_op jit(solution)/shard_map/scatter | solution.py:86
  148.0 250.6 %all-reduce.2.cloned.1.call-done = f32[512,512]{1,0:T(8,128)} async-done(((f32[512,512]{1,0:T(8,128)}), f32[512,512]{1,0:T(8,128)}) %all-reduce.2.cloned.1.call-update) | async-done | bytes 1048592 | tf_op jit(solution)/shard_map/psum | solution.py:73
  398.7 2.3 copy.19
  (5 shorter events, 0.1 us)
Async XLA Ops:
  7.2 71.3 %copy-start = (f32[512,512]{1,0:T(8,128)S(1)}, f32[512,512]{1,0:T(8,128)}, u32[]{:S(2)}) copy-start(f32[512,512]{1,0:T(8,128)} %param.13) | copy-start | bytes 3145732
  7.2 20.7 %copy-start.5 = (f32[512,8]{0,1:T(8,128)S(1)}, f32[512,8]{0,1:T(8,128)}, u32[]{:S(2)}) copy-start(f32[512,8]{0,1:T(8,128)} %param.14) | copy-start | bytes 49156
  7.2 20.8 %copy-start.6 = (s32[512,8]{0,1:T(8,128)S(1)}, s32[512,8]{0,1:T(8,128)}, u32[]{:S(2)}) copy-start(s32[512,8]{0,1:T(8,128)} %param.15) | copy-start | bytes 49156
  7.2 3.6 copy-start.8
  7.2 59.3 %all-gather.4.cloned.1.call-start = ((), (), s32[]{:S(2)}) async-start(), calls=%async_computation.3 | async-start | bytes 6291456 | tf_op jit(solution)/shard_map/all_gather | solution.py:56
  11.6 26.8 %all-to-all-start = ((s32[128,1,2]{2,1,0:T(1,128)}), s32[128,1,2]{2,1,0:T(1,128)S(1)}, u32[]{:S(2)}, u32[]{:S(2)}) async-start(s32[128,1,2]{2,1,0:T(1,128)} %bitcast.16), calls=%async_computation | async-start | bytes 131072 | tf_op jit(solution)/shard_map/all_to_all | solution.py:40
  42.6 22.7 %all-to-all-start.1 = ((f32[128,2,512]{2,1,0:T(2,128)}), f32[128,2,512]{2,1,0:T(2,128)S(1)}, u32[]{:S(2)}, u32[]{:S(2)}) async-start(f32[128,2,512]{2,1,0:T(2,128)} %reshape.78), calls=%async_computation.1 | async-start | bytes 1048576 | tf_op jit(solution)/shard_map/all_to_all | solution.py:42
  48.8 89.3 %all-gather.6.cloned.1.call-start = ((), (), s32[]{:S(2)}) async-start(), calls=%async_computation.5 | async-start | bytes 3145728 | tf_op jit(solution)/shard_map/all_gather | solution.py:84
  59.8 2.5 copy-start.1
  66.5 9.6 %copy-start.2 = (f32[256,512]{1,0:T(8,128)S(1)}, f32[256,512]{1,0:T(8,128)}, u32[]{:S(2)}) copy-start(f32[256,512]{1,0:T(8,128)} %reshape.74) | copy-start | bytes 1572868
  66.5 9.7 %copy-start.3 = (f32[512,512]{1,0:T(8,128)S(1)}, f32[512,512]{1,0:T(8,128)}, u32[]{:S(2)}) copy-start(f32[512,512]{1,0:T(8,128)} %param.11) | copy-start | bytes 3145732
  78.5 43.7 %copy-start.7 = (s32[1,1024]{1,0:T(1,128)S(1)}, s32[1,1024]{1,0:T(1,128)}, u32[]{:S(2)}) copy-start(s32[1,1024]{1,0:T(1,128)} %param.19) | copy-start | bytes 12292
  122.1 5.2 %copy-start.4 = (f32[512,512]{1,0:T(8,128)S(1)}, f32[512,512]{1,0:T(8,128)}, u32[]{:S(2)}) copy-start(f32[512,512]{1,0:T(8,128)} %get-tuple-element.20) | copy-start | bytes 3145732
  122.1 276.6 %all-reduce.2.cloned.1.call-start = ((), (), s32[]{:S(2)}) async-start(), calls=%async_computation.4 | async-start | bytes 2097152 | tf_op jit(solution)/shard_map/psum | solution.py:73
Sparse Core Ops, SparseCore 0:
  10.9 23.5 all-gather.3
  122.2 15.8 all-gather.5
  143.5 255.1 all-reduce.1
where the time goes:
time: 409 us; the launch traced here: 407 us
  waiting for transfers between devices  263 us (64%)
  blocking collectives  38.6 us (9%)
  matrix products  32.6 us (8%)
  local copies, waits for them, and re-layouts  25.9 us (6%)
  starting transfers between devices  22.8 us (6%)
  between operations  14 us (3%)
  other arithmetic  10.7 us (3%)
    psum x1, waiting for transfers between devices, body(): lax.psum(term * (BETA / math.sqrt(all_nodes)), ('batch', 'hist', 'rep'))  251 us
    all_to_all x1, blocking collectives, body(): lax.all_to_all(outgoing, ('batch', 'hist'), split_axis=0, concat_axis=0,...  38.6 us
    all_to_all x1, starting transfers between devices, body(): lax.all_to_all(halo_rows[0], ('batch', 'hist'), split_axis=0, concat_axis...  16.3 us
    add x1, other arithmetic, body(): tile + jnp.where(neighbors[:, slot:slot + 1] == column_ids, edge_weight[:...  10.7 us
    all_to_all x1, waiting for transfers between devices, body(): lax.all_to_all(halo_rows[0], ('batch', 'hist'), split_axis=0, concat_axis...  10.4 us
    dot_general x1, matrix products, body(): jnp.dot(hot_tile, lax.all_gather(hot_history, 'rep', axis=0, tiled=True),...  9.63 us
    unnamed x21, local copies, waits for them, and re-layouts  9.08 us
  transfers between devices with their start and end apart: 5, of which 3 were waited for; matrix products, arithmetic and copies ran while one was open for 11% of the time, Pallas kernels for 0%

commit v1 on v0

v1 whole, which is shorter than its diff:
```python
import math

import jax
import jax.numpy as jnp
from jax import lax
from jax.sharding import PartitionSpec as P

ALPHA = 0.1
BETA = math.log(1.5)
HIGH = lax.Precision.HIGH
OWN = ("batch", "hist")
SWAP = [(0, 1), (1, 0)]


def dot(a, b, dims=(((1,), (0,)), ((), ()))):
    return lax.dot_general(a, b, dims, precision=HIGH, preferred_element_type=jnp.float32)


def exchange(v):
    return lax.all_to_all(v, OWN, split_axis=0, concat_axis=0, tiled=True)


def pair(mine, core):
    other = lax.ppermute(mine, "rep", SWAP)
    first = jnp.where(core == 0, mine, other)
    second = jnp.where(core == 0, other, mine)
    return jnp.concatenate([first, second], axis=0)


def body(
    node_input,
    initial,
    cotangent,
    weight,
    edge_weight,
    neighbors,
    halo_rows,
    cold_history,
    hot_history,
    dest_rows,
):
    local_rows, width = node_input.shape
    owners = lax.axis_size(OWN)
    core = lax.axis_index("rep")
    halo_count = owners * halo_rows.shape[2]
    found = cold_history[exchange(halo_rows[0])]
    halo = exchange(found).reshape(halo_count, width)
    hot = pair(hot_history, core)
    ids = lax.broadcasted_iota(jnp.int32, (1, local_rows), 1)
    tile = jnp.zeros((local_rows, local_rows), jnp.float32)
    for slot in range(2, neighbors.shape[1]):
        tile = tile + jnp.where(
            neighbors[:, slot : slot + 1] == ids, edge_weight[:, slot : slot + 1], 0.0
        )
    hot_rows = hot[neighbors[:, 1] - local_rows - halo_count]
    agg = dot(tile, node_input) + edge_weight[:, 1:2] * hot_rows
    halo_ids = lax.broadcasted_iota(jnp.int32, (1, halo_count), 1) + local_rows
    halo_tile = jnp.where(neighbors[:, :1] == halo_ids, edge_weight[:, :1], 0.0)
    agg = agg + dot(halo_tile, halo)
    z = (1.0 - ALPHA) * agg + ALPHA * initial
    u = (1.0 - BETA) * z + BETA * dot(z, weight)
    embed, pull = jax.vjp(lambda v: jax.nn.gelu(v, approximate=True), u)
    du = pull(cotangent)[0]
    all_nodes = local_rows * lax.axis_size(("batch", "hist", "rep"))
    term = dot(z, du, (((0,), (0,)), ((), ()))) * (BETA / math.sqrt(all_nodes))
    half = width // 2
    keep = lax.dynamic_slice_in_dim(term, core * half, half, 0)
    give = lax.dynamic_slice_in_dim(term, (1 - core) * half, half, 0)
    keep = keep + lax.ppermute(give, "rep", SWAP)
    outgoing = jnp.concatenate(
        [embed.reshape(owners, -1, 128), keep.reshape(owners, -1, 128)], axis=1
    )
    arrived = exchange(outgoing)
    cut = local_rows * width // owners // 128
    piece = jnp.sum(arrived[:, cut:], axis=0)
    pieces = exchange(jnp.broadcast_to(piece[None], (owners,) + piece.shape))
    grad_weight = pair(pieces.reshape(half, width), core)
    dz = (1.0 - BETA) * du + BETA * dot(du, weight, (((1,), (1,)), ((), ())))
    grad_input = (1.0 - ALPHA) * dot(tile, dz, (((0,), (0,)), ((), ())))
    received = pair(arrived[:, :cut].reshape(local_rows, width), core)
    new_history = cold_history.at[dest_rows[0]].set(received, unique_indices=True)
    return (grad_weight, grad_input, new_history)


def solution(mesh):
    return jax.shard_map(
        body,
        mesh=mesh,
        in_specs=(
            P(("batch", "hist", "rep"), None),
            P(("batch", "hist", "rep"), None),
            P(("batch", "hist", "rep"), None),
            P(),
            P(("batch", "hist", "rep"), None),
            P(("batch", "hist", "rep"), None),
            P(("batch", "hist", "rep"), None, None),
            P(("batch", "hist"), None),
            P("rep", None),
            P(("batch", "hist"), None),
        ),
        out_specs=(P(), P(("batch", "hist", "rep"), None), P(("batch", "hist"), None)),
        check_vma=False,
    )
```

time: 409 us -> 176 us (0.43)
  waiting for transfers between devices: 263 us -> 20.6 us
  blocking collectives: 38.6 us -> 69.2 us
  matrix products: 32.6 us -> 17.5 us
  between operations: 14 us -> 0.93 us
  other arithmetic: 10.7 us -> 20.6 us
  local copies, waits for them, and re-layouts: 25.9 us -> 18.6 us
  starting transfers between devices: 22.8 us -> 28.4 us
    psum x1 -> x0, waiting for transfers between devices: 251 us -> none  [body(): lax.psum(term * (BETA / math.sqrt(all_nodes)), ('batch', 'hist', 'rep'))]
    all_to_all x1 -> x2, blocking collectives: 38.6 us -> 69.2 us  [exchange(): return lax.all_to_all(v, OWN, split_axis=0, concat_axis=0, tiled=True)]
    dot_general x7 -> x6, matrix products: 32.6 us -> 17.5 us  [dot(): lax.dot_general(a, b, dims, precision=HIGH, preferred_element_type=jnp.fl...]
    ppermute x0 -> x4, starting transfers between devices: none -> 12.5 us  [the longest x3 8.83 us: pair(): other = lax.ppermute(mine, 'rep', SWAP)]
    all_to_all x2, waiting for transfers between devices: 10.4 us -> 18.8 us  [exchange(): return lax.all_to_all(v, OWN, split_axis=0, concat_axis=0, tiled=True)]
    scatter x0 -> x1, other arithmetic: none -> 8.3 us  [body(): cold_history.at[dest_rows[0]].set(received, unique_indices=True)]
    scatter x1 -> x0, local copies, waits for them, and re-layouts: 7.98 us -> none  [body(): new_history = cold_history.at[dest_rows[0]].set(received)]
    add x1 -> x3, other arithmetic: 10.7 us -> 3.1 us  [the longest x1 1.82 us: body(): z = (1.0 - ALPHA) * agg + ALPHA * initial]
  transfers between devices with their start and end apart: 5 -> 6, of which waited for: 3 -> 3; matrix products, arithmetic and copies ran while one was open for 11% -> 18% of each run, Pallas kernels for 0% -> 0%
where the time goes in v1:
time: 176 us
  blocking collectives  69.2 us (39%)
  starting transfers between devices  28.4 us (16%)
  other arithmetic  20.6 us (12%)
  waiting for transfers between devices  20.6 us (12%)
  local copies, waits for them, and re-layouts  18.6 us (11%)
  matrix products  17.5 us (10%)
    all_to_all x2, blocking collectives, exchange(): return lax.all_to_all(v, OWN, split_axis=0, concat_axis=0, tiled=True)  69.2 us
    all_to_all x2, waiting for transfers between devices, exchange(): return lax.all_to_all(v, OWN, split_axis=0, concat_axis=0, tiled=True)  18.8 us
    dot_general x6, matrix products, dot(): lax.dot_general(a, b, dims, precision=HIGH, preferred_element_type=jnp.fl...  17.5 us
    all_to_all x2, starting transfers between devices, exchange(): return lax.all_to_all(v, OWN, split_axis=0, concat_axis=0, tiled=True)  15.9 us
    ppermute x3, starting transfers between devices, pair(): other = lax.ppermute(mine, 'rep', SWAP)  8.83 us
    scatter x1, other arithmetic, body(): cold_history.at[dest_rows[0]].set(received, unique_indices=True)  8.3 us
    select_n x3, other arithmetic, pair(): first = jnp.where(core == 0, mine, other)  5.48 us
    unnamed x22, local copies, waits for them, and re-layouts  4.69 us
  transfers between devices with their start and end apart: 6, of which 3 were waited for; matrix products, arithmetic and copies ran while one was open for 18% of the time, Pallas kernels for 0%

profile of v1, /device:TPU:1, one launch (start us, length us, event | category | flops | bytes accessed | tf_op | source)
XLA Modules:
  0.0 175.7 jit_solution(17027917452980716915)
XLA Ops:
  0.6 0.0 copy-start
  0.6 0.0 copy-start.8
  0.7 3.6 %copy.17 = f32[1280,512]{1,0:T(8,128)} copy(f32[1280,512]{1,0:T(8,128)} %param.17) | data formatting | bytes 5242880
  4.2 3.2 %collective-permute-start = (f32[1024,512]{1,0:T(8,128)}, f32[1024,512]{1,0:T(8,128)}, u32[]{:S(2)}, u32[]{:S(2)}) collective-permute-start(f32[1024,512]{1,0:T(8,128)} %param.18), channel_id=1, source_target_pairs={{0,1},{1,0},{2,3},{3,2},{4,5},{5,4},{6,7},{7,6},{8,9},{9,8},{10,11... | collective-permute-start | bytes 6291464 | tf_op jit(solution)/shard_map/ppermute | solution.py:24
  7.5 0.0 copy-done.8
  7.5 0.1 copy.14
  7.6 24.1 %all_to_all.28 = s32[128,1,2]{2,1,0:T(1,128)S(1)} all-to-all(s32[128,1,2]{2,1,0:T(1,128)S(1)} %bitcast.32), channel_id=1, replica_groups=mesh['batch'=32,'hist'=4,'rep'=2] {'batch','hist'}, dimensions={0} | all-to-all | bytes 2048 | tf_op jit(solution)/shard_map/all_to_all | solution.py:20
  31.7 0.1 reshape.101
  31.9 3.0 %gather_fusion.1 = f32[256,512]{1,0:T(8,128)S(1)} fusion(f32[1280,512]{1,0:T(8,128)} %copy.17, s32[1024]{0:T(1024)S(1)} %pad_clamp_fusion), kind=kCustom, calls=%fused_computation.1 | custom fusion | bytes 1049600 | tf_op jit(solution)/shard_map/gather | solution.py:46
  34.8 0.0 copy-start.5
  34.8 0.0 copy-start.6
  34.9 1.1 reshape.100
  36.0 6.4 %all-to-all-start.1 = ((f32[128,2,512]{2,1,0:T(2,128)}), f32[128,2,512]{2,1,0:T(2,128)S(1)}, u32[]{:S(2)}, u32[]{:S(2)}) async-start(f32[128,2,512]{2,1,0:T(2,128)} %reshape.100), calls=%async_computation.1 | async-start | bytes 1048576 | tf_op jit(solution)/shard_map/all_to_all | solution.py:20
  42.3 0.0 copy-done.5
  42.4 0.0 copy-done.6
  42.4 4.2 %fusion.14 = f32[512,512]{1,0:T(8,128)} fusion(f32[512,512]{1,0:T(8,128)} %param.10, f32[512]{0:T(512)S(1)} %bitcast.50, s32[512]{0:T(512)S(1)} %bitcast.38, f32[512]{0:T(512)S(1)} %bitcast.52, s32[512]{0:T(512)S(1)} %bitcast.40, f32[512]{0:T(512)S(1)} %bitcast.54, s32[512]{0:T(512)S(1)} %bitcast.42, f32[512]{0:T(512)S(1)} %bitcast.56, ...), kind=kOutput, calls=%fused_computation.39 | convolution fusion | flops 809762816 | bytes 2121728 | tf_op jit(solution)/shard_map/dot_general | solution.py:16
  46.6 12.1 %all-to-all-done.1 = f32[128,2,512]{2,1,0:T(2,128)S(1)} async-done(((f32[128,2,512]{2,1,0:T(2,128)}), f32[128,2,512]{2,1,0:T(2,128)S(1)}, u32[]{:S(2)}, u32[]{:S(2)}) %all-to-all-start.1) | async-done | bytes 524320 | tf_op jit(solution)/shard_map/all_to_all | solution.py:20
  58.7 0.4 reshape.86
  59.1 0.6 fusion.12
  59.7 0.0 collective-permute-done
  59.7 2.7 %broadcast_select_fusion.1 = (f32[1024,512]{1,0:T(8,128)S(1)}, f32[1024,512]{1,0:T(8,128)S(1)}) fusion(f32[1024,512]{1,0:T(8,128)} %param.18, f32[1024,512]{1,0:T(8,128)} %collective-permute-done, pred[]{:T(512)S(6)} %eq.113), kind=kLoop, calls=%fused_computation.33 | loop fusion | flops 1048576 | bytes 8388609 | tf_op jit(solution)/shard_map/jit(_where)/select_n | solution.py:25
  62.5 2.4 %pad_maximum_fusion = f32[2048,512]{1,0:T(8,128)} fusion(f32[1024,512]{1,0:T(8,128)S(1)} %get-tuple-element.4, f32[1024,512]{1,0:T(8,128)S(1)} %get-tuple-element.3), kind=kLoop, calls=%fused_computation.3 | loop fusion | flops 1048576 | bytes 8388608 | tf_op jit(solution)/shard_map/concatenate | solution.py:27
  64.9 4.2 %gather_fusion = f32[512,512]{1,0:T(8,128)S(1)} fusion(f32[2048,512]{1,0:T(8,128)} %pad_maximum_fusion, s32[1024]{0:T(1024)S(1)} %pad_clamp_fusion.1), kind=kCustom, calls=%fused_computation | custom fusion | bytes 2099200 | tf_op jit(solution)/shard_map/gather | solution.py:55
  69.1 1.8 %multiply_add_fusion = f32[512,512]{1,0:T(8,128)S(1)} fusion(f32[512,512]{1,0:T(8,128)} %param.11, f32[512,512]{1,0:T(8,128)S(1)} %fusion.12, f32[512,512]{1,0:T(8,128)} %fusion.14, f32[512,512]{1,0:T(8,128)S(1)} %gather_fusion, f32[512]{0:T(512)S(1)} %bitcast.33), kind=kLoop, calls=%fused_computation.24 | loop fusion | flops 1572864 | bytes 5244928 | tf_op jit(solution)/shard_map/add | solution.py:60
  70.9 0.0 copy-done
  70.9 0.0 copy-start.9
  70.9 1.3 multiply_multiply_fusion.2
  72.3 0.0 copy-start.4
  72.3 0.0 copy-done.9
  72.3 1.7 convolution_multiply_fusion.2
  74.0 0.0 copy-done.4
  74.0 0.0 copy-start.3
  74.0 1.0 copy-done.3
  75.0 0.8 constant_dynamic-slice_fusion
  75.8 3.7 %collective-permute-start.1 = (f32[256,512]{1,0:T(8,128)}, f32[256,512]{1,0:T(8,128)}, u32[]{:S(2)}, u32[]{:S(2)}) collective-permute-start(f32[256,512]{1,0:T(8,128)} %constant_dynamic-slice_fusion), channel_id=1, source_target_pairs={{0,1},{1,0},{2,3},{3,2},{4,5},{5,4},{6,7},{7,6},{8,9},{9,8},{10,11... | collective-permute-start | bytes 1572872 | tf_op jit(solution)/shard_map/ppermute | solution.py:69
  79.5 0.1 reshape.87
  79.6 1.8 %collective-permute-done.1 = f32[256,512]{1,0:T(8,128)} collective-permute-done((f32[256,512]{1,0:T(8,128)}, f32[256,512]{1,0:T(8,128)}, u32[]{:S(2)}, u32[]{:S(2)}) %collective-permute-start.1) | collective-permute-done | bytes 524320 | tf_op jit(solution)/shard_map/ppermute | solution.py:69
  81.4 1.3 dynamic-slice_add_fusion
  82.7 0.1 pad_maximum_fusion.1
  82.8 45.0 %all_to_all.27 = f32[128,24,128]{2,1,0:T(8,128)S(1)} all-to-all(f32[128,24,128]{2,1,0:T(8,128)S(1)} %pad_maximum_fusion.1), channel_id=1, replica_groups=mesh['batch'=32,'hist'=4,'rep'=2] {'batch','hist'}, dimensions={0} | all-to-all | bytes 3145728 | tf_op jit(solution)/shard_map/all_to_all | solution.py:20
  127.8 0.1 slice_reduce_fusion
  128.0 0.8 broadcast_in_dim.93
  128.8 9.5 %all-to-all-start.3 = ((f32[128,8,128]{2,1,0:T(8,128)}), f32[128,8,128]{2,1,0:T(8,128)S(1)}, u32[]{:S(2)}, u32[]{:S(2)}) async-start(f32[128,8,128]{2,1,0:T(8,128)} %broadcast_in_dim.93), calls=%async_computation.3 | async-start | bytes 1048576 | tf_op jit(solution)/shard_map/all_to_all | solution.py:20
  138.3 0.0 copy-start.7
  138.3 1.1 slice.77
  139.4 1.4 reshape.90
  140.8 0.0 copy-start.1
  140.8 1.6 collective-permute-start.3
  142.4 0.0 copy-done.7
  142.4 5.3 %fusion.4 = f32[512,512]{1,0:T(8,128)} fusion(f32[512,512]{1,0:T(8,128)S(1)} %copy-done, f32[512,512]{1,0:T(8,128)} %copy-done.4, f32[512,512]{1,0:T(8,128)} %param.12), kind=kOutput, calls=%fused_computation.13 | convolution fusion | flops 816054272 | bytes 4194304 | tf_op jit(solution)/shard_map/dot_general | solution.py:16
  147.8 0.0 copy-done.1
  147.8 6.6 %all-to-all-done.3 = f32[128,8,128]{2,1,0:T(8,128)S(1)} async-done(((f32[128,8,128]{2,1,0:T(8,128)}), f32[128,8,128]{2,1,0:T(8,128)S(1)}, u32[]{:S(2)}, u32[]{:S(2)}) %all-to-all-start.3) | async-done | bytes 524320 | tf_op jit(solution)/shard_map/all_to_all | solution.py:20
  154.4 0.9 reshape.89
  155.3 0.0 copy-start.2
  155.3 4.0 %collective-permute-start.2 = (f32[256,512]{1,0:T(8,128)}, f32[256,512]{1,0:T(8,128)}, u32[]{:S(2)}, u32[]{:S(2)}) collective-permute-start(f32[256,512]{1,0:T(8,128)} %reshape.89), channel_id=1, source_target_pairs={{0,1},{1,0},{2,3},{3,2},{4,5},{5,4},{6,7},{7,6},{8,9},{9,8},{10,11... | collective-permute-start | bytes 1572872 | tf_op jit(solution)/shard_map/ppermute | solution.py:24
  159.3 4.3 %convolution_multiply_fusion = f32[512,512]{1,0:T(8,128)} fusion(f32[512,512]{1,0:T(8,128)} %fusion.4, f32[512]{0:T(512)S(1)} %bitcast.51, s32[512]{0:T(512)S(1)} %bitcast.39, f32[512]{0:T(512)S(1)} %bitcast.53, s32[512]{0:T(512)S(1)} %bitcast.41, f32[512]{0:T(512)S(1)} %bitcast.55, s32[512]{0:T(512)S(1)} %bitcast.43, f32[512]{0:T(512)S(1)} %bitcast.57, ...), kind=kOutput, calls=%fused_computation.11 | convolution fusion | flops 810024960 | bytes 2121728 | tf_op jit(solution)/shard_map/dot_general | solution.py:16
  163.6 0.0 collective-permute-done.3
  163.6 0.0 copy-done.2
  163.6 1.5 broadcast_select_fusion.3
  165.0 8.3 %scatter_custom_fusion = f32[1280,512]{1,0:T(8,128)} fusion(f32[1280,512]{1,0:T(8,128)} %copy.17, s32[1024]{0:T(1024)S(1)} %bitcast.37, f32[512,512]{1,0:T(8,128)S(1)} %get-tuple-element.6, f32[]{:T(128)} %constant.53, f32[512,512]{1,0:T(8,128)S(1)} %get-tuple-element.5), kind=kCustom, calls=%fused_computation.4 | custom fusion | flops 524288 | bytes 4719104 | tf_op jit(solution)/shard_map/scatter | solution.py:81
  173.3 0.0 collective-permute-done.2
  173.3 1.3 broadcast_select_fusion.5
  174.7 1.0 pad_maximum_fusion.2
  (8 shorter events, 0.1 us)
Async XLA Ops:
  0.6 70.3 %copy-start = (f32[512,512]{1,0:T(8,128)S(1)}, f32[512,512]{1,0:T(8,128)}, u32[]{:S(2)}) copy-start(f32[512,512]{1,0:T(8,128)} %param.13) | copy-start | bytes 3145732
  0.6 6.8 %copy-start.8 = (s32[1,128,2]{1,2,0:T(2,128)S(1)}, s32[1,128,2]{1,2,0:T(2,128)}, u32[]{:S(2)}) copy-start(s32[1,128,2]{1,2,0:T(2,128)} %param.16) | copy-start | bytes 3076
  4.2 55.5 %collective-permute-start = (f32[1024,512]{1,0:T(8,128)}, f32[1024,512]{1,0:T(8,128)}, u32[]{:S(2)}, u32[]{:S(2)}) collective-permute-start(f32[1024,512]{1,0:T(8,128)} %param.18), channel_id=1, source_target_pairs={{0,1},{1,0},{2,3},{3,2},{4,5},{5,4},{6,7},{7,6},{8,9},{9,8},{10,11... | collective-permute-start | bytes 6291464 | tf_op jit(solution)/shard_map/ppermute | solution.py:24
  34.8 7.5 %copy-start.5 = (s32[512,8]{0,1:T(8,128)S(1)}, s32[512,8]{0,1:T(8,128)}, u32[]{:S(2)}) copy-start(s32[512,8]{0,1:T(8,128)} %param.15) | copy-start | bytes 49156
  34.8 7.5 %copy-start.6 = (f32[512,8]{0,1:T(8,128)S(1)}, f32[512,8]{0,1:T(8,128)}, u32[]{:S(2)}) copy-start(f32[512,8]{0,1:T(8,128)} %param.14) | copy-start | bytes 49156
  36.0 22.8 %all-to-all-start.1 = ((f32[128,2,512]{2,1,0:T(2,128)}), f32[128,2,512]{2,1,0:T(2,128)S(1)}, u32[]{:S(2)}, u32[]{:S(2)}) async-start(f32[128,2,512]{2,1,0:T(2,128)} %reshape.100), calls=%async_computation.1 | async-start | bytes 1048576 | tf_op jit(solution)/shard_map/all_to_all | solution.py:20
  70.9 1.4 copy-start.9
  72.3 1.7 copy-start.4
  74.0 1.0 copy-start.3
  75.8 5.6 %collective-permute-start.1 = (f32[256,512]{1,0:T(8,128)}, f32[256,512]{1,0:T(8,128)}, u32[]{:S(2)}, u32[]{:S(2)}) collective-permute-start(f32[256,512]{1,0:T(8,128)} %constant_dynamic-slice_fusion), channel_id=1, source_target_pairs={{0,1},{1,0},{2,3},{3,2},{4,5},{5,4},{6,7},{7,6},{8,9},{9,8},{10,11... | collective-permute-start | bytes 1572872 | tf_op jit(solution)/shard_map/ppermute | solution.py:69
  128.8 25.6 %all-to-all-start.3 = ((f32[128,8,128]{2,1,0:T(8,128)}), f32[128,8,128]{2,1,0:T(8,128)S(1)}, u32[]{:S(2)}, u32[]{:S(2)}) async-start(f32[128,8,128]{2,1,0:T(8,128)} %broadcast_in_dim.93), calls=%async_computation.3 | async-start | bytes 1048576 | tf_op jit(solution)/shard_map/all_to_all | solution.py:20
  138.3 4.1 %copy-start.7 = (s32[1,1024]{1,0:T(1,128)S(1)}, s32[1,1024]{1,0:T(1,128)}, u32[]{:S(2)}) copy-start(s32[1,1024]{1,0:T(1,128)} %param.19) | copy-start | bytes 12292
  140.8 7.0 %copy-start.1 = (f32[512,512]{1,0:T(8,128)}, f32[512,512]{1,0:T(8,128)S(1)}, u32[]{:S(2)}) copy-start(f32[512,512]{1,0:T(8,128)S(1)} %reshape.90) | copy-start | bytes 3145732
  140.8 22.8 %collective-permute-start.3 = (f32[512,512]{1,0:T(8,128)S(1)}, f32[512,512]{1,0:T(8,128)}, u32[]{:S(2)}, u32[]{:S(2)}) collective-permute-start(f32[512,512]{1,0:T(8,128)S(1)} %reshape.90), channel_id=1, source_target_pairs={{0,1},{1,0},{2,3},{3,2},{4,5},{5,4},{6,7},{7,6},{8,9},{9,8},{10,11... | collective-permute-start | bytes 3145736 | tf_op jit(solution)/shard_map/ppermute | solution.py:24
  155.3 8.3 %copy-start.2 = (f32[512,512]{1,0:T(8,128)S(1)}, f32[512,512]{1,0:T(8,128)}, u32[]{:S(2)}) copy-start(f32[512,512]{1,0:T(8,128)} %copy-done.1) | copy-start | bytes 3145732
  155.3 18.0 %collective-permute-start.2 = (f32[256,512]{1,0:T(8,128)}, f32[256,512]{1,0:T(8,128)}, u32[]{:S(2)}, u32[]{:S(2)}) collective-permute-start(f32[256,512]{1,0:T(8,128)} %reshape.89), channel_id=1, source_target_pairs={{0,1},{1,0},{2,3},{3,2},{4,5},{5,4},{6,7},{7,6},{8,9},{9,8},{10,11... | collective-permute-start | bytes 1572872 | tf_op jit(solution)/shard_map/ppermute | solution.py:24

commit v2 on v1

v2 whole, which is shorter than its diff:
```python
import math

import jax
import jax.numpy as jnp
from jax import lax
from jax.experimental import pallas as pl
from jax.experimental.pallas import tpu as pltpu
from jax.sharding import PartitionSpec as P

ALPHA = 0.1
BETA = math.log(1.5)
OWN = ("batch", "hist")
SWAP = [(0, 1), (1, 0)]
F32 = jnp.float32
BF16 = jnp.bfloat16
GELU_C = math.sqrt(2.0 / math.pi)
GELU_A = 0.044715
VMEM = pl.BlockSpec(memory_space=pltpu.VMEM)
SMEM = pl.BlockSpec(memory_space=pltpu.SMEM)
MIB = 1 << 20


def dot(a, b, left=1, right=0):
    return lax.dot_general(a, b, (((left,), (right,)), ((), ())), preferred_element_type=F32)


def split(v):
    high = v.astype(BF16)
    return high, (v - high.astype(F32)).astype(BF16)


def dot3(a, b, left=1, right=0):
    return dot(a[0], b[0], left, right) + (dot(a[0], b[1], left, right) + dot(a[1], b[0], left, right))


def lanes(rows, columns):
    return lax.broadcasted_iota(jnp.int32, (rows, columns), 1)


def one_hot(column, count):
    return (column == lanes(column.shape[0], count)).astype(BF16)


def call(kernel, outs, args, scalars=0, scratch=(), limit=16, flops=0, aliases=None):
    count = sum(math.prod(o[0]) for o in outs) * 4 + sum(math.prod(a.shape) for a in args) * 4
    return pl.pallas_call(
        kernel,
        out_shape=[jax.ShapeDtypeStruct(*o) for o in outs],
        in_specs=[SMEM] * scalars + [VMEM] * (len(args) - scalars),
        out_specs=[VMEM] * len(outs),
        scratch_shapes=list(scratch),
        input_output_aliases=aliases or {},
        compiler_params=pltpu.CompilerParams(vmem_limit_bytes=limit * MIB),
        cost_estimate=pl.CostEstimate(flops=flops, bytes_accessed=count, transcendentals=0),
    )(*args)


def gather_kernel(idx_ref, cold_ref, out_ref):
    owners, per = idx_ref.shape
    high, low = split(cold_ref[...])
    pick = jnp.concatenate(
        [one_hot(idx_ref[:, s : s + 1], cold_ref.shape[0]) for s in range(per)], axis=0
    )
    found = dot(pick, high) + dot(pick, low)
    for s in range(per):
        for l in range(4):
            out_ref[pl.ds(s * 4 + l, owners, stride=per * 4), :] = found[
                s * owners : (s + 1) * owners, l * 128 : (l + 1) * 128
            ]


def prepare_kernel(
    core_ref, nbr_ref, ew_ref, node_ref, init_ref, mine_ref, other_ref,
    part_ref, high_ref, low_ref, pick_ref, *, halo_count,
):
    rows = node_ref.shape[0]
    core = core_ref[0]
    nbr = nbr_ref[...]
    ew = ew_ref[...]
    ids = lanes(rows, rows)
    tile = jnp.zeros((rows, rows), F32)
    for k in range(2, nbr.shape[1]):
        tile = tile + jnp.where(nbr[:, k : k + 1] == ids, ew[:, k : k + 1], 0.0)
    tiles = split(tile)
    high_ref[...] = tiles[0]
    low_ref[...] = tiles[1]
    half = mine_ref.shape[0]
    hot = nbr[:, 1:2] - (rows + halo_count)
    picked = jnp.zeros((rows, node_ref.shape[1]), F32)
    for ref, start in ((mine_ref, core * half), (other_ref, (1 - core) * half)):
        choose = one_hot(hot - start, half)
        for part in split(ref[...]):
            picked = picked + dot(choose, part)
    agg = dot3(tiles, split(node_ref[...])) + ew[:, 1:2] * picked
    part_ref[...] = (1.0 - ALPHA) * agg + ALPHA * init_ref[...]
    place = nbr[:, :1] - rows
    pick_ref[...] = one_hot((place & 1) * (halo_count // 2) + (place >> 1), halo_count)


def layer_kernel(
    core_ref, halo_ref, pick_ref, ew_ref, part_ref, weight_ref, cot_ref,
    embed_ref, keep_ref, give_ref, du_ref, term_ref,
):
    owners = halo_ref.shape[0] // 8
    halo = jnp.concatenate(
        [
            jnp.concatenate(
                [halo_ref[pl.ds(s * 4 + l, owners, stride=8), :] for l in range(4)], axis=1
            )
            for s in range(2)
        ],
        axis=0,
    )
    pick = pick_ref[...]
    high, low = split(halo)
    z = part_ref[...] + ((1.0 - ALPHA) * ew_ref[:, :1]) * (dot(pick, high) + dot(pick, low))
    zs = split(z)
    u = (1.0 - BETA) * z + BETA * dot3(zs, split(weight_ref[...]))
    square = u * u
    bent = jnp.tanh(GELU_C * (u + GELU_A * (square * u)))
    embed_ref[...] = (0.5 * u) * (1.0 + bent)
    slope = 0.5 * (1.0 + bent) + (0.5 * u) * (1.0 - bent * bent) * (
        GELU_C * (1.0 + (3.0 * GELU_A) * square)
    )
    du = cot_ref[...] * slope
    du_ref[...] = du
    term_ref[...] = dot3(zs, split(du), 0, 0)
    half = term_ref.shape[0] // 2
    core = core_ref[0]
    keep_ref[...] = term_ref[pl.ds(pl.multiple_of(core * half, half), half), :]
    give_ref[...] = term_ref[pl.ds(pl.multiple_of((1 - core) * half, half), half), :]


def pack_kernel(embed_ref, keep_ref, got_ref, out_ref):
    groups = out_ref.shape[0]
    top = lax.broadcasted_iota(jnp.int32, (groups, 2, 8, 128), 2) < 4
    for pair in range(2):
        x, y = (
            embed_ref[:, l * 128 : (l + 1) * 128].reshape(groups, 2, 8, 128)
            for l in (2 * pair, 2 * pair + 1)
        )
        even = jnp.where(top, x, pltpu.roll(y, 4, 2))
        odd = jnp.where(top, pltpu.roll(x, 4, 2), y)
        for h in range(2):
            out_ref[:, 2 * h, 8 * pair : 8 * pair + 8, :] = even[:, h]
            out_ref[:, 2 * h + 1, 8 * pair : 8 * pair + 8, :] = odd[:, h]
    for l in range(4):
        at = slice(l * 128, (l + 1) * 128)
        out_ref[:, l, 16:24, :] = (keep_ref[:, at] + got_ref[:, at]).reshape(groups, 8, 128)


def backward_kernel(du_ref, weight_ref, high_ref, low_ref, out_ref):
    du = du_ref[...]
    dz = (1.0 - BETA) * du + BETA * dot3(split(du), split(weight_ref[...]), 1, 1)
    out_ref[...] = (1.0 - ALPHA) * dot3((high_ref[...], low_ref[...]), split(dz), 0, 0)


def sum_kernel(arrived_ref, piece_ref, recv_ref, *, scale):
    piece = jnp.sum(arrived_ref[:, 16:24, :], axis=0) * scale
    piece_ref[...] = jnp.broadcast_to(piece[None], piece_ref.shape)
    recv_ref[...] = arrived_ref[:, :16, :]


def history_kernel(core_ref, dest_ref, mine_ref, other_ref, cold_ref, out_ref, high_ref, low_ref):
    core = core_ref[0]
    owners = mine_ref.shape[0] // 16
    rows = 4 * owners
    for r, ref in enumerate((mine_ref, other_ref)):
        for s in range(4):
            for l in range(4):
                high, low = split(ref[pl.ds(4 * l + s, owners, stride=16), :])
                at = pl.ds(r * rows + s * owners, owners)
                high_ref[at, l * 128 : (l + 1) * 128] = high
                low_ref[at, l * 128 : (l + 1) * 128] = low
    dest = jnp.concatenate(
        [dest_ref[pl.ds(core, 1), :], dest_ref[pl.ds(1 - core, 1), :]], axis=1
    )
    step = 256
    for start in range(0, cold_ref.shape[0], step):
        ids = lax.broadcasted_iota(jnp.int32, (step, 2 * rows), 0) + start
        hit = jnp.where(ids == dest, 1.0, 0.0)
        count = jnp.sum(hit, axis=1, keepdims=True)
        place = hit.astype(BF16)
        written = dot(place, high_ref[...]) + dot(place, low_ref[...])
        at = pl.ds(start, step)
        out_ref[at, :] = jnp.where(count > 0.5, written, cold_ref[at, :])


def assemble_kernel(core_ref, mine_ref, other_ref, out_ref):
    core = core_ref[0]
    half = out_ref.shape[0] // 2
    for ref, which in ((mine_ref, core), (other_ref, 1 - core)):
        at = pl.ds(pl.multiple_of(which * half, half), half)
        for l in range(4):
            out_ref[at, l * 128 : (l + 1) * 128] = ref[:, l].reshape(half, 128)


def exchange(v):
    return lax.all_to_all(v, OWN, split_axis=0, concat_axis=0, tiled=True)


def swap(v):
    return lax.ppermute(v, "rep", SWAP)


def body(
    node_input,
    initial,
    cotangent,
    weight,
    edge_weight,
    neighbors,
    halo_rows,
    cold_history,
    hot_history,
    dest_rows,
):
    rows, width = node_input.shape
    owners = lax.axis_size(OWN)
    halo_count = owners * halo_rows.shape[2]
    core = lax.axis_index("rep").astype(jnp.int32).reshape(1)
    full = (rows, width)
    wanted = exchange(halo_rows[0])
    part, high, low, pick = call(
        lambda *r: prepare_kernel(*r, halo_count=halo_count),
        [(full, F32), ((rows, rows), BF16), ((rows, rows), BF16), ((rows, halo_count), BF16)],
        (core, neighbors, edge_weight, node_input, initial, hot_history, swap(hot_history)),
        scalars=1,
        flops=6 * 10**9,
    )
    wanted, part = lax.optimization_barrier((wanted, part))
    (found,) = call(
        gather_kernel,
        [((halo_count * 4, 128), F32)],
        (wanted, cold_history),
        flops=10**9,
    )
    halo = exchange(found)
    half = (rows // 2, width)
    embed, keep, give, du = call(
        layer_kernel,
        [(full, F32), (half, F32), (half, F32), (full, F32)],
        (core, halo, pick, edge_weight, part, weight, cotangent),
        scalars=1,
        scratch=[pltpu.VMEM((width, width), F32)],
        flops=2 * 10**9,
    )
    (outgoing,) = call(
        pack_kernel, [((owners // 4, 4, 24, 128), F32)], (embed, keep, swap(give))
    )
    arrived = exchange(outgoing.reshape(owners * 24, 128)).reshape(owners, 24, 128)
    (grad_input,) = call(
        backward_kernel, [(full, F32)], (du, weight, high, low), flops=2 * 10**9
    )
    arrived, grad_input = lax.optimization_barrier((arrived, grad_input))
    all_nodes = rows * lax.axis_size(("batch", "hist", "rep"))
    piece, recv = call(
        lambda *r: sum_kernel(*r, scale=BETA / math.sqrt(all_nodes)),
        [((owners, 8, 128), F32), ((owners, 16, 128), F32)],
        (arrived,),
    )
    pieces = exchange(piece.reshape(owners * 8, 128))
    recv = recv.reshape(owners * 16, 128)
    dest = jnp.transpose(dest_rows.reshape(2, owners, 4), (0, 2, 1)).reshape(2, rows)
    (new_history,) = call(
        history_kernel,
        [(cold_history.shape, F32)],
        (core, dest, recv, swap(recv), cold_history),
        scalars=1,
        scratch=[pltpu.VMEM((2 * rows, width), BF16), pltpu.VMEM((2 * rows, width), BF16)],
        flops=4 * 10**9,
    )
    pieces, new_history = lax.optimization_barrier((pieces, new_history))
    shape = (owners // 4, 4, 8, 128)
    (grad_weight,) = call(
        assemble_kernel,
        [((width, width), F32)],
        (core, pieces.reshape(shape), swap(pieces).reshape(shape)),
        scalars=1,
    )
    return (grad_weight, grad_input, new_history)


def solution(mesh):
    return jax.shard_map(
        body,
        mesh=mesh,
        in_specs=(
            P(("batch", "hist", "rep"), None),
            P(("batch", "hist", "rep"), None),
            P(("batch", "hist", "rep"), None),
            P(),
            P(("batch", "hist", "rep"), None),
            P(("batch", "hist", "rep"), None),
            P(("batch", "hist", "rep"), None, None),
            P(("batch", "hist"), None),
            P("rep", None),
            P(("batch", "hist"), None),
        ),
        out_specs=(P(), P(("batch", "hist", "rep"), None), P(("batch", "hist"), None)),
        check_vma=False,
    )
```

time: 176 us -> 155 us (0.88)
  blocking collectives: 69.2 us -> 30 us
  waiting for transfers between devices: 20.6 us -> 45.9 us
  other arithmetic: 20.6 us -> 0.66 us
  Pallas kernels: 0 us -> 19.5 us
  matrix products: 17.5 us -> 0 us
  starting transfers between devices: 28.4 us -> 39.8 us
    all_to_all x2 -> x1, blocking collectives: 69.2 us -> 30 us  [exchange(): return lax.all_to_all(v, OWN, split_axis=0, concat_axis=0, tiled=True)]
    all_to_all x2 -> x3, waiting for transfers between devices: 18.8 us -> 42.8 us  [exchange(): return lax.all_to_all(v, OWN, split_axis=0, concat_axis=0, tiled=True)]
    pallas_call x0 -> x8, Pallas kernels: none -> 19.5 us  [call(): pl.pallas_call(kernel, out_shape=[jax.ShapeDtypeStruct(*o) for o in outs]...]
    dot_general x6 -> x0, matrix products: 17.5 us -> none  [dot(): lax.dot_general(a, b, dims, precision=HIGH, preferred_element_type=jnp.fl...]
    unnamed x22 -> x43, local copies, waits for them, and re-layouts: 4.69 us -> 17.1 us
    all_to_all x2 -> x3, starting transfers between devices: 15.9 us -> 27.8 us  [exchange(): return lax.all_to_all(v, OWN, split_axis=0, concat_axis=0, tiled=True)]
    scatter x1 -> x0, other arithmetic: 8.3 us -> none  [body(): cold_history.at[dest_rows[0]].set(received, unique_indices=True)]
    gather x3 -> x0, local copies, waits for them, and re-layouts: 8.26 us -> none  [the longest x1 4.21 us: body(): hot_rows = hot[neighbors[:, 1] - local_rows - halo_count]]
  transfers between devices with their start and end apart: 6 -> 7, of which waited for: 3 -> 4; matrix products, arithmetic and copies ran while one was open for 18% -> 3% of each run, Pallas kernels for 0% -> 8%
where the time goes in v2:
time: 155 us; the launch traced here: 154 us
  waiting for transfers between devices  45.9 us (30%)
  starting transfers between devices  39.8 us (26%)
  blocking collectives  30 us (19%)
  Pallas kernels  19.5 us (13%)
  local copies, waits for them, and re-layouts  17.4 us (11%)
    all_to_all x3, waiting for transfers between devices, exchange(): return lax.all_to_all(v, OWN, split_axis=0, concat_axis=0, tiled=True)  42.8 us
    all_to_all x1, blocking collectives, exchange(): return lax.all_to_all(v, OWN, split_axis=0, concat_axis=0, tiled=True)  30 us
    all_to_all x3, starting transfers between devices, exchange(): return lax.all_to_all(v, OWN, split_axis=0, concat_axis=0, tiled=True)  27.8 us
    pallas_call x8, Pallas kernels, call(): pl.pallas_call(kernel, out_shape=[jax.ShapeDtypeStruct(*o) for o in outs]...  19.5 us
    unnamed x43, local copies, waits for them, and re-layouts  17.1 us
    ppermute x4, starting transfers between devices, swap(): return lax.ppermute(v, 'rep', SWAP)  12 us
  transfers between devices with their start and end apart: 7, of which 4 were waited for; matrix products, arithmetic and copies ran while one was open for 3% of the time, Pallas kernels for 8%

profile of v2, /device:TPU:1, one launch (start us, length us, event | category | flops | bytes accessed | tf_op | source)
XLA Modules:
  0.0 154.1 jit_solution(5847999628445748875)
XLA Ops:
  0.6 3.3 %collective-permute-start = (f32[1024,512]{1,0:T(8,128)}, f32[1024,512]{1,0:T(8,128)S(1)}, u32[]{:S(2)}, u32[]{:S(2)}) collective-permute-start(f32[1024,512]{1,0:T(8,128)} %r_5_.1), channel_id=1, source_target_pairs={{0,1},{1,0},{2,3},{3,2},{4,5},{5,4},{6,7},{7,6},{8,9},{9,8},{10,11... | collective-permute-start | bytes 6291464 | tf_op jit(solution)/shard_map/ppermute | solution.py:203
  4.0 1.4 copy.23
  5.4 13.8 %all-to-all-start = ((s32[128,1,2]{2,1,0:T(1,128)}), s32[128,1,2]{2,1,0:T(1,128)S(1)}, u32[]{:S(2)}, u32[]{:S(2)}) async-start(s32[128,1,2]{2,1,0:T(1,128)} %bitcast.1), calls=%async_computation | async-start | bytes 131072 | tf_op jit(solution)/shard_map/all_to_all | solution.py:199
  19.1 0.8 copy.25.r_2_.ew_ref
  20.0 0.8 copy.24.r_1_
  20.8 0.0 collective-permute-done.r_6_
  20.8 0.0 copy-start.3
  20.9 1.3 copy-done.3
  22.2 0.0 copy-start.2
  22.2 1.6 %copy-done.2 = f32[1024,512]{1,0:T(8,128)S(1)} copy-done((f32[1024,512]{1,0:T(8,128)S(1)}, f32[1024,512]{1,0:T(8,128)}, u32[]{:S(2)}) %copy-start.2) | copy-done | bytes 2097176
  23.8 0.0 copy-start.4
  23.8 1.6 %copy-done.4 = f32[1024,512]{1,0:T(8,128)S(1)} copy-done((f32[1024,512]{1,0:T(8,128)S(1)}, f32[1024,512]{1,0:T(8,128)}, u32[]{:S(2)}) %copy-start.4) | copy-done | bytes 2097176
  25.4 0.0 copy-start.5
  25.4 1.2 copy-done.5
  26.6 0.0 copy-start.6
  26.6 1.2 copy-done.6
  27.8 0.0 copy-start
  27.8 4.0 %shard_map.121 = (f32[512,512]{1,0:T(8,128)S(1)}, bf16[512,512]{1,0:T(8,128)(2,1)S(1)}, bf16[512,512]{1,0:T(8,128)(2,1)S(1)}, bf16[512,256]{1,0:T(8,128)(2,1)S(1)}) custom-call(s32[1]{0:T(128)} %bitcast.r_0_.core_ref, s32[512,8]{1,0:T(8,128)S(1)} %copy.24.r_1_, f32[512,8]{1,0:T(8,128)S(1)} %copy.25.r_2_.ew_ref, f32[512,512]{1,0:T(8,128)S(1)} %copy-done.5, ...), custom_call_target="tpu_custom_call" | custom-call | flops 6000000000 | bytes 9994244 | tf_op jit(solution)/shard_map/pallas_call | solution.py:46
  31.8 0.0 copy-start.12
  31.8 1.0 copy-done.12
  32.8 0.0 copy-start.14
  32.8 0.8 copy-done.14
  33.6 0.0 copy-start.16
  33.6 0.8 copy-done.16
  34.4 0.0 all-to-all-done
  34.4 0.0 copy-done
  34.4 0.0 copy-start.7
  34.4 0.0 copy-start.8
  34.4 0.0 copy-start.13
  34.4 0.9 shard_map.122
  35.4 30.0 %all_to_all.41 = f32[128,8,128]{2,1,0:T(8,128)S(1)} all-to-all(f32[128,8,128]{2,1,0:T(8,128)S(1)} %bitcast.19), channel_id=1, replica_groups=mesh['batch'=32,'hist'=4,'rep'=2] {'batch','hist'}, dimensions={0} | all-to-all | bytes 1048576 | tf_op jit(solution)/shard_map/all_to_all | solution.py:199
  65.4 0.0 copy-done.7
  65.4 0.0 copy-done.8
  65.4 0.0 copy-done.13
  65.4 3.1 %shard_map.123 = (f32[512,512]{1,0:T(8,128)S(1)}, f32[256,512]{1,0:T(8,128)S(1)}, f32[256,512]{1,0:T(8,128)S(1)}, f32[512,512]{1,0:T(8,128)S(1)}) custom-call(s32[1]{0:T(128)} %bitcast.r_0_.core_ref, f32[1024,128]{1,0:T(8,128)S(1)} %bitcast.18, bf16[512,256]{1,0:T(8,128)(2,1)S(1)} %get-tuple-element.21.pick_ref, f32[512,8]{1,0:T(8,128)S(1)} %copy.25.r_2_.ew_ref, ...), custom_call_target="tpu_custom_call" | custom-call | flops 2000000000 | bytes 7356420 | tf_op jit(solution)/shard_map/pallas_call | solution.py:46
  68.5 0.0 copy-start.10
  68.5 3.6 %collective-permute-start.1 = (f32[256,512]{1,0:T(8,128)S(1)}, f32[256,512]{1,0:T(8,128)S(1)}, u32[]{:S(2)}, u32[]{:S(2)}) collective-permute-start(f32[256,512]{1,0:T(8,128)S(1)} %get-tuple-element.25), channel_id=1, source_target_pairs={{0,1},{1,0},{2,3},{3,2},{4,5},{5,4},{6,7},{7,6},{8,9},{9,8},{10,11... | collective-permute-start | bytes 1572872 | tf_op jit(solution)/shard_map/ppermute | solution.py:203
  72.2 1.5 collective-permute-done.1.got_ref
  73.7 1.4 shard_map.124
  75.1 0.0 copy-done.10
  75.1 6.8 %all-to-all-start.2 = ((f32[128,24,128]{2,1,0:T(8,128)}), f32[128,24,128]{2,1,0:T(8,128)S(1)}, u32[]{:S(2)}, u32[]{:S(2)}) async-start(f32[128,24,128]{2,1,0:T(8,128)} %bitcast.5), calls=%async_computation.2 | async-start | bytes 3145728 | tf_op jit(solution)/shard_map/all_to_all | solution.py:199
  81.9 0.0 copy-done.9
  81.9 0.0 copy-done.15
  81.9 0.0 copy-start.11
  81.9 1.2 copy-done.11
  83.1 1.0 copy-done.17
  84.2 2.9 %shard_map.125 = f32[512,512]{1,0:T(8,128)} custom-call(f32[512,512]{1,0:T(8,128)S(1)} %copy-done.11, f32[512,512]{1,0:T(8,128)S(1)} %copy-done.9, bf16[512,512]{1,0:T(8,128)(2,1)S(1)} %copy-done.15, bf16[512,512]{1,0:T(8,128)(2,1)S(1)} %copy-done.17), custom_call_target="tpu_custom_call" | custom-call | flops 2000000000 | bytes 5242880 | tf_op jit(solution)/shard_map/pallas_call | solution.py:46
  87.1 33.3 %all-to-all-done.2.r_0_ = f32[128,24,128]{2,1,0:T(8,128)S(1)} async-done(((f32[128,24,128]{2,1,0:T(8,128)}), f32[128,24,128]{2,1,0:T(8,128)S(1)}, u32[]{:S(2)}, u32[]{:S(2)}) %all-to-all-start.2) | async-done | bytes 1572896 | tf_op jit(solution)/shard_map/all_to_all | solution.py:199
  120.4 1.0 shard_map.126
  121.4 3.2 %collective-permute-start.2 = (f32[2048,128]{1,0:T(8,128)S(1)}, f32[2048,128]{1,0:T(8,128)S(1)}, u32[]{:S(2)}, u32[]{:S(2)}) collective-permute-start(f32[2048,128]{1,0:T(8,128)S(1)} %bitcast.22), channel_id=1, source_target_pairs={{0,1},{1,0},{2,3},{3,2},{4,5},{5,4},{6,7},{7,6},{8,9},{9,8},{10,11... | collective-permute-start | bytes 3145736 | tf_op jit(solution)/shard_map/ppermute | solution.py:203
  124.6 7.3 %all-to-all-start.3 = ((f32[128,8,128]{2,1,0:T(8,128)}), f32[128,8,128]{2,1,0:T(8,128)S(1)}, u32[]{:S(2)}, u32[]{:S(2)}) async-start(f32[128,8,128]{2,1,0:T(8,128)} %get-tuple-element.30), calls=%async_computation.3 | async-start | bytes 1048576 | tf_op jit(solution)/shard_map/all_to_all | solution.py:199
  131.9 0.5 broadcast.3
  132.4 0.0 copy-done.18
  132.4 0.7 reduce.3
  133.1 0.1 reshape.40
  133.2 0.1 copy.27
  133.3 0.0 collective-permute-done.2.other_ref
  133.3 0.0 copy-start.1
  133.3 1.7 %copy-done.1 = f32[1280,512]{1,0:T(8,128)S(1)} copy-done((f32[1280,512]{1,0:T(8,128)S(1)}, f32[1280,512]{1,0:T(8,128)}, u32[]{:S(2)}) %copy-start.1) | copy-done | bytes 2621464
  135.1 5.2 %shard_map.127 = f32[1280,512]{1,0:T(8,128)} custom-call(s32[1]{0:T(128)} %bitcast.r_0_.core_ref, s32[2,512]{1,0:T(2,128)S(1)} %bitcast.21, f32[2048,128]{1,0:T(8,128)S(1)} %bitcast.23, f32[2048,128]{1,0:T(8,128)S(1)} %collective-permute-done.2.other_ref, f32[1280,512]{1,0:T(8,128)S(1)} %copy-done.1), custom_call_target="tpu_custom_call" | custom-call | flops 4000000000 | bytes 7344132 | tf_op jit(solution)/shard_map/pallas_call | solution.py:46
  140.2 9.5 %all-to-all-done.3 = f32[128,8,128]{2,1,0:T(8,128)S(1)} async-done(((f32[128,8,128]{2,1,0:T(8,128)}), f32[128,8,128]{2,1,0:T(8,128)S(1)}, u32[]{:S(2)}, u32[]{:S(2)}) %all-to-all-start.3) | async-done | bytes 524320 | tf_op jit(solution)/shard_map/all_to_all | solution.py:199
  149.7 1.8 %collective-permute-start.3 = (f32[1024,128]{1,0:T(8,128)S(1)}, f32[1024,128]{1,0:T(8,128)S(1)}, u32[]{:S(2)}, u32[]{:S(2)}) collective-permute-start(f32[1024,128]{1,0:T(8,128)S(1)} %bitcast.15), channel_id=1, source_target_pairs={{0,1},{1,0},{2,3},{3,2},{4,5},{5,4},{6,7},{7,6},{8,9},{9,8},{10,11... | collective-permute-start | bytes 1572872 | tf_op jit(solution)/shard_map/ppermute | solution.py:203
  151.5 1.5 collective-permute-done.3
  153.1 1.0 shard_map.128
  (5 shorter events, 0.0 us)
Async XLA Ops:
  0.6 20.2 %collective-permute-start = (f32[1024,512]{1,0:T(8,128)}, f32[1024,512]{1,0:T(8,128)S(1)}, u32[]{:S(2)}, u32[]{:S(2)}) collective-permute-start(f32[1024,512]{1,0:T(8,128)} %r_5_.1), channel_id=1, source_target_pairs={{0,1},{1,0},{2,3},{3,2},{4,5},{5,4},{6,7},{7,6},{8,9},{9,8},{10,11... | collective-permute-start | bytes 6291464 | tf_op jit(solution)/shard_map/ppermute | solution.py:203
  5.4 29.1 %all-to-all-start = ((s32[128,1,2]{2,1,0:T(1,128)}), s32[128,1,2]{2,1,0:T(1,128)S(1)}, u32[]{:S(2)}, u32[]{:S(2)}) async-start(s32[128,1,2]{2,1,0:T(1,128)} %bitcast.1), calls=%async_computation | async-start | bytes 131072 | tf_op jit(solution)/shard_map/all_to_all | solution.py:199
  20.8 1.3 copy-start.3
  22.2 1.6 %copy-start.2 = (f32[1024,512]{1,0:T(8,128)S(1)}, f32[1024,512]{1,0:T(8,128)}, u32[]{:S(2)}) copy-start(f32[1024,512]{1,0:T(8,128)} %r_5_.1) | copy-start | bytes 6291460
  23.8 1.6 %copy-start.4 = (f32[1024,512]{1,0:T(8,128)S(1)}, f32[1024,512]{1,0:T(8,128)}, u32[]{:S(2)}) copy-start(f32[1024,512]{1,0:T(8,128)} %copy-done.3) | copy-start | bytes 6291460
  25.4 1.2 copy-start.5
  26.6 1.2 copy-start.6
  27.8 6.6 %copy-start = (f32[1280,512]{1,0:T(8,128)S(1)}, f32[1280,512]{1,0:T(8,128)}, u32[]{:S(2)}) copy-start(f32[1280,512]{1,0:T(8,128)} %cold_ref.3) | copy-start | bytes 7864324
  31.8 1.0 copy-start.12
  32.8 0.8 copy-start.14
  33.6 0.8 copy-start.16
  34.4 31.0 %copy-start.7 = (f32[512,512]{1,0:T(8,128)S(1)}, f32[512,512]{1,0:T(8,128)}, u32[]{:S(2)}) copy-start(f32[512,512]{1,0:T(8,128)} %cot_ref.1) | copy-start | bytes 3145732
  34.4 31.0 %copy-start.8 = (f32[512,512]{1,0:T(8,128)S(1)}, f32[512,512]{1,0:T(8,128)}, u32[]{:S(2)}) copy-start(f32[512,512]{1,0:T(8,128)} %weight_ref.3) | copy-start | bytes 3145732
  34.4 31.0 %copy-start.13 = (f32[512,512]{1,0:T(8,128)S(1)}, f32[512,512]{1,0:T(8,128)}, u32[]{:S(2)}) copy-start(f32[512,512]{1,0:T(8,128)} %copy-done.12) | copy-start | bytes 3145732
  68.5 6.6 %copy-start.10 = (f32[512,512]{1,0:T(8,128)}, f32[512,512]{1,0:T(8,128)S(1)}, u32[]{:S(2)}) copy-start(f32[512,512]{1,0:T(8,128)S(1)} %get-tuple-element.26.du_ref) | copy-start | bytes 3145732
  68.5 5.2 %collective-permute-start.1 = (f32[256,512]{1,0:T(8,128)S(1)}, f32[256,512]{1,0:T(8,128)S(1)}, u32[]{:S(2)}, u32[]{:S(2)}) collective-permute-start(f32[256,512]{1,0:T(8,128)S(1)} %get-tuple-element.25), channel_id=1, source_target_pairs={{0,1},{1,0},{2,3},{3,2},{4,5},{5,4},{6,7},{7,6},{8,9},{9,8},{10,11... | collective-permute-start | bytes 1572872 | tf_op jit(solution)/shard_map/ppermute | solution.py:203
  75.1 6.8 %copy-start.9 = (f32[512,512]{1,0:T(8,128)S(1)}, f32[512,512]{1,0:T(8,128)}, u32[]{:S(2)}) copy-start(f32[512,512]{1,0:T(8,128)} %weight_ref.3) | copy-start | bytes 3145732
  75.1 6.8 %copy-start.15 = (bf16[512,512]{1,0:T(8,128)(2,1)S(1)}, bf16[512,512]{1,0:T(8,128)(2,1)}, u32[]{:S(2)}) copy-start(bf16[512,512]{1,0:T(8,128)(2,1)} %copy-done.14) | copy-start | bytes 1572868
  75.1 45.3 %all-to-all-start.2 = ((f32[128,24,128]{2,1,0:T(8,128)}), f32[128,24,128]{2,1,0:T(8,128)S(1)}, u32[]{:S(2)}, u32[]{:S(2)}) async-start(f32[128,24,128]{2,1,0:T(8,128)} %bitcast.5), calls=%async_computation.2 | async-start | bytes 3145728 | tf_op jit(solution)/shard_map/all_to_all | solution.py:199
  81.9 1.2 copy-start.11
  83.1 1.0 copy-start.17
  87.1 45.3 %copy-start.18 = (s32[1,1024]{1,0:T(1,128)S(1)}, s32[1,1024]{1,0:T(1,128)}, u32[]{:S(2)}) copy-start(s32[1,1024]{1,0:T(1,128)} %param.19) | copy-start | bytes 12292
  121.4 12.0 %collective-permute-start.2 = (f32[2048,128]{1,0:T(8,128)S(1)}, f32[2048,128]{1,0:T(8,128)S(1)}, u32[]{:S(2)}, u32[]{:S(2)}) collective-permute-start(f32[2048,128]{1,0:T(8,128)S(1)} %bitcast.22), channel_id=1, source_target_pairs={{0,1},{1,0},{2,3},{3,2},{4,5},{5,4},{6,7},{7,6},{8,9},{9,8},{10,11... | collective-permute-start | bytes 3145736 | tf_op jit(solution)/shard_map/ppermute | solution.py:203
  124.6 25.2 %all-to-all-start.3 = ((f32[128,8,128]{2,1,0:T(8,128)}), f32[128,8,128]{2,1,0:T(8,128)S(1)}, u32[]{:S(2)}, u32[]{:S(2)}) async-start(f32[128,8,128]{2,1,0:T(8,128)} %get-tuple-element.30), calls=%async_computation.3 | async-start | bytes 1048576 | tf_op jit(solution)/shard_map/all_to_all | solution.py:199
  133.3 1.8 %copy-start.1 = (f32[1280,512]{1,0:T(8,128)S(1)}, f32[1280,512]{1,0:T(8,128)}, u32[]{:S(2)}) copy-start(f32[1280,512]{1,0:T(8,128)} %cold_ref.3) | copy-start | bytes 7864324
  149.7 3.3 %collective-permute-start.3 = (f32[1024,128]{1,0:T(8,128)S(1)}, f32[1024,128]{1,0:T(8,128)S(1)}, u32[]{:S(2)}, u32[]{:S(2)}) collective-permute-start(f32[1024,128]{1,0:T(8,128)S(1)} %bitcast.15), channel_id=1, source_target_pairs={{0,1},{1,0},{2,3},{3,2},{4,5},{5,4},{6,7},{7,6},{8,9},{9,8},{10,11... | collective-permute-start | bytes 1572872 | tf_op jit(solution)/shard_map/ppermute | solution.py:203

commit v3 on v2

--- a/solution.py
+++ b/solution.py
@@ -1,3 +1,4 @@
+import functools
 import math
 
 import jax
@@ -10,7 +11,6 @@
 ALPHA = 0.1
 BETA = math.log(1.5)
 OWN = ("batch", "hist")
-SWAP = [(0, 1), (1, 0)]
 F32 = jnp.float32
 BF16 = jnp.bfloat16
 GELU_C = math.sqrt(2.0 / math.pi)
@@ -41,7 +41,7 @@
     return (column == lanes(column.shape[0], count)).astype(BF16)
 
 
-def call(kernel, outs, args, scalars=0, scratch=(), limit=16, flops=0, aliases=None):
+def call(kernel, outs, args, scalars=0, scratch=(), limit=8, flops=0, aliases=None):
     count = sum(math.prod(o[0]) for o in outs) * 4 + sum(math.prod(a.shape) for a in args) * 4
     return pl.pallas_call(
         kernel,
@@ -98,8 +98,7 @@
 
 
 def layer_kernel(
-    core_ref, halo_ref, pick_ref, ew_ref, part_ref, weight_ref, cot_ref,
-    embed_ref, keep_ref, give_ref, du_ref, term_ref,
+    halo_ref, pick_ref, ew_ref, part_ref, weight_ref, out_ref, high_ref, low_ref, u_ref
 ):
     owners = halo_ref.shape[0] // 8
     halo = jnp.concatenate(
@@ -115,28 +114,16 @@
     high, low = split(halo)
     z = part_ref[...] + ((1.0 - ALPHA) * ew_ref[:, :1]) * (dot(pick, high) + dot(pick, low))
     zs = split(z)
+    high_ref[...] = zs[0]
+    low_ref[...] = zs[1]
     u = (1.0 - BETA) * z + BETA * dot3(zs, split(weight_ref[...]))
-    square = u * u
-    bent = jnp.tanh(GELU_C * (u + GELU_A * (square * u)))
-    embed_ref[...] = (0.5 * u) * (1.0 + bent)
-    slope = 0.5 * (1.0 + bent) + (0.5 * u) * (1.0 - bent * bent) * (
-        GELU_C * (1.0 + (3.0 * GELU_A) * square)
-    )
-    du = cot_ref[...] * slope
-    du_ref[...] = du
-    term_ref[...] = dot3(zs, split(du), 0, 0)
-    half = term_ref.shape[0] // 2
-    core = core_ref[0]
-    keep_ref[...] = term_ref[pl.ds(pl.multiple_of(core * half, half), half), :]
-    give_ref[...] = term_ref[pl.ds(pl.multiple_of((1 - core) * half, half), half), :]
-
-
-def pack_kernel(embed_ref, keep_ref, got_ref, out_ref):
+    u_ref[...] = u
+    embed = (0.5 * u) * (1.0 + jnp.tanh(GELU_C * (u + GELU_A * (u * u * u))))
     groups = out_ref.shape[0]
     top = lax.broadcasted_iota(jnp.int32, (groups, 2, 8, 128), 2) < 4
     for pair in range(2):
         x, y = (
-            embed_ref[:, l * 128 : (l + 1) * 128].reshape(groups, 2, 8, 128)
+            embed[:, l * 128 : (l + 1) * 128].reshape(groups, 2, 8, 128)
             for l in (2 * pair, 2 * pair + 1)
         )
         even = jnp.where(top, x, pltpu.roll(y, 4, 2))
@@ -144,21 +131,54 @@
         for h in range(2):
             out_ref[:, 2 * h, 8 * pair : 8 * pair + 8, :] = even[:, h]
             out_ref[:, 2 * h + 1, 8 * pair : 8 * pair + 8, :] = odd[:, h]
-    for l in range(4):
-        at = slice(l * 128, (l + 1) * 128)
-        out_ref[:, l, 16:24, :] = (keep_ref[:, at] + got_ref[:, at]).reshape(groups, 8, 128)
+
+
+def weight_kernel(
+    core_ref, u_ref, high_ref, low_ref, cot_ref, keep_ref, give_ref, du_ref, term_ref
+):
+    u = u_ref[...]
+    square = u * u
+    bent = jnp.tanh(GELU_C * (u + GELU_A * (square * u)))
+    slope = 0.5 * (1.0 + bent) + (0.5 * u) * (1.0 - bent * bent) * (
+        GELU_C * (1.0 + (3.0 * GELU_A) * square)
+    )
+    du = cot_ref[...] * slope
+    du_ref[...] = du
+    term_ref[...] = dot3((high_ref[...], low_ref[...]), split(du), 0, 0)
+    half = term_ref.shape[0] // 2
+    core = core_ref[0]
+    keep_ref[...] = term_ref[pl.ds(pl.multiple_of(core * half, half), half), :]
+    give_ref[...] = term_ref[pl.ds(pl.multiple_of((1 - core) * half, half), half), :]
+
+
+def scatter_kernel(me_ref, *refs):
+    terms, outs, total_ref = refs[: -1 - 4], refs[-1 - 4 : -1], refs[-1]
+    total_ref[...] = functools.reduce(lambda x, y: x + y, [t[...] for t in terms])
+    size = outs[0].shape[0]
+    for shift, out in enumerate(outs):
+        at = jnp.bitwise_xor(me_ref[0], shift) * size
+        out[...] = total_ref[pl.ds(pl.multiple_of(at, size), size), :]
+
+
+def total_kernel(*refs):
+    terms = [t[...] for t in refs[:-1]]
+    while len(terms) > 1:
+        terms = [x + y for x, y in zip(terms[::2], terms[1::2])]
+    refs[-1][...] = terms[0]
+
+
+def join_kernel(me_ref, *refs, scale=None):
+    size = refs[0].shape[0]
+    for shift, part in enumerate(refs[:-1]):
+        at = jnp.bitwise_xor(me_ref[0], shift) * size
+        value = part[...] if scale is None else part[...] * scale
+        refs[-1][pl.ds(pl.multiple_of(at, size), size), :] = value
 
 
 def backward_kernel(du_ref, weight_ref, high_ref, low_ref, out_ref):
     du = du_ref[...]
     dz = (1.0 - BETA) * du + BETA * dot3(split(du), split(weight_ref[...]), 1, 1)
     out_ref[...] = (1.0 - ALPHA) * dot3((high_ref[...], low_ref[...]), split(dz), 0, 0)
-
-
-def sum_kernel(arrived_ref, piece_ref, recv_ref, *, scale):
-    piece = jnp.sum(arrived_ref[:, 16:24, :], axis=0) * scale
-    piece_ref[...] = jnp.broadcast_to(piece[None], piece_ref.shape)
-    recv_ref[...] = arrived_ref[:, :16, :]
 
 
 def history_kernel(core_ref, dest_ref, mine_ref, other_ref, cold_ref, out_ref, high_ref, low_ref):
@@ -186,21 +206,48 @@
         out_ref[at, :] = jnp.where(count > 0.5, written, cold_ref[at, :])
 
 
-def assemble_kernel(core_ref, mine_ref, other_ref, out_ref):
-    core = core_ref[0]
-    half = out_ref.shape[0] // 2
-    for ref, which in ((mine_ref, core), (other_ref, 1 - core)):
-        at = pl.ds(pl.multiple_of(which * half, half), half)
-        for l in range(4):
-            out_ref[at, l * 128 : (l + 1) * 128] = ref[:, l].reshape(half, 128)
-
-
 def exchange(v):
     return lax.all_to_all(v, OWN, split_axis=0, concat_axis=0, tiled=True)
 
 
 def swap(v):
-    return lax.ppermute(v, "rep", SWAP)
+    return lax.ppermute(v, "rep", [(0, 1), (1, 0)])
+
+
+def move(v, axis, mask):
+    count = lax.axis_size(axis)
+    return lax.ppermute(v, axis, [(i, i ^ mask) for i in range(count)])
+
+
+def scatter(me, axis, unit, *terms):
+    size = terms[0].shape[0] // 4
+    piece = ((size, terms[0].shape[1]), F32)
+    outs = call(
+        scatter_kernel,
+        [piece] * 4,
+        (me,) + terms,
+        scalars=1,
+        scratch=[pltpu.VMEM(terms[0].shape, F32)],
+    )
+    return [outs[0]] + [move(outs[shift], axis, shift * unit) for shift in (1, 2, 3)]
+
+
+def total(*terms):
+    return call(total_kernel, [(terms[0].shape, F32)], terms)[0]
+
+
+def join(me, parts, scale=None):
+    rows, width = parts[0].shape
+    return call(
+        functools.partial(join_kernel, scale=scale),
+        [((rows * len(parts), width), F32)],
+        (me,) + tuple(parts),
+        scalars=1,
+    )[0]
+
+
+def gather(me, axis, unit, v):
+    return join(me, [v] + [move(v, axis, shift * unit) for shift in (1, 2, 3)])
 
 
 def body(
@@ -226,58 +273,62 @@
         [(full, F32), ((rows, rows), BF16), ((rows, rows), BF16), ((rows, halo_count), BF16)],
         (core, neighbors, edge_weight, node_input, initial, hot_history, swap(hot_history)),
         scalars=1,
+        limit=60,
         flops=6 * 10**9,
     )
-    wanted, part = lax.optimization_barrier((wanted, part))
     (found,) = call(
         gather_kernel,
         [((halo_count * 4, 128), F32)],
         (wanted, cold_history),
+        limit=60,
         flops=10**9,
     )
-    halo = exchange(found)
+    halo, part = lax.optimization_barrier((exchange(found), part))
+    outgoing, z_high, z_low, u = call(
+        layer_kernel,
+        [((owners // 4, 4, 16, 128), F32), (full, BF16), (full, BF16), (full, F32)],
+        (halo, pick, edge_weight, part, weight),
+        limit=60,
+        flops=2 * 10**9,
+    )
+    arrived = exchange(outgoing.reshape(owners * 16, 128))
     half = (rows // 2, width)
-    embed, keep, give, du = call(
-        layer_kernel,
-        [(full, F32), (half, F32), (half, F32), (full, F32)],
-        (core, halo, pick, edge_weight, part, weight, cotangent),
+    keep, give, du = call(
+        weight_kernel,
+        [(half, F32), (half, F32), (full, F32)],
+        (core, u, z_high, z_low, cotangent),
         scalars=1,
         scratch=[pltpu.VMEM((width, width), F32)],
-        flops=2 * 10**9,
-    )
-    (outgoing,) = call(
-        pack_kernel, [((owners // 4, 4, 24, 128), F32)], (embed, keep, swap(give))
-    )
-    arrived = exchange(outgoing.reshape(owners * 24, 128)).reshape(owners, 24, 128)
+        limit=60,
+        flops=10**9,
+    )
     (grad_input,) = call(
-        backward_kernel, [(full, F32)], (du, weight, high, low), flops=2 * 10**9
-    )
-    arrived, grad_input = lax.optimization_barrier((arrived, grad_input))
-    all_nodes = rows * lax.axis_size(("batch", "hist", "rep"))
-    piece, recv = call(
-        lambda *r: sum_kernel(*r, scale=BETA / math.sqrt(all_nodes)),
-        [((owners, 8, 128), F32), ((owners, 16, 128), F32)],
-        (arrived,),
-    )
-    pieces = exchange(piece.reshape(owners * 8, 128))
-    recv = recv.reshape(owners * 16, 128)
+        backward_kernel, [(full, F32)], (du, weight, high, low), limit=60, flops=2 * 10**9
+    )
+    at_x = lax.axis_index("hist").astype(jnp.int32).reshape(1)
+    batch = lax.axis_index("batch").astype(jnp.int32).reshape(1)
+    depth = lax.axis_size("batch") // 4
+    at_y = batch // depth
+    parts = scatter(at_x, "hist", 1, keep, swap(give))
+    parts = scatter(at_y, "batch", depth, *parts)
+    summed = total(*parts)
+    summed = total(summed, *[move(summed, "batch", mask) for mask in (2, 4, 6)])
+    arrived, summed, grad_input = lax.optimization_barrier((arrived, summed, grad_input))
     dest = jnp.transpose(dest_rows.reshape(2, owners, 4), (0, 2, 1)).reshape(2, rows)
     (new_history,) = call(
         history_kernel,
         [(cold_history.shape, F32)],
-        (core, dest, recv, swap(recv), cold_history),
+        (core, dest, arrived, swap(arrived), cold_history),
         scalars=1,
         scratch=[pltpu.VMEM((2 * rows, width), BF16), pltpu.VMEM((2 * rows, width), BF16)],
+        limit=24,
         flops=4 * 10**9,
     )
-    pieces, new_history = lax.optimization_barrier((pieces, new_history))
-    shape = (owners // 4, 4, 8, 128)
-    (grad_weight,) = call(
-        assemble_kernel,
-        [((width, width), F32)],
-        (core, pieces.reshape(shape), swap(pieces).reshape(shape)),
-        scalars=1,
-    )
+    summed = total(summed, move(summed, "batch", 1))
+    summed = gather(at_y, "batch", depth, summed)
+    summed = gather(at_x, "hist", 1, summed)
+    all_nodes = rows * lax.axis_size(("batch", "hist", "rep"))
+    grad_weight = join(core, [summed, swap(summed)], BETA / math.sqrt(all_nodes))
     return (grad_weight, grad_input, new_history)
 
 

time: 155 us -> 149 us (0.961)
  waiting for transfers between devices: 45.9 us -> 31 us
  Pallas kernels: 19.5 us -> 32.3 us
  starting transfers between devices: 39.8 us -> 51.4 us
  local copies, waits for them, and re-layouts: 17.4 us -> 8.08 us
  blocking collectives: 30 us -> 24.5 us
    all_to_all x3 -> x2, waiting for transfers between devices: 42.8 us -> 5.75 us  [exchange(): return lax.all_to_all(v, OWN, split_axis=0, concat_axis=0, tiled=True)]
    ppermute x4 -> x20, starting transfers between devices: 12 us -> 36.9 us  [the longest x16 22.5 us: move(): return lax.ppermute(v, axis, [(i, i ^ mask) for i in range(count)])]
    ppermute x4 -> x20, waiting for transfers between devices: 3.08 us -> 25.3 us  [the longest x16 23.4 us: move(): return lax.ppermute(v, axis, [(i, i ^ mask) for i in range(count)])]
    all_to_all x3 -> x2, starting transfers between devices: 27.8 us -> 14.6 us  [exchange(): return lax.all_to_all(v, OWN, split_axis=0, concat_axis=0, tiled=True)]
    pallas_call x8 -> x14, Pallas kernels: 19.5 us -> 32.3 us  [call(): pl.pallas_call(kernel, out_shape=[jax.ShapeDtypeStruct(*o) for o in outs]...]
    unnamed x43 -> x19, local copies, waits for them, and re-layouts: 17.1 us -> 7.88 us
    all_to_all x1, blocking collectives: 30 us -> 24.5 us  [exchange(): return lax.all_to_all(v, OWN, split_axis=0, concat_axis=0, tiled=True)]
  transfers between devices with their start and end apart: 7 -> 22, of which waited for: 4 -> 14; matrix products, arithmetic and copies ran while one was open for 3% -> 3% of each run, Pallas kernels for 8% -> 15%
where the time goes in v3:
time: 149 us
  starting transfers between devices  51.4 us (34%)
  Pallas kernels  32.3 us (22%)
  waiting for transfers between devices  31 us (21%)
  blocking collectives  24.5 us (16%)
  local copies, waits for them, and re-layouts  8.08 us (5%)
    pallas_call x14, Pallas kernels, call(): pl.pallas_call(kernel, out_shape=[jax.ShapeDtypeStruct(*o) for o in outs]...  32.3 us
    all_to_all x1, blocking collectives, exchange(): return lax.all_to_all(v, OWN, split_axis=0, concat_axis=0, tiled=True)  24.5 us
    ppermute x16, waiting for transfers between devices, move(): return lax.ppermute(v, axis, [(i, i ^ mask) for i in range(count)])  23.4 us
    ppermute x16, starting transfers between devices, move(): return lax.ppermute(v, axis, [(i, i ^ mask) for i in range(count)])  22.5 us
    all_to_all x2, starting transfers between devices, exchange(): return lax.all_to_all(v, OWN, split_axis=0, concat_axis=0, tiled=True)  14.6 us
    ppermute x4, starting transfers between devices, swap(): return lax.ppermute(v, 'rep', [(0, 1), (1, 0)])  14.4 us
    unnamed x19, local copies, waits for them, and re-layouts  7.88 us
    all_to_all x2, waiting for transfers between devices, exchange(): return lax.all_to_all(v, OWN, split_axis=0, concat_axis=0, tiled=True)  5.75 us
  transfers between devices with their start and end apart: 22, of which 14 were waited for; matrix products, arithmetic and copies ran while one was open for 3% of the time, Pallas kernels for 15%

profile of v3, /device:TPU:1, one launch (start us, length us, event | category | flops | bytes accessed | tf_op | source)
XLA Modules:
  0.0 148.8 jit_solution(17852099595790256386)
XLA Ops:
  0.7 3.3 %collective-permute-start = (f32[1024,512]{1,0:T(8,128)}, f32[1024,512]{1,0:T(8,128)S(1)}, u32[]{:S(2)}, u32[]{:S(2)}) collective-permute-start(f32[1024,512]{1,0:T(8,128)} %r_5_.1), channel_id=1, source_target_pairs={{0,1},{1,0},{2,3},{3,2},{4,5},{5,4},{6,7},{7,6},{8,9},{9,8},{10,11... | collective-permute-start | bytes 6291464 | tf_op jit(solution)/shard_map/ppermute | solution.py:214
  4.0 0.8 copy.23
  4.8 24.5 %all_to_all.35 = s32[128,1,2]{2,1,0:T(1,128)} all-to-all(s32[128,1,2]{2,1,0:T(1,128)S(1)} %bitcast.21), channel_id=1, replica_groups=mesh['batch'=32,'hist'=4,'rep'=2] {'batch','hist'}, dimensions={0} | all-to-all | bytes 2048 | tf_op jit(solution)/shard_map/all_to_all | solution.py:210
  29.3 3.5 %shard_map.121 = f32[1024,128]{1,0:T(8,128)} custom-call(s32[128,2]{1,0:T(8,128)} %bitcast.22, f32[1280,512]{1,0:T(8,128)} %cold_ref.3), custom_call_target="tpu_custom_call" | custom-call | flops 1000000000 | bytes 3146752 | tf_op jit(solution)/shard_map/pallas_call | solution.py:46
  32.8 6.2 %all-to-all-start.1 = ((f32[128,8,128]{2,1,0:T(8,128)}), f32[128,8,128]{2,1,0:T(8,128)S(1)}, u32[]{:S(2)}, u32[]{:S(2)}) async-start(f32[128,8,128]{2,1,0:T(8,128)} %bitcast.19), calls=%async_computation.1 | async-start | bytes 1048576 | tf_op jit(solution)/shard_map/all_to_all | solution.py:210
  39.0 0.9 copy.25.r_2_.ew_ref
  39.9 0.8 copy.24.r_1_
  40.7 0.0 collective-permute-done.r_6_
  40.7 1.3 copy-done.6
  42.0 7.9 %shard_map.122 = (f32[512,512]{1,0:T(8,128)}, bf16[512,512]{1,0:T(8,128)(2,1)}, bf16[512,512]{1,0:T(8,128)(2,1)}, bf16[512,256]{1,0:T(8,128)(2,1)}) custom-call(s32[1]{0:T(128)} %bitcast.r_0_.core_ref.me_ref, s32[512,8]{1,0:T(8,128)} %copy.24.r_1_, f32[512,8]{1,0:T(8,128)} %copy.25.r_2_.ew_ref, f32[512,512]{1,0:T(8,128)} %r_3_.1, f32[512,512]{1,0:T(8,128)} %r_4_.1, ...), custom_call_target="tpu_custom_call" | custom-call | flops 6000000000 | bytes 9994244 | tf_op jit(solution)/shard_map/pallas_call | solution.py:46
  49.9 5.7 %all-to-all-done.1 = f32[128,8,128]{2,1,0:T(8,128)S(1)} async-done(((f32[128,8,128]{2,1,0:T(8,128)}), f32[128,8,128]{2,1,0:T(8,128)S(1)}, u32[]{:S(2)}, u32[]{:S(2)}) %all-to-all-start.1) | async-done | bytes 524320 | tf_op jit(solution)/shard_map/all_to_all | solution.py:210
  55.7 0.8 copy-done.2
  56.5 4.9 %shard_map.123 = (f32[32,4,16,128]{3,2,1,0:T(8,128)}, bf16[512,512]{1,0:T(8,128)(2,1)}, bf16[512,512]{1,0:T(8,128)(2,1)}, f32[512,512]{1,0:T(8,128)}) custom-call(f32[1024,128]{1,0:T(8,128)} %bitcast.18, bf16[512,256]{1,0:T(8,128)(2,1)} %get-tuple-element.29.pick_ref, f32[512,8]{1,0:T(8,128)} %copy.25.r_2_.ew_ref, f32[512,512]{1,0:T(8,128)} %get-tuple-element.30.part_ref, ...), custom_call_target="tpu_custom_call" | custom-call | flops 2000000000 | bytes 7356416 | tf_op jit(solution)/shard_map/pallas_call | solution.py:46
  61.3 8.4 %all-to-all-start.2 = ((f32[128,16,128]{2,1,0:T(8,128)}), f32[128,16,128]{2,1,0:T(8,128)S(1)}, u32[]{:S(2)}, u32[]{:S(2)}) async-start(f32[128,16,128]{2,1,0:T(8,128)} %bitcast.17), calls=%async_computation.2 | async-start | bytes 2097152 | tf_op jit(solution)/shard_map/all_to_all | solution.py:210
  69.7 4.8 %shard_map.124 = (f32[256,512]{1,0:T(8,128)}, f32[256,512]{1,0:T(8,128)}, f32[512,512]{1,0:T(8,128)}) custom-call(s32[1]{0:T(128)} %bitcast.r_0_.core_ref.me_ref, f32[512,512]{1,0:T(8,128)} %get-tuple-element.32.u_ref, bf16[512,512]{1,0:T(8,128)(2,1)} %get-tuple-element.33.high_ref, bf16[512,512]{1,0:T(8,128)(2,1)} %get-tuple-element.34.low_ref, ...), custom_call_target="tpu_custom_call" | custom-call | flops 1000000000 | bytes 6291460 | tf_op jit(solution)/shard_map/pallas_call | solution.py:46
  74.5 2.2 %collective-permute-start.1 = (f32[256,512]{1,0:T(8,128)}, f32[256,512]{1,0:T(8,128)S(1)}, u32[]{:S(2)}, u32[]{:S(2)}) collective-permute-start(f32[256,512]{1,0:T(8,128)} %get-tuple-element.36), channel_id=1, source_target_pairs={{0,1},{1,0},{2,3},{3,2},{4,5},{5,4},{6,7},{7,6},{8,9},{9,8},{10,11... | collective-permute-start | bytes 1572872 | tf_op jit(solution)/shard_map/ppermute | solution.py:214
  76.7 1.7 %collective-permute-done.1.refs_1_ = f32[256,512]{1,0:T(8,128)S(1)} collective-permute-done((f32[256,512]{1,0:T(8,128)}, f32[256,512]{1,0:T(8,128)S(1)}, u32[]{:S(2)}, u32[]{:S(2)}) %collective-permute-start.1) | collective-permute-done | bytes 524320 | tf_op jit(solution)/shard_map/ppermute | solution.py:214
  78.5 1.0 copy-done
  79.5 0.1 shard_map.125
  79.6 0.9 collective-permute-start.2
  80.5 2.4 %collective-permute-start.3 = (f32[64,512]{1,0:T(8,128)S(1)}, f32[64,512]{1,0:T(8,128)S(1)}, u32[]{:S(2)}, u32[]{:S(2)}) collective-permute-start(f32[64,512]{1,0:T(8,128)S(1)} %get-tuple-element.39), channel_id=1, source_target_pairs={{0,4},{2,6},{4,0},{6,2},{1,5},{3,7},{5,1},{7,3},{8,12},{10,14},{12... | collective-permute-start | bytes 393224 | tf_op jit(solution)/shard_map/ppermute | solution.py:219
  82.9 0.6 collective-permute-start.4
  83.5 2.0 %collective-permute-done.2.refs_1_ = f32[64,512]{1,0:T(8,128)S(1)} collective-permute-done((f32[64,512]{1,0:T(8,128)S(1)}, f32[64,512]{1,0:T(8,128)S(1)}, u32[]{:S(2)}, u32[]{:S(2)}) %collective-permute-start.2) | collective-permute-done | bytes 131104 | tf_op jit(solution)/shard_map/ppermute | solution.py:219
  85.5 8.2 %collective-permute-done.3.refs_2_ = f32[64,512]{1,0:T(8,128)S(1)} collective-permute-done((f32[64,512]{1,0:T(8,128)S(1)}, f32[64,512]{1,0:T(8,128)S(1)}, u32[]{:S(2)}, u32[]{:S(2)}) %collective-permute-start.3) | collective-permute-done | bytes 131104 | tf_op jit(solution)/shard_map/ppermute | solution.py:219
  93.7 1.8 %collective-permute-done.4.refs_3_ = f32[64,512]{1,0:T(8,128)S(1)} collective-permute-done((f32[64,512]{1,0:T(8,128)S(1)}, f32[64,512]{1,0:T(8,128)S(1)}, u32[]{:S(2)}, u32[]{:S(2)}) %collective-permute-start.4) | collective-permute-done | bytes 131104 | tf_op jit(solution)/shard_map/ppermute | solution.py:219
  95.5 1.4 collective-permute-start.5
  96.9 2.8 %collective-permute-start.6 = (f32[16,512]{1,0:T(8,128)S(1)}, f32[16,512]{1,0:T(8,128)S(1)}, u32[]{:S(2)}, u32[]{:S(2)}) collective-permute-start(f32[16,512]{1,0:T(8,128)S(1)} %get-tuple-element.43), channel_id=1, source_target_pairs={{0,128},{8,136},{16,144},{24,152},{32,160},{40,168},{48,176},{56,1... | collective-permute-start | bytes 98312 | tf_op jit(solution)/shard_map/ppermute | solution.py:219
  99.7 0.0 collective-permute-start.7
  99.7 0.0 collective-permute-done.5.refs_1_
  99.7 1.6 %collective-permute-done.6.refs_2_ = f32[16,512]{1,0:T(8,128)S(1)} collective-permute-done((f32[16,512]{1,0:T(8,128)S(1)}, f32[16,512]{1,0:T(8,128)S(1)}, u32[]{:S(2)}, u32[]{:S(2)}) %collective-permute-start.6) | collective-permute-done | bytes 32800 | tf_op jit(solution)/shard_map/ppermute | solution.py:219
  101.4 2.3 %collective-permute-done.7.refs_3_ = f32[16,512]{1,0:T(8,128)S(1)} collective-permute-done((f32[16,512]{1,0:T(8,128)S(1)}, f32[16,512]{1,0:T(8,128)S(1)}, u32[]{:S(2)}, u32[]{:S(2)}) %collective-permute-start.7) | collective-permute-done | bytes 32800 | tf_op jit(solution)/shard_map/ppermute | solution.py:219
  103.7 2.8 %collective-permute-start.10 = (f32[16,512]{1,0:T(8,128)S(1)}, f32[16,512]{1,0:T(8,128)S(1)}, u32[]{:S(2)}, u32[]{:S(2)}) collective-permute-start(f32[16,512]{1,0:T(8,128)S(1)} %shard_map.127.refs_0_), channel_id=1, source_target_pairs={{0,48},{8,56},{16,32},{24,40},{32,16},{40,24},{48,0},{56,8},{64,11... | collective-permute-start | bytes 98312 | tf_op jit(solution)/shard_map/ppermute | solution.py:219
  106.5 2.1 %collective-permute-start.8 = (f32[16,512]{1,0:T(8,128)S(1)}, f32[16,512]{1,0:T(8,128)S(1)}, u32[]{:S(2)}, u32[]{:S(2)}) collective-permute-start(f32[16,512]{1,0:T(8,128)S(1)} %shard_map.127.refs_0_), channel_id=1, source_target_pairs={{0,16},{8,24},{16,0},{24,8},{32,48},{40,56},{48,32},{56,40},{64,80... | collective-permute-start | bytes 98312 | tf_op jit(solution)/shard_map/ppermute | solution.py:219
  108.5 0.9 collective-permute-start.9
  109.4 4.8 %shard_map.129 = f32[512,512]{1,0:T(8,128)} custom-call(f32[512,512]{1,0:T(8,128)} %get-tuple-element.45.du_ref, f32[512,512]{1,0:T(8,128)} %weight_ref.3, bf16[512,512]{1,0:T(8,128)(2,1)} %get-tuple-element.46.high_ref, bf16[512,512]{1,0:T(8,128)(2,1)} %get-tuple-element.47.low_ref), custom_call_target="tpu_custom_call" | custom-call | flops 2000000000 | bytes 5242880 | tf_op jit(solution)/shard_map/pallas_call | solution.py:46
  114.2 0.0 collective-permute-done.10.refs_3_
  114.2 0.0 collective-permute-done.8.refs_1_
  114.2 1.0 collective-permute-done.9.refs_2_
  115.2 0.0 all-to-all-done.2
  115.2 5.0 %collective-permute-start.19 = (f32[2048,128]{1,0:T(8,128)S(1)}, f32[2048,128]{1,0:T(8,128)S(1)}, u32[]{:S(2)}, u32[]{:S(2)}) collective-permute-start(f32[2048,128]{1,0:T(8,128)S(1)} %bitcast.14), channel_id=1, source_target_pairs={{0,1},{1,0},{2,3},{3,2},{4,5},{5,4},{6,7},{7,6},{8,9},{9,8},{10,11... | collective-permute-start | bytes 3145736 | tf_op jit(solution)/shard_map/ppermute | solution.py:214
  120.2 0.5 collective-permute-start.11
  120.7 2.2 %collective-permute-done.11.refs_1_ = f32[16,512]{1,0:T(8,128)S(1)} collective-permute-done((f32[16,512]{1,0:T(8,128)S(1)}, f32[16,512]{1,0:T(8,128)S(1)}, u32[]{:S(2)}, u32[]{:S(2)}) %collective-permute-start.11) | collective-permute-done | bytes 32800 | tf_op jit(solution)/shard_map/ppermute | solution.py:219
  123.0 0.0 collective-permute-start.12
  123.0 0.9 collective-permute-start.13
  123.9 3.0 %collective-permute-start.14 = (f32[16,512]{1,0:T(8,128)S(1)}, f32[16,512]{1,0:T(8,128)S(1)}, u32[]{:S(2)}, u32[]{:S(2)}) collective-permute-start(f32[16,512]{1,0:T(8,128)S(1)} %shard_map.130.refs_0_), channel_id=1, source_target_pairs={{0,192},{8,200},{16,208},{24,216},{32,224},{40,232},{48,240},{56,2... | collective-permute-start | bytes 98312 | tf_op jit(solution)/shard_map/ppermute | solution.py:219
  126.8 0.0 collective-permute-done.12.refs_1_
  126.9 0.5 collective-permute-done.13.refs_2_
  127.4 0.8 collective-permute-done.14.refs_3_
  128.2 0.3 collective-permute-start.15
  128.5 1.1 collective-permute-start.16
  129.6 2.8 %collective-permute-start.17 = (f32[64,512]{1,0:T(8,128)S(1)}, f32[64,512]{1,0:T(8,128)S(1)}, u32[]{:S(2)}, u32[]{:S(2)}) collective-permute-start(f32[64,512]{1,0:T(8,128)S(1)} %shard_map.131.refs_0_), channel_id=1, source_target_pairs={{0,6},{2,4},{4,2},{6,0},{1,7},{3,5},{5,3},{7,1},{8,14},{10,12},{12... | collective-permute-start | bytes 393224 | tf_op jit(solution)/shard_map/ppermute | solution.py:219
  132.3 0.0 collective-permute-done.15.refs_1_
  132.3 1.8 %collective-permute-done.16.refs_2_ = f32[64,512]{1,0:T(8,128)S(1)} collective-permute-done((f32[64,512]{1,0:T(8,128)S(1)}, f32[64,512]{1,0:T(8,128)S(1)}, u32[]{:S(2)}, u32[]{:S(2)}) %collective-permute-start.16) | collective-permute-done | bytes 131104 | tf_op jit(solution)/shard_map/ppermute | solution.py:219
  134.1 1.2 collective-permute-done.17.refs_3_
  135.3 3.9 %collective-permute-start.18 = (f32[256,512]{1,0:T(8,128)S(1)}, f32[256,512]{1,0:T(8,128)S(1)}, u32[]{:S(2)}, u32[]{:S(2)}) collective-permute-start(f32[256,512]{1,0:T(8,128)S(1)} %shard_map.132.refs_0_), channel_id=1, source_target_pairs={{0,1},{1,0},{2,3},{3,2},{4,5},{5,4},{6,7},{7,6},{8,9},{9,8},{10,11... | collective-permute-start | bytes 1572872 | tf_op jit(solution)/shard_map/ppermute | solution.py:214
  139.2 0.5 broadcast.7
  139.8 0.7 reduce.3
  140.4 0.1 reshape.37
  140.6 0.1 copy.27
  140.6 0.1 collective-permute-done.18.refs_1_
  140.8 1.1 shard_map.133
  141.8 0.0 collective-permute-done.19.other_ref
  141.8 1.7 %copy-done.1 = f32[1280,512]{1,0:T(8,128)S(1)} copy-done((f32[1280,512]{1,0:T(8,128)S(1)}, f32[1280,512]{1,0:T(8,128)}, u32[]{:S(2)}) %copy-start.1) | copy-done | bytes 2621464
  143.6 5.2 %shard_map.134 = f32[1280,512]{1,0:T(8,128)} custom-call(s32[1]{0:T(128)} %bitcast.r_0_.core_ref.me_ref, s32[2,512]{1,0:T(2,128)S(1)} %bitcast.16, f32[2048,128]{1,0:T(8,128)S(1)} %bitcast.15, f32[2048,128]{1,0:T(8,128)S(1)} %collective-permute-done.19.other_ref, f32[1280,512]{1,0:T(8,128)S(1)} %copy-done.1), custom_call_target="tpu_custom_call" | custom-call | flops 4000000000 | bytes 7344132 | tf_op jit(solution)/shard_map/pallas_call | solution.py:46
  (17 shorter events, 0.1 us)
Async XLA Ops:
  0.6 38.4 %copy-start.3 = (f32[512,8]{0,1:T(8,128)S(1)}, f32[512,8]{0,1:T(8,128)}, u32[]{:S(2)}) copy-start(f32[512,8]{0,1:T(8,128)} %param.14) | copy-start | bytes 49156
  0.6 39.3 %copy-start.4 = (s32[512,8]{0,1:T(8,128)S(1)}, s32[512,8]{0,1:T(8,128)}, u32[]{:S(2)}) copy-start(s32[512,8]{0,1:T(8,128)} %param.15) | copy-start | bytes 49156
  0.7 40.1 %collective-permute-start = (f32[1024,512]{1,0:T(8,128)}, f32[1024,512]{1,0:T(8,128)S(1)}, u32[]{:S(2)}, u32[]{:S(2)}) collective-permute-start(f32[1024,512]{1,0:T(8,128)} %r_5_.1), channel_id=1, source_target_pairs={{0,1},{1,0},{2,3},{3,2},{4,5},{5,4},{6,7},{7,6},{8,9},{9,8},{10,11... | collective-permute-start | bytes 6291464 | tf_op jit(solution)/shard_map/ppermute | solution.py:214
  32.8 22.8 %all-to-all-start.1 = ((f32[128,8,128]{2,1,0:T(8,128)}), f32[128,8,128]{2,1,0:T(8,128)S(1)}, u32[]{:S(2)}, u32[]{:S(2)}) async-start(f32[128,8,128]{2,1,0:T(8,128)} %bitcast.19), calls=%async_computation.1 | async-start | bytes 1048576 | tf_op jit(solution)/shard_map/all_to_all | solution.py:210
  40.7 1.3 copy-start.6
  55.7 0.8 copy-start.2
  61.3 53.9 %all-to-all-start.2 = ((f32[128,16,128]{2,1,0:T(8,128)}), f32[128,16,128]{2,1,0:T(8,128)S(1)}, u32[]{:S(2)}, u32[]{:S(2)}) async-start(f32[128,16,128]{2,1,0:T(8,128)} %bitcast.17), calls=%async_computation.2 | async-start | bytes 2097152 | tf_op jit(solution)/shard_map/all_to_all | solution.py:210
  74.5 4.0 %collective-permute-start.1 = (f32[256,512]{1,0:T(8,128)}, f32[256,512]{1,0:T(8,128)S(1)}, u32[]{:S(2)}, u32[]{:S(2)}) collective-permute-start(f32[256,512]{1,0:T(8,128)} %get-tuple-element.36), channel_id=1, source_target_pairs={{0,1},{1,0},{2,3},{3,2},{4,5},{5,4},{6,7},{7,6},{8,9},{9,8},{10,11... | collective-permute-start | bytes 1572872 | tf_op jit(solution)/shard_map/ppermute | solution.py:214
  78.5 1.0 copy-start
  79.6 6.0 %collective-permute-start.2 = (f32[64,512]{1,0:T(8,128)S(1)}, f32[64,512]{1,0:T(8,128)S(1)}, u32[]{:S(2)}, u32[]{:S(2)}) collective-permute-start(f32[64,512]{1,0:T(8,128)S(1)} %get-tuple-element.38), channel_id=1, source_target_pairs={{0,2},{2,0},{4,6},{6,4},{1,3},{3,1},{5,7},{7,5},{8,10},{10,8},{12,... | collective-permute-start | bytes 393224 | tf_op jit(solution)/shard_map/ppermute | solution.py:219
  80.5 13.2 %collective-permute-start.3 = (f32[64,512]{1,0:T(8,128)S(1)}, f32[64,512]{1,0:T(8,128)S(1)}, u32[]{:S(2)}, u32[]{:S(2)}) collective-permute-start(f32[64,512]{1,0:T(8,128)S(1)} %get-tuple-element.39), channel_id=1, source_target_pairs={{0,4},{2,6},{4,0},{6,2},{1,5},{3,7},{5,1},{7,3},{8,12},{10,14},{12... | collective-permute-start | bytes 393224 | tf_op jit(solution)/shard_map/ppermute | solution.py:219
  82.9 12.5 %collective-permute-start.4 = (f32[64,512]{1,0:T(8,128)S(1)}, f32[64,512]{1,0:T(8,128)S(1)}, u32[]{:S(2)}, u32[]{:S(2)}) collective-permute-start(f32[64,512]{1,0:T(8,128)S(1)} %get-tuple-element.40), channel_id=1, source_target_pairs={{0,6},{2,4},{4,2},{6,0},{1,7},{3,5},{5,3},{7,1},{8,14},{10,12},{12... | collective-permute-start | bytes 393224 | tf_op jit(solution)/shard_map/ppermute | solution.py:219
  95.5 4.2 %collective-permute-start.5 = (f32[16,512]{1,0:T(8,128)S(1)}, f32[16,512]{1,0:T(8,128)S(1)}, u32[]{:S(2)}, u32[]{:S(2)}) collective-permute-start(f32[16,512]{1,0:T(8,128)S(1)} %get-tuple-element.42), channel_id=1, source_target_pairs={{0,64},{8,72},{16,80},{24,88},{32,96},{40,104},{48,112},{56,120},{... | collective-permute-start | bytes 98312 | tf_op jit(solution)/shard_map/ppermute | solution.py:219
  96.9 4.5 %collective-permute-start.6 = (f32[16,512]{1,0:T(8,128)S(1)}, f32[16,512]{1,0:T(8,128)S(1)}, u32[]{:S(2)}, u32[]{:S(2)}) collective-permute-start(f32[16,512]{1,0:T(8,128)S(1)} %get-tuple-element.43), channel_id=1, source_target_pairs={{0,128},{8,136},{16,144},{24,152},{32,160},{40,168},{48,176},{56,1... | collective-permute-start | bytes 98312 | tf_op jit(solution)/shard_map/ppermute | solution.py:219
  99.7 4.0 %collective-permute-start.7 = (f32[16,512]{1,0:T(8,128)S(1)}, f32[16,512]{1,0:T(8,128)S(1)}, u32[]{:S(2)}, u32[]{:S(2)}) collective-permute-start(f32[16,512]{1,0:T(8,128)S(1)} %get-tuple-element.44), channel_id=1, source_target_pairs={{0,192},{8,200},{16,208},{24,216},{32,224},{40,232},{48,240},{56,2... | collective-permute-start | bytes 98312 | tf_op jit(solution)/shard_map/ppermute | solution.py:219
  103.7 10.5 %collective-permute-start.10 = (f32[16,512]{1,0:T(8,128)S(1)}, f32[16,512]{1,0:T(8,128)S(1)}, u32[]{:S(2)}, u32[]{:S(2)}) collective-permute-start(f32[16,512]{1,0:T(8,128)S(1)} %shard_map.127.refs_0_), channel_id=1, source_target_pairs={{0,48},{8,56},{16,32},{24,40},{32,16},{40,24},{48,0},{56,8},{64,11... | collective-permute-start | bytes 98312 | tf_op jit(solution)/shard_map/ppermute | solution.py:219
  106.5 7.7 %collective-permute-start.8 = (f32[16,512]{1,0:T(8,128)S(1)}, f32[16,512]{1,0:T(8,128)S(1)}, u32[]{:S(2)}, u32[]{:S(2)}) collective-permute-start(f32[16,512]{1,0:T(8,128)S(1)} %shard_map.127.refs_0_), channel_id=1, source_target_pairs={{0,16},{8,24},{16,0},{24,8},{32,48},{40,56},{48,32},{56,40},{64,80... | collective-permute-start | bytes 98312 | tf_op jit(solution)/shard_map/ppermute | solution.py:219
  108.5 6.7 %collective-permute-start.9 = (f32[16,512]{1,0:T(8,128)S(1)}, f32[16,512]{1,0:T(8,128)S(1)}, u32[]{:S(2)}, u32[]{:S(2)}) collective-permute-start(f32[16,512]{1,0:T(8,128)S(1)} %shard_map.127.refs_0_), channel_id=1, source_target_pairs={{0,32},{8,40},{16,48},{24,56},{32,0},{40,8},{48,16},{56,24},{64,96... | collective-permute-start | bytes 98312 | tf_op jit(solution)/shard_map/ppermute | solution.py:219
  109.4 30.3 %copy-start.5 = (s32[1,1024]{1,0:T(1,128)S(1)}, s32[1,1024]{1,0:T(1,128)}, u32[]{:S(2)}) copy-start(s32[1,1024]{1,0:T(1,128)} %param.19) | copy-start | bytes 12292
  115.2 26.6 %collective-permute-start.19 = (f32[2048,128]{1,0:T(8,128)S(1)}, f32[2048,128]{1,0:T(8,128)S(1)}, u32[]{:S(2)}, u32[]{:S(2)}) collective-permute-start(f32[2048,128]{1,0:T(8,128)S(1)} %bitcast.14), channel_id=1, source_target_pairs={{0,1},{1,0},{2,3},{3,2},{4,5},{5,4},{6,7},{7,6},{8,9},{9,8},{10,11... | collective-permute-start | bytes 3145736 | tf_op jit(solution)/shard_map/ppermute | solution.py:214
  120.2 2.8 %collective-permute-start.11 = (f32[16,512]{1,0:T(8,128)S(1)}, f32[16,512]{1,0:T(8,128)S(1)}, u32[]{:S(2)}, u32[]{:S(2)}) collective-permute-start(f32[16,512]{1,0:T(8,128)S(1)} %shard_map.128.refs_0_), channel_id=1, source_target_pairs={{0,8},{8,0},{16,24},{24,16},{32,40},{40,32},{48,56},{56,48},{64,72... | collective-permute-start | bytes 98312 | tf_op jit(solution)/shard_map/ppermute | solution.py:219
  123.0 3.9 %collective-permute-start.12 = (f32[16,512]{1,0:T(8,128)S(1)}, f32[16,512]{1,0:T(8,128)S(1)}, u32[]{:S(2)}, u32[]{:S(2)}) collective-permute-start(f32[16,512]{1,0:T(8,128)S(1)} %shard_map.130.refs_0_), channel_id=1, source_target_pairs={{0,64},{8,72},{16,80},{24,88},{32,96},{40,104},{48,112},{56,120},{... | collective-permute-start | bytes 98312 | tf_op jit(solution)/shard_map/ppermute | solution.py:219
  123.0 4.4 %collective-permute-start.13 = (f32[16,512]{1,0:T(8,128)S(1)}, f32[16,512]{1,0:T(8,128)S(1)}, u32[]{:S(2)}, u32[]{:S(2)}) collective-permute-start(f32[16,512]{1,0:T(8,128)S(1)} %shard_map.130.refs_0_), channel_id=1, source_target_pairs={{0,128},{8,136},{16,144},{24,152},{32,160},{40,168},{48,176},{56,1... | collective-permute-start | bytes 98312 | tf_op jit(solution)/shard_map/ppermute | solution.py:219
  123.9 4.3 %collective-permute-start.14 = (f32[16,512]{1,0:T(8,128)S(1)}, f32[16,512]{1,0:T(8,128)S(1)}, u32[]{:S(2)}, u32[]{:S(2)}) collective-permute-start(f32[16,512]{1,0:T(8,128)S(1)} %shard_map.130.refs_0_), channel_id=1, source_target_pairs={{0,192},{8,200},{16,208},{24,216},{32,224},{40,232},{48,240},{56,2... | collective-permute-start | bytes 98312 | tf_op jit(solution)/shard_map/ppermute | solution.py:219
  128.2 4.2 %collective-permute-start.15 = (f32[64,512]{1,0:T(8,128)S(1)}, f32[64,512]{1,0:T(8,128)S(1)}, u32[]{:S(2)}, u32[]{:S(2)}) collective-permute-start(f32[64,512]{1,0:T(8,128)S(1)} %shard_map.131.refs_0_), channel_id=1, source_target_pairs={{0,2},{2,0},{4,6},{6,4},{1,3},{3,1},{5,7},{7,5},{8,10},{10,8},{12,... | collective-permute-start | bytes 393224 | tf_op jit(solution)/shard_map/ppermute | solution.py:219
  128.5 5.6 %collective-permute-start.16 = (f32[64,512]{1,0:T(8,128)S(1)}, f32[64,512]{1,0:T(8,128)S(1)}, u32[]{:S(2)}, u32[]{:S(2)}) collective-permute-start(f32[64,512]{1,0:T(8,128)S(1)} %shard_map.131.refs_0_), channel_id=1, source_target_pairs={{0,4},{2,6},{4,0},{6,2},{1,5},{3,7},{5,1},{7,3},{8,12},{10,14},{12... | collective-permute-start | bytes 393224 | tf_op jit(solution)/shard_map/ppermute | solution.py:219
  129.6 5.7 %collective-permute-start.17 = (f32[64,512]{1,0:T(8,128)S(1)}, f32[64,512]{1,0:T(8,128)S(1)}, u32[]{:S(2)}, u32[]{:S(2)}) collective-permute-start(f32[64,512]{1,0:T(8,128)S(1)} %shard_map.131.refs_0_), channel_id=1, source_target_pairs={{0,6},{2,4},{4,2},{6,0},{1,7},{3,5},{5,3},{7,1},{8,14},{10,12},{12... | collective-permute-start | bytes 393224 | tf_op jit(solution)/shard_map/ppermute | solution.py:219
  135.3 5.4 %collective-permute-start.18 = (f32[256,512]{1,0:T(8,128)S(1)}, f32[256,512]{1,0:T(8,128)S(1)}, u32[]{:S(2)}, u32[]{:S(2)}) collective-permute-start(f32[256,512]{1,0:T(8,128)S(1)} %shard_map.132.refs_0_), channel_id=1, source_target_pairs={{0,1},{1,0},{2,3},{3,2},{4,5},{5,4},{6,7},{7,6},{8,9},{9,8},{10,11... | collective-permute-start | bytes 1572872 | tf_op jit(solution)/shard_map/ppermute | solution.py:214
  141.8 1.7 %copy-start.1 = (f32[1280,512]{1,0:T(8,128)S(1)}, f32[1280,512]{1,0:T(8,128)}, u32[]{:S(2)}) copy-start(f32[1280,512]{1,0:T(8,128)} %cold_ref.3) | copy-start | bytes 7864324

commit v4 on v3

v4 whole, which is shorter than its diff:
```python
import functools
import math

import jax
import jax.numpy as jnp
from jax import lax
from jax.experimental import pallas as pl
from jax.experimental.pallas import tpu as pltpu
from jax.sharding import PartitionSpec as P

ALPHA = 0.1
BETA = math.log(1.5)
OWN = ("batch", "hist")
F32 = jnp.float32
BF16 = jnp.bfloat16
GELU_C = math.sqrt(2.0 / math.pi)
GELU_A = 0.044715
VMEM = pl.BlockSpec(memory_space=pltpu.VMEM)
SMEM = pl.BlockSpec(memory_space=pltpu.SMEM)
HBM = pl.BlockSpec(memory_space=pltpu.HBM)
MIB = 1 << 20


def dot(a, b, left=1, right=0):
    return lax.dot_general(a, b, (((left,), (right,)), ((), ())), preferred_element_type=F32)


def split(v):
    high = v.astype(BF16)
    return high, (v - high.astype(F32)).astype(BF16)


def dot3(a, b, left=1, right=0):
    return dot(a[0], b[0], left, right) + (dot(a[0], b[1], left, right) + dot(a[1], b[0], left, right))


def lanes(rows, columns):
    return lax.broadcasted_iota(jnp.int32, (rows, columns), 1)


def one_hot(column, count):
    return (column == lanes(column.shape[0], count)).astype(BF16)


class Source:
    def __init__(self, ref, buffer, sem, rows=None):
        rows = rows or ref.shape[0]
        self.buffer, self.copies, self.shape = buffer, [], ref.shape
        for i in range(ref.shape[0] // rows):
            at = (pl.ds(i * rows, rows),) + (slice(None),) * (len(ref.shape) - 1)
            copy = pltpu.make_async_copy(ref.at[at], buffer.at[at], sem.at[i])
            copy.start()
            self.copies.append(copy)

    def __getitem__(self, index):
        for copy in self.copies:
            copy.wait()
        self.copies = []
        return self.buffer[index]

    def part(self, i):
        self.copies[i].wait()


class Sink:
    def __init__(self, ref, buffer, sem, rows=None):
        self.ref, self.buffer, self.sem = ref, buffer, sem
        self.rows, self.copies = rows or ref.shape[0], []
        self.shape = ref.shape

    def __setitem__(self, index, value):
        self.buffer[index] = value

    def push(self, i=0):
        at = (pl.ds(i * self.rows, self.rows),) + (slice(None),) * (len(self.shape) - 1)
        copy = pltpu.make_async_copy(self.buffer.at[at], self.ref.at[at], self.sem.at[i])
        copy.start()
        self.copies.append(copy)


def call(kernel, outs, args, spaces=None, scratch=(), limit=8, flops=0, rows=None):
    spaces = spaces or "v" * (len(args) + len(outs))
    shapes = [(a.shape, a.dtype) for a in args] + list(outs)
    where = {"s": SMEM, "v": VMEM, "h": HBM}
    remote = [i for i, space in enumerate(spaces) if space == "h"]
    buffers = [pltpu.VMEM(*shapes[i]) for i in remote]
    sems = [pltpu.SemaphoreType.DMA((shapes[i][0][0] // rows if rows else 1,)) for i in remote]

    def wrapped(*refs):
        refs, rest = list(refs[: len(shapes)]), refs[len(shapes) :]
        sinks = []
        for n, i in enumerate(remote):
            kind = Source if i < len(args) else Sink
            refs[i] = kind(refs[i], rest[n], rest[len(remote) + n], rows)
            if kind is Sink:
                sinks.append(refs[i])
        kernel(*refs, *rest[2 * len(remote) :])
        for sink in sinks:
            for copy in sink.copies:
                copy.wait()

    count = sum(math.prod(shape) * 4 for shape, _ in shapes)
    return pl.pallas_call(
        wrapped,
        out_shape=[jax.ShapeDtypeStruct(*o) for o in outs],
        in_specs=[where[c] for c in spaces[: len(args)]],
        out_specs=[where[c] for c in spaces[len(args) :]],
        scratch_shapes=buffers + sems + list(scratch),
        compiler_params=pltpu.CompilerParams(vmem_limit_bytes=limit * MIB),
        cost_estimate=pl.CostEstimate(flops=flops, bytes_accessed=count, transcendentals=0),
    )(*args)


def gather_kernel(idx_ref, cold_ref, out_ref):
    owners, per = idx_ref.shape
    step = cold_ref.shape[0] // len(cold_ref.copies)
    found = jnp.zeros((per * owners, cold_ref.shape[1]), F32)
    for block in range(len(cold_ref.copies)):
        cold_ref.part(block)
        high, low = split(cold_ref.buffer[block * step : (block + 1) * step, :])
        pick = jnp.concatenate(
            [one_hot(idx_ref[:, s : s + 1] - block * step, step) for s in range(per)], axis=0
        )
        found = found + (dot(pick, high) + dot(pick, low))
    for s in range(per):
        for l in range(4):
            out_ref[pl.ds(s * 4 + l, owners, stride=per * 4), :] = found[
                s * owners : (s + 1) * owners, l * 128 : (l + 1) * 128
            ]


def hot_kernel(core_ref, nbr_ref, ew_ref, mine_ref, other_ref, out_ref, *, start):
    core = core_ref[0]
    half = mine_ref.shape[0]
    hot = nbr_ref[...].T[:, 1:2] - start
    picked = jnp.zeros(out_ref.shape, F32)
    for ref, base in ((mine_ref, core * half), (other_ref, (1 - core) * half)):
        choose = one_hot(hot - base, half)
        for part in split(ref[...]):
            picked = picked + dot(choose, part)
    out_ref[...] = ew_ref[...].T[:, 1:2] * picked
    out_ref.push()


def local_kernel(
    nbr_ref, ew_ref, node_ref, init_ref, hot_ref, part_ref, high_ref, low_ref, pick_ref
):
    rows = node_ref.shape[0]
    halo_count = pick_ref.shape[1]
    nbr = nbr_ref[...].T
    ew = ew_ref[...].T
    ids = lanes(rows, rows)
    tile = jnp.zeros((rows, rows), F32)
    for k in range(2, nbr.shape[1]):
        tile = tile + jnp.where(nbr[:, k : k + 1] == ids, ew[:, k : k + 1], 0.0)
    tiles = split(tile)
    high_ref[...] = tiles[0]
    low_ref[...] = tiles[1]
    high_ref.push()
    low_ref.push()
    agg = dot3(tiles, split(node_ref[...])) + hot_ref[...]
    part_ref[...] = (1.0 - ALPHA) * agg + ALPHA * init_ref[...]
    part_ref.push()
    place = nbr[:, :1] - rows
    pick_ref[...] = one_hot((place & 1) * (halo_count // 2) + (place >> 1), halo_count)
    pick_ref.push()


def layer_kernel(
    core_ref, halo_ref, pick_ref, ew_ref, part_ref, weight_ref, cot_ref,
    out_ref, keep_ref, give_ref, du_ref, term_ref,
):
    owners = halo_ref.shape[0] // 8
    halo = jnp.concatenate(
        [
            jnp.concatenate(
                [halo_ref[pl.ds(s * 4 + l, owners, stride=8), :] for l in range(4)], axis=1
            )
            for s in range(2)
        ],
        axis=0,
    )
    pick = pick_ref[...]
    high, low = split(halo)
    ew = ew_ref[...].T[:, :1]
    z = part_ref[...] + ((1.0 - ALPHA) * ew) * (dot(pick, high) + dot(pick, low))
    zs = split(z)
    u = (1.0 - BETA) * z + BETA * dot3(zs, split(weight_ref[...]))
    square = u * u
    bent = jnp.tanh(GELU_C * (u + GELU_A * (square * u)))
    embed = (0.5 * u) * (1.0 + bent)
    slope = 0.5 * (1.0 + bent) + (0.5 * u) * (1.0 - bent * bent) * (
        GELU_C * (1.0 + (3.0 * GELU_A) * square)
    )
    du = cot_ref[...] * slope
    du_ref[...] = du
    du_ref.push()
    groups = out_ref.shape[0]
    top = lax.broadcasted_iota(jnp.int32, (groups, 2, 8, 128), 2) < 4
    for pair in range(2):
        x, y = (
            embed[:, l * 128 : (l + 1) * 128].reshape(groups, 2, 8, 128)
            for l in (2 * pair, 2 * pair + 1)
        )
        even = jnp.where(top, x, pltpu.roll(y, 4, 2))
        odd = jnp.where(top, pltpu.roll(x, 4, 2), y)
        for h in range(2):
            out_ref[:, 2 * h, 8 * pair : 8 * pair + 8, :] = even[:, h]
            out_ref[:, 2 * h + 1, 8 * pair : 8 * pair + 8, :] = odd[:, h]
    out_ref.push()
    term_ref[...] = dot3(zs, split(du), 0, 0)
    half = term_ref.shape[0] // 2
    core = core_ref[0]
    keep_ref[...] = term_ref[pl.ds(pl.multiple_of(core * half, half), half), :]
    give_ref[...] = term_ref[pl.ds(pl.multiple_of((1 - core) * half, half), half), :]


def scatter_kernel(me_ref, *refs):
    terms, outs, total_ref = refs[: -1 - 4], refs[-1 - 4 : -1], refs[-1]
    total_ref[...] = functools.reduce(lambda x, y: x + y, [t[...] for t in terms])
    size = outs[0].shape[0]
    for shift, out in enumerate(outs):
        at = jnp.bitwise_xor(me_ref[0], shift) * size
        out[...] = total_ref[pl.ds(pl.multiple_of(at, size), size), :]


def total_kernel(*refs):
    terms = [t[...] for t in refs[:-1]]
    while len(terms) > 1:
        terms = [x + y for x, y in zip(terms[::2], terms[1::2])]
    refs[-1][...] = terms[0]


def join_kernel(me_ref, *refs, scale=None):
    size = refs[0].shape[0]
    for shift, part in enumerate(refs[:-1]):
        at = jnp.bitwise_xor(me_ref[0], shift) * size
        value = part[...] if scale is None else part[...] * scale
        refs[-1][pl.ds(pl.multiple_of(at, size), size), :] = value


def backward_kernel(du_ref, weight_ref, high_ref, low_ref, out_ref):
    du = du_ref[...]
    dz = (1.0 - BETA) * du + BETA * dot3(split(du), split(weight_ref[...]), 1, 1)
    out_ref[...] = (1.0 - ALPHA) * dot3((high_ref[...], low_ref[...]), split(dz), 0, 0)
    out_ref.push()


def history_kernel(which_ref, dest_ref, recv_ref, base_ref, out_ref, high_ref, low_ref):
    owners = recv_ref.shape[0] // 16
    for s in range(4):
        for l in range(4):
            high, low = split(recv_ref[pl.ds(4 * l + s, owners, stride=16), :])
            at = slice(s * owners, (s + 1) * owners)
            high_ref[at, l * 128 : (l + 1) * 128] = high
            low_ref[at, l * 128 : (l + 1) * 128] = low
    dest = dest_ref[pl.ds(which_ref[0], 1), :]
    step = out_ref.rows
    for block in range(out_ref.shape[0] // step):
        ids = lax.broadcasted_iota(jnp.int32, (step, dest.shape[1]), 0) + block * step
        hit = jnp.where(ids == dest, 1.0, 0.0)
        count = jnp.sum(hit, axis=1, keepdims=True)
        place = hit.astype(BF16)
        written = dot(place, high_ref[...]) + dot(place, low_ref[...])
        at = slice(block * step, (block + 1) * step)
        base_ref.part(block)
        out_ref[at, :] = jnp.where(count > 0.5, written, base_ref.buffer[at, :])
        out_ref.push(block)


def write_rows(which, dest, recv, base):
    rows, width = dest.shape[1], base.shape[1]
    return call(
        history_kernel,
        [(base.shape, F32)],
        (which, dest, recv, base),
        spaces="svvhh",
        scratch=[pltpu.VMEM((rows, width), BF16), pltpu.VMEM((rows, width), BF16)],
        limit=52,
        flops=2 * 10**9,
        rows=256,
    )[0]


def exchange(v):
    return lax.all_to_all(v, OWN, split_axis=0, concat_axis=0, tiled=True)


def swap(v):
    return lax.ppermute(v, "rep", [(0, 1), (1, 0)])


def move(v, axis, mask):
    count = lax.axis_size(axis)
    return lax.ppermute(v, axis, [(i, i ^ mask) for i in range(count)])


def scatter(me, *terms):
    size = terms[0].shape[0] // 4
    return call(
        scatter_kernel,
        [((size, terms[0].shape[1]), F32)] * 4,
        (me,) + terms,
        spaces="s" + "v" * (len(terms) + 4),
        scratch=[pltpu.VMEM(terms[0].shape, F32)],
    )


def trade(pieces, axis, unit):
    return [pieces[0]] + [move(pieces[shift], axis, shift * unit) for shift in (1, 2, 3)]


def total(*terms):
    return call(total_kernel, [(terms[0].shape, F32)], terms)[0]


def join(me, parts, scale=None):
    rows, width = parts[0].shape
    return call(
        functools.partial(join_kernel, scale=scale),
        [((rows * len(parts), width), F32)],
        (me,) + tuple(parts),
        spaces="s" + "v" * (len(parts) + 1),
    )[0]


def together(*values):
    return lax.optimization_barrier(values)


def body(
    node_input,
    initial,
    cotangent,
    weight,
    edge_weight,
    neighbors,
    halo_rows,
    cold_history,
    hot_history,
    dest_rows,
):
    rows, width = node_input.shape
    owners = lax.axis_size(OWN)
    halo_count = owners * halo_rows.shape[2]
    core = lax.axis_index("rep").astype(jnp.int32).reshape(1)
    at_x = lax.axis_index("hist").astype(jnp.int32).reshape(1)
    depth = lax.axis_size("batch") // 4
    at_y = lax.div(lax.axis_index("batch").astype(jnp.int32), jnp.int32(depth)).reshape(1)
    full = (rows, width)
    half = (rows // 2, width)
    nbr = neighbors.T
    ew = edge_weight.T
    dest = jnp.transpose(dest_rows.reshape(2, owners, 4), (0, 2, 1)).reshape(2, rows)

    wanted = exchange(halo_rows[0])
    (hot,) = call(
        functools.partial(hot_kernel, start=rows + halo_count),
        [(full, F32)],
        (core, nbr, ew, hot_history, swap(hot_history)),
        spaces="svvhhh",
        limit=60,
        flops=4 * 10**9,
    )
    wanted, hot, dest = together(wanted, hot, dest)
    (found,) = call(
        gather_kernel,
        [((halo_count * 4, 128), F32)],
        (wanted, cold_history),
        spaces="vhv",
        rows=256,
        limit=60,
        flops=10**9,
    )
    halo = exchange(found)
    part, high, low, pick = call(
        local_kernel,
        [(full, F32), ((rows, rows), BF16), ((rows, rows), BF16), ((rows, halo_count), BF16)],
        (nbr, ew, node_input, initial, hot),
        spaces="vvhhhhhhh",
        limit=60,
        flops=2 * 10**9,
    )
    halo, part = together(halo, part)
    outgoing, keep, give, du = call(
        layer_kernel,
        [((owners // 4, 4, 16, 128), F32), (half, F32), (half, F32), (full, F32)],
        (core, halo, pick, ew, part, weight, cotangent),
        spaces="svhvhhhhvvh",
        scratch=[pltpu.VMEM((width, width), F32)],
        limit=52,
        flops=3 * 10**9,
    )
    pieces = scatter(at_x, keep, swap(give))
    outgoing, *pieces = together(outgoing, *pieces)
    arrived = exchange(outgoing.reshape(owners * 16, 128))
    pieces = scatter(at_y, *trade(pieces, "hist", 1))
    summed = total(*trade(pieces, "batch", depth))
    (grad_input,) = call(
        backward_kernel,
        [(full, F32)],
        (du, weight, high, low),
        spaces="hhhhh",
        limit=60,
        flops=2 * 10**9,
    )
    summed = together(summed, *[move(summed, "batch", mask) for mask in (2, 4, 6)], grad_input)
    grad_input = summed[-1]
    summed = total(*summed[:-1])
    summed = total(summed, move(summed, "batch", 1))
    arrived, summed = together(arrived, summed)
    arrived_other = swap(arrived)
    parts = trade([summed] * 4, "batch", depth)
    history = write_rows(core, dest, arrived, cold_history)
    *parts, history = together(*parts, history)
    summed = join(at_y, parts)
    parts = trade([summed] * 4, "hist", 1)
    history = write_rows(1 - core, dest, arrived_other, history)
    *parts, history = together(*parts, history)
    summed = join(at_x, parts)
    all_nodes = rows * lax.axis_size(("batch", "hist", "rep"))
    grad_weight = join(core, [summed, swap(summed)], BETA / math.sqrt(all_nodes))
    return (grad_weight, grad_input, history)


def solution(mesh):
    return jax.shard_map(
        body,
        mesh=mesh,
        in_specs=(
            P(("batch", "hist", "rep"), None),
            P(("batch", "hist", "rep"), None),
            P(("batch", "hist", "rep"), None),
            P(),
            P(("batch", "hist", "rep"), None),
            P(("batch", "hist", "rep"), None),
            P(("batch", "hist", "rep"), None, None),
            P(("batch", "hist"), None),
            P("rep", None),
            P(("batch", "hist"), None),
        ),
        out_specs=(P(), P(("batch", "hist", "rep"), None), P(("batch", "hist"), None)),
        check_vma=False,
    )
```

time: 149 us -> 150 us (level)
  blocking collectives: 24.5 us -> 0 us
  starting transfers between devices: 51.4 us -> 72.1 us
  waiting for transfers between devices: 31 us -> 34.6 us
  local copies, waits for them, and re-layouts: 8.08 us -> 5.04 us
  Pallas kernels: 32.3 us -> 35.3 us
    all_to_all x1 -> x0, blocking collectives: 24.5 us -> none  [exchange(): return lax.all_to_all(v, OWN, split_axis=0, concat_axis=0, tiled=True)]
    all_to_all x2 -> x3, starting transfers between devices: 14.6 us -> 32.7 us  [exchange(): return lax.all_to_all(v, OWN, split_axis=0, concat_axis=0, tiled=True)]
    all_to_all x2 -> x3, waiting for transfers between devices: 5.75 us -> 13 us  [exchange(): return lax.all_to_all(v, OWN, split_axis=0, concat_axis=0, tiled=True)]
    ppermute x16, waiting for transfers between devices: 23.4 us -> 18.5 us  [move(): return lax.ppermute(v, axis, [(i, i ^ mask) for i in range(count)])]
    pallas_call x14 -> x15, Pallas kernels: 32.3 us -> 35.3 us  [call(): pl.pallas_call(wrapped, out_shape=[jax.ShapeDtypeStruct(*o) for o in outs...]
    unnamed x19 -> x11, local copies, waits for them, and re-layouts: 7.88 us -> 4.84 us
    ppermute x16, starting transfers between devices: 22.5 us -> 25.3 us  [move(): return lax.ppermute(v, axis, [(i, i ^ mask) for i in range(count)])]
  transfers between devices with their start and end apart: 22 -> 23, of which waited for: 14 -> 12; matrix products, arithmetic and copies ran while one was open for 3% -> 2% of each run, Pallas kernels for 15% -> 16%
where the time goes in v4:
time: 150 us; the launch traced here: 149 us
  starting transfers between devices  72.1 us (48%)
  Pallas kernels  35.3 us (24%)
  waiting for transfers between devices  34.6 us (23%)
  local copies, waits for them, and re-layouts  5.04 us (3%)
    pallas_call x15, Pallas kernels, call(): pl.pallas_call(wrapped, out_shape=[jax.ShapeDtypeStruct(*o) for o in outs...  35.3 us
    all_to_all x3, starting transfers between devices, exchange(): return lax.all_to_all(v, OWN, split_axis=0, concat_axis=0, tiled=True)  32.7 us
    ppermute x16, starting transfers between devices, move(): return lax.ppermute(v, axis, [(i, i ^ mask) for i in range(count)])  25.3 us
    ppermute x16, waiting for transfers between devices, move(): return lax.ppermute(v, axis, [(i, i ^ mask) for i in range(count)])  18.5 us
    ppermute x4, starting transfers between devices, swap(): return lax.ppermute(v, 'rep', [(0, 1), (1, 0)])  14.1 us
    all_to_all x3, waiting for transfers between devices, exchange(): return lax.all_to_all(v, OWN, split_axis=0, concat_axis=0, tiled=True)  13 us
    unnamed x11, local copies, waits for them, and re-layouts  4.84 us
    ppermute x4, waiting for transfers between devices, swap(): return lax.ppermute(v, 'rep', [(0, 1), (1, 0)])  3.08 us
  transfers between devices with their start and end apart: 23, of which 12 were waited for; matrix products, arithmetic and copies ran while one was open for 2% of the time, Pallas kernels for 16%

profile of v4, /device:TPU:1, one launch (start us, length us, event | category | flops | bytes accessed | tf_op | source)
XLA Modules:
  0.0 149.3 jit_solution(2589450197765347933)
XLA Ops:
  0.6 3.3 %collective-permute-start = (f32[1024,512]{1,0:T(8,128)}, f32[1024,512]{1,0:T(8,128)S(1)}, u32[]{:S(2)}, u32[]{:S(2)}) collective-permute-start(f32[1024,512]{1,0:T(8,128)} %refs_3_.3), channel_id=1, source_target_pairs={{0,1},{1,0},{2,3},{3,2},{4,5},{5,4},{6,7},{7,6},{8,9},{9,8},{10,11... | collective-permute-start | bytes 6291464 | tf_op jit(solution)/shard_map/ppermute | solution.py:290
  4.0 1.4 copy.17
  5.4 13.8 %all-to-all-start = ((s32[128,1,2]{2,1,0:T(1,128)}), s32[128,1,2]{2,1,0:T(1,128)S(1)}, u32[]{:S(2)}, u32[]{:S(2)}) async-start(s32[128,1,2]{2,1,0:T(1,128)} %bitcast.3), calls=%async_computation | async-start | bytes 131072 | tf_op jit(solution)/shard_map/all_to_all | solution.py:286
  19.2 0.5 broadcast.3
  19.7 1.3 reduce.3
  21.0 0.1 reshape.33
  21.2 0.1 copy.18
  21.2 0.0 collective-permute-done.refs_4_
  21.2 0.0 copy-start.3
  21.3 1.3 copy-done.3
  22.6 6.0 %shard_map.121.refs_4_ = f32[512,512]{1,0:T(8,128)} custom-call(s32[1]{0:T(128)} %bitcast.refs_0_, s32[8,512]{1,0:T(8,128)} %bitcast.29, f32[8,512]{1,0:T(8,128)} %bitcast.21, f32[1024,512]{1,0:T(8,128)} %refs_3_.3, f32[1024,512]{1,0:T(8,128)} %copy-done.3), custom_call_target="tpu_custom_call" | custom-call | flops 4000000000 | bytes 5275652 | tf_op jit(solution)/shard_map/pallas_call | solution.py:103
  28.5 1.1 all-to-all-done
  29.6 0.6 copy-done.2
  30.3 4.0 %shard_map.122 = f32[1024,128]{1,0:T(8,128)} custom-call(s32[128,2]{1,0:T(8,128)} %bitcast.27, f32[1280,512]{1,0:T(8,128)} %refs_3_.5), custom_call_target="tpu_custom_call" | custom-call | flops 1000000000 | bytes 3146752 | tf_op jit(solution)/shard_map/pallas_call | solution.py:103
  34.3 12.3 %all-to-all-start.1 = ((f32[128,8,128]{2,1,0:T(8,128)}), f32[128,8,128]{2,1,0:T(8,128)S(1)}, u32[]{:S(2)}, u32[]{:S(2)}) async-start(f32[128,8,128]{2,1,0:T(8,128)} %bitcast.25), calls=%async_computation.1 | async-start | bytes 1048576 | tf_op jit(solution)/shard_map/all_to_all | solution.py:286
  46.6 0.0 copy-start
  46.6 4.9 %shard_map.123 = (f32[512,512]{1,0:T(8,128)}, bf16[512,512]{1,0:T(8,128)(2,1)}, bf16[512,512]{1,0:T(8,128)(2,1)}, bf16[512,256]{1,0:T(8,128)(2,1)}) custom-call(s32[8,512]{1,0:T(8,128)} %bitcast.30, f32[8,512]{1,0:T(8,128)} %bitcast.22, f32[512,512]{1,0:T(8,128)} %refs_2_.1, f32[512,512]{1,0:T(8,128)} %refs_3_.4, f32[512,512]{1,0:T(8,128)} %shard_map.121.refs_4_), custom_call_target="tpu_custom_call" | custom-call | flops 2000000000 | bytes 6848512 | tf_op jit(solution)/shard_map/pallas_call | solution.py:103
  51.5 11.9 %all-to-all-done.1 = f32[128,8,128]{2,1,0:T(8,128)S(1)} async-done(((f32[128,8,128]{2,1,0:T(8,128)}), f32[128,8,128]{2,1,0:T(8,128)S(1)}, u32[]{:S(2)}, u32[]{:S(2)}) %all-to-all-start.1) | async-done | bytes 524320 | tf_op jit(solution)/shard_map/all_to_all | solution.py:286
  63.4 0.9 copy-done.1
  64.4 5.6 %shard_map.124 = (f32[32,4,16,128]{3,2,1,0:T(8,128)}, f32[256,512]{1,0:T(8,128)S(1)}, f32[256,512]{1,0:T(8,128)S(1)}, f32[512,512]{1,0:T(8,128)}) custom-call(s32[1]{0:T(128)} %bitcast.refs_0_, f32[1024,128]{1,0:T(8,128)S(1)} %bitcast.18, bf16[512,256]{1,0:T(8,128)(2,1)S(1)} %copy-done.1, f32[8,512]{1,0:T(8,128)S(1)} %bitcast.23, ...), custom_call_target="tpu_custom_call" | custom-call | flops 3000000000 | bytes 7356420 | tf_op jit(solution)/shard_map/pallas_call | solution.py:103
  70.0 3.5 %collective-permute-start.1 = (f32[256,512]{1,0:T(8,128)S(1)}, f32[256,512]{1,0:T(8,128)S(1)}, u32[]{:S(2)}, u32[]{:S(2)}) collective-permute-start(f32[256,512]{1,0:T(8,128)S(1)} %get-tuple-element.54), channel_id=1, source_target_pairs={{0,1},{1,0},{2,3},{3,2},{4,5},{5,4},{6,7},{7,6},{8,9},{9,8},{10,11... | collective-permute-start | bytes 1572872 | tf_op jit(solution)/shard_map/ppermute | solution.py:290
  73.5 1.5 %collective-permute-done.1.refs_2_ = f32[256,512]{1,0:T(8,128)S(1)} collective-permute-done((f32[256,512]{1,0:T(8,128)S(1)}, f32[256,512]{1,0:T(8,128)S(1)}, u32[]{:S(2)}, u32[]{:S(2)}) %collective-permute-start.1) | collective-permute-done | bytes 524320 | tf_op jit(solution)/shard_map/ppermute | solution.py:290
  75.0 0.1 shard_map.125
  75.1 6.6 %all-to-all-start.2 = ((f32[128,16,128]{2,1,0:T(8,128)}), f32[128,16,128]{2,1,0:T(8,128)S(1)}, u32[]{:S(2)}, u32[]{:S(2)}) async-start(f32[128,16,128]{2,1,0:T(8,128)} %bitcast.24), calls=%async_computation.2 | async-start | bytes 2097152 | tf_op jit(solution)/shard_map/all_to_all | solution.py:286
  81.7 0.7 collective-permute-start.2
  82.4 2.4 %collective-permute-start.3 = (f32[64,512]{1,0:T(8,128)S(1)}, f32[64,512]{1,0:T(8,128)S(1)}, u32[]{:S(2)}, u32[]{:S(2)}) collective-permute-start(f32[64,512]{1,0:T(8,128)S(1)} %get-tuple-element.62), channel_id=1, source_target_pairs={{0,4},{2,6},{4,0},{6,2},{1,5},{3,7},{5,1},{7,3},{8,12},{10,14},{12... | collective-permute-start | bytes 393224 | tf_op jit(solution)/shard_map/ppermute | solution.py:295
  84.8 0.9 collective-permute-start.4
  85.7 3.0 %collective-permute-done.2.refs_2_ = f32[64,512]{1,0:T(8,128)S(1)} collective-permute-done((f32[64,512]{1,0:T(8,128)S(1)}, f32[64,512]{1,0:T(8,128)S(1)}, u32[]{:S(2)}, u32[]{:S(2)}) %collective-permute-start.2) | collective-permute-done | bytes 131104 | tf_op jit(solution)/shard_map/ppermute | solution.py:295
  88.7 6.1 %collective-permute-done.3.refs_3_ = f32[64,512]{1,0:T(8,128)S(1)} collective-permute-done((f32[64,512]{1,0:T(8,128)S(1)}, f32[64,512]{1,0:T(8,128)S(1)}, u32[]{:S(2)}, u32[]{:S(2)}) %collective-permute-start.3) | collective-permute-done | bytes 131104 | tf_op jit(solution)/shard_map/ppermute | solution.py:295
  94.8 1.5 %collective-permute-done.4.refs_4_ = f32[64,512]{1,0:T(8,128)S(1)} collective-permute-done((f32[64,512]{1,0:T(8,128)S(1)}, f32[64,512]{1,0:T(8,128)S(1)}, u32[]{:S(2)}, u32[]{:S(2)}) %collective-permute-start.4) | collective-permute-done | bytes 131104 | tf_op jit(solution)/shard_map/ppermute | solution.py:295
  96.4 1.6 %collective-permute-start.5 = (f32[16,512]{1,0:T(8,128)S(1)}, f32[16,512]{1,0:T(8,128)S(1)}, u32[]{:S(2)}, u32[]{:S(2)}) collective-permute-start(f32[16,512]{1,0:T(8,128)S(1)} %get-tuple-element.65), channel_id=1, source_target_pairs={{0,64},{8,72},{16,80},{24,88},{32,96},{40,104},{48,112},{56,120},{... | collective-permute-start | bytes 98312 | tf_op jit(solution)/shard_map/ppermute | solution.py:295
  98.0 2.8 %collective-permute-start.6 = (f32[16,512]{1,0:T(8,128)S(1)}, f32[16,512]{1,0:T(8,128)S(1)}, u32[]{:S(2)}, u32[]{:S(2)}) collective-permute-start(f32[16,512]{1,0:T(8,128)S(1)} %get-tuple-element.66), channel_id=1, source_target_pairs={{0,128},{8,136},{16,144},{24,152},{32,160},{40,168},{48,176},{56,1... | collective-permute-start | bytes 98312 | tf_op jit(solution)/shard_map/ppermute | solution.py:295
  100.8 0.0 collective-permute-start.7
  100.8 0.0 collective-permute-done.5.refs_1_
  100.8 2.4 %collective-permute-done.6.refs_2_ = f32[16,512]{1,0:T(8,128)S(1)} collective-permute-done((f32[16,512]{1,0:T(8,128)S(1)}, f32[16,512]{1,0:T(8,128)S(1)}, u32[]{:S(2)}, u32[]{:S(2)}) %collective-permute-start.6) | collective-permute-done | bytes 32800 | tf_op jit(solution)/shard_map/ppermute | solution.py:295
  103.2 2.0 %collective-permute-done.7.refs_3_ = f32[16,512]{1,0:T(8,128)S(1)} collective-permute-done((f32[16,512]{1,0:T(8,128)S(1)}, f32[16,512]{1,0:T(8,128)S(1)}, u32[]{:S(2)}, u32[]{:S(2)}) %collective-permute-start.7) | collective-permute-done | bytes 32800 | tf_op jit(solution)/shard_map/ppermute | solution.py:295
  105.2 4.7 %collective-permute-start.10 = (f32[16,512]{1,0:T(8,128)S(1)}, f32[16,512]{1,0:T(8,128)S(1)}, u32[]{:S(2)}, u32[]{:S(2)}) collective-permute-start(f32[16,512]{1,0:T(8,128)S(1)} %shard_map.127.refs_0_), channel_id=1, source_target_pairs={{0,48},{8,56},{16,32},{24,40},{32,16},{40,24},{48,0},{56,8},{64,11... | collective-permute-start | bytes 98312 | tf_op jit(solution)/shard_map/ppermute | solution.py:295
  109.9 0.3 collective-permute-start.8
  110.2 2.1 %collective-permute-start.9 = (f32[16,512]{1,0:T(8,128)S(1)}, f32[16,512]{1,0:T(8,128)S(1)}, u32[]{:S(2)}, u32[]{:S(2)}) collective-permute-start(f32[16,512]{1,0:T(8,128)S(1)} %shard_map.127.refs_0_), channel_id=1, source_target_pairs={{0,32},{8,40},{16,48},{24,56},{32,0},{40,8},{48,16},{56,24},{64,96... | collective-permute-start | bytes 98312 | tf_op jit(solution)/shard_map/ppermute | solution.py:295
  112.3 4.6 %shard_map.128 = f32[512,512]{1,0:T(8,128)} custom-call(f32[512,512]{1,0:T(8,128)} %get-tuple-element.68.refs_0_, f32[512,512]{1,0:T(8,128)} %refs_1_.3, bf16[512,512]{1,0:T(8,128)(2,1)} %get-tuple-element.69.refs_2_, bf16[512,512]{1,0:T(8,128)(2,1)} %get-tuple-element.70.refs_3_), custom_call_target="tpu_custom_call" | custom-call | flops 2000000000 | bytes 5242880 | tf_op jit(solution)/shard_map/pallas_call | solution.py:103
  116.9 0.0 collective-permute-done.10.refs_3_
  116.9 0.0 collective-permute-done.8.refs_1_
  117.0 0.3 collective-permute-done.9.refs_2_
  117.2 2.0 %collective-permute-start.11 = (f32[16,512]{1,0:T(8,128)S(1)}, f32[16,512]{1,0:T(8,128)S(1)}, u32[]{:S(2)}, u32[]{:S(2)}) collective-permute-start(f32[16,512]{1,0:T(8,128)S(1)} %shard_map.129.refs_0_), channel_id=1, source_target_pairs={{0,8},{8,0},{16,24},{24,16},{32,40},{40,32},{48,56},{56,48},{64,72... | collective-permute-start | bytes 98312 | tf_op jit(solution)/shard_map/ppermute | solution.py:295
  119.2 1.8 %collective-permute-done.11.refs_1_ = f32[16,512]{1,0:T(8,128)S(1)} collective-permute-done((f32[16,512]{1,0:T(8,128)S(1)}, f32[16,512]{1,0:T(8,128)S(1)}, u32[]{:S(2)}, u32[]{:S(2)}) %collective-permute-start.11) | collective-permute-done | bytes 32800 | tf_op jit(solution)/shard_map/ppermute | solution.py:295
  121.0 0.0 all-to-all-done.2
  121.0 5.8 %collective-permute-start.18 = (f32[2048,128]{1,0:T(8,128)S(1)}, f32[2048,128]{1,0:T(8,128)S(1)}, u32[]{:S(2)}, u32[]{:S(2)}) collective-permute-start(f32[2048,128]{1,0:T(8,128)S(1)} %bitcast.16), channel_id=1, source_target_pairs={{0,1},{1,0},{2,3},{3,2},{4,5},{5,4},{6,7},{7,6},{8,9},{9,8},{10,11... | collective-permute-start | bytes 3145736 | tf_op jit(solution)/shard_map/ppermute | solution.py:290
  126.9 0.0 collective-permute-start.12
  126.9 0.9 collective-permute-start.13
  127.8 3.0 %collective-permute-start.14 = (f32[16,512]{1,0:T(8,128)S(1)}, f32[16,512]{1,0:T(8,128)S(1)}, u32[]{:S(2)}, u32[]{:S(2)}) collective-permute-start(f32[16,512]{1,0:T(8,128)S(1)} %shard_map.130.refs_1_), channel_id=1, source_target_pairs={{0,192},{8,200},{16,208},{24,216},{32,224},{40,232},{48,240},{56,2... | collective-permute-start | bytes 98312 | tf_op jit(solution)/shard_map/ppermute | solution.py:295
  130.8 4.5 %shard_map.131.refs_3_ = f32[1280,512]{1,0:T(8,128)} custom-call(s32[1]{0:T(128)} %bitcast.refs_0_, s32[2,512]{1,0:T(2,128)S(1)} %bitcast.19, f32[2048,128]{1,0:T(8,128)S(1)} %bitcast.17, f32[1280,512]{1,0:T(8,128)} %refs_3_.5), custom_call_target="tpu_custom_call" | custom-call | flops 2000000000 | bytes 6295556 | tf_op jit(solution)/shard_map/pallas_call | solution.py:103
  135.3 0.0 collective-permute-done.12.refs_2_
  135.3 0.0 collective-permute-done.13.refs_3_
  135.3 0.0 collective-permute-done.14.refs_4_
  135.3 0.1 collective-permute-start.15
  135.4 1.9 %collective-permute-start.16 = (f32[64,512]{1,0:T(8,128)S(1)}, f32[64,512]{1,0:T(8,128)S(1)}, u32[]{:S(2)}, u32[]{:S(2)}) collective-permute-start(f32[64,512]{1,0:T(8,128)S(1)} %shard_map.132.refs_1_), channel_id=1, source_target_pairs={{0,4},{2,6},{4,0},{6,2},{1,5},{3,7},{5,1},{7,3},{8,12},{10,14},{12... | collective-permute-start | bytes 393224 | tf_op jit(solution)/shard_map/ppermute | solution.py:295
  137.3 2.0 %collective-permute-start.17 = (f32[64,512]{1,0:T(8,128)S(1)}, f32[64,512]{1,0:T(8,128)S(1)}, u32[]{:S(2)}, u32[]{:S(2)}) collective-permute-start(f32[64,512]{1,0:T(8,128)S(1)} %shard_map.132.refs_1_), channel_id=1, source_target_pairs={{0,6},{2,4},{4,2},{6,0},{1,7},{3,5},{5,3},{7,1},{8,14},{10,12},{12... | collective-permute-start | bytes 393224 | tf_op jit(solution)/shard_map/ppermute | solution.py:295
  139.3 0.0 collective-permute-done.18.refs_2_
  139.3 4.5 %shard_map.133 = f32[1280,512]{1,0:T(8,128)} custom-call(s32[1]{0:T(128)S(6)} %sub.3.refs_0_, s32[2,512]{1,0:T(2,128)S(1)} %bitcast.20, f32[2048,128]{1,0:T(8,128)S(1)} %collective-permute-done.18.refs_2_, f32[1280,512]{1,0:T(8,128)} %shard_map.131.refs_3_), custom_call_target="tpu_custom_call" | custom-call | flops 2000000000 | bytes 6295556 | tf_op jit(solution)/shard_map/pallas_call | solution.py:103
  143.8 0.0 collective-permute-done.15.refs_2_
  143.8 1.4 collective-permute-done.17.refs_4_
  145.3 1.4 collective-permute-start.19
  146.7 1.5 %collective-permute-done.19.refs_2_ = f32[256,512]{1,0:T(8,128)S(1)} collective-permute-done((f32[256,512]{1,0:T(8,128)S(1)}, f32[256,512]{1,0:T(8,128)S(1)}, u32[]{:S(2)}, u32[]{:S(2)}) %collective-permute-start.19) | collective-permute-done | bytes 524320 | tf_op jit(solution)/shard_map/ppermute | solution.py:290
  148.2 1.1 shard_map.135
  (11 shorter events, 0.1 us)
Async XLA Ops:
  0.6 20.6 %collective-permute-start = (f32[1024,512]{1,0:T(8,128)}, f32[1024,512]{1,0:T(8,128)S(1)}, u32[]{:S(2)}, u32[]{:S(2)}) collective-permute-start(f32[1024,512]{1,0:T(8,128)} %refs_3_.3), channel_id=1, source_target_pairs={{0,1},{1,0},{2,3},{3,2},{4,5},{5,4},{6,7},{7,6},{8,9},{9,8},{10,11... | collective-permute-start | bytes 6291464 | tf_op jit(solution)/shard_map/ppermute | solution.py:290
  5.4 24.3 %all-to-all-start = ((s32[128,1,2]{2,1,0:T(1,128)}), s32[128,1,2]{2,1,0:T(1,128)S(1)}, u32[]{:S(2)}, u32[]{:S(2)}) async-start(s32[128,1,2]{2,1,0:T(1,128)} %bitcast.3), calls=%async_computation | async-start | bytes 131072 | tf_op jit(solution)/shard_map/all_to_all | solution.py:286
  21.2 1.3 copy-start.3
  29.6 0.6 copy-start.2
  34.3 29.1 %all-to-all-start.1 = ((f32[128,8,128]{2,1,0:T(8,128)}), f32[128,8,128]{2,1,0:T(8,128)S(1)}, u32[]{:S(2)}, u32[]{:S(2)}) async-start(f32[128,8,128]{2,1,0:T(8,128)} %bitcast.25), calls=%async_computation.1 | async-start | bytes 1048576 | tf_op jit(solution)/shard_map/all_to_all | solution.py:286
  46.6 16.8 %copy-start = (f32[512,8]{0,1:T(8,128)S(1)}, f32[512,8]{0,1:T(8,128)}, u32[]{:S(2)}) copy-start(f32[512,8]{0,1:T(8,128)} %param.14) | copy-start | bytes 49156
  63.4 1.0 copy-start.1
  70.0 5.0 %collective-permute-start.1 = (f32[256,512]{1,0:T(8,128)S(1)}, f32[256,512]{1,0:T(8,128)S(1)}, u32[]{:S(2)}, u32[]{:S(2)}) collective-permute-start(f32[256,512]{1,0:T(8,128)S(1)} %get-tuple-element.54), channel_id=1, source_target_pairs={{0,1},{1,0},{2,3},{3,2},{4,5},{5,4},{6,7},{7,6},{8,9},{9,8},{10,11... | collective-permute-start | bytes 1572872 | tf_op jit(solution)/shard_map/ppermute | solution.py:290
  75.1 45.9 %all-to-all-start.2 = ((f32[128,16,128]{2,1,0:T(8,128)}), f32[128,16,128]{2,1,0:T(8,128)S(1)}, u32[]{:S(2)}, u32[]{:S(2)}) async-start(f32[128,16,128]{2,1,0:T(8,128)} %bitcast.24), calls=%async_computation.2 | async-start | bytes 2097152 | tf_op jit(solution)/shard_map/all_to_all | solution.py:286
  81.7 7.0 %collective-permute-start.2 = (f32[64,512]{1,0:T(8,128)S(1)}, f32[64,512]{1,0:T(8,128)S(1)}, u32[]{:S(2)}, u32[]{:S(2)}) collective-permute-start(f32[64,512]{1,0:T(8,128)S(1)} %get-tuple-element.61), channel_id=1, source_target_pairs={{0,2},{2,0},{4,6},{6,4},{1,3},{3,1},{5,7},{7,5},{8,10},{10,8},{12,... | collective-permute-start | bytes 393224 | tf_op jit(solution)/shard_map/ppermute | solution.py:295
  82.4 12.4 %collective-permute-start.3 = (f32[64,512]{1,0:T(8,128)S(1)}, f32[64,512]{1,0:T(8,128)S(1)}, u32[]{:S(2)}, u32[]{:S(2)}) collective-permute-start(f32[64,512]{1,0:T(8,128)S(1)} %get-tuple-element.62), channel_id=1, source_target_pairs={{0,4},{2,6},{4,0},{6,2},{1,5},{3,7},{5,1},{7,3},{8,12},{10,14},{12... | collective-permute-start | bytes 393224 | tf_op jit(solution)/shard_map/ppermute | solution.py:295
  84.8 11.5 %collective-permute-start.4 = (f32[64,512]{1,0:T(8,128)S(1)}, f32[64,512]{1,0:T(8,128)S(1)}, u32[]{:S(2)}, u32[]{:S(2)}) collective-permute-start(f32[64,512]{1,0:T(8,128)S(1)} %get-tuple-element.63), channel_id=1, source_target_pairs={{0,6},{2,4},{4,2},{6,0},{1,7},{3,5},{5,3},{7,1},{8,14},{10,12},{12... | collective-permute-start | bytes 393224 | tf_op jit(solution)/shard_map/ppermute | solution.py:295
  96.4 4.4 %collective-permute-start.5 = (f32[16,512]{1,0:T(8,128)S(1)}, f32[16,512]{1,0:T(8,128)S(1)}, u32[]{:S(2)}, u32[]{:S(2)}) collective-permute-start(f32[16,512]{1,0:T(8,128)S(1)} %get-tuple-element.65), channel_id=1, source_target_pairs={{0,64},{8,72},{16,80},{24,88},{32,96},{40,104},{48,112},{56,120},{... | collective-permute-start | bytes 98312 | tf_op jit(solution)/shard_map/ppermute | solution.py:295
  98.0 5.3 %collective-permute-start.6 = (f32[16,512]{1,0:T(8,128)S(1)}, f32[16,512]{1,0:T(8,128)S(1)}, u32[]{:S(2)}, u32[]{:S(2)}) collective-permute-start(f32[16,512]{1,0:T(8,128)S(1)} %get-tuple-element.66), channel_id=1, source_target_pairs={{0,128},{8,136},{16,144},{24,152},{32,160},{40,168},{48,176},{56,1... | collective-permute-start | bytes 98312 | tf_op jit(solution)/shard_map/ppermute | solution.py:295
  100.8 4.4 %collective-permute-start.7 = (f32[16,512]{1,0:T(8,128)S(1)}, f32[16,512]{1,0:T(8,128)S(1)}, u32[]{:S(2)}, u32[]{:S(2)}) collective-permute-start(f32[16,512]{1,0:T(8,128)S(1)} %get-tuple-element.67), channel_id=1, source_target_pairs={{0,192},{8,200},{16,208},{24,216},{32,224},{40,232},{48,240},{56,2... | collective-permute-start | bytes 98312 | tf_op jit(solution)/shard_map/ppermute | solution.py:295
  105.2 11.8 %collective-permute-start.10 = (f32[16,512]{1,0:T(8,128)S(1)}, f32[16,512]{1,0:T(8,128)S(1)}, u32[]{:S(2)}, u32[]{:S(2)}) collective-permute-start(f32[16,512]{1,0:T(8,128)S(1)} %shard_map.127.refs_0_), channel_id=1, source_target_pairs={{0,48},{8,56},{16,32},{24,40},{32,16},{40,24},{48,0},{56,8},{64,11... | collective-permute-start | bytes 98312 | tf_op jit(solution)/shard_map/ppermute | solution.py:295
  109.9 7.0 %collective-permute-start.8 = (f32[16,512]{1,0:T(8,128)S(1)}, f32[16,512]{1,0:T(8,128)S(1)}, u32[]{:S(2)}, u32[]{:S(2)}) collective-permute-start(f32[16,512]{1,0:T(8,128)S(1)} %shard_map.127.refs_0_), channel_id=1, source_target_pairs={{0,16},{8,24},{16,0},{24,8},{32,48},{40,56},{48,32},{56,40},{64,80... | collective-permute-start | bytes 98312 | tf_op jit(solution)/shard_map/ppermute | solution.py:295
  110.2 7.0 %collective-permute-start.9 = (f32[16,512]{1,0:T(8,128)S(1)}, f32[16,512]{1,0:T(8,128)S(1)}, u32[]{:S(2)}, u32[]{:S(2)}) collective-permute-start(f32[16,512]{1,0:T(8,128)S(1)} %shard_map.127.refs_0_), channel_id=1, source_target_pairs={{0,32},{8,40},{16,48},{24,56},{32,0},{40,8},{48,16},{56,24},{64,96... | collective-permute-start | bytes 98312 | tf_op jit(solution)/shard_map/ppermute | solution.py:295
  117.2 3.8 %collective-permute-start.11 = (f32[16,512]{1,0:T(8,128)S(1)}, f32[16,512]{1,0:T(8,128)S(1)}, u32[]{:S(2)}, u32[]{:S(2)}) collective-permute-start(f32[16,512]{1,0:T(8,128)S(1)} %shard_map.129.refs_0_), channel_id=1, source_target_pairs={{0,8},{8,0},{16,24},{24,16},{32,40},{40,32},{48,56},{56,48},{64,72... | collective-permute-start | bytes 98312 | tf_op jit(solution)/shard_map/ppermute | solution.py:295
  121.0 18.2 %collective-permute-start.18 = (f32[2048,128]{1,0:T(8,128)S(1)}, f32[2048,128]{1,0:T(8,128)S(1)}, u32[]{:S(2)}, u32[]{:S(2)}) collective-permute-start(f32[2048,128]{1,0:T(8,128)S(1)} %bitcast.16), channel_id=1, source_target_pairs={{0,1},{1,0},{2,3},{3,2},{4,5},{5,4},{6,7},{7,6},{8,9},{9,8},{10,11... | collective-permute-start | bytes 3145736 | tf_op jit(solution)/shard_map/ppermute | solution.py:290
  126.9 8.4 %collective-permute-start.12 = (f32[16,512]{1,0:T(8,128)S(1)}, f32[16,512]{1,0:T(8,128)S(1)}, u32[]{:S(2)}, u32[]{:S(2)}) collective-permute-start(f32[16,512]{1,0:T(8,128)S(1)} %shard_map.130.refs_1_), channel_id=1, source_target_pairs={{0,64},{8,72},{16,80},{24,88},{32,96},{40,104},{48,112},{56,120},{... | collective-permute-start | bytes 98312 | tf_op jit(solution)/shard_map/ppermute | solution.py:295
  126.9 8.4 %collective-permute-start.13 = (f32[16,512]{1,0:T(8,128)S(1)}, f32[16,512]{1,0:T(8,128)S(1)}, u32[]{:S(2)}, u32[]{:S(2)}) collective-permute-start(f32[16,512]{1,0:T(8,128)S(1)} %shard_map.130.refs_1_), channel_id=1, source_target_pairs={{0,128},{8,136},{16,144},{24,152},{32,160},{40,168},{48,176},{56,1... | collective-permute-start | bytes 98312 | tf_op jit(solution)/shard_map/ppermute | solution.py:295
  127.8 7.5 %collective-permute-start.14 = (f32[16,512]{1,0:T(8,128)S(1)}, f32[16,512]{1,0:T(8,128)S(1)}, u32[]{:S(2)}, u32[]{:S(2)}) collective-permute-start(f32[16,512]{1,0:T(8,128)S(1)} %shard_map.130.refs_1_), channel_id=1, source_target_pairs={{0,192},{8,200},{16,208},{24,216},{32,224},{40,232},{48,240},{56,2... | collective-permute-start | bytes 98312 | tf_op jit(solution)/shard_map/ppermute | solution.py:295
  135.3 8.4 %collective-permute-start.15 = (f32[64,512]{1,0:T(8,128)S(1)}, f32[64,512]{1,0:T(8,128)S(1)}, u32[]{:S(2)}, u32[]{:S(2)}) collective-permute-start(f32[64,512]{1,0:T(8,128)S(1)} %shard_map.132.refs_1_), channel_id=1, source_target_pairs={{0,2},{2,0},{4,6},{6,4},{1,3},{3,1},{5,7},{7,5},{8,10},{10,8},{12,... | collective-permute-start | bytes 393224 | tf_op jit(solution)/shard_map/ppermute | solution.py:295
  135.4 8.3 %collective-permute-start.16 = (f32[64,512]{1,0:T(8,128)S(1)}, f32[64,512]{1,0:T(8,128)S(1)}, u32[]{:S(2)}, u32[]{:S(2)}) collective-permute-start(f32[64,512]{1,0:T(8,128)S(1)} %shard_map.132.refs_1_), channel_id=1, source_target_pairs={{0,4},{2,6},{4,0},{6,2},{1,5},{3,7},{5,1},{7,3},{8,12},{10,14},{12... | collective-permute-start | bytes 393224 | tf_op jit(solution)/shard_map/ppermute | solution.py:295
  137.3 7.9 %collective-permute-start.17 = (f32[64,512]{1,0:T(8,128)S(1)}, f32[64,512]{1,0:T(8,128)S(1)}, u32[]{:S(2)}, u32[]{:S(2)}) collective-permute-start(f32[64,512]{1,0:T(8,128)S(1)} %shard_map.132.refs_1_), channel_id=1, source_target_pairs={{0,6},{2,4},{4,2},{6,0},{1,7},{3,5},{5,3},{7,1},{8,14},{10,12},{12... | collective-permute-start | bytes 393224 | tf_op jit(solution)/shard_map/ppermute | solution.py:295
  145.3 3.0 %collective-permute-start.19 = (f32[256,512]{1,0:T(8,128)S(1)}, f32[256,512]{1,0:T(8,128)S(1)}, u32[]{:S(2)}, u32[]{:S(2)}) collective-permute-start(f32[256,512]{1,0:T(8,128)S(1)} %shard_map.134.refs_1_), channel_id=1, source_target_pairs={{0,1},{1,0},{2,3},{3,2},{4,5},{5,4},{6,7},{7,6},{8,9},{9,8},{10,11... | collective-permute-start | bytes 1572872 | tf_op jit(solution)/shard_map/ppermute | solution.py:290

commit v5 on v4

--- a/solution.py
+++ b/solution.py
@@ -129,26 +129,19 @@
             ]
 
 
-def hot_kernel(core_ref, nbr_ref, ew_ref, mine_ref, other_ref, out_ref, *, start):
-    core = core_ref[0]
-    half = mine_ref.shape[0]
-    hot = nbr_ref[...].T[:, 1:2] - start
-    picked = jnp.zeros(out_ref.shape, F32)
-    for ref, base in ((mine_ref, core * half), (other_ref, (1 - core) * half)):
-        choose = one_hot(hot - base, half)
-        for part in split(ref[...]):
-            picked = picked + dot(choose, part)
-    out_ref[...] = ew_ref[...].T[:, 1:2] * picked
-    out_ref.push()
-
-
-def local_kernel(
-    nbr_ref, ew_ref, node_ref, init_ref, hot_ref, part_ref, high_ref, low_ref, pick_ref
+def prepare_kernel(
+    core_ref, nbr_ref, ew_ref, mine_ref, other_ref, node_ref, init_ref,
+    part_ref, high_ref, low_ref, pick_ref,
 ):
     rows = node_ref.shape[0]
     halo_count = pick_ref.shape[1]
+    half = mine_ref.shape[0]
+    core = core_ref[0]
     nbr = nbr_ref[...].T
     ew = ew_ref[...].T
+    place = nbr[:, :1] - rows
+    pick_ref[...] = one_hot((place & 1) * (halo_count // 2) + (place >> 1), halo_count)
+    pick_ref.push()
     ids = lanes(rows, rows)
     tile = jnp.zeros((rows, rows), F32)
     for k in range(2, nbr.shape[1]):
@@ -158,12 +151,15 @@
     low_ref[...] = tiles[1]
     high_ref.push()
     low_ref.push()
-    agg = dot3(tiles, split(node_ref[...])) + hot_ref[...]
+    hot = nbr[:, 1:2] - (rows + halo_count)
+    picked = jnp.zeros((rows, node_ref.shape[1]), F32)
+    for ref, base in ((mine_ref, core * half), (other_ref, (1 - core) * half)):
+        choose = one_hot(hot - base, half)
+        for piece in split(ref[...]):
+            picked = picked + dot(choose, piece)
+    agg = dot3(tiles, split(node_ref[...])) + ew[:, 1:2] * picked
     part_ref[...] = (1.0 - ALPHA) * agg + ALPHA * init_ref[...]
     part_ref.push()
-    place = nbr[:, :1] - rows
-    pick_ref[...] = one_hot((place & 1) * (halo_count // 2) + (place >> 1), halo_count)
-    pick_ref.push()
 
 
 def layer_kernel(
@@ -246,18 +242,25 @@
     out_ref.push()
 
 
-def history_kernel(which_ref, dest_ref, recv_ref, base_ref, out_ref, high_ref, low_ref):
-    owners = recv_ref.shape[0] // 16
-    for s in range(4):
-        for l in range(4):
-            high, low = split(recv_ref[pl.ds(4 * l + s, owners, stride=16), :])
-            at = slice(s * owners, (s + 1) * owners)
-            high_ref[at, l * 128 : (l + 1) * 128] = high
-            low_ref[at, l * 128 : (l + 1) * 128] = low
-    dest = dest_ref[pl.ds(which_ref[0], 1), :]
+def history_kernel(
+    core_ref, dest_ref, mine_ref, other_ref, base_ref, out_ref, high_ref, low_ref
+):
+    owners = mine_ref.shape[0] // 16
+    rows = 4 * owners
+    for r, ref in enumerate((mine_ref, other_ref)):
+        for s in range(4):
+            for l in range(4):
+                high, low = split(ref[pl.ds(4 * l + s, owners, stride=16), :])
+                at = slice(r * rows + s * owners, r * rows + (s + 1) * owners)
+                high_ref[at, l * 128 : (l + 1) * 128] = high
+                low_ref[at, l * 128 : (l + 1) * 128] = low
+    core = core_ref[0]
+    dest = jnp.concatenate(
+        [dest_ref[pl.ds(core, 1), :], dest_ref[pl.ds(1 - core, 1), :]], axis=1
+    )
     step = out_ref.rows
     for block in range(out_ref.shape[0] // step):
-        ids = lax.broadcasted_iota(jnp.int32, (step, dest.shape[1]), 0) + block * step
+        ids = lax.broadcasted_iota(jnp.int32, (step, 2 * rows), 0) + block * step
         hit = jnp.where(ids == dest, 1.0, 0.0)
         count = jnp.sum(hit, axis=1, keepdims=True)
         place = hit.astype(BF16)
@@ -268,16 +271,16 @@
         out_ref.push(block)
 
 
-def write_rows(which, dest, recv, base):
-    rows, width = dest.shape[1], base.shape[1]
+def write_rows(core, dest, mine, other, base):
+    rows, width = 2 * dest.shape[1], base.shape[1]
     return call(
         history_kernel,
         [(base.shape, F32)],
-        (which, dest, recv, base),
-        spaces="svvhh",
+        (core, dest, mine, other, base),
+        spaces="svvvhh",
         scratch=[pltpu.VMEM((rows, width), BF16), pltpu.VMEM((rows, width), BF16)],
         limit=52,
-        flops=2 * 10**9,
+        flops=4 * 10**9,
         rows=256,
     )[0]
 
@@ -354,15 +357,6 @@
     dest = jnp.transpose(dest_rows.reshape(2, owners, 4), (0, 2, 1)).reshape(2, rows)
 
     wanted = exchange(halo_rows[0])
-    (hot,) = call(
-        functools.partial(hot_kernel, start=rows + halo_count),
-        [(full, F32)],
-        (core, nbr, ew, hot_history, swap(hot_history)),
-        spaces="svvhhh",
-        limit=60,
-        flops=4 * 10**9,
-    )
-    wanted, hot, dest = together(wanted, hot, dest)
     (found,) = call(
         gather_kernel,
         [((halo_count * 4, 128), F32)],
@@ -374,12 +368,12 @@
     )
     halo = exchange(found)
     part, high, low, pick = call(
-        local_kernel,
+        prepare_kernel,
         [(full, F32), ((rows, rows), BF16), ((rows, rows), BF16), ((rows, halo_count), BF16)],
-        (nbr, ew, node_input, initial, hot),
-        spaces="vvhhhhhhh",
+        (core, nbr, ew, hot_history, swap(hot_history), node_input, initial),
+        spaces="svvhhhhhhhh",
         limit=60,
-        flops=2 * 10**9,
+        flops=6 * 10**9,
     )
     halo, part = together(halo, part)
     outgoing, keep, give, du = call(
@@ -391,11 +385,8 @@
         limit=52,
         flops=3 * 10**9,
     )
-    pieces = scatter(at_x, keep, swap(give))
-    outgoing, *pieces = together(outgoing, *pieces)
-    arrived = exchange(outgoing.reshape(owners * 16, 128))
-    pieces = scatter(at_y, *trade(pieces, "hist", 1))
-    summed = total(*trade(pieces, "batch", depth))
+    got, dest = together(swap(give), dest)
+    pieces = trade(scatter(at_x, keep, got), "hist", 1)
     (grad_input,) = call(
         backward_kernel,
         [(full, F32)],
@@ -404,18 +395,17 @@
         limit=60,
         flops=2 * 10**9,
     )
-    summed = together(summed, *[move(summed, "batch", mask) for mask in (2, 4, 6)], grad_input)
-    grad_input = summed[-1]
-    summed = total(*summed[:-1])
+    *pieces, grad_input = together(*pieces, grad_input)
+    pieces = trade(scatter(at_y, *pieces), "batch", depth)
+    outgoing, grad_input = together(outgoing, grad_input)
+    arrived = exchange(outgoing.reshape(owners * 16, 128))
+    summed = total(*pieces)
+    summed = total(summed, *[move(summed, "batch", mask) for mask in (2, 4, 6)])
     summed = total(summed, move(summed, "batch", 1))
+    summed = join(at_y, trade([summed] * 4, "batch", depth))
     arrived, summed = together(arrived, summed)
-    arrived_other = swap(arrived)
-    parts = trade([summed] * 4, "batch", depth)
-    history = write_rows(core, dest, arrived, cold_history)
-    *parts, history = together(*parts, history)
-    summed = join(at_y, parts)
     parts = trade([summed] * 4, "hist", 1)
-    history = write_rows(1 - core, dest, arrived_other, history)
+    history = write_rows(core, dest, arrived, swap(arrived), cold_history)
     *parts, history = together(*parts, history)
     summed = join(at_x, parts)
     all_nodes = rows * lax.axis_size(("batch", "hist", "rep"))

time: 150 us -> 147 us (0.980)
  blocking collectives: 0 us -> 24.4 us
  starting transfers between devices: 72.1 us -> 50.7 us
  Pallas kernels: 35.3 us -> 29.7 us
    all_to_all x0 -> x1, blocking collectives: none -> 24.4 us  [exchange(): return lax.all_to_all(v, OWN, split_axis=0, concat_axis=0, tiled=True)]
    all_to_all x3 -> x2, starting transfers between devices: 32.7 us -> 13.7 us  [exchange(): return lax.all_to_all(v, OWN, split_axis=0, concat_axis=0, tiled=True)]
    ppermute x16, waiting for transfers between devices: 18.5 us -> 27 us  [move(): return lax.ppermute(v, axis, [(i, i ^ mask) for i in range(count)])]
    all_to_all x3 -> x2, waiting for transfers between devices: 13 us -> 7.25 us  [exchange(): return lax.all_to_all(v, OWN, split_axis=0, concat_axis=0, tiled=True)]
    pallas_call x15 -> x13, Pallas kernels: 35.3 us -> 29.7 us  [call(): pl.pallas_call(wrapped, out_shape=[jax.ShapeDtypeStruct(*o) for o in outs...]
    ppermute x16, starting transfers between devices: 25.3 us -> 22.5 us  [move(): return lax.ppermute(v, axis, [(i, i ^ mask) for i in range(count)])]
    unnamed x11 -> x13, local copies, waits for them, and re-layouts: 4.84 us -> 4.54 us
  transfers between devices with their start and end apart: 23 -> 22, of which waited for: 12 -> 12; matrix products, arithmetic and copies ran while one was open for 2% -> 1% of each run, Pallas kernels for 16% -> 16%
where the time goes in v5:
time: 147 us
  starting transfers between devices  50.7 us (34%)
  waiting for transfers between devices  36 us (24%)
  Pallas kernels  29.7 us (20%)
  blocking collectives  24.4 us (17%)
  local copies, waits for them, and re-layouts  4.75 us (3%)
    pallas_call x13, Pallas kernels, call(): pl.pallas_call(wrapped, out_shape=[jax.ShapeDtypeStruct(*o) for o in outs...  29.7 us
    ppermute x16, waiting for transfers between devices, move(): return lax.ppermute(v, axis, [(i, i ^ mask) for i in range(count)])  27 us
    all_to_all x1, blocking collectives, exchange(): return lax.all_to_all(v, OWN, split_axis=0, concat_axis=0, tiled=True)  24.4 us
    ppermute x16, starting transfers between devices, move(): return lax.ppermute(v, axis, [(i, i ^ mask) for i in range(count)])  22.5 us
    ppermute x4, starting transfers between devices, swap(): return lax.ppermute(v, 'rep', [(0, 1), (1, 0)])  14.5 us
    all_to_all x2, starting transfers between devices, exchange(): return lax.all_to_all(v, OWN, split_axis=0, concat_axis=0, tiled=True)  13.7 us
    all_to_all x2, waiting for transfers between devices, exchange(): return lax.all_to_all(v, OWN, split_axis=0, concat_axis=0, tiled=True)  7.25 us
    unnamed x13, local copies, waits for them, and re-layouts  4.54 us
  transfers between devices with their start and end apart: 22, of which 12 were waited for; matrix products, arithmetic and copies ran while one was open for 1% of the time, Pallas kernels for 16%

profile of v5, /device:TPU:1, one launch (start us, length us, event | category | flops | bytes accessed | tf_op | source)
XLA Modules:
  0.0 147.0 jit_solution(16292109722469845039)
XLA Ops:
  0.6 3.3 %collective-permute-start = (f32[1024,512]{1,0:T(8,128)}, f32[1024,512]{1,0:T(8,128)S(1)}, u32[]{:S(2)}, u32[]{:S(2)}) collective-permute-start(f32[1024,512]{1,0:T(8,128)} %refs_3_.1), channel_id=1, source_target_pairs={{0,1},{1,0},{2,3},{3,2},{4,5},{5,4},{6,7},{7,6},{8,9},{9,8},{10,11... | collective-permute-start | bytes 6291464 | tf_op jit(solution)/shard_map/ppermute | solution.py:293
  4.0 0.8 copy.17
  4.7 24.4 %all_to_all.35 = s32[128,1,2]{2,1,0:T(1,128)} all-to-all(s32[128,1,2]{2,1,0:T(1,128)S(1)} %bitcast.24), channel_id=1, replica_groups=mesh['batch'=32,'hist'=4,'rep'=2] {'batch','hist'}, dimensions={0} | all-to-all | bytes 2048 | tf_op jit(solution)/shard_map/all_to_all | solution.py:289
  29.1 4.0 %shard_map.121 = f32[1024,128]{1,0:T(8,128)} custom-call(s32[128,2]{1,0:T(8,128)} %bitcast.25, f32[1280,512]{1,0:T(8,128)} %refs_4_.1), custom_call_target="tpu_custom_call" | custom-call | flops 1000000000 | bytes 3146752 | tf_op jit(solution)/shard_map/pallas_call | solution.py:103
  33.1 6.4 %all-to-all-start.1 = ((f32[128,8,128]{2,1,0:T(8,128)}), f32[128,8,128]{2,1,0:T(8,128)S(1)}, u32[]{:S(2)}, u32[]{:S(2)}) async-start(f32[128,8,128]{2,1,0:T(8,128)} %bitcast.22), calls=%async_computation.1 | async-start | bytes 1048576 | tf_op jit(solution)/shard_map/all_to_all | solution.py:289
  39.5 0.0 collective-permute-done.refs_4_
  39.5 0.0 copy-start.3
  39.5 1.3 copy-done.3
  40.9 0.0 copy-start
  40.9 7.5 %shard_map.122 = (f32[512,512]{1,0:T(8,128)}, bf16[512,512]{1,0:T(8,128)(2,1)}, bf16[512,512]{1,0:T(8,128)(2,1)}, bf16[512,256]{1,0:T(8,128)(2,1)}) custom-call(s32[1]{0:T(128)} %bitcast.refs_0_, s32[8,512]{1,0:T(8,128)} %bitcast.27, f32[8,512]{1,0:T(8,128)} %bitcast.20, f32[1024,512]{1,0:T(8,128)} %refs_3_.1, f32[1024,512]{1,0:T(8,128)} %copy-done.3, ...), custom_call_target="tpu_custom_call" | custom-call | flops 6000000000 | bytes 9994244 | tf_op jit(solution)/shard_map/pallas_call | solution.py:103
  48.4 7.3 %all-to-all-done.1 = f32[128,8,128]{2,1,0:T(8,128)S(1)} async-done(((f32[128,8,128]{2,1,0:T(8,128)}), f32[128,8,128]{2,1,0:T(8,128)S(1)}, u32[]{:S(2)}, u32[]{:S(2)}) %all-to-all-start.1) | async-done | bytes 524320 | tf_op jit(solution)/shard_map/all_to_all | solution.py:289
  55.6 0.0 copy-done
  55.7 0.9 copy-done.1
  56.6 5.6 %shard_map.123 = (f32[32,4,16,128]{3,2,1,0:T(8,128)}, f32[256,512]{1,0:T(8,128)S(1)}, f32[256,512]{1,0:T(8,128)S(1)}, f32[512,512]{1,0:T(8,128)}) custom-call(s32[1]{0:T(128)} %bitcast.refs_0_, f32[1024,128]{1,0:T(8,128)S(1)} %bitcast.18, bf16[512,256]{1,0:T(8,128)(2,1)S(1)} %copy-done.1, f32[8,512]{1,0:T(8,128)S(1)} %bitcast.21, ...), custom_call_target="tpu_custom_call" | custom-call | flops 3000000000 | bytes 7356420 | tf_op jit(solution)/shard_map/pallas_call | solution.py:103
  62.2 4.1 %collective-permute-start.1 = (f32[256,512]{1,0:T(8,128)S(1)}, f32[256,512]{1,0:T(8,128)S(1)}, u32[]{:S(2)}, u32[]{:S(2)}) collective-permute-start(f32[256,512]{1,0:T(8,128)S(1)} %get-tuple-element.43), channel_id=1, source_target_pairs={{0,1},{1,0},{2,3},{3,2},{4,5},{5,4},{6,7},{7,6},{8,9},{9,8},{10,11... | collective-permute-start | bytes 1572872 | tf_op jit(solution)/shard_map/ppermute | solution.py:293
  66.3 0.5 broadcast.3
  66.8 0.0 copy-done.2
  66.8 0.7 reduce.3
  67.5 0.1 reshape.32
  67.6 0.1 copy.18
  67.7 0.1 collective-permute-done.1.refs_2_
  67.8 0.1 shard_map.124
  67.9 0.4 collective-permute-start.2
  68.3 1.8 %collective-permute-start.3 = (f32[64,512]{1,0:T(8,128)S(1)}, f32[64,512]{1,0:T(8,128)S(1)}, u32[]{:S(2)}, u32[]{:S(2)}) collective-permute-start(f32[64,512]{1,0:T(8,128)S(1)} %get-tuple-element.47), channel_id=1, source_target_pairs={{0,4},{2,6},{4,0},{6,2},{1,5},{3,7},{5,1},{7,3},{8,12},{10,14},{12... | collective-permute-start | bytes 393224 | tf_op jit(solution)/shard_map/ppermute | solution.py:298
  70.1 1.7 %collective-permute-start.4 = (f32[64,512]{1,0:T(8,128)S(1)}, f32[64,512]{1,0:T(8,128)S(1)}, u32[]{:S(2)}, u32[]{:S(2)}) collective-permute-start(f32[64,512]{1,0:T(8,128)S(1)} %get-tuple-element.48), channel_id=1, source_target_pairs={{0,6},{2,4},{4,2},{6,0},{1,7},{3,5},{5,3},{7,1},{8,14},{10,12},{12... | collective-permute-start | bytes 393224 | tf_op jit(solution)/shard_map/ppermute | solution.py:298
  71.9 4.6 %shard_map.125 = f32[512,512]{1,0:T(8,128)} custom-call(f32[512,512]{1,0:T(8,128)} %get-tuple-element.49.refs_0_, f32[512,512]{1,0:T(8,128)} %refs_1_.3, bf16[512,512]{1,0:T(8,128)(2,1)} %get-tuple-element.50.refs_2_, bf16[512,512]{1,0:T(8,128)(2,1)} %get-tuple-element.51.refs_3_), custom_call_target="tpu_custom_call" | custom-call | flops 2000000000 | bytes 5242880 | tf_op jit(solution)/shard_map/pallas_call | solution.py:103
  76.5 0.0 collective-permute-done.2.refs_2_
  76.5 0.0 collective-permute-done.3.refs_3_
  76.5 2.2 %collective-permute-done.4.refs_4_ = f32[64,512]{1,0:T(8,128)S(1)} collective-permute-done((f32[64,512]{1,0:T(8,128)S(1)}, f32[64,512]{1,0:T(8,128)S(1)}, u32[]{:S(2)}, u32[]{:S(2)}) %collective-permute-start.4) | collective-permute-done | bytes 131104 | tf_op jit(solution)/shard_map/ppermute | solution.py:298
  78.7 7.4 %all-to-all-start.2 = ((f32[128,16,128]{2,1,0:T(8,128)}), f32[128,16,128]{2,1,0:T(8,128)S(1)}, u32[]{:S(2)}, u32[]{:S(2)}) async-start(f32[128,16,128]{2,1,0:T(8,128)} %bitcast.9), calls=%async_computation.2 | async-start | bytes 2097152 | tf_op jit(solution)/shard_map/all_to_all | solution.py:289
  86.2 0.8 collective-permute-start.5
  86.9 2.8 %collective-permute-start.6 = (f32[16,512]{1,0:T(8,128)S(1)}, f32[16,512]{1,0:T(8,128)S(1)}, u32[]{:S(2)}, u32[]{:S(2)}) collective-permute-start(f32[16,512]{1,0:T(8,128)S(1)} %get-tuple-element.60), channel_id=1, source_target_pairs={{0,128},{8,136},{16,144},{24,152},{32,160},{40,168},{48,176},{56,1... | collective-permute-start | bytes 98312 | tf_op jit(solution)/shard_map/ppermute | solution.py:298
  89.7 0.4 collective-permute-start.7
  90.1 0.0 collective-permute-done.5.refs_1_
  90.1 2.4 %collective-permute-done.6.refs_2_ = f32[16,512]{1,0:T(8,128)S(1)} collective-permute-done((f32[16,512]{1,0:T(8,128)S(1)}, f32[16,512]{1,0:T(8,128)S(1)}, u32[]{:S(2)}, u32[]{:S(2)}) %collective-permute-start.6) | collective-permute-done | bytes 32800 | tf_op jit(solution)/shard_map/ppermute | solution.py:298
  92.5 2.9 %collective-permute-done.7.refs_3_ = f32[16,512]{1,0:T(8,128)S(1)} collective-permute-done((f32[16,512]{1,0:T(8,128)S(1)}, f32[16,512]{1,0:T(8,128)S(1)}, u32[]{:S(2)}, u32[]{:S(2)}) %collective-permute-start.7) | collective-permute-done | bytes 32800 | tf_op jit(solution)/shard_map/ppermute | solution.py:298
  95.4 3.0 %collective-permute-start.10 = (f32[16,512]{1,0:T(8,128)S(1)}, f32[16,512]{1,0:T(8,128)S(1)}, u32[]{:S(2)}, u32[]{:S(2)}) collective-permute-start(f32[16,512]{1,0:T(8,128)S(1)} %shard_map.127.refs_0_), channel_id=1, source_target_pairs={{0,48},{8,56},{16,32},{24,40},{32,16},{40,24},{48,0},{56,8},{64,11... | collective-permute-start | bytes 98312 | tf_op jit(solution)/shard_map/ppermute | solution.py:298
  98.4 2.5 %collective-permute-start.8 = (f32[16,512]{1,0:T(8,128)S(1)}, f32[16,512]{1,0:T(8,128)S(1)}, u32[]{:S(2)}, u32[]{:S(2)}) collective-permute-start(f32[16,512]{1,0:T(8,128)S(1)} %shard_map.127.refs_0_), channel_id=1, source_target_pairs={{0,16},{8,24},{16,0},{24,8},{32,48},{40,56},{48,32},{56,40},{64,80... | collective-permute-start | bytes 98312 | tf_op jit(solution)/shard_map/ppermute | solution.py:298
  100.8 0.3 collective-permute-start.9
  101.1 8.8 %collective-permute-done.10.refs_3_ = f32[16,512]{1,0:T(8,128)S(1)} collective-permute-done((f32[16,512]{1,0:T(8,128)S(1)}, f32[16,512]{1,0:T(8,128)S(1)}, u32[]{:S(2)}, u32[]{:S(2)}) %collective-permute-start.10) | collective-permute-done | bytes 32800 | tf_op jit(solution)/shard_map/ppermute | solution.py:298
  109.9 0.0 collective-permute-done.8.refs_1_
  109.9 3.9 %collective-permute-done.9.refs_2_ = f32[16,512]{1,0:T(8,128)S(1)} collective-permute-done((f32[16,512]{1,0:T(8,128)S(1)}, f32[16,512]{1,0:T(8,128)S(1)}, u32[]{:S(2)}, u32[]{:S(2)}) %collective-permute-start.9) | collective-permute-done | bytes 32800 | tf_op jit(solution)/shard_map/ppermute | solution.py:298
  113.8 1.1 collective-permute-start.11
  114.9 2.0 %collective-permute-done.11.refs_1_ = f32[16,512]{1,0:T(8,128)S(1)} collective-permute-done((f32[16,512]{1,0:T(8,128)S(1)}, f32[16,512]{1,0:T(8,128)S(1)}, u32[]{:S(2)}, u32[]{:S(2)}) %collective-permute-start.11) | collective-permute-done | bytes 32800 | tf_op jit(solution)/shard_map/ppermute | solution.py:298
  117.0 1.0 collective-permute-start.12
  118.0 2.7 %collective-permute-start.13 = (f32[16,512]{1,0:T(8,128)S(1)}, f32[16,512]{1,0:T(8,128)S(1)}, u32[]{:S(2)}, u32[]{:S(2)}) collective-permute-start(f32[16,512]{1,0:T(8,128)S(1)} %shard_map.129.refs_1_), channel_id=1, source_target_pairs={{0,128},{8,136},{16,144},{24,152},{32,160},{40,168},{48,176},{56,1... | collective-permute-start | bytes 98312 | tf_op jit(solution)/shard_map/ppermute | solution.py:298
  120.7 0.2 collective-permute-start.14
  120.8 0.0 collective-permute-done.12.refs_2_
  120.8 1.5 %collective-permute-done.13.refs_3_ = f32[16,512]{1,0:T(8,128)S(1)} collective-permute-done((f32[16,512]{1,0:T(8,128)S(1)}, f32[16,512]{1,0:T(8,128)S(1)}, u32[]{:S(2)}, u32[]{:S(2)}) %collective-permute-start.13) | collective-permute-done | bytes 32800 | tf_op jit(solution)/shard_map/ppermute | solution.py:298
  122.3 2.3 %collective-permute-done.14.refs_4_ = f32[16,512]{1,0:T(8,128)S(1)} collective-permute-done((f32[16,512]{1,0:T(8,128)S(1)}, f32[16,512]{1,0:T(8,128)S(1)}, u32[]{:S(2)}, u32[]{:S(2)}) %collective-permute-start.14) | collective-permute-done | bytes 32800 | tf_op jit(solution)/shard_map/ppermute | solution.py:298
  124.6 0.0 all-to-all-done.2
  124.7 6.2 %collective-permute-start.18 = (f32[2048,128]{1,0:T(8,128)S(1)}, f32[2048,128]{1,0:T(8,128)S(1)}, u32[]{:S(2)}, u32[]{:S(2)}) collective-permute-start(f32[2048,128]{1,0:T(8,128)S(1)} %bitcast.16), channel_id=1, source_target_pairs={{0,1},{1,0},{2,3},{3,2},{4,5},{5,4},{6,7},{7,6},{8,9},{9,8},{10,11... | collective-permute-start | bytes 3145736 | tf_op jit(solution)/shard_map/ppermute | solution.py:293
  130.9 1.2 collective-permute-start.15
  132.1 2.4 %collective-permute-start.16 = (f32[64,512]{1,0:T(8,128)S(1)}, f32[64,512]{1,0:T(8,128)S(1)}, u32[]{:S(2)}, u32[]{:S(2)}) collective-permute-start(f32[64,512]{1,0:T(8,128)S(1)} %shard_map.130.refs_1_), channel_id=1, source_target_pairs={{0,4},{2,6},{4,0},{6,2},{1,5},{3,7},{5,1},{7,3},{8,12},{10,14},{12... | collective-permute-start | bytes 393224 | tf_op jit(solution)/shard_map/ppermute | solution.py:298
  134.5 0.3 collective-permute-start.17
  134.7 0.0 collective-permute-done.18.refs_3_
  134.7 1.0 copy-done.4
  135.7 6.6 %shard_map.131 = f32[1280,512]{1,0:T(8,128)} custom-call(s32[1]{0:T(128)} %bitcast.refs_0_, s32[2,512]{1,0:T(2,128)S(1)} %bitcast.19, f32[2048,128]{1,0:T(8,128)S(1)} %bitcast.17, f32[2048,128]{1,0:T(8,128)} %copy-done.4, f32[1280,512]{1,0:T(8,128)} %refs_4_.1), custom_call_target="tpu_custom_call" | custom-call | flops 4000000000 | bytes 7344132 | tf_op jit(solution)/shard_map/pallas_call | solution.py:103
  142.4 0.0 collective-permute-done.15.refs_2_
  142.4 0.0 collective-permute-done.16.refs_3_
  142.4 1.1 collective-permute-done.17.refs_4_
  143.5 0.9 collective-permute-start.19
  144.4 1.5 %collective-permute-done.19.refs_2_ = f32[256,512]{1,0:T(8,128)S(1)} collective-permute-done((f32[256,512]{1,0:T(8,128)S(1)}, f32[256,512]{1,0:T(8,128)S(1)}, u32[]{:S(2)}, u32[]{:S(2)}) %collective-permute-start.19) | collective-permute-done | bytes 524320 | tf_op jit(solution)/shard_map/ppermute | solution.py:293
  145.9 1.1 shard_map.133
  (10 shorter events, 0.1 us)
Async XLA Ops:
  0.6 38.9 %collective-permute-start = (f32[1024,512]{1,0:T(8,128)}, f32[1024,512]{1,0:T(8,128)S(1)}, u32[]{:S(2)}, u32[]{:S(2)}) collective-permute-start(f32[1024,512]{1,0:T(8,128)} %refs_3_.1), channel_id=1, source_target_pairs={{0,1},{1,0},{2,3},{3,2},{4,5},{5,4},{6,7},{7,6},{8,9},{9,8},{10,11... | collective-permute-start | bytes 6291464 | tf_op jit(solution)/shard_map/ppermute | solution.py:293
  33.1 22.5 %all-to-all-start.1 = ((f32[128,8,128]{2,1,0:T(8,128)}), f32[128,8,128]{2,1,0:T(8,128)S(1)}, u32[]{:S(2)}, u32[]{:S(2)}) async-start(f32[128,8,128]{2,1,0:T(8,128)} %bitcast.22), calls=%async_computation.1 | async-start | bytes 1048576 | tf_op jit(solution)/shard_map/all_to_all | solution.py:289
  39.5 1.3 copy-start.3
  40.9 14.8 %copy-start = (f32[512,8]{0,1:T(8,128)S(1)}, f32[512,8]{0,1:T(8,128)}, u32[]{:S(2)}) copy-start(f32[512,8]{0,1:T(8,128)} %param.14) | copy-start | bytes 49156
  55.7 1.0 copy-start.1
  56.6 10.2 %copy-start.2 = (s32[1,1024]{1,0:T(1,128)S(1)}, s32[1,1024]{1,0:T(1,128)}, u32[]{:S(2)}) copy-start(s32[1,1024]{1,0:T(1,128)} %param.19) | copy-start | bytes 12292
  62.2 5.6 %collective-permute-start.1 = (f32[256,512]{1,0:T(8,128)S(1)}, f32[256,512]{1,0:T(8,128)S(1)}, u32[]{:S(2)}, u32[]{:S(2)}) collective-permute-start(f32[256,512]{1,0:T(8,128)S(1)} %get-tuple-element.43), channel_id=1, source_target_pairs={{0,1},{1,0},{2,3},{3,2},{4,5},{5,4},{6,7},{7,6},{8,9},{9,8},{10,11... | collective-permute-start | bytes 1572872 | tf_op jit(solution)/shard_map/ppermute | solution.py:293
  67.9 8.6 %collective-permute-start.2 = (f32[64,512]{1,0:T(8,128)S(1)}, f32[64,512]{1,0:T(8,128)S(1)}, u32[]{:S(2)}, u32[]{:S(2)}) collective-permute-start(f32[64,512]{1,0:T(8,128)S(1)} %get-tuple-element.46), channel_id=1, source_target_pairs={{0,2},{2,0},{4,6},{6,4},{1,3},{3,1},{5,7},{7,5},{8,10},{10,8},{12,... | collective-permute-start | bytes 393224 | tf_op jit(solution)/shard_map/ppermute | solution.py:298
  68.3 8.2 %collective-permute-start.3 = (f32[64,512]{1,0:T(8,128)S(1)}, f32[64,512]{1,0:T(8,128)S(1)}, u32[]{:S(2)}, u32[]{:S(2)}) collective-permute-start(f32[64,512]{1,0:T(8,128)S(1)} %get-tuple-element.47), channel_id=1, source_target_pairs={{0,4},{2,6},{4,0},{6,2},{1,5},{3,7},{5,1},{7,3},{8,12},{10,14},{12... | collective-permute-start | bytes 393224 | tf_op jit(solution)/shard_map/ppermute | solution.py:298
  70.1 8.6 %collective-permute-start.4 = (f32[64,512]{1,0:T(8,128)S(1)}, f32[64,512]{1,0:T(8,128)S(1)}, u32[]{:S(2)}, u32[]{:S(2)}) collective-permute-start(f32[64,512]{1,0:T(8,128)S(1)} %get-tuple-element.48), channel_id=1, source_target_pairs={{0,6},{2,4},{4,2},{6,0},{1,7},{3,5},{5,3},{7,1},{8,14},{10,12},{12... | collective-permute-start | bytes 393224 | tf_op jit(solution)/shard_map/ppermute | solution.py:298
  78.7 45.9 %all-to-all-start.2 = ((f32[128,16,128]{2,1,0:T(8,128)}), f32[128,16,128]{2,1,0:T(8,128)S(1)}, u32[]{:S(2)}, u32[]{:S(2)}) async-start(f32[128,16,128]{2,1,0:T(8,128)} %bitcast.9), calls=%async_computation.2 | async-start | bytes 2097152 | tf_op jit(solution)/shard_map/all_to_all | solution.py:289
  86.2 3.9 %collective-permute-start.5 = (f32[16,512]{1,0:T(8,128)S(1)}, f32[16,512]{1,0:T(8,128)S(1)}, u32[]{:S(2)}, u32[]{:S(2)}) collective-permute-start(f32[16,512]{1,0:T(8,128)S(1)} %get-tuple-element.59), channel_id=1, source_target_pairs={{0,64},{8,72},{16,80},{24,88},{32,96},{40,104},{48,112},{56,120},{... | collective-permute-start | bytes 98312 | tf_op jit(solution)/shard_map/ppermute | solution.py:298
  86.9 5.6 %collective-permute-start.6 = (f32[16,512]{1,0:T(8,128)S(1)}, f32[16,512]{1,0:T(8,128)S(1)}, u32[]{:S(2)}, u32[]{:S(2)}) collective-permute-start(f32[16,512]{1,0:T(8,128)S(1)} %get-tuple-element.60), channel_id=1, source_target_pairs={{0,128},{8,136},{16,144},{24,152},{32,160},{40,168},{48,176},{56,1... | collective-permute-start | bytes 98312 | tf_op jit(solution)/shard_map/ppermute | solution.py:298
  89.7 5.6 %collective-permute-start.7 = (f32[16,512]{1,0:T(8,128)S(1)}, f32[16,512]{1,0:T(8,128)S(1)}, u32[]{:S(2)}, u32[]{:S(2)}) collective-permute-start(f32[16,512]{1,0:T(8,128)S(1)} %get-tuple-element.61), channel_id=1, source_target_pairs={{0,192},{8,200},{16,208},{24,216},{32,224},{40,232},{48,240},{56,2... | collective-permute-start | bytes 98312 | tf_op jit(solution)/shard_map/ppermute | solution.py:298
  95.4 14.5 %collective-permute-start.10 = (f32[16,512]{1,0:T(8,128)S(1)}, f32[16,512]{1,0:T(8,128)S(1)}, u32[]{:S(2)}, u32[]{:S(2)}) collective-permute-start(f32[16,512]{1,0:T(8,128)S(1)} %shard_map.127.refs_0_), channel_id=1, source_target_pairs={{0,48},{8,56},{16,32},{24,40},{32,16},{40,24},{48,0},{56,8},{64,11... | collective-permute-start | bytes 98312 | tf_op jit(solution)/shard_map/ppermute | solution.py:298
  98.4 11.5 %collective-permute-start.8 = (f32[16,512]{1,0:T(8,128)S(1)}, f32[16,512]{1,0:T(8,128)S(1)}, u32[]{:S(2)}, u32[]{:S(2)}) collective-permute-start(f32[16,512]{1,0:T(8,128)S(1)} %shard_map.127.refs_0_), channel_id=1, source_target_pairs={{0,16},{8,24},{16,0},{24,8},{32,48},{40,56},{48,32},{56,40},{64,80... | collective-permute-start | bytes 98312 | tf_op jit(solution)/shard_map/ppermute | solution.py:298
  100.8 13.0 %collective-permute-start.9 = (f32[16,512]{1,0:T(8,128)S(1)}, f32[16,512]{1,0:T(8,128)S(1)}, u32[]{:S(2)}, u32[]{:S(2)}) collective-permute-start(f32[16,512]{1,0:T(8,128)S(1)} %shard_map.127.refs_0_), channel_id=1, source_target_pairs={{0,32},{8,40},{16,48},{24,56},{32,0},{40,8},{48,16},{56,24},{64,96... | collective-permute-start | bytes 98312 | tf_op jit(solution)/shard_map/ppermute | solution.py:298
  113.8 3.1 %collective-permute-start.11 = (f32[16,512]{1,0:T(8,128)S(1)}, f32[16,512]{1,0:T(8,128)S(1)}, u32[]{:S(2)}, u32[]{:S(2)}) collective-permute-start(f32[16,512]{1,0:T(8,128)S(1)} %shard_map.128.refs_0_), channel_id=1, source_target_pairs={{0,8},{8,0},{16,24},{24,16},{32,40},{40,32},{48,56},{56,48},{64,72... | collective-permute-start | bytes 98312 | tf_op jit(solution)/shard_map/ppermute | solution.py:298
  117.0 3.9 %collective-permute-start.12 = (f32[16,512]{1,0:T(8,128)S(1)}, f32[16,512]{1,0:T(8,128)S(1)}, u32[]{:S(2)}, u32[]{:S(2)}) collective-permute-start(f32[16,512]{1,0:T(8,128)S(1)} %shard_map.129.refs_1_), channel_id=1, source_target_pairs={{0,64},{8,72},{16,80},{24,88},{32,96},{40,104},{48,112},{56,120},{... | collective-permute-start | bytes 98312 | tf_op jit(solution)/shard_map/ppermute | solution.py:298
  118.0 4.3 %collective-permute-start.13 = (f32[16,512]{1,0:T(8,128)S(1)}, f32[16,512]{1,0:T(8,128)S(1)}, u32[]{:S(2)}, u32[]{:S(2)}) collective-permute-start(f32[16,512]{1,0:T(8,128)S(1)} %shard_map.129.refs_1_), channel_id=1, source_target_pairs={{0,128},{8,136},{16,144},{24,152},{32,160},{40,168},{48,176},{56,1... | collective-permute-start | bytes 98312 | tf_op jit(solution)/shard_map/ppermute | solution.py:298
  120.7 4.0 %collective-permute-start.14 = (f32[16,512]{1,0:T(8,128)S(1)}, f32[16,512]{1,0:T(8,128)S(1)}, u32[]{:S(2)}, u32[]{:S(2)}) collective-permute-start(f32[16,512]{1,0:T(8,128)S(1)} %shard_map.129.refs_1_), channel_id=1, source_target_pairs={{0,192},{8,200},{16,208},{24,216},{32,224},{40,232},{48,240},{56,2... | collective-permute-start | bytes 98312 | tf_op jit(solution)/shard_map/ppermute | solution.py:298
  124.7 10.1 %collective-permute-start.18 = (f32[2048,128]{1,0:T(8,128)S(1)}, f32[2048,128]{1,0:T(8,128)S(1)}, u32[]{:S(2)}, u32[]{:S(2)}) collective-permute-start(f32[2048,128]{1,0:T(8,128)S(1)} %bitcast.16), channel_id=1, source_target_pairs={{0,1},{1,0},{2,3},{3,2},{4,5},{5,4},{6,7},{7,6},{8,9},{9,8},{10,11... | collective-permute-start | bytes 3145736 | tf_op jit(solution)/shard_map/ppermute | solution.py:293
  130.9 11.5 %collective-permute-start.15 = (f32[64,512]{1,0:T(8,128)S(1)}, f32[64,512]{1,0:T(8,128)S(1)}, u32[]{:S(2)}, u32[]{:S(2)}) collective-permute-start(f32[64,512]{1,0:T(8,128)S(1)} %shard_map.130.refs_1_), channel_id=1, source_target_pairs={{0,2},{2,0},{4,6},{6,4},{1,3},{3,1},{5,7},{7,5},{8,10},{10,8},{12,... | collective-permute-start | bytes 393224 | tf_op jit(solution)/shard_map/ppermute | solution.py:298
  132.1 10.3 %collective-permute-start.16 = (f32[64,512]{1,0:T(8,128)S(1)}, f32[64,512]{1,0:T(8,128)S(1)}, u32[]{:S(2)}, u32[]{:S(2)}) collective-permute-start(f32[64,512]{1,0:T(8,128)S(1)} %shard_map.130.refs_1_), channel_id=1, source_target_pairs={{0,4},{2,6},{4,0},{6,2},{1,5},{3,7},{5,1},{7,3},{8,12},{10,14},{12... | collective-permute-start | bytes 393224 | tf_op jit(solution)/shard_map/ppermute | solution.py:298
  134.5 9.0 %collective-permute-start.17 = (f32[64,512]{1,0:T(8,128)S(1)}, f32[64,512]{1,0:T(8,128)S(1)}, u32[]{:S(2)}, u32[]{:S(2)}) collective-permute-start(f32[64,512]{1,0:T(8,128)S(1)} %shard_map.130.refs_1_), channel_id=1, source_target_pairs={{0,6},{2,4},{4,2},{6,0},{1,7},{3,5},{5,3},{7,1},{8,14},{10,12},{12... | collective-permute-start | bytes 393224 | tf_op jit(solution)/shard_map/ppermute | solution.py:298
  134.7 1.0 copy-start.4
  143.5 2.4 %collective-permute-start.19 = (f32[256,512]{1,0:T(8,128)S(1)}, f32[256,512]{1,0:T(8,128)S(1)}, u32[]{:S(2)}, u32[]{:S(2)}) collective-permute-start(f32[256,512]{1,0:T(8,128)S(1)} %shard_map.132.refs_1_), channel_id=1, source_target_pairs={{0,1},{1,0},{2,3},{3,2},{4,5},{5,4},{6,7},{7,6},{8,9},{9,8},{10,11... | collective-permute-start | bytes 1572872 | tf_op jit(solution)/shard_map/ppermute | solution.py:293

commit v6 on v5

--- a/solution.py
+++ b/solution.py
@@ -115,12 +115,11 @@
     owners, per = idx_ref.shape
     step = cold_ref.shape[0] // len(cold_ref.copies)
     found = jnp.zeros((per * owners, cold_ref.shape[1]), F32)
-    for block in range(len(cold_ref.copies)):
+    idx = jnp.concatenate([idx_ref[:, s : s + 1] for s in range(per)], axis=0)
+    picks = [one_hot(idx - block * step, step) for block in range(len(cold_ref.copies))]
+    for block, pick in enumerate(picks):
         cold_ref.part(block)
         high, low = split(cold_ref.buffer[block * step : (block + 1) * step, :])
-        pick = jnp.concatenate(
-            [one_hot(idx_ref[:, s : s + 1] - block * step, step) for s in range(per)], axis=0
-        )
         found = found + (dot(pick, high) + dot(pick, low))
     for s in range(per):
         for l in range(4):
@@ -131,17 +130,13 @@
 
 def prepare_kernel(
     core_ref, nbr_ref, ew_ref, mine_ref, other_ref, node_ref, init_ref,
-    part_ref, high_ref, low_ref, pick_ref,
+    part_ref, high_ref, low_ref, *, halo_count,
 ):
     rows = node_ref.shape[0]
-    halo_count = pick_ref.shape[1]
     half = mine_ref.shape[0]
     core = core_ref[0]
     nbr = nbr_ref[...].T
     ew = ew_ref[...].T
-    place = nbr[:, :1] - rows
-    pick_ref[...] = one_hot((place & 1) * (halo_count // 2) + (place >> 1), halo_count)
-    pick_ref.push()
     ids = lanes(rows, rows)
     tile = jnp.zeros((rows, rows), F32)
     for k in range(2, nbr.shape[1]):
@@ -163,7 +158,7 @@
 
 
 def layer_kernel(
-    core_ref, halo_ref, pick_ref, ew_ref, part_ref, weight_ref, cot_ref,
+    core_ref, halo_ref, nbr_ref, ew_ref, part_ref, weight_ref, cot_ref,
     out_ref, keep_ref, give_ref, du_ref, term_ref,
 ):
     owners = halo_ref.shape[0] // 8
@@ -176,7 +171,8 @@
         ],
         axis=0,
     )
-    pick = pick_ref[...]
+    place = nbr_ref[...].T[:, :1] - part_ref.shape[0]
+    pick = one_hot((place & 1) * owners + (place >> 1), 2 * owners)
     high, low = split(halo)
     ew = ew_ref[...].T[:, :1]
     z = part_ref[...] + ((1.0 - ALPHA) * ew) * (dot(pick, high) + dot(pick, low))
@@ -242,25 +238,18 @@
     out_ref.push()
 
 
-def history_kernel(
-    core_ref, dest_ref, mine_ref, other_ref, base_ref, out_ref, high_ref, low_ref
-):
-    owners = mine_ref.shape[0] // 16
-    rows = 4 * owners
-    for r, ref in enumerate((mine_ref, other_ref)):
-        for s in range(4):
-            for l in range(4):
-                high, low = split(ref[pl.ds(4 * l + s, owners, stride=16), :])
-                at = slice(r * rows + s * owners, r * rows + (s + 1) * owners)
-                high_ref[at, l * 128 : (l + 1) * 128] = high
-                low_ref[at, l * 128 : (l + 1) * 128] = low
-    core = core_ref[0]
-    dest = jnp.concatenate(
-        [dest_ref[pl.ds(core, 1), :], dest_ref[pl.ds(1 - core, 1), :]], axis=1
-    )
+def history_kernel(which_ref, dest_ref, recv_ref, base_ref, out_ref, high_ref, low_ref):
+    owners = recv_ref.shape[0] // 16
+    for s in range(4):
+        for l in range(4):
+            high, low = split(recv_ref[pl.ds(4 * l + s, owners, stride=16), :])
+            at = slice(s * owners, (s + 1) * owners)
+            high_ref[at, l * 128 : (l + 1) * 128] = high
+            low_ref[at, l * 128 : (l + 1) * 128] = low
+    dest = dest_ref[pl.ds(which_ref[0], 1), :]
     step = out_ref.rows
     for block in range(out_ref.shape[0] // step):
-        ids = lax.broadcasted_iota(jnp.int32, (step, 2 * rows), 0) + block * step
+        ids = lax.broadcasted_iota(jnp.int32, (step, dest.shape[1]), 0) + block * step
         hit = jnp.where(ids == dest, 1.0, 0.0)
         count = jnp.sum(hit, axis=1, keepdims=True)
         place = hit.astype(BF16)
@@ -271,16 +260,16 @@
         out_ref.push(block)
 
 
-def write_rows(core, dest, mine, other, base):
-    rows, width = 2 * dest.shape[1], base.shape[1]
+def write_rows(which, dest, recv, base):
+    rows, width = dest.shape[1], base.shape[1]
     return call(
         history_kernel,
         [(base.shape, F32)],
-        (core, dest, mine, other, base),
-        spaces="svvvhh",
+        (which, dest, recv, base),
+        spaces="svvhh",
         scratch=[pltpu.VMEM((rows, width), BF16), pltpu.VMEM((rows, width), BF16)],
         limit=52,
-        flops=4 * 10**9,
+        flops=2 * 10**9,
         rows=256,
     )[0]
 
@@ -367,11 +356,11 @@
         flops=10**9,
     )
     halo = exchange(found)
-    part, high, low, pick = call(
-        prepare_kernel,
-        [(full, F32), ((rows, rows), BF16), ((rows, rows), BF16), ((rows, halo_count), BF16)],
+    part, high, low = call(
+        functools.partial(prepare_kernel, halo_count=halo_count),
+        [(full, F32), ((rows, rows), BF16), ((rows, rows), BF16)],
         (core, nbr, ew, hot_history, swap(hot_history), node_input, initial),
-        spaces="svvhhhhhhhh",
+        spaces="svvhhhhhhh",
         limit=60,
         flops=6 * 10**9,
     )
@@ -379,8 +368,8 @@
     outgoing, keep, give, du = call(
         layer_kernel,
         [((owners // 4, 4, 16, 128), F32), (half, F32), (half, F32), (full, F32)],
-        (core, halo, pick, ew, part, weight, cotangent),
-        spaces="svhvhhhhvvh",
+        (core, halo, nbr, ew, part, weight, cotangent),
+        spaces="svvvhhhhvvh",
         scratch=[pltpu.VMEM((width, width), F32)],
         limit=52,
         flops=3 * 10**9,
@@ -397,15 +386,18 @@
     )
     *pieces, grad_input = together(*pieces, grad_input)
     pieces = trade(scatter(at_y, *pieces), "batch", depth)
-    outgoing, grad_input = together(outgoing, grad_input)
     arrived = exchange(outgoing.reshape(owners * 16, 128))
     summed = total(*pieces)
     summed = total(summed, *[move(summed, "batch", mask) for mask in (2, 4, 6)])
     summed = total(summed, move(summed, "batch", 1))
-    summed = join(at_y, trade([summed] * 4, "batch", depth))
     arrived, summed = together(arrived, summed)
+    arrived_other = swap(arrived)
+    parts = trade([summed] * 4, "batch", depth)
+    history = write_rows(core, dest, arrived, cold_history)
+    *parts, history = together(*parts, history)
+    summed = join(at_y, parts)
     parts = trade([summed] * 4, "hist", 1)
-    history = write_rows(core, dest, arrived, swap(arrived), cold_history)
+    history = write_rows(1 - core, dest, arrived_other, history)
     *parts, history = together(*parts, history)
     summed = join(at_x, parts)
     all_nodes = rows * lax.axis_size(("batch", "hist", "rep"))

time: 147 us -> 142 us (0.966)
  waiting for transfers between devices: 36 us -> 29.7 us
  Pallas kernels: 29.7 us -> 31.8 us
  local copies, waits for them, and re-layouts: 4.75 us -> 2.83 us
    ppermute x16, waiting for transfers between devices: 27 us -> 20.7 us  [move(): return lax.ppermute(v, axis, [(i, i ^ mask) for i in range(count)])]
    pallas_call x13 -> x14, Pallas kernels: 29.7 us -> 31.8 us  [call(): pl.pallas_call(wrapped, out_shape=[jax.ShapeDtypeStruct(*o) for o in outs...]
    unnamed x13 -> x11, local copies, waits for them, and re-layouts: 4.54 us -> 2.63 us
  transfers between devices with their start and end apart: 22 -> 22, of which waited for: 12 -> 11; matrix products, arithmetic and copies ran while one was open for 1% -> 2% of each run, Pallas kernels for 16% -> 18%
where the time goes in v6:
time: 142 us
  starting transfers between devices  51.5 us (36%)
  Pallas kernels  31.8 us (22%)
  waiting for transfers between devices  29.7 us (21%)
  blocking collectives  24.4 us (17%)
  local copies, waits for them, and re-layouts  2.83 us (2%)
    pallas_call x14, Pallas kernels, call(): pl.pallas_call(wrapped, out_shape=[jax.ShapeDtypeStruct(*o) for o in outs...  31.8 us
    all_to_all x1, blocking collectives, exchange(): return lax.all_to_all(v, OWN, split_axis=0, concat_axis=0, tiled=True)  24.4 us
    ppermute x16, starting transfers between devices, move(): return lax.ppermute(v, axis, [(i, i ^ mask) for i in range(count)])  23.2 us
    ppermute x16, waiting for transfers between devices, move(): return lax.ppermute(v, axis, [(i, i ^ mask) for i in range(count)])  20.7 us
    all_to_all x2, starting transfers between devices, exchange(): return lax.all_to_all(v, OWN, split_axis=0, concat_axis=0, tiled=True)  15.1 us
    ppermute x4, starting transfers between devices, swap(): return lax.ppermute(v, 'rep', [(0, 1), (1, 0)])  13.3 us
    all_to_all x2, waiting for transfers between devices, exchange(): return lax.all_to_all(v, OWN, split_axis=0, concat_axis=0, tiled=True)  7.32 us
  transfers between devices with their start and end apart: 22, of which 11 were waited for; matrix products, arithmetic and copies ran while one was open for 2% of the time, Pallas kernels for 18%

profile of v6, /device:TPU:1, one launch (start us, length us, event | category | flops | bytes accessed | tf_op | source)
XLA Modules:
  0.0 141.8 jit_solution(12016766890199899821)
XLA Ops:
  0.6 3.3 %collective-permute-start = (f32[1024,512]{1,0:T(8,128)}, f32[1024,512]{1,0:T(8,128)S(1)}, u32[]{:S(2)}, u32[]{:S(2)}) collective-permute-start(f32[1024,512]{1,0:T(8,128)} %refs_3_.2), channel_id=1, source_target_pairs={{0,1},{1,0},{2,3},{3,2},{4,5},{5,4},{6,7},{7,6},{8,9},{9,8},{10,11... | collective-permute-start | bytes 6291464 | tf_op jit(solution)/shard_map/ppermute | solution.py:282
  4.0 0.8 copy.17
  4.7 24.4 %all_to_all.35 = s32[128,1,2]{2,1,0:T(1,128)} all-to-all(s32[128,1,2]{2,1,0:T(1,128)S(1)} %bitcast.28), channel_id=1, replica_groups=mesh['batch'=32,'hist'=4,'rep'=2] {'batch','hist'}, dimensions={0} | all-to-all | bytes 2048 | tf_op jit(solution)/shard_map/all_to_all | solution.py:278
  29.1 3.9 %shard_map.121 = f32[1024,128]{1,0:T(8,128)} custom-call(s32[128,2]{1,0:T(8,128)} %bitcast.29, f32[1280,512]{1,0:T(8,128)} %refs_3_.3), custom_call_target="tpu_custom_call" | custom-call | flops 1000000000 | bytes 3146752 | tf_op jit(solution)/shard_map/pallas_call | solution.py:103
  33.1 6.4 %all-to-all-start.1 = ((f32[128,8,128]{2,1,0:T(8,128)}), f32[128,8,128]{2,1,0:T(8,128)S(1)}, u32[]{:S(2)}, u32[]{:S(2)}) async-start(f32[128,8,128]{2,1,0:T(8,128)} %bitcast.26), calls=%async_computation.1 | async-start | bytes 1048576 | tf_op jit(solution)/shard_map/all_to_all | solution.py:278
  39.4 0.0 collective-permute-done.refs_4_
  39.5 0.0 copy-start.3
  39.5 1.3 copy-done.3
  40.8 0.0 copy-start
  40.8 7.5 %shard_map.122 = (f32[512,512]{1,0:T(8,128)}, bf16[512,512]{1,0:T(8,128)(2,1)}, bf16[512,512]{1,0:T(8,128)(2,1)}) custom-call(s32[1]{0:T(128)} %bitcast.refs_0_, s32[8,512]{1,0:T(8,128)} %bitcast.21, f32[8,512]{1,0:T(8,128)} %bitcast.23, f32[1024,512]{1,0:T(8,128)} %refs_3_.2, f32[1024,512]{1,0:T(8,128)} %copy-done.3, f32[512,512]{1,0:T(8,128)} %refs_5_.2, ...), custom_call_target="tpu_custom_call" | custom-call | flops 6000000000 | bytes 9469956 | tf_op jit(solution)/shard_map/pallas_call | solution.py:103
  48.3 7.3 %all-to-all-done.1 = f32[128,8,128]{2,1,0:T(8,128)S(1)} async-done(((f32[128,8,128]{2,1,0:T(8,128)}), f32[128,8,128]{2,1,0:T(8,128)S(1)}, u32[]{:S(2)}, u32[]{:S(2)}) %all-to-all-start.1) | async-done | bytes 524320 | tf_op jit(solution)/shard_map/all_to_all | solution.py:278
  55.6 0.0 copy-done
  55.6 0.0 copy-done.1
  55.6 5.6 %shard_map.123 = (f32[32,4,16,128]{3,2,1,0:T(8,128)}, f32[256,512]{1,0:T(8,128)S(1)}, f32[256,512]{1,0:T(8,128)S(1)}, f32[512,512]{1,0:T(8,128)}) custom-call(s32[1]{0:T(128)} %bitcast.refs_0_, f32[1024,128]{1,0:T(8,128)S(1)} %bitcast.18, s32[8,512]{1,0:T(8,128)S(1)} %bitcast.22, f32[8,512]{1,0:T(8,128)S(1)} %bitcast.24, ...), custom_call_target="tpu_custom_call" | custom-call | flops 3000000000 | bytes 6848516 | tf_op jit(solution)/shard_map/pallas_call | solution.py:103
  61.2 8.7 %all-to-all-start.2 = ((f32[128,16,128]{2,1,0:T(8,128)}), f32[128,16,128]{2,1,0:T(8,128)S(1)}, u32[]{:S(2)}, u32[]{:S(2)}) async-start(f32[128,16,128]{2,1,0:T(8,128)} %bitcast.25), calls=%async_computation.2 | async-start | bytes 2097152 | tf_op jit(solution)/shard_map/all_to_all | solution.py:278
  69.9 2.3 %collective-permute-start.1 = (f32[256,512]{1,0:T(8,128)S(1)}, f32[256,512]{1,0:T(8,128)S(1)}, u32[]{:S(2)}, u32[]{:S(2)}) collective-permute-start(f32[256,512]{1,0:T(8,128)S(1)} %get-tuple-element.44), channel_id=1, source_target_pairs={{0,1},{1,0},{2,3},{3,2},{4,5},{5,4},{6,7},{7,6},{8,9},{9,8},{10,11... | collective-permute-start | bytes 1572872 | tf_op jit(solution)/shard_map/ppermute | solution.py:282
  72.3 0.5 broadcast.3
  72.8 0.0 copy-done.2
  72.8 0.7 reduce.3
  73.4 0.1 reshape.33
  73.6 0.1 copy.18
  73.7 0.1 collective-permute-done.1.refs_2_
  73.8 0.1 shard_map.124
  73.9 0.9 collective-permute-start.2
  74.8 2.4 %collective-permute-start.3 = (f32[64,512]{1,0:T(8,128)S(1)}, f32[64,512]{1,0:T(8,128)S(1)}, u32[]{:S(2)}, u32[]{:S(2)}) collective-permute-start(f32[64,512]{1,0:T(8,128)S(1)} %get-tuple-element.48), channel_id=1, source_target_pairs={{0,4},{2,6},{4,0},{6,2},{1,5},{3,7},{5,1},{7,3},{8,12},{10,14},{12... | collective-permute-start | bytes 393224 | tf_op jit(solution)/shard_map/ppermute | solution.py:287
  77.2 0.6 collective-permute-start.4
  77.8 4.6 %shard_map.125 = f32[512,512]{1,0:T(8,128)} custom-call(f32[512,512]{1,0:T(8,128)} %get-tuple-element.50.refs_0_, f32[512,512]{1,0:T(8,128)} %refs_1_.3, bf16[512,512]{1,0:T(8,128)(2,1)} %get-tuple-element.51.refs_2_, bf16[512,512]{1,0:T(8,128)(2,1)} %get-tuple-element.52.refs_3_), custom_call_target="tpu_custom_call" | custom-call | flops 2000000000 | bytes 5242880 | tf_op jit(solution)/shard_map/pallas_call | solution.py:103
  82.5 0.0 collective-permute-done.2.refs_2_
  82.5 5.5 %collective-permute-done.3.refs_3_ = f32[64,512]{1,0:T(8,128)S(1)} collective-permute-done((f32[64,512]{1,0:T(8,128)S(1)}, f32[64,512]{1,0:T(8,128)S(1)}, u32[]{:S(2)}, u32[]{:S(2)}) %collective-permute-start.3) | collective-permute-done | bytes 131104 | tf_op jit(solution)/shard_map/ppermute | solution.py:287
  88.0 1.3 collective-permute-done.4.refs_4_
  89.4 1.4 collective-permute-start.5
  90.8 2.8 %collective-permute-start.6 = (f32[16,512]{1,0:T(8,128)S(1)}, f32[16,512]{1,0:T(8,128)S(1)}, u32[]{:S(2)}, u32[]{:S(2)}) collective-permute-start(f32[16,512]{1,0:T(8,128)S(1)} %get-tuple-element.59), channel_id=1, source_target_pairs={{0,128},{8,136},{16,144},{24,152},{32,160},{40,168},{48,176},{56,1... | collective-permute-start | bytes 98312 | tf_op jit(solution)/shard_map/ppermute | solution.py:287
  93.6 0.0 collective-permute-start.7
  93.6 0.0 collective-permute-done.5.refs_1_
  93.6 2.9 %collective-permute-done.6.refs_2_ = f32[16,512]{1,0:T(8,128)S(1)} collective-permute-done((f32[16,512]{1,0:T(8,128)S(1)}, f32[16,512]{1,0:T(8,128)S(1)}, u32[]{:S(2)}, u32[]{:S(2)}) %collective-permute-start.6) | collective-permute-done | bytes 32800 | tf_op jit(solution)/shard_map/ppermute | solution.py:287
  96.5 1.9 %collective-permute-done.7.refs_3_ = f32[16,512]{1,0:T(8,128)S(1)} collective-permute-done((f32[16,512]{1,0:T(8,128)S(1)}, f32[16,512]{1,0:T(8,128)S(1)}, u32[]{:S(2)}, u32[]{:S(2)}) %collective-permute-start.7) | collective-permute-done | bytes 32800 | tf_op jit(solution)/shard_map/ppermute | solution.py:287
  98.3 4.0 %collective-permute-start.10 = (f32[16,512]{1,0:T(8,128)S(1)}, f32[16,512]{1,0:T(8,128)S(1)}, u32[]{:S(2)}, u32[]{:S(2)}) collective-permute-start(f32[16,512]{1,0:T(8,128)S(1)} %shard_map.127.refs_0_), channel_id=1, source_target_pairs={{0,48},{8,56},{16,32},{24,40},{32,16},{40,24},{48,0},{56,8},{64,11... | collective-permute-start | bytes 98312 | tf_op jit(solution)/shard_map/ppermute | solution.py:287
  102.3 0.4 collective-permute-start.8
  102.8 1.8 %collective-permute-start.9 = (f32[16,512]{1,0:T(8,128)S(1)}, f32[16,512]{1,0:T(8,128)S(1)}, u32[]{:S(2)}, u32[]{:S(2)}) collective-permute-start(f32[16,512]{1,0:T(8,128)S(1)} %shard_map.127.refs_0_), channel_id=1, source_target_pairs={{0,32},{8,40},{16,48},{24,56},{32,0},{40,8},{48,16},{56,24},{64,96... | collective-permute-start | bytes 98312 | tf_op jit(solution)/shard_map/ppermute | solution.py:287
  104.5 0.0 collective-permute-done.10.refs_3_
  104.5 2.1 %collective-permute-done.8.refs_1_ = f32[16,512]{1,0:T(8,128)S(1)} collective-permute-done((f32[16,512]{1,0:T(8,128)S(1)}, f32[16,512]{1,0:T(8,128)S(1)}, u32[]{:S(2)}, u32[]{:S(2)}) %collective-permute-start.8) | collective-permute-done | bytes 32800 | tf_op jit(solution)/shard_map/ppermute | solution.py:287
  106.6 3.1 %collective-permute-done.9.refs_2_ = f32[16,512]{1,0:T(8,128)S(1)} collective-permute-done((f32[16,512]{1,0:T(8,128)S(1)}, f32[16,512]{1,0:T(8,128)S(1)}, u32[]{:S(2)}, u32[]{:S(2)}) %collective-permute-start.9) | collective-permute-done | bytes 32800 | tf_op jit(solution)/shard_map/ppermute | solution.py:287
  109.7 1.0 collective-permute-start.11
  110.7 2.5 %collective-permute-done.11.refs_1_ = f32[16,512]{1,0:T(8,128)S(1)} collective-permute-done((f32[16,512]{1,0:T(8,128)S(1)}, f32[16,512]{1,0:T(8,128)S(1)}, u32[]{:S(2)}, u32[]{:S(2)}) %collective-permute-start.11) | collective-permute-done | bytes 32800 | tf_op jit(solution)/shard_map/ppermute | solution.py:287
  113.2 0.0 all-to-all-done.2
  113.2 6.2 %collective-permute-start.18 = (f32[2048,128]{1,0:T(8,128)S(1)}, f32[2048,128]{1,0:T(8,128)S(1)}, u32[]{:S(2)}, u32[]{:S(2)}) collective-permute-start(f32[2048,128]{1,0:T(8,128)S(1)} %bitcast.16), channel_id=1, source_target_pairs={{0,1},{1,0},{2,3},{3,2},{4,5},{5,4},{6,7},{7,6},{8,9},{9,8},{10,11... | collective-permute-start | bytes 3145736 | tf_op jit(solution)/shard_map/ppermute | solution.py:282
  119.4 0.0 collective-permute-start.12
  119.4 1.2 collective-permute-start.13
  120.6 2.7 %collective-permute-start.14 = (f32[16,512]{1,0:T(8,128)S(1)}, f32[16,512]{1,0:T(8,128)S(1)}, u32[]{:S(2)}, u32[]{:S(2)}) collective-permute-start(f32[16,512]{1,0:T(8,128)S(1)} %shard_map.129.refs_1_), channel_id=1, source_target_pairs={{0,192},{8,200},{16,208},{24,216},{32,224},{40,232},{48,240},{56,2... | collective-permute-start | bytes 98312 | tf_op jit(solution)/shard_map/ppermute | solution.py:287
  123.3 4.5 %shard_map.130.refs_3_ = f32[1280,512]{1,0:T(8,128)} custom-call(s32[1]{0:T(128)} %bitcast.refs_0_, s32[2,512]{1,0:T(2,128)S(1)} %bitcast.19, f32[2048,128]{1,0:T(8,128)S(1)} %bitcast.17, f32[1280,512]{1,0:T(8,128)} %refs_3_.3), custom_call_target="tpu_custom_call" | custom-call | flops 2000000000 | bytes 6295556 | tf_op jit(solution)/shard_map/pallas_call | solution.py:103
  127.8 0.0 collective-permute-done.12.refs_2_
  127.8 0.0 collective-permute-done.13.refs_3_
  127.8 0.0 collective-permute-done.14.refs_4_
  127.8 0.1 collective-permute-start.15
  127.9 1.8 %collective-permute-start.16 = (f32[64,512]{1,0:T(8,128)S(1)}, f32[64,512]{1,0:T(8,128)S(1)}, u32[]{:S(2)}, u32[]{:S(2)}) collective-permute-start(f32[64,512]{1,0:T(8,128)S(1)} %shard_map.131.refs_1_), channel_id=1, source_target_pairs={{0,4},{2,6},{4,0},{6,2},{1,5},{3,7},{5,1},{7,3},{8,12},{10,14},{12... | collective-permute-start | bytes 393224 | tf_op jit(solution)/shard_map/ppermute | solution.py:287
  129.8 2.0 %collective-permute-start.17 = (f32[64,512]{1,0:T(8,128)S(1)}, f32[64,512]{1,0:T(8,128)S(1)}, u32[]{:S(2)}, u32[]{:S(2)}) collective-permute-start(f32[64,512]{1,0:T(8,128)S(1)} %shard_map.131.refs_1_), channel_id=1, source_target_pairs={{0,6},{2,4},{4,2},{6,0},{1,7},{3,5},{5,3},{7,1},{8,14},{10,12},{12... | collective-permute-start | bytes 393224 | tf_op jit(solution)/shard_map/ppermute | solution.py:287
  131.8 0.0 collective-permute-done.18.refs_2_
  131.8 4.5 %shard_map.132 = f32[1280,512]{1,0:T(8,128)} custom-call(s32[1]{0:T(128)S(6)} %sub.3.refs_0_, s32[2,512]{1,0:T(2,128)S(1)} %bitcast.20, f32[2048,128]{1,0:T(8,128)S(1)} %collective-permute-done.18.refs_2_, f32[1280,512]{1,0:T(8,128)} %shard_map.130.refs_3_), custom_call_target="tpu_custom_call" | custom-call | flops 2000000000 | bytes 6295556 | tf_op jit(solution)/shard_map/pallas_call | solution.py:103
  136.2 0.0 collective-permute-done.15.refs_2_
  136.3 0.0 collective-permute-done.16.refs_3_
  136.3 1.4 %collective-permute-done.17.refs_4_ = f32[64,512]{1,0:T(8,128)S(1)} collective-permute-done((f32[64,512]{1,0:T(8,128)S(1)}, f32[64,512]{1,0:T(8,128)S(1)}, u32[]{:S(2)}, u32[]{:S(2)}) %collective-permute-start.17) | collective-permute-done | bytes 131104 | tf_op jit(solution)/shard_map/ppermute | solution.py:287
  137.7 1.4 %collective-permute-start.19 = (f32[256,512]{1,0:T(8,128)S(1)}, f32[256,512]{1,0:T(8,128)S(1)}, u32[]{:S(2)}, u32[]{:S(2)}) collective-permute-start(f32[256,512]{1,0:T(8,128)S(1)} %shard_map.133.refs_1_), channel_id=1, source_target_pairs={{0,1},{1,0},{2,3},{3,2},{4,5},{5,4},{6,7},{7,6},{8,9},{9,8},{10,11... | collective-permute-start | bytes 1572872 | tf_op jit(solution)/shard_map/ppermute | solution.py:282
  139.2 1.5 %collective-permute-done.19.refs_2_ = f32[256,512]{1,0:T(8,128)S(1)} collective-permute-done((f32[256,512]{1,0:T(8,128)S(1)}, f32[256,512]{1,0:T(8,128)S(1)}, u32[]{:S(2)}, u32[]{:S(2)}) %collective-permute-start.19) | collective-permute-done | bytes 524320 | tf_op jit(solution)/shard_map/ppermute | solution.py:282
  140.7 1.1 shard_map.134
  (9 shorter events, 0.1 us)
Async XLA Ops:
  0.6 38.8 %collective-permute-start = (f32[1024,512]{1,0:T(8,128)}, f32[1024,512]{1,0:T(8,128)S(1)}, u32[]{:S(2)}, u32[]{:S(2)}) collective-permute-start(f32[1024,512]{1,0:T(8,128)} %refs_3_.2), channel_id=1, source_target_pairs={{0,1},{1,0},{2,3},{3,2},{4,5},{5,4},{6,7},{7,6},{8,9},{9,8},{10,11... | collective-permute-start | bytes 6291464 | tf_op jit(solution)/shard_map/ppermute | solution.py:282
  33.1 22.5 %all-to-all-start.1 = ((f32[128,8,128]{2,1,0:T(8,128)}), f32[128,8,128]{2,1,0:T(8,128)S(1)}, u32[]{:S(2)}, u32[]{:S(2)}) async-start(f32[128,8,128]{2,1,0:T(8,128)} %bitcast.26), calls=%async_computation.1 | async-start | bytes 1048576 | tf_op jit(solution)/shard_map/all_to_all | solution.py:278
  39.5 1.3 copy-start.3
  40.8 14.8 %copy-start = (s32[512,8]{0,1:T(8,128)S(1)}, s32[512,8]{0,1:T(8,128)}, u32[]{:S(2)}) copy-start(s32[512,8]{0,1:T(8,128)} %param.15) | copy-start | bytes 49156
  40.8 14.8 %copy-start.1 = (f32[512,8]{0,1:T(8,128)S(1)}, f32[512,8]{0,1:T(8,128)}, u32[]{:S(2)}) copy-start(f32[512,8]{0,1:T(8,128)} %param.14) | copy-start | bytes 49156
  55.6 17.2 %copy-start.2 = (s32[1,1024]{1,0:T(1,128)S(1)}, s32[1,1024]{1,0:T(1,128)}, u32[]{:S(2)}) copy-start(s32[1,1024]{1,0:T(1,128)} %param.19) | copy-start | bytes 12292
  61.2 52.0 %all-to-all-start.2 = ((f32[128,16,128]{2,1,0:T(8,128)}), f32[128,16,128]{2,1,0:T(8,128)S(1)}, u32[]{:S(2)}, u32[]{:S(2)}) async-start(f32[128,16,128]{2,1,0:T(8,128)} %bitcast.25), calls=%async_computation.2 | async-start | bytes 2097152 | tf_op jit(solution)/shard_map/all_to_all | solution.py:278
  69.9 3.9 %collective-permute-start.1 = (f32[256,512]{1,0:T(8,128)S(1)}, f32[256,512]{1,0:T(8,128)S(1)}, u32[]{:S(2)}, u32[]{:S(2)}) collective-permute-start(f32[256,512]{1,0:T(8,128)S(1)} %get-tuple-element.44), channel_id=1, source_target_pairs={{0,1},{1,0},{2,3},{3,2},{4,5},{5,4},{6,7},{7,6},{8,9},{9,8},{10,11... | collective-permute-start | bytes 1572872 | tf_op jit(solution)/shard_map/ppermute | solution.py:282
  73.9 8.6 %collective-permute-start.2 = (f32[64,512]{1,0:T(8,128)S(1)}, f32[64,512]{1,0:T(8,128)S(1)}, u32[]{:S(2)}, u32[]{:S(2)}) collective-permute-start(f32[64,512]{1,0:T(8,128)S(1)} %get-tuple-element.47), channel_id=1, source_target_pairs={{0,2},{2,0},{4,6},{6,4},{1,3},{3,1},{5,7},{7,5},{8,10},{10,8},{12,... | collective-permute-start | bytes 393224 | tf_op jit(solution)/shard_map/ppermute | solution.py:287
  74.8 13.2 %collective-permute-start.3 = (f32[64,512]{1,0:T(8,128)S(1)}, f32[64,512]{1,0:T(8,128)S(1)}, u32[]{:S(2)}, u32[]{:S(2)}) collective-permute-start(f32[64,512]{1,0:T(8,128)S(1)} %get-tuple-element.48), channel_id=1, source_target_pairs={{0,4},{2,6},{4,0},{6,2},{1,5},{3,7},{5,1},{7,3},{8,12},{10,14},{12... | collective-permute-start | bytes 393224 | tf_op jit(solution)/shard_map/ppermute | solution.py:287
  77.2 12.1 %collective-permute-start.4 = (f32[64,512]{1,0:T(8,128)S(1)}, f32[64,512]{1,0:T(8,128)S(1)}, u32[]{:S(2)}, u32[]{:S(2)}) collective-permute-start(f32[64,512]{1,0:T(8,128)S(1)} %get-tuple-element.49), channel_id=1, source_target_pairs={{0,6},{2,4},{4,2},{6,0},{1,7},{3,5},{5,3},{7,1},{8,14},{10,12},{12... | collective-permute-start | bytes 393224 | tf_op jit(solution)/shard_map/ppermute | solution.py:287
  89.4 4.2 %collective-permute-start.5 = (f32[16,512]{1,0:T(8,128)S(1)}, f32[16,512]{1,0:T(8,128)S(1)}, u32[]{:S(2)}, u32[]{:S(2)}) collective-permute-start(f32[16,512]{1,0:T(8,128)S(1)} %get-tuple-element.58), channel_id=1, source_target_pairs={{0,64},{8,72},{16,80},{24,88},{32,96},{40,104},{48,112},{56,120},{... | collective-permute-start | bytes 98312 | tf_op jit(solution)/shard_map/ppermute | solution.py:287
  90.8 5.7 %collective-permute-start.6 = (f32[16,512]{1,0:T(8,128)S(1)}, f32[16,512]{1,0:T(8,128)S(1)}, u32[]{:S(2)}, u32[]{:S(2)}) collective-permute-start(f32[16,512]{1,0:T(8,128)S(1)} %get-tuple-element.59), channel_id=1, source_target_pairs={{0,128},{8,136},{16,144},{24,152},{32,160},{40,168},{48,176},{56,1... | collective-permute-start | bytes 98312 | tf_op jit(solution)/shard_map/ppermute | solution.py:287
  93.6 4.7 %collective-permute-start.7 = (f32[16,512]{1,0:T(8,128)S(1)}, f32[16,512]{1,0:T(8,128)S(1)}, u32[]{:S(2)}, u32[]{:S(2)}) collective-permute-start(f32[16,512]{1,0:T(8,128)S(1)} %get-tuple-element.60), channel_id=1, source_target_pairs={{0,192},{8,200},{16,208},{24,216},{32,224},{40,232},{48,240},{56,2... | collective-permute-start | bytes 98312 | tf_op jit(solution)/shard_map/ppermute | solution.py:287
  98.3 6.2 %collective-permute-start.10 = (f32[16,512]{1,0:T(8,128)S(1)}, f32[16,512]{1,0:T(8,128)S(1)}, u32[]{:S(2)}, u32[]{:S(2)}) collective-permute-start(f32[16,512]{1,0:T(8,128)S(1)} %shard_map.127.refs_0_), channel_id=1, source_target_pairs={{0,48},{8,56},{16,32},{24,40},{32,16},{40,24},{48,0},{56,8},{64,11... | collective-permute-start | bytes 98312 | tf_op jit(solution)/shard_map/ppermute | solution.py:287
  102.3 4.3 %collective-permute-start.8 = (f32[16,512]{1,0:T(8,128)S(1)}, f32[16,512]{1,0:T(8,128)S(1)}, u32[]{:S(2)}, u32[]{:S(2)}) collective-permute-start(f32[16,512]{1,0:T(8,128)S(1)} %shard_map.127.refs_0_), channel_id=1, source_target_pairs={{0,16},{8,24},{16,0},{24,8},{32,48},{40,56},{48,32},{56,40},{64,80... | collective-permute-start | bytes 98312 | tf_op jit(solution)/shard_map/ppermute | solution.py:287
  102.8 6.9 %collective-permute-start.9 = (f32[16,512]{1,0:T(8,128)S(1)}, f32[16,512]{1,0:T(8,128)S(1)}, u32[]{:S(2)}, u32[]{:S(2)}) collective-permute-start(f32[16,512]{1,0:T(8,128)S(1)} %shard_map.127.refs_0_), channel_id=1, source_target_pairs={{0,32},{8,40},{16,48},{24,56},{32,0},{40,8},{48,16},{56,24},{64,96... | collective-permute-start | bytes 98312 | tf_op jit(solution)/shard_map/ppermute | solution.py:287
  109.7 3.5 %collective-permute-start.11 = (f32[16,512]{1,0:T(8,128)S(1)}, f32[16,512]{1,0:T(8,128)S(1)}, u32[]{:S(2)}, u32[]{:S(2)}) collective-permute-start(f32[16,512]{1,0:T(8,128)S(1)} %shard_map.128.refs_0_), channel_id=1, source_target_pairs={{0,8},{8,0},{16,24},{24,16},{32,40},{40,32},{48,56},{56,48},{64,72... | collective-permute-start | bytes 98312 | tf_op jit(solution)/shard_map/ppermute | solution.py:287
  113.2 18.5 %collective-permute-start.18 = (f32[2048,128]{1,0:T(8,128)S(1)}, f32[2048,128]{1,0:T(8,128)S(1)}, u32[]{:S(2)}, u32[]{:S(2)}) collective-permute-start(f32[2048,128]{1,0:T(8,128)S(1)} %bitcast.16), channel_id=1, source_target_pairs={{0,1},{1,0},{2,3},{3,2},{4,5},{5,4},{6,7},{7,6},{8,9},{9,8},{10,11... | collective-permute-start | bytes 3145736 | tf_op jit(solution)/shard_map/ppermute | solution.py:282
  119.4 8.4 %collective-permute-start.12 = (f32[16,512]{1,0:T(8,128)S(1)}, f32[16,512]{1,0:T(8,128)S(1)}, u32[]{:S(2)}, u32[]{:S(2)}) collective-permute-start(f32[16,512]{1,0:T(8,128)S(1)} %shard_map.129.refs_1_), channel_id=1, source_target_pairs={{0,64},{8,72},{16,80},{24,88},{32,96},{40,104},{48,112},{56,120},{... | collective-permute-start | bytes 98312 | tf_op jit(solution)/shard_map/ppermute | solution.py:287
  119.4 8.4 %collective-permute-start.13 = (f32[16,512]{1,0:T(8,128)S(1)}, f32[16,512]{1,0:T(8,128)S(1)}, u32[]{:S(2)}, u32[]{:S(2)}) collective-permute-start(f32[16,512]{1,0:T(8,128)S(1)} %shard_map.129.refs_1_), channel_id=1, source_target_pairs={{0,128},{8,136},{16,144},{24,152},{32,160},{40,168},{48,176},{56,1... | collective-permute-start | bytes 98312 | tf_op jit(solution)/shard_map/ppermute | solution.py:287
  120.6 7.2 %collective-permute-start.14 = (f32[16,512]{1,0:T(8,128)S(1)}, f32[16,512]{1,0:T(8,128)S(1)}, u32[]{:S(2)}, u32[]{:S(2)}) collective-permute-start(f32[16,512]{1,0:T(8,128)S(1)} %shard_map.129.refs_1_), channel_id=1, source_target_pairs={{0,192},{8,200},{16,208},{24,216},{32,224},{40,232},{48,240},{56,2... | collective-permute-start | bytes 98312 | tf_op jit(solution)/shard_map/ppermute | solution.py:287
  127.8 8.4 %collective-permute-start.15 = (f32[64,512]{1,0:T(8,128)S(1)}, f32[64,512]{1,0:T(8,128)S(1)}, u32[]{:S(2)}, u32[]{:S(2)}) collective-permute-start(f32[64,512]{1,0:T(8,128)S(1)} %shard_map.131.refs_1_), channel_id=1, source_target_pairs={{0,2},{2,0},{4,6},{6,4},{1,3},{3,1},{5,7},{7,5},{8,10},{10,8},{12,... | collective-permute-start | bytes 393224 | tf_op jit(solution)/shard_map/ppermute | solution.py:287
  127.9 8.3 %collective-permute-start.16 = (f32[64,512]{1,0:T(8,128)S(1)}, f32[64,512]{1,0:T(8,128)S(1)}, u32[]{:S(2)}, u32[]{:S(2)}) collective-permute-start(f32[64,512]{1,0:T(8,128)S(1)} %shard_map.131.refs_1_), channel_id=1, source_target_pairs={{0,4},{2,6},{4,0},{6,2},{1,5},{3,7},{5,1},{7,3},{8,12},{10,14},{12... | collective-permute-start | bytes 393224 | tf_op jit(solution)/shard_map/ppermute | solution.py:287
  129.8 7.9 %collective-permute-start.17 = (f32[64,512]{1,0:T(8,128)S(1)}, f32[64,512]{1,0:T(8,128)S(1)}, u32[]{:S(2)}, u32[]{:S(2)}) collective-permute-start(f32[64,512]{1,0:T(8,128)S(1)} %shard_map.131.refs_1_), channel_id=1, source_target_pairs={{0,6},{2,4},{4,2},{6,0},{1,7},{3,5},{5,3},{7,1},{8,14},{10,12},{12... | collective-permute-start | bytes 393224 | tf_op jit(solution)/shard_map/ppermute | solution.py:287
  137.7 3.0 %collective-permute-start.19 = (f32[256,512]{1,0:T(8,128)S(1)}, f32[256,512]{1,0:T(8,128)S(1)}, u32[]{:S(2)}, u32[]{:S(2)}) collective-permute-start(f32[256,512]{1,0:T(8,128)S(1)} %shard_map.133.refs_1_), channel_id=1, source_target_pairs={{0,1},{1,0},{2,3},{3,2},{4,5},{5,4},{6,7},{7,6},{8,9},{9,8},{10,11... | collective-permute-start | bytes 1572872 | tf_op jit(solution)/shard_map/ppermute | solution.py:282

commit v7 on v6

--- a/solution.py
+++ b/solution.py
@@ -388,8 +388,10 @@
     pieces = trade(scatter(at_y, *pieces), "batch", depth)
     arrived = exchange(outgoing.reshape(owners * 16, 128))
     summed = total(*pieces)
-    summed = total(summed, *[move(summed, "batch", mask) for mask in (2, 4, 6)])
-    summed = total(summed, move(summed, "batch", 1))
+    mask = 1
+    while mask < depth:
+        summed = total(summed, move(summed, "batch", mask))
+        mask *= 2
     arrived, summed = together(arrived, summed)
     arrived_other = swap(arrived)
     parts = trade([summed] * 4, "batch", depth)

time: 142 us -> 141 us (level)
    ppermute x16 -> x15, waiting for transfers between devices: 20.7 us -> 18.4 us  [move(): return lax.ppermute(v, axis, [(i, i ^ mask) for i in range(count)])]
    ppermute x16 -> x15, starting transfers between devices: 23.2 us -> 23.8 us  [move(): return lax.ppermute(v, axis, [(i, i ^ mask) for i in range(count)])]
    pallas_call x14 -> x15, Pallas kernels: 31.8 us -> 31.8 us  [call(): pl.pallas_call(wrapped, out_shape=[jax.ShapeDtypeStruct(*o) for o in outs...]
  transfers between devices with their start and end apart: 22 -> 21, of which waited for: 11 -> 11; matrix products, arithmetic and copies ran while one was open for 2% -> 2% of each run, Pallas kernels for 18% -> 18%
where the time goes in v7:
time: 141 us; the launch traced here: 140 us
  starting transfers between devices  52.5 us (37%)
  Pallas kernels  31.8 us (23%)
  waiting for transfers between devices  28.7 us (20%)
  blocking collectives  24.4 us (17%)
  local copies, waits for them, and re-layouts  1.52 us (1%)
    pallas_call x15, Pallas kernels, call(): pl.pallas_call(wrapped, out_shape=[jax.ShapeDtypeStruct(*o) for o in outs...  31.8 us
    all_to_all x1, blocking collectives, exchange(): return lax.all_to_all(v, OWN, split_axis=0, concat_axis=0, tiled=True)  24.4 us
    ppermute x15, starting transfers between devices, move(): return lax.ppermute(v, axis, [(i, i ^ mask) for i in range(count)])  23.8 us
    ppermute x15, waiting for transfers between devices, move(): return lax.ppermute(v, axis, [(i, i ^ mask) for i in range(count)])  18.4 us
    all_to_all x2, starting transfers between devices, exchange(): return lax.all_to_all(v, OWN, split_axis=0, concat_axis=0, tiled=True)  15.1 us
    ppermute x4, starting transfers between devices, swap(): return lax.ppermute(v, 'rep', [(0, 1), (1, 0)])  13.6 us
    all_to_all x2, waiting for transfers between devices, exchange(): return lax.all_to_all(v, OWN, split_axis=0, concat_axis=0, tiled=True)  8.64 us
  transfers between devices with their start and end apart: 21, of which 11 were waited for; matrix products, arithmetic and copies ran while one was open for 2% of the time, Pallas kernels for 18%

profile of v7, /device:TPU:1, one launch (start us, length us, event | category | flops | bytes accessed | tf_op | source)
XLA Modules:
  0.0 140.4 jit_solution(12823375053070774205)
XLA Ops:
  0.6 3.3 %collective-permute-start = (f32[1024,512]{1,0:T(8,128)}, f32[1024,512]{1,0:T(8,128)}, u32[]{:S(2)}, u32[]{:S(2)}) collective-permute-start(f32[1024,512]{1,0:T(8,128)} %refs_3_.2), channel_id=1, source_target_pairs={{0,1},{1,0},{2,3},{3,2},{4,5},{5,4},{6,7},{7,6},{8,9},{9,8},{10,11... | collective-permute-start | bytes 6291464 | tf_op jit(solution)/shard_map/ppermute | solution.py:282
  4.0 0.8 copy.17
  4.7 24.4 %all_to_all.35 = s32[128,1,2]{2,1,0:T(1,128)} all-to-all(s32[128,1,2]{2,1,0:T(1,128)S(1)} %bitcast.28), channel_id=1, replica_groups=mesh['batch'=32,'hist'=4,'rep'=2] {'batch','hist'}, dimensions={0} | all-to-all | bytes 2048 | tf_op jit(solution)/shard_map/all_to_all | solution.py:278
  29.1 3.9 %shard_map.121 = f32[1024,128]{1,0:T(8,128)} custom-call(s32[128,2]{1,0:T(8,128)} %bitcast.29, f32[1280,512]{1,0:T(8,128)} %refs_3_.3), custom_call_target="tpu_custom_call" | custom-call | flops 1000000000 | bytes 3146752 | tf_op jit(solution)/shard_map/pallas_call | solution.py:103
  33.1 6.4 %all-to-all-start.1 = ((f32[128,8,128]{2,1,0:T(8,128)}), f32[128,8,128]{2,1,0:T(8,128)S(1)}, u32[]{:S(2)}, u32[]{:S(2)}) async-start(f32[128,8,128]{2,1,0:T(8,128)} %bitcast.26), calls=%async_computation.1 | async-start | bytes 1048576 | tf_op jit(solution)/shard_map/all_to_all | solution.py:278
  39.5 0.0 collective-permute-done.refs_4_
  39.5 0.0 copy-start
  39.5 0.0 copy-start.1
  39.5 7.5 %shard_map.122 = (f32[512,512]{1,0:T(8,128)}, bf16[512,512]{1,0:T(8,128)(2,1)}, bf16[512,512]{1,0:T(8,128)(2,1)}) custom-call(s32[1]{0:T(128)} %bitcast.refs_0_, s32[8,512]{1,0:T(8,128)} %bitcast.21, f32[8,512]{1,0:T(8,128)} %bitcast.23, f32[1024,512]{1,0:T(8,128)} %refs_3_.2, f32[1024,512]{1,0:T(8,128)} %collective-permute-done.refs_4_, ...), custom_call_target="tpu_custom_call" | custom-call | flops 6000000000 | bytes 9469956 | tf_op jit(solution)/shard_map/pallas_call | solution.py:103
  47.0 8.6 %all-to-all-done.1 = f32[128,8,128]{2,1,0:T(8,128)S(1)} async-done(((f32[128,8,128]{2,1,0:T(8,128)}), f32[128,8,128]{2,1,0:T(8,128)S(1)}, u32[]{:S(2)}, u32[]{:S(2)}) %all-to-all-start.1) | async-done | bytes 524320 | tf_op jit(solution)/shard_map/all_to_all | solution.py:278
  55.6 0.0 copy-done
  55.6 0.0 copy-done.1
  55.6 0.0 copy-start.2
  55.6 5.6 %shard_map.123 = (f32[32,4,16,128]{3,2,1,0:T(8,128)}, f32[256,512]{1,0:T(8,128)S(1)}, f32[256,512]{1,0:T(8,128)S(1)}, f32[512,512]{1,0:T(8,128)}) custom-call(s32[1]{0:T(128)} %bitcast.refs_0_, f32[1024,128]{1,0:T(8,128)S(1)} %bitcast.18, s32[8,512]{1,0:T(8,128)S(1)} %bitcast.22, f32[8,512]{1,0:T(8,128)S(1)} %bitcast.24, ...), custom_call_target="tpu_custom_call" | custom-call | flops 3000000000 | bytes 6848516 | tf_op jit(solution)/shard_map/pallas_call | solution.py:103
  61.2 8.7 %all-to-all-start.2 = ((f32[128,16,128]{2,1,0:T(8,128)}), f32[128,16,128]{2,1,0:T(8,128)S(1)}, u32[]{:S(2)}, u32[]{:S(2)}) async-start(f32[128,16,128]{2,1,0:T(8,128)} %bitcast.25), calls=%async_computation.2 | async-start | bytes 2097152 | tf_op jit(solution)/shard_map/all_to_all | solution.py:278
  70.0 2.3 %collective-permute-start.1 = (f32[256,512]{1,0:T(8,128)S(1)}, f32[256,512]{1,0:T(8,128)S(1)}, u32[]{:S(2)}, u32[]{:S(2)}) collective-permute-start(f32[256,512]{1,0:T(8,128)S(1)} %get-tuple-element.44), channel_id=1, source_target_pairs={{0,1},{1,0},{2,3},{3,2},{4,5},{5,4},{6,7},{7,6},{8,9},{9,8},{10,11... | collective-permute-start | bytes 1572872 | tf_op jit(solution)/shard_map/ppermute | solution.py:282
  72.3 0.5 broadcast.3
  72.8 0.0 copy-done.2
  72.8 0.7 reduce.3
  73.5 0.1 reshape.33
  73.6 0.1 copy.18
  73.7 0.1 collective-permute-done.1.refs_2_
  73.8 0.1 shard_map.124
  73.9 0.9 collective-permute-start.2
  74.8 2.4 %collective-permute-start.3 = (f32[64,512]{1,0:T(8,128)S(1)}, f32[64,512]{1,0:T(8,128)S(1)}, u32[]{:S(2)}, u32[]{:S(2)}) collective-permute-start(f32[64,512]{1,0:T(8,128)S(1)} %get-tuple-element.48), channel_id=1, source_target_pairs={{0,4},{2,6},{4,0},{6,2},{1,5},{3,7},{5,1},{7,3},{8,12},{10,14},{12... | collective-permute-start | bytes 393224 | tf_op jit(solution)/shard_map/ppermute | solution.py:287
  77.2 0.6 collective-permute-start.4
  77.8 4.6 %shard_map.125 = f32[512,512]{1,0:T(8,128)} custom-call(f32[512,512]{1,0:T(8,128)} %get-tuple-element.50.refs_0_, f32[512,512]{1,0:T(8,128)} %refs_1_.3, bf16[512,512]{1,0:T(8,128)(2,1)} %get-tuple-element.51.refs_2_, bf16[512,512]{1,0:T(8,128)(2,1)} %get-tuple-element.52.refs_3_), custom_call_target="tpu_custom_call" | custom-call | flops 2000000000 | bytes 5242880 | tf_op jit(solution)/shard_map/pallas_call | solution.py:103
  82.5 0.0 collective-permute-done.2.refs_2_
  82.5 5.5 %collective-permute-done.3.refs_3_ = f32[64,512]{1,0:T(8,128)S(1)} collective-permute-done((f32[64,512]{1,0:T(8,128)S(1)}, f32[64,512]{1,0:T(8,128)S(1)}, u32[]{:S(2)}, u32[]{:S(2)}) %collective-permute-start.3) | collective-permute-done | bytes 131104 | tf_op jit(solution)/shard_map/ppermute | solution.py:287
  88.0 1.4 collective-permute-done.4.refs_4_
  89.4 1.4 collective-permute-start.5
  90.8 2.8 %collective-permute-start.6 = (f32[16,512]{1,0:T(8,128)S(1)}, f32[16,512]{1,0:T(8,128)S(1)}, u32[]{:S(2)}, u32[]{:S(2)}) collective-permute-start(f32[16,512]{1,0:T(8,128)S(1)} %get-tuple-element.59), channel_id=1, source_target_pairs={{0,128},{8,136},{16,144},{24,152},{32,160},{40,168},{48,176},{56,1... | collective-permute-start | bytes 98312 | tf_op jit(solution)/shard_map/ppermute | solution.py:287
  93.6 0.0 collective-permute-start.7
  93.6 0.0 collective-permute-done.5.refs_1_
  93.6 2.9 %collective-permute-done.6.refs_2_ = f32[16,512]{1,0:T(8,128)S(1)} collective-permute-done((f32[16,512]{1,0:T(8,128)S(1)}, f32[16,512]{1,0:T(8,128)S(1)}, u32[]{:S(2)}, u32[]{:S(2)}) %collective-permute-start.6) | collective-permute-done | bytes 32800 | tf_op jit(solution)/shard_map/ppermute | solution.py:287
  96.5 1.9 %collective-permute-done.7.refs_3_ = f32[16,512]{1,0:T(8,128)S(1)} collective-permute-done((f32[16,512]{1,0:T(8,128)S(1)}, f32[16,512]{1,0:T(8,128)S(1)}, u32[]{:S(2)}, u32[]{:S(2)}) %collective-permute-start.7) | collective-permute-done | bytes 32800 | tf_op jit(solution)/shard_map/ppermute | solution.py:287
  98.4 1.6 %collective-permute-start.8 = (f32[16,512]{1,0:T(8,128)S(1)}, f32[16,512]{1,0:T(8,128)S(1)}, u32[]{:S(2)}, u32[]{:S(2)}) collective-permute-start(f32[16,512]{1,0:T(8,128)S(1)} %shard_map.127.refs_0_), channel_id=1, source_target_pairs={{0,8},{8,0},{16,24},{24,16},{32,40},{40,32},{48,56},{56,48},{64,72... | collective-permute-start | bytes 98312 | tf_op jit(solution)/shard_map/ppermute | solution.py:287
  99.9 1.3 collective-permute-done.8.refs_1_
  101.2 2.1 %collective-permute-start.9 = (f32[16,512]{1,0:T(8,128)S(1)}, f32[16,512]{1,0:T(8,128)S(1)}, u32[]{:S(2)}, u32[]{:S(2)}) collective-permute-start(f32[16,512]{1,0:T(8,128)S(1)} %shard_map.128.refs_0_), channel_id=1, source_target_pairs={{0,16},{8,24},{16,0},{24,8},{32,48},{40,56},{48,32},{56,40},{64,80... | collective-permute-start | bytes 98312 | tf_op jit(solution)/shard_map/ppermute | solution.py:287
  103.3 1.7 %collective-permute-done.9.refs_1_ = f32[16,512]{1,0:T(8,128)S(1)} collective-permute-done((f32[16,512]{1,0:T(8,128)S(1)}, f32[16,512]{1,0:T(8,128)S(1)}, u32[]{:S(2)}, u32[]{:S(2)}) %collective-permute-start.9) | collective-permute-done | bytes 32800 | tf_op jit(solution)/shard_map/ppermute | solution.py:287
  105.0 4.2 %collective-permute-start.10 = (f32[16,512]{1,0:T(8,128)S(1)}, f32[16,512]{1,0:T(8,128)S(1)}, u32[]{:S(2)}, u32[]{:S(2)}) collective-permute-start(f32[16,512]{1,0:T(8,128)S(1)} %shard_map.129.refs_0_), channel_id=1, source_target_pairs={{0,32},{8,40},{16,48},{24,56},{32,0},{40,8},{48,16},{56,24},{64,96... | collective-permute-start | bytes 98312 | tf_op jit(solution)/shard_map/ppermute | solution.py:287
  109.2 2.4 %collective-permute-done.10.refs_1_ = f32[16,512]{1,0:T(8,128)S(1)} collective-permute-done((f32[16,512]{1,0:T(8,128)S(1)}, f32[16,512]{1,0:T(8,128)S(1)}, u32[]{:S(2)}, u32[]{:S(2)}) %collective-permute-start.10) | collective-permute-done | bytes 32800 | tf_op jit(solution)/shard_map/ppermute | solution.py:287
  111.7 0.0 all-to-all-done.2
  111.7 6.5 %collective-permute-start.17 = (f32[2048,128]{1,0:T(8,128)S(1)}, f32[2048,128]{1,0:T(8,128)S(1)}, u32[]{:S(2)}, u32[]{:S(2)}) collective-permute-start(f32[2048,128]{1,0:T(8,128)S(1)} %bitcast.16), channel_id=1, source_target_pairs={{0,1},{1,0},{2,3},{3,2},{4,5},{5,4},{6,7},{7,6},{8,9},{9,8},{10,11... | collective-permute-start | bytes 3145736 | tf_op jit(solution)/shard_map/ppermute | solution.py:282
  118.2 0.0 collective-permute-start.11
  118.2 0.9 collective-permute-start.12
  119.1 3.0 %collective-permute-start.13 = (f32[16,512]{1,0:T(8,128)S(1)}, f32[16,512]{1,0:T(8,128)S(1)}, u32[]{:S(2)}, u32[]{:S(2)}) collective-permute-start(f32[16,512]{1,0:T(8,128)S(1)} %shard_map.130.refs_1_), channel_id=1, source_target_pairs={{0,192},{8,200},{16,208},{24,216},{32,224},{40,232},{48,240},{56,2... | collective-permute-start | bytes 98312 | tf_op jit(solution)/shard_map/ppermute | solution.py:287
  122.1 4.5 %shard_map.131.refs_3_ = f32[1280,512]{1,0:T(8,128)} custom-call(s32[1]{0:T(128)} %bitcast.refs_0_, s32[2,512]{1,0:T(2,128)S(1)} %bitcast.19, f32[2048,128]{1,0:T(8,128)S(1)} %bitcast.17, f32[1280,512]{1,0:T(8,128)} %refs_3_.3), custom_call_target="tpu_custom_call" | custom-call | flops 2000000000 | bytes 6295556 | tf_op jit(solution)/shard_map/pallas_call | solution.py:103
  126.5 0.0 collective-permute-done.11.refs_2_
  126.5 0.0 collective-permute-done.12.refs_3_
  126.5 0.0 collective-permute-done.13.refs_4_
  126.6 0.1 collective-permute-start.14
  126.7 1.8 %collective-permute-start.15 = (f32[64,512]{1,0:T(8,128)S(1)}, f32[64,512]{1,0:T(8,128)S(1)}, u32[]{:S(2)}, u32[]{:S(2)}) collective-permute-start(f32[64,512]{1,0:T(8,128)S(1)} %shard_map.132.refs_1_), channel_id=1, source_target_pairs={{0,4},{2,6},{4,0},{6,2},{1,5},{3,7},{5,1},{7,3},{8,12},{10,14},{12... | collective-permute-start | bytes 393224 | tf_op jit(solution)/shard_map/ppermute | solution.py:287
  128.4 2.1 %collective-permute-start.16 = (f32[64,512]{1,0:T(8,128)S(1)}, f32[64,512]{1,0:T(8,128)S(1)}, u32[]{:S(2)}, u32[]{:S(2)}) collective-permute-start(f32[64,512]{1,0:T(8,128)S(1)} %shard_map.132.refs_1_), channel_id=1, source_target_pairs={{0,6},{2,4},{4,2},{6,0},{1,7},{3,5},{5,3},{7,1},{8,14},{10,12},{12... | collective-permute-start | bytes 393224 | tf_op jit(solution)/shard_map/ppermute | solution.py:287
  130.5 0.0 collective-permute-done.17.refs_2_
  130.5 4.5 %shard_map.133 = f32[1280,512]{1,0:T(8,128)} custom-call(s32[1]{0:T(128)S(6)} %sub.3.refs_0_, s32[2,512]{1,0:T(2,128)S(1)} %bitcast.20, f32[2048,128]{1,0:T(8,128)S(1)} %collective-permute-done.17.refs_2_, f32[1280,512]{1,0:T(8,128)} %shard_map.131.refs_3_), custom_call_target="tpu_custom_call" | custom-call | flops 2000000000 | bytes 6295556 | tf_op jit(solution)/shard_map/pallas_call | solution.py:103
  135.0 0.0 collective-permute-done.14.refs_2_
  135.0 0.0 collective-permute-done.15.refs_3_
  135.0 1.3 collective-permute-done.16.refs_4_
  136.4 1.4 %collective-permute-start.18 = (f32[256,512]{1,0:T(8,128)S(1)}, f32[256,512]{1,0:T(8,128)S(1)}, u32[]{:S(2)}, u32[]{:S(2)}) collective-permute-start(f32[256,512]{1,0:T(8,128)S(1)} %shard_map.134.refs_1_), channel_id=1, source_target_pairs={{0,1},{1,0},{2,3},{3,2},{4,5},{5,4},{6,7},{7,6},{8,9},{9,8},{10,11... | collective-permute-start | bytes 1572872 | tf_op jit(solution)/shard_map/ppermute | solution.py:282
  137.8 1.5 %collective-permute-done.18.refs_2_ = f32[256,512]{1,0:T(8,128)S(1)} collective-permute-done((f32[256,512]{1,0:T(8,128)S(1)}, f32[256,512]{1,0:T(8,128)S(1)}, u32[]{:S(2)}, u32[]{:S(2)}) %collective-permute-start.18) | collective-permute-done | bytes 524320 | tf_op jit(solution)/shard_map/ppermute | solution.py:282
  139.4 1.1 shard_map.135
  (8 shorter events, 0.1 us)
Async XLA Ops:
  0.6 38.8 %collective-permute-start = (f32[1024,512]{1,0:T(8,128)}, f32[1024,512]{1,0:T(8,128)}, u32[]{:S(2)}, u32[]{:S(2)}) collective-permute-start(f32[1024,512]{1,0:T(8,128)} %refs_3_.2), channel_id=1, source_target_pairs={{0,1},{1,0},{2,3},{3,2},{4,5},{5,4},{6,7},{7,6},{8,9},{9,8},{10,11... | collective-permute-start | bytes 6291464 | tf_op jit(solution)/shard_map/ppermute | solution.py:282
  33.1 22.5 %all-to-all-start.1 = ((f32[128,8,128]{2,1,0:T(8,128)}), f32[128,8,128]{2,1,0:T(8,128)S(1)}, u32[]{:S(2)}, u32[]{:S(2)}) async-start(f32[128,8,128]{2,1,0:T(8,128)} %bitcast.26), calls=%async_computation.1 | async-start | bytes 1048576 | tf_op jit(solution)/shard_map/all_to_all | solution.py:278
  39.5 16.1 %copy-start = (s32[512,8]{0,1:T(8,128)S(1)}, s32[512,8]{0,1:T(8,128)}, u32[]{:S(2)}) copy-start(s32[512,8]{0,1:T(8,128)} %param.15) | copy-start | bytes 49156
  39.5 16.1 %copy-start.1 = (f32[512,8]{0,1:T(8,128)S(1)}, f32[512,8]{0,1:T(8,128)}, u32[]{:S(2)}) copy-start(f32[512,8]{0,1:T(8,128)} %param.14) | copy-start | bytes 49156
  55.6 17.2 %copy-start.2 = (s32[1,1024]{1,0:T(1,128)S(1)}, s32[1,1024]{1,0:T(1,128)}, u32[]{:S(2)}) copy-start(s32[1,1024]{1,0:T(1,128)} %param.19) | copy-start | bytes 12292
  61.2 50.4 %all-to-all-start.2 = ((f32[128,16,128]{2,1,0:T(8,128)}), f32[128,16,128]{2,1,0:T(8,128)S(1)}, u32[]{:S(2)}, u32[]{:S(2)}) async-start(f32[128,16,128]{2,1,0:T(8,128)} %bitcast.25), calls=%async_computation.2 | async-start | bytes 2097152 | tf_op jit(solution)/shard_map/all_to_all | solution.py:278
  70.0 3.9 %collective-permute-start.1 = (f32[256,512]{1,0:T(8,128)S(1)}, f32[256,512]{1,0:T(8,128)S(1)}, u32[]{:S(2)}, u32[]{:S(2)}) collective-permute-start(f32[256,512]{1,0:T(8,128)S(1)} %get-tuple-element.44), channel_id=1, source_target_pairs={{0,1},{1,0},{2,3},{3,2},{4,5},{5,4},{6,7},{7,6},{8,9},{9,8},{10,11... | collective-permute-start | bytes 1572872 | tf_op jit(solution)/shard_map/ppermute | solution.py:282
  73.9 8.6 %collective-permute-start.2 = (f32[64,512]{1,0:T(8,128)S(1)}, f32[64,512]{1,0:T(8,128)S(1)}, u32[]{:S(2)}, u32[]{:S(2)}) collective-permute-start(f32[64,512]{1,0:T(8,128)S(1)} %get-tuple-element.47), channel_id=1, source_target_pairs={{0,2},{2,0},{4,6},{6,4},{1,3},{3,1},{5,7},{7,5},{8,10},{10,8},{12,... | collective-permute-start | bytes 393224 | tf_op jit(solution)/shard_map/ppermute | solution.py:287
  74.8 13.2 %collective-permute-start.3 = (f32[64,512]{1,0:T(8,128)S(1)}, f32[64,512]{1,0:T(8,128)S(1)}, u32[]{:S(2)}, u32[]{:S(2)}) collective-permute-start(f32[64,512]{1,0:T(8,128)S(1)} %get-tuple-element.48), channel_id=1, source_target_pairs={{0,4},{2,6},{4,0},{6,2},{1,5},{3,7},{5,1},{7,3},{8,12},{10,14},{12... | collective-permute-start | bytes 393224 | tf_op jit(solution)/shard_map/ppermute | solution.py:287
  77.2 12.1 %collective-permute-start.4 = (f32[64,512]{1,0:T(8,128)S(1)}, f32[64,512]{1,0:T(8,128)S(1)}, u32[]{:S(2)}, u32[]{:S(2)}) collective-permute-start(f32[64,512]{1,0:T(8,128)S(1)} %get-tuple-element.49), channel_id=1, source_target_pairs={{0,6},{2,4},{4,2},{6,0},{1,7},{3,5},{5,3},{7,1},{8,14},{10,12},{12... | collective-permute-start | bytes 393224 | tf_op jit(solution)/shard_map/ppermute | solution.py:287
  89.4 4.2 %collective-permute-start.5 = (f32[16,512]{1,0:T(8,128)S(1)}, f32[16,512]{1,0:T(8,128)S(1)}, u32[]{:S(2)}, u32[]{:S(2)}) collective-permute-start(f32[16,512]{1,0:T(8,128)S(1)} %get-tuple-element.58), channel_id=1, source_target_pairs={{0,64},{8,72},{16,80},{24,88},{32,96},{40,104},{48,112},{56,120},{... | collective-permute-start | bytes 98312 | tf_op jit(solution)/shard_map/ppermute | solution.py:287
  90.8 5.7 %collective-permute-start.6 = (f32[16,512]{1,0:T(8,128)S(1)}, f32[16,512]{1,0:T(8,128)S(1)}, u32[]{:S(2)}, u32[]{:S(2)}) collective-permute-start(f32[16,512]{1,0:T(8,128)S(1)} %get-tuple-element.59), channel_id=1, source_target_pairs={{0,128},{8,136},{16,144},{24,152},{32,160},{40,168},{48,176},{56,1... | collective-permute-start | bytes 98312 | tf_op jit(solution)/shard_map/ppermute | solution.py:287
  93.6 4.7 %collective-permute-start.7 = (f32[16,512]{1,0:T(8,128)S(1)}, f32[16,512]{1,0:T(8,128)S(1)}, u32[]{:S(2)}, u32[]{:S(2)}) collective-permute-start(f32[16,512]{1,0:T(8,128)S(1)} %get-tuple-element.60), channel_id=1, source_target_pairs={{0,192},{8,200},{16,208},{24,216},{32,224},{40,232},{48,240},{56,2... | collective-permute-start | bytes 98312 | tf_op jit(solution)/shard_map/ppermute | solution.py:287
  98.4 2.9 %collective-permute-start.8 = (f32[16,512]{1,0:T(8,128)S(1)}, f32[16,512]{1,0:T(8,128)S(1)}, u32[]{:S(2)}, u32[]{:S(2)}) collective-permute-start(f32[16,512]{1,0:T(8,128)S(1)} %shard_map.127.refs_0_), channel_id=1, source_target_pairs={{0,8},{8,0},{16,24},{24,16},{32,40},{40,32},{48,56},{56,48},{64,72... | collective-permute-start | bytes 98312 | tf_op jit(solution)/shard_map/ppermute | solution.py:287
  101.2 3.7 %collective-permute-start.9 = (f32[16,512]{1,0:T(8,128)S(1)}, f32[16,512]{1,0:T(8,128)S(1)}, u32[]{:S(2)}, u32[]{:S(2)}) collective-permute-start(f32[16,512]{1,0:T(8,128)S(1)} %shard_map.128.refs_0_), channel_id=1, source_target_pairs={{0,16},{8,24},{16,0},{24,8},{32,48},{40,56},{48,32},{56,40},{64,80... | collective-permute-start | bytes 98312 | tf_op jit(solution)/shard_map/ppermute | solution.py:287
  105.0 6.7 %collective-permute-start.10 = (f32[16,512]{1,0:T(8,128)S(1)}, f32[16,512]{1,0:T(8,128)S(1)}, u32[]{:S(2)}, u32[]{:S(2)}) collective-permute-start(f32[16,512]{1,0:T(8,128)S(1)} %shard_map.129.refs_0_), channel_id=1, source_target_pairs={{0,32},{8,40},{16,48},{24,56},{32,0},{40,8},{48,16},{56,24},{64,96... | collective-permute-start | bytes 98312 | tf_op jit(solution)/shard_map/ppermute | solution.py:287
  111.7 18.8 %collective-permute-start.17 = (f32[2048,128]{1,0:T(8,128)S(1)}, f32[2048,128]{1,0:T(8,128)S(1)}, u32[]{:S(2)}, u32[]{:S(2)}) collective-permute-start(f32[2048,128]{1,0:T(8,128)S(1)} %bitcast.16), channel_id=1, source_target_pairs={{0,1},{1,0},{2,3},{3,2},{4,5},{5,4},{6,7},{7,6},{8,9},{9,8},{10,11... | collective-permute-start | bytes 3145736 | tf_op jit(solution)/shard_map/ppermute | solution.py:282
  118.2 8.3 %collective-permute-start.11 = (f32[16,512]{1,0:T(8,128)S(1)}, f32[16,512]{1,0:T(8,128)S(1)}, u32[]{:S(2)}, u32[]{:S(2)}) collective-permute-start(f32[16,512]{1,0:T(8,128)S(1)} %shard_map.130.refs_1_), channel_id=1, source_target_pairs={{0,64},{8,72},{16,80},{24,88},{32,96},{40,104},{48,112},{56,120},{... | collective-permute-start | bytes 98312 | tf_op jit(solution)/shard_map/ppermute | solution.py:287
  118.2 8.4 %collective-permute-start.12 = (f32[16,512]{1,0:T(8,128)S(1)}, f32[16,512]{1,0:T(8,128)S(1)}, u32[]{:S(2)}, u32[]{:S(2)}) collective-permute-start(f32[16,512]{1,0:T(8,128)S(1)} %shard_map.130.refs_1_), channel_id=1, source_target_pairs={{0,128},{8,136},{16,144},{24,152},{32,160},{40,168},{48,176},{56,1... | collective-permute-start | bytes 98312 | tf_op jit(solution)/shard_map/ppermute | solution.py:287
  119.1 7.5 %collective-permute-start.13 = (f32[16,512]{1,0:T(8,128)S(1)}, f32[16,512]{1,0:T(8,128)S(1)}, u32[]{:S(2)}, u32[]{:S(2)}) collective-permute-start(f32[16,512]{1,0:T(8,128)S(1)} %shard_map.130.refs_1_), channel_id=1, source_target_pairs={{0,192},{8,200},{16,208},{24,216},{32,224},{40,232},{48,240},{56,2... | collective-permute-start | bytes 98312 | tf_op jit(solution)/shard_map/ppermute | solution.py:287
  126.6 8.4 %collective-permute-start.14 = (f32[64,512]{1,0:T(8,128)S(1)}, f32[64,512]{1,0:T(8,128)S(1)}, u32[]{:S(2)}, u32[]{:S(2)}) collective-permute-start(f32[64,512]{1,0:T(8,128)S(1)} %shard_map.132.refs_1_), channel_id=1, source_target_pairs={{0,2},{2,0},{4,6},{6,4},{1,3},{3,1},{5,7},{7,5},{8,10},{10,8},{12,... | collective-permute-start | bytes 393224 | tf_op jit(solution)/shard_map/ppermute | solution.py:287
  126.7 8.3 %collective-permute-start.15 = (f32[64,512]{1,0:T(8,128)S(1)}, f32[64,512]{1,0:T(8,128)S(1)}, u32[]{:S(2)}, u32[]{:S(2)}) collective-permute-start(f32[64,512]{1,0:T(8,128)S(1)} %shard_map.132.refs_1_), channel_id=1, source_target_pairs={{0,4},{2,6},{4,0},{6,2},{1,5},{3,7},{5,1},{7,3},{8,12},{10,14},{12... | collective-permute-start | bytes 393224 | tf_op jit(solution)/shard_map/ppermute | solution.py:287
  128.4 7.9 %collective-permute-start.16 = (f32[64,512]{1,0:T(8,128)S(1)}, f32[64,512]{1,0:T(8,128)S(1)}, u32[]{:S(2)}, u32[]{:S(2)}) collective-permute-start(f32[64,512]{1,0:T(8,128)S(1)} %shard_map.132.refs_1_), channel_id=1, source_target_pairs={{0,6},{2,4},{4,2},{6,0},{1,7},{3,5},{5,3},{7,1},{8,14},{10,12},{12... | collective-permute-start | bytes 393224 | tf_op jit(solution)/shard_map/ppermute | solution.py:287
  136.4 3.0 %collective-permute-start.18 = (f32[256,512]{1,0:T(8,128)S(1)}, f32[256,512]{1,0:T(8,128)S(1)}, u32[]{:S(2)}, u32[]{:S(2)}) collective-permute-start(f32[256,512]{1,0:T(8,128)S(1)} %shard_map.134.refs_1_), channel_id=1, source_target_pairs={{0,1},{1,0},{2,3},{3,2},{4,5},{5,4},{6,7},{7,6},{8,9},{9,8},{10,11... | collective-permute-start | bytes 1572872 | tf_op jit(solution)/shard_map/ppermute | solution.py:282

commit v8 on v7

--- a/solution.py
+++ b/solution.py
@@ -6,11 +6,14 @@
 from jax import lax
 from jax.experimental import pallas as pl
 from jax.experimental.pallas import tpu as pltpu
+from jax.sharding import Mesh
 from jax.sharding import PartitionSpec as P
 
 ALPHA = 0.1
 BETA = math.log(1.5)
-OWN = ("batch", "hist")
+OWN = ("y", "z", "hist")
+PLANE = ("y", "hist")
+ALL = ("y", "z", "hist", "rep")
 F32 = jnp.float32
 BF16 = jnp.bfloat16
 GELU_C = math.sqrt(2.0 / math.pi)
@@ -223,12 +226,18 @@
     refs[-1][...] = terms[0]
 
 
-def join_kernel(me_ref, *refs, scale=None):
-    size = refs[0].shape[0]
-    for shift, part in enumerate(refs[:-1]):
-        at = jnp.bitwise_xor(me_ref[0], shift) * size
-        value = part[...] if scale is None else part[...] * scale
-        refs[-1][pl.ds(pl.multiple_of(at, size), size), :] = value
+def spread_kernel(mine_ref, other_ref, out_ref):
+    out_ref[...] = jnp.broadcast_to((mine_ref[...] + other_ref[...])[None], out_ref.shape)
+
+
+def assemble_kernel(core_ref, mine_ref, other_ref, out_ref, *, scale):
+    half = out_ref.shape[0] // 2
+    size = mine_ref.shape[1]
+    for ref, which in ((mine_ref, core_ref[0]), (other_ref, 1 - core_ref[0])):
+        for y in range(4):
+            for x in range(4):
+                at = which * half + (x * 4 + y) * size
+                out_ref[pl.ds(pl.multiple_of(at, size), size), :] = ref[y * 4 + x] * scale
 
 
 def backward_kernel(du_ref, weight_ref, high_ref, low_ref, out_ref):
@@ -274,8 +283,8 @@
     )[0]
 
 
-def exchange(v):
-    return lax.all_to_all(v, OWN, split_axis=0, concat_axis=0, tiled=True)
+def exchange(v, axes=OWN):
+    return lax.all_to_all(v, axes, split_axis=0, concat_axis=0, tiled=True)
 
 
 def swap(v):
@@ -298,22 +307,12 @@
     )
 
 
-def trade(pieces, axis, unit):
-    return [pieces[0]] + [move(pieces[shift], axis, shift * unit) for shift in (1, 2, 3)]
+def trade(pieces, axis):
+    return [pieces[0]] + [move(pieces[shift], axis, shift) for shift in (1, 2, 3)]
 
 
 def total(*terms):
     return call(total_kernel, [(terms[0].shape, F32)], terms)[0]
-
-
-def join(me, parts, scale=None):
-    rows, width = parts[0].shape
-    return call(
-        functools.partial(join_kernel, scale=scale),
-        [((rows * len(parts), width), F32)],
-        (me,) + tuple(parts),
-        spaces="s" + "v" * (len(parts) + 1),
-    )[0]
 
 
 def together(*values):
@@ -337,8 +336,7 @@
     halo_count = owners * halo_rows.shape[2]
     core = lax.axis_index("rep").astype(jnp.int32).reshape(1)
     at_x = lax.axis_index("hist").astype(jnp.int32).reshape(1)
-    depth = lax.axis_size("batch") // 4
-    at_y = lax.div(lax.axis_index("batch").astype(jnp.int32), jnp.int32(depth)).reshape(1)
+    at_y = lax.axis_index("y").astype(jnp.int32).reshape(1)
     full = (rows, width)
     half = (rows // 2, width)
     nbr = neighbors.T
@@ -375,7 +373,7 @@
         flops=3 * 10**9,
     )
     got, dest = together(swap(give), dest)
-    pieces = trade(scatter(at_x, keep, got), "hist", 1)
+    pieces = trade(scatter(at_x, keep, got), "hist")
     (grad_input,) = call(
         backward_kernel,
         [(full, F32)],
@@ -385,44 +383,51 @@
         flops=2 * 10**9,
     )
     *pieces, grad_input = together(*pieces, grad_input)
-    pieces = trade(scatter(at_y, *pieces), "batch", depth)
+    pieces = trade(scatter(at_y, *pieces), "y")
     arrived = exchange(outgoing.reshape(owners * 16, 128))
     summed = total(*pieces)
     mask = 1
-    while mask < depth:
-        summed = total(summed, move(summed, "batch", mask))
+    while 2 * mask < lax.axis_size("z"):
+        summed = total(summed, move(summed, "z", mask))
         mask *= 2
-    arrived, summed = together(arrived, summed)
+    plane = lax.axis_size(PLANE)
+    (spread,) = call(
+        spread_kernel, [((plane,) + summed.shape, F32)], (summed, move(summed, "z", mask))
+    )
+    arrived, spread = together(arrived, spread)
     arrived_other = swap(arrived)
-    parts = trade([summed] * 4, "batch", depth)
+    gathered = exchange(spread, PLANE)
     history = write_rows(core, dest, arrived, cold_history)
-    *parts, history = together(*parts, history)
-    summed = join(at_y, parts)
-    parts = trade([summed] * 4, "hist", 1)
     history = write_rows(1 - core, dest, arrived_other, history)
-    *parts, history = together(*parts, history)
-    summed = join(at_x, parts)
-    all_nodes = rows * lax.axis_size(("batch", "hist", "rep"))
-    grad_weight = join(core, [summed, swap(summed)], BETA / math.sqrt(all_nodes))
+    gathered, history = together(gathered, history)
+    all_nodes = rows * lax.axis_size(ALL)
+    (grad_weight,) = call(
+        functools.partial(assemble_kernel, scale=BETA / math.sqrt(all_nodes)),
+        [((width, width), F32)],
+        (core, gathered, swap(gathered)),
+        spaces="svvv",
+    )
     return (grad_weight, grad_input, history)
 
 
 def solution(mesh):
+    batch, hist, rep = mesh.devices.shape
+    mesh = Mesh(mesh.devices.reshape(4, batch // 4, hist, rep), ALL)
     return jax.shard_map(
         body,
         mesh=mesh,
         in_specs=(
-            P(("batch", "hist", "rep"), None),
-            P(("batch", "hist", "rep"), None),
-            P(("batch", "hist", "rep"), None),
+            P(ALL, None),
+            P(ALL, None),
+            P(ALL, None),
             P(),
-            P(("batch", "hist", "rep"), None),
-            P(("batch", "hist", "rep"), None),
-            P(("batch", "hist", "rep"), None, None),
-            P(("batch", "hist"), None),
+            P(ALL, None),
+            P(ALL, None),
+            P(ALL, None, None),
+            P(OWN, None),
             P("rep", None),
-            P(("batch", "hist"), None),
+            P(OWN, None),
         ),
-        out_specs=(P(), P(("batch", "hist", "rep"), None), P(("batch", "hist"), None)),
+        out_specs=(P(), P(ALL, None), P(OWN, None)),
         check_vma=False,
     )

time: 141 us -> 138 us (0.979)
  starting transfers between devices: 52.5 us -> 47.9 us
    ppermute x15 -> x9, starting transfers between devices: 23.8 us -> 16.1 us  [move(): return lax.ppermute(v, axis, [(i, i ^ mask) for i in range(count)])]
    all_to_all x2 -> x3, starting transfers between devices: 15.1 us -> 18.7 us  [exchange(): return lax.all_to_all(v, axes, split_axis=0, concat_axis=0, tiled=True)]
    ppermute x15 -> x9, waiting for transfers between devices: 18.4 us -> 17 us  [move(): return lax.ppermute(v, axis, [(i, i ^ mask) for i in range(count)])]
    all_to_all x2 -> x3, waiting for transfers between devices: 8.64 us -> 9.78 us  [exchange(): return lax.all_to_all(v, axes, split_axis=0, concat_axis=0, tiled=True)]
    pallas_call x15 -> x13, Pallas kernels: 31.8 us -> 32.6 us  [call(): pl.pallas_call(wrapped, out_shape=[jax.ShapeDtypeStruct(*o) for o in outs...]
  transfers between devices with their start and end apart: 21 -> 16, of which waited for: 11 -> 11; matrix products, arithmetic and copies ran while one was open for 2% -> 2% of each run, Pallas kernels for 18% -> 19%
where the time goes in v8:
time: 138 us
  starting transfers between devices  47.9 us (35%)
  Pallas kernels  32.6 us (24%)
  waiting for transfers between devices  28.5 us (21%)
  blocking collectives  24.4 us (18%)
  local copies, waits for them, and re-layouts  2.85 us (2%)
    pallas_call x13, Pallas kernels, call(): pl.pallas_call(wrapped, out_shape=[jax.ShapeDtypeStruct(*o) for o in outs...  32.6 us
    all_to_all x1, blocking collectives, exchange(): return lax.all_to_all(v, axes, split_axis=0, concat_axis=0, tiled=True)  24.4 us
    all_to_all x3, starting transfers between devices, exchange(): return lax.all_to_all(v, axes, split_axis=0, concat_axis=0, tiled=True)  18.7 us
    ppermute x9, waiting for transfers between devices, move(): return lax.ppermute(v, axis, [(i, i ^ mask) for i in range(count)])  17 us
    ppermute x9, starting transfers between devices, move(): return lax.ppermute(v, axis, [(i, i ^ mask) for i in range(count)])  16.1 us
    ppermute x4, starting transfers between devices, swap(): return lax.ppermute(v, 'rep', [(0, 1), (1, 0)])  13.1 us
    all_to_all x3, waiting for transfers between devices, exchange(): return lax.all_to_all(v, axes, split_axis=0, concat_axis=0, tiled=True)  9.78 us
  transfers between devices with their start and end apart: 16, of which 11 were waited for; matrix products, arithmetic and copies ran while one was open for 2% of the time, Pallas kernels for 19%

profile of v8, /device:TPU:1, one launch (start us, length us, event | category | flops | bytes accessed | tf_op | source)
XLA Modules:
  0.0 137.5 jit_solution(18078274355211225922)
XLA Ops:
  0.6 3.3 %collective-permute-start = (f32[1024,512]{1,0:T(8,128)}, f32[1024,512]{1,0:T(8,128)S(1)}, u32[]{:S(2)}, u32[]{:S(2)}) collective-permute-start(f32[1024,512]{1,0:T(8,128)} %refs_3_.2), channel_id=1, source_target_pairs={{0,1},{1,0},{2,3},{3,2},{4,5},{5,4},{6,7},{7,6},{8,9},{9,8},{10,11... | collective-permute-start | bytes 6291464 | tf_op jit(solution)/shard_map/ppermute | solution.py:291
  4.0 0.8 copy.17
  4.7 24.4 %all_to_all.40 = s32[128,1,2]{2,1,0:T(1,128)} all-to-all(s32[128,1,2]{2,1,0:T(1,128)S(1)} %bitcast.28), channel_id=1, replica_groups=mesh['y'=4,'z'=8,'hist'=4,'rep'=2] {'y','z','hist'}, dimensions={0} | all-to-all | bytes 2048 | tf_op jit(solution)/shard_map/all_to_all | solution.py:287
  29.1 3.9 %shard_map.121 = f32[1024,128]{1,0:T(8,128)} custom-call(s32[128,2]{1,0:T(8,128)} %bitcast.29, f32[1280,512]{1,0:T(8,128)} %refs_3_.3), custom_call_target="tpu_custom_call" | custom-call | flops 1000000000 | bytes 3146752 | tf_op jit(solution)/shard_map/pallas_call | solution.py:106
  33.1 6.4 %all-to-all-start.1 = ((f32[128,8,128]{2,1,0:T(8,128)}), f32[128,8,128]{2,1,0:T(8,128)S(1)}, u32[]{:S(2)}, u32[]{:S(2)}) async-start(f32[128,8,128]{2,1,0:T(8,128)} %bitcast.26), calls=%async_computation.1 | async-start | bytes 1048576 | tf_op jit(solution)/shard_map/all_to_all | solution.py:287
  39.4 0.0 collective-permute-done.refs_4_
  39.5 0.0 copy-start.3
  39.5 1.3 copy-done.3
  40.8 0.0 copy-start
  40.8 0.0 copy-start.1
  40.8 7.5 %shard_map.122 = (f32[512,512]{1,0:T(8,128)}, bf16[512,512]{1,0:T(8,128)(2,1)}, bf16[512,512]{1,0:T(8,128)(2,1)}) custom-call(s32[1]{0:T(128)} %bitcast.refs_0_, s32[8,512]{1,0:T(8,128)} %bitcast.21, f32[8,512]{1,0:T(8,128)} %bitcast.23, f32[1024,512]{1,0:T(8,128)} %refs_3_.2, f32[1024,512]{1,0:T(8,128)} %copy-done.3, f32[512,512]{1,0:T(8,128)} %refs_5_.2, ...), custom_call_target="tpu_custom_call" | custom-call | flops 6000000000 | bytes 9469956 | tf_op jit(solution)/shard_map/pallas_call | solution.py:106
  48.3 7.3 %all-to-all-done.1 = f32[128,8,128]{2,1,0:T(8,128)S(1)} async-done(((f32[128,8,128]{2,1,0:T(8,128)}), f32[128,8,128]{2,1,0:T(8,128)S(1)}, u32[]{:S(2)}, u32[]{:S(2)}) %all-to-all-start.1) | async-done | bytes 524320 | tf_op jit(solution)/shard_map/all_to_all | solution.py:287
  55.6 0.0 copy-done
  55.6 0.0 copy-done.1
  55.6 0.0 copy-start.2
  55.6 5.6 %shard_map.123 = (f32[32,4,16,128]{3,2,1,0:T(8,128)}, f32[256,512]{1,0:T(8,128)S(1)}, f32[256,512]{1,0:T(8,128)S(1)}, f32[512,512]{1,0:T(8,128)}) custom-call(s32[1]{0:T(128)} %bitcast.refs_0_, f32[1024,128]{1,0:T(8,128)S(1)} %bitcast.18, s32[8,512]{1,0:T(8,128)S(1)} %bitcast.22, f32[8,512]{1,0:T(8,128)S(1)} %bitcast.24, ...), custom_call_target="tpu_custom_call" | custom-call | flops 3000000000 | bytes 6848516 | tf_op jit(solution)/shard_map/pallas_call | solution.py:106
  61.2 8.7 %all-to-all-start.2 = ((f32[128,16,128]{2,1,0:T(8,128)}), f32[128,16,128]{2,1,0:T(8,128)S(1)}, u32[]{:S(2)}, u32[]{:S(2)}) async-start(f32[128,16,128]{2,1,0:T(8,128)} %bitcast.25), calls=%async_computation.2 | async-start | bytes 2097152 | tf_op jit(solution)/shard_map/all_to_all | solution.py:287
  69.9 2.3 %collective-permute-start.1 = (f32[256,512]{1,0:T(8,128)S(1)}, f32[256,512]{1,0:T(8,128)S(1)}, u32[]{:S(2)}, u32[]{:S(2)}) collective-permute-start(f32[256,512]{1,0:T(8,128)S(1)} %get-tuple-element.36), channel_id=1, source_target_pairs={{0,1},{1,0},{2,3},{3,2},{4,5},{5,4},{6,7},{7,6},{8,9},{9,8},{10,11... | collective-permute-start | bytes 1572872 | tf_op jit(solution)/shard_map/ppermute | solution.py:291
  72.2 0.5 broadcast.3
  72.8 0.0 copy-done.2
  72.8 0.6 reduce.3
  73.4 0.1 reshape.33
  73.5 0.1 copy.18
  73.6 0.1 collective-permute-done.1.refs_2_
  73.8 0.1 shard_map.124
  73.9 0.9 collective-permute-start.2
  74.8 2.4 %collective-permute-start.3 = (f32[64,512]{1,0:T(8,128)S(1)}, f32[64,512]{1,0:T(8,128)S(1)}, u32[]{:S(2)}, u32[]{:S(2)}) collective-permute-start(f32[64,512]{1,0:T(8,128)S(1)} %get-tuple-element.40), channel_id=1, source_target_pairs={{0,4},{2,6},{4,0},{6,2},{1,5},{3,7},{5,1},{7,3},{8,12},{10,14},{12... | collective-permute-start | bytes 393224 | tf_op jit(solution)/shard_map/ppermute | solution.py:296
  77.2 0.6 collective-permute-start.4
  77.8 4.6 %shard_map.125 = f32[512,512]{1,0:T(8,128)} custom-call(f32[512,512]{1,0:T(8,128)} %get-tuple-element.42.refs_0_, f32[512,512]{1,0:T(8,128)} %refs_1_.3, bf16[512,512]{1,0:T(8,128)(2,1)} %get-tuple-element.43.refs_2_, bf16[512,512]{1,0:T(8,128)(2,1)} %get-tuple-element.44.refs_3_), custom_call_target="tpu_custom_call" | custom-call | flops 2000000000 | bytes 5242880 | tf_op jit(solution)/shard_map/pallas_call | solution.py:106
  82.4 0.0 collective-permute-done.2.refs_2_
  82.4 5.5 %collective-permute-done.3.refs_3_ = f32[64,512]{1,0:T(8,128)S(1)} collective-permute-done((f32[64,512]{1,0:T(8,128)S(1)}, f32[64,512]{1,0:T(8,128)S(1)}, u32[]{:S(2)}, u32[]{:S(2)}) %collective-permute-start.3) | collective-permute-done | bytes 131104 | tf_op jit(solution)/shard_map/ppermute | solution.py:296
  88.0 1.3 collective-permute-done.4.refs_4_
  89.4 1.4 collective-permute-start.5
  90.7 2.8 %collective-permute-start.6 = (f32[16,512]{1,0:T(8,128)S(1)}, f32[16,512]{1,0:T(8,128)S(1)}, u32[]{:S(2)}, u32[]{:S(2)}) collective-permute-start(f32[16,512]{1,0:T(8,128)S(1)} %get-tuple-element.51), channel_id=1, source_target_pairs={{0,128},{64,192},{128,0},{192,64},{1,129},{65,193},{129,1},{193,65... | collective-permute-start | bytes 98312 | tf_op jit(solution)/shard_map/ppermute | solution.py:296
  93.6 0.0 collective-permute-start.7
  93.6 0.0 collective-permute-done.5.refs_1_
  93.6 2.9 %collective-permute-done.6.refs_2_ = f32[16,512]{1,0:T(8,128)S(1)} collective-permute-done((f32[16,512]{1,0:T(8,128)S(1)}, f32[16,512]{1,0:T(8,128)S(1)}, u32[]{:S(2)}, u32[]{:S(2)}) %collective-permute-start.6) | collective-permute-done | bytes 32800 | tf_op jit(solution)/shard_map/ppermute | solution.py:296
  96.4 1.9 %collective-permute-done.7.refs_3_ = f32[16,512]{1,0:T(8,128)S(1)} collective-permute-done((f32[16,512]{1,0:T(8,128)S(1)}, f32[16,512]{1,0:T(8,128)S(1)}, u32[]{:S(2)}, u32[]{:S(2)}) %collective-permute-start.7) | collective-permute-done | bytes 32800 | tf_op jit(solution)/shard_map/ppermute | solution.py:296
  98.3 1.6 %collective-permute-start.8 = (f32[16,512]{1,0:T(8,128)S(1)}, f32[16,512]{1,0:T(8,128)S(1)}, u32[]{:S(2)}, u32[]{:S(2)}) collective-permute-start(f32[16,512]{1,0:T(8,128)S(1)} %shard_map.127.refs_0_), channel_id=1, source_target_pairs={{0,8},{8,0},{16,24},{24,16},{32,40},{40,32},{48,56},{56,48},{1,9},... | collective-permute-start | bytes 98312 | tf_op jit(solution)/shard_map/ppermute | solution.py:296
  99.9 1.3 collective-permute-done.8.refs_1_
  101.2 2.1 %collective-permute-start.9 = (f32[16,512]{1,0:T(8,128)S(1)}, f32[16,512]{1,0:T(8,128)S(1)}, u32[]{:S(2)}, u32[]{:S(2)}) collective-permute-start(f32[16,512]{1,0:T(8,128)S(1)} %shard_map.128.refs_0_), channel_id=1, source_target_pairs={{0,16},{8,24},{16,0},{24,8},{32,48},{40,56},{48,32},{56,40},{1,17}... | collective-permute-start | bytes 98312 | tf_op jit(solution)/shard_map/ppermute | solution.py:296
  103.3 1.7 %collective-permute-done.9.refs_1_ = f32[16,512]{1,0:T(8,128)S(1)} collective-permute-done((f32[16,512]{1,0:T(8,128)S(1)}, f32[16,512]{1,0:T(8,128)S(1)}, u32[]{:S(2)}, u32[]{:S(2)}) %collective-permute-start.9) | collective-permute-done | bytes 32800 | tf_op jit(solution)/shard_map/ppermute | solution.py:296
  104.9 4.2 %collective-permute-start.10 = (f32[16,512]{1,0:T(8,128)S(1)}, f32[16,512]{1,0:T(8,128)S(1)}, u32[]{:S(2)}, u32[]{:S(2)}) collective-permute-start(f32[16,512]{1,0:T(8,128)S(1)} %shard_map.129.refs_0_), channel_id=1, source_target_pairs={{0,32},{8,40},{16,48},{24,56},{32,0},{40,8},{48,16},{56,24},{1,33}... | collective-permute-start | bytes 98312 | tf_op jit(solution)/shard_map/ppermute | solution.py:296
  109.2 2.4 %collective-permute-done.10.refs_1_ = f32[16,512]{1,0:T(8,128)S(1)} collective-permute-done((f32[16,512]{1,0:T(8,128)S(1)}, f32[16,512]{1,0:T(8,128)S(1)}, u32[]{:S(2)}, u32[]{:S(2)}) %collective-permute-start.10) | collective-permute-done | bytes 32800 | tf_op jit(solution)/shard_map/ppermute | solution.py:296
  111.6 0.9 shard_map.130
  112.5 0.0 all-to-all-done.2
  112.5 6.4 %collective-permute-start.11 = (f32[2048,128]{1,0:T(8,128)S(1)}, f32[2048,128]{1,0:T(8,128)S(1)}, u32[]{:S(2)}, u32[]{:S(2)}) collective-permute-start(f32[2048,128]{1,0:T(8,128)S(1)} %bitcast.16), channel_id=1, source_target_pairs={{0,1},{1,0},{2,3},{3,2},{4,5},{5,4},{6,7},{7,6},{8,9},{9,8},{10,11... | collective-permute-start | bytes 3145736 | tf_op jit(solution)/shard_map/ppermute | solution.py:291
  118.9 3.6 %all-to-all-start.3 = ((f32[16,16,512]{2,1,0:T(8,128)}), f32[16,16,512]{2,1,0:T(8,128)S(1)}, u32[]{:S(2)}, u32[]{:S(2)}) async-start(f32[16,16,512]{2,1,0:T(8,128)} %shard_map.130), calls=%async_computation.3 | async-start | bytes 1048576 | tf_op jit(solution)/shard_map/all_to_all | solution.py:287
  122.5 4.4 %shard_map.131.refs_3_ = f32[1280,512]{1,0:T(8,128)} custom-call(s32[1]{0:T(128)} %bitcast.refs_0_, s32[2,512]{1,0:T(2,128)S(1)} %bitcast.19, f32[2048,128]{1,0:T(8,128)S(1)} %bitcast.17, f32[1280,512]{1,0:T(8,128)} %refs_3_.3), custom_call_target="tpu_custom_call" | custom-call | flops 2000000000 | bytes 6295556 | tf_op jit(solution)/shard_map/pallas_call | solution.py:106
  126.9 0.0 collective-permute-done.11.refs_2_
  126.9 4.4 %shard_map.132 = f32[1280,512]{1,0:T(8,128)} custom-call(s32[1]{0:T(128)S(6)} %sub.3.refs_0_, s32[2,512]{1,0:T(2,128)S(1)} %bitcast.20, f32[2048,128]{1,0:T(8,128)S(1)} %collective-permute-done.11.refs_2_, f32[1280,512]{1,0:T(8,128)} %shard_map.131.refs_3_), custom_call_target="tpu_custom_call" | custom-call | flops 2000000000 | bytes 6295556 | tf_op jit(solution)/shard_map/pallas_call | solution.py:106
  131.4 2.5 %all-to-all-done.3.refs_1_ = f32[16,16,512]{2,1,0:T(8,128)S(1)} async-done(((f32[16,16,512]{2,1,0:T(8,128)}), f32[16,16,512]{2,1,0:T(8,128)S(1)}, u32[]{:S(2)}, u32[]{:S(2)}) %all-to-all-start.3) | async-done | bytes 524320 | tf_op jit(solution)/shard_map/all_to_all | solution.py:287
  133.8 1.1 collective-permute-start.12
  134.9 1.5 %collective-permute-done.12.refs_2_ = f32[16,16,512]{2,1,0:T(8,128)S(1)} collective-permute-done((f32[16,16,512]{2,1,0:T(8,128)S(1)}, f32[16,16,512]{2,1,0:T(8,128)S(1)}, u32[]{:S(2)}, u32[]{:S(2)}) %collective-permute-start.12) | collective-permute-done | bytes 524320 | tf_op jit(solution)/shard_map/ppermute | solution.py:291
  136.5 1.1 shard_map.133
  (5 shorter events, 0.1 us)
Async XLA Ops:
  0.6 38.8 %collective-permute-start = (f32[1024,512]{1,0:T(8,128)}, f32[1024,512]{1,0:T(8,128)S(1)}, u32[]{:S(2)}, u32[]{:S(2)}) collective-permute-start(f32[1024,512]{1,0:T(8,128)} %refs_3_.2), channel_id=1, source_target_pairs={{0,1},{1,0},{2,3},{3,2},{4,5},{5,4},{6,7},{7,6},{8,9},{9,8},{10,11... | collective-permute-start | bytes 6291464 | tf_op jit(solution)/shard_map/ppermute | solution.py:291
  33.1 22.5 %all-to-all-start.1 = ((f32[128,8,128]{2,1,0:T(8,128)}), f32[128,8,128]{2,1,0:T(8,128)S(1)}, u32[]{:S(2)}, u32[]{:S(2)}) async-start(f32[128,8,128]{2,1,0:T(8,128)} %bitcast.26), calls=%async_computation.1 | async-start | bytes 1048576 | tf_op jit(solution)/shard_map/all_to_all | solution.py:287
  39.5 1.3 copy-start.3
  40.8 14.8 %copy-start = (s32[512,8]{0,1:T(8,128)S(1)}, s32[512,8]{0,1:T(8,128)}, u32[]{:S(2)}) copy-start(s32[512,8]{0,1:T(8,128)} %param.15) | copy-start | bytes 49156
  40.8 14.8 %copy-start.1 = (f32[512,8]{0,1:T(8,128)S(1)}, f32[512,8]{0,1:T(8,128)}, u32[]{:S(2)}) copy-start(f32[512,8]{0,1:T(8,128)} %param.14) | copy-start | bytes 49156
  55.6 17.2 %copy-start.2 = (s32[1,1024]{1,0:T(1,128)S(1)}, s32[1,1024]{1,0:T(1,128)}, u32[]{:S(2)}) copy-start(s32[1,1024]{1,0:T(1,128)} %param.19) | copy-start | bytes 12292
  61.2 51.3 %all-to-all-start.2 = ((f32[128,16,128]{2,1,0:T(8,128)}), f32[128,16,128]{2,1,0:T(8,128)S(1)}, u32[]{:S(2)}, u32[]{:S(2)}) async-start(f32[128,16,128]{2,1,0:T(8,128)} %bitcast.25), calls=%async_computation.2 | async-start | bytes 2097152 | tf_op jit(solution)/shard_map/all_to_all | solution.py:287
  69.9 3.9 %collective-permute-start.1 = (f32[256,512]{1,0:T(8,128)S(1)}, f32[256,512]{1,0:T(8,128)S(1)}, u32[]{:S(2)}, u32[]{:S(2)}) collective-permute-start(f32[256,512]{1,0:T(8,128)S(1)} %get-tuple-element.36), channel_id=1, source_target_pairs={{0,1},{1,0},{2,3},{3,2},{4,5},{5,4},{6,7},{7,6},{8,9},{9,8},{10,11... | collective-permute-start | bytes 1572872 | tf_op jit(solution)/shard_map/ppermute | solution.py:291
  73.9 8.6 %collective-permute-start.2 = (f32[64,512]{1,0:T(8,128)S(1)}, f32[64,512]{1,0:T(8,128)S(1)}, u32[]{:S(2)}, u32[]{:S(2)}) collective-permute-start(f32[64,512]{1,0:T(8,128)S(1)} %get-tuple-element.39), channel_id=1, source_target_pairs={{0,2},{2,0},{4,6},{6,4},{1,3},{3,1},{5,7},{7,5},{8,10},{10,8},{12,... | collective-permute-start | bytes 393224 | tf_op jit(solution)/shard_map/ppermute | solution.py:296
  74.8 13.2 %collective-permute-start.3 = (f32[64,512]{1,0:T(8,128)S(1)}, f32[64,512]{1,0:T(8,128)S(1)}, u32[]{:S(2)}, u32[]{:S(2)}) collective-permute-start(f32[64,512]{1,0:T(8,128)S(1)} %get-tuple-element.40), channel_id=1, source_target_pairs={{0,4},{2,6},{4,0},{6,2},{1,5},{3,7},{5,1},{7,3},{8,12},{10,14},{12... | collective-permute-start | bytes 393224 | tf_op jit(solution)/shard_map/ppermute | solution.py:296
  77.2 12.1 %collective-permute-start.4 = (f32[64,512]{1,0:T(8,128)S(1)}, f32[64,512]{1,0:T(8,128)S(1)}, u32[]{:S(2)}, u32[]{:S(2)}) collective-permute-start(f32[64,512]{1,0:T(8,128)S(1)} %get-tuple-element.41), channel_id=1, source_target_pairs={{0,6},{2,4},{4,2},{6,0},{1,7},{3,5},{5,3},{7,1},{8,14},{10,12},{12... | collective-permute-start | bytes 393224 | tf_op jit(solution)/shard_map/ppermute | solution.py:296
  89.4 4.2 %collective-permute-start.5 = (f32[16,512]{1,0:T(8,128)S(1)}, f32[16,512]{1,0:T(8,128)S(1)}, u32[]{:S(2)}, u32[]{:S(2)}) collective-permute-start(f32[16,512]{1,0:T(8,128)S(1)} %get-tuple-element.50), channel_id=1, source_target_pairs={{0,64},{64,0},{128,192},{192,128},{1,65},{65,1},{129,193},{193,129... | collective-permute-start | bytes 98312 | tf_op jit(solution)/shard_map/ppermute | solution.py:296
  90.7 5.7 %collective-permute-start.6 = (f32[16,512]{1,0:T(8,128)S(1)}, f32[16,512]{1,0:T(8,128)S(1)}, u32[]{:S(2)}, u32[]{:S(2)}) collective-permute-start(f32[16,512]{1,0:T(8,128)S(1)} %get-tuple-element.51), channel_id=1, source_target_pairs={{0,128},{64,192},{128,0},{192,64},{1,129},{65,193},{129,1},{193,65... | collective-permute-start | bytes 98312 | tf_op jit(solution)/shard_map/ppermute | solution.py:296
  93.6 4.7 %collective-permute-start.7 = (f32[16,512]{1,0:T(8,128)S(1)}, f32[16,512]{1,0:T(8,128)S(1)}, u32[]{:S(2)}, u32[]{:S(2)}) collective-permute-start(f32[16,512]{1,0:T(8,128)S(1)} %get-tuple-element.52), channel_id=1, source_target_pairs={{0,192},{64,128},{128,64},{192,0},{1,193},{65,129},{129,65},{193,1... | collective-permute-start | bytes 98312 | tf_op jit(solution)/shard_map/ppermute | solution.py:296
  98.3 2.9 %collective-permute-start.8 = (f32[16,512]{1,0:T(8,128)S(1)}, f32[16,512]{1,0:T(8,128)S(1)}, u32[]{:S(2)}, u32[]{:S(2)}) collective-permute-start(f32[16,512]{1,0:T(8,128)S(1)} %shard_map.127.refs_0_), channel_id=1, source_target_pairs={{0,8},{8,0},{16,24},{24,16},{32,40},{40,32},{48,56},{56,48},{1,9},... | collective-permute-start | bytes 98312 | tf_op jit(solution)/shard_map/ppermute | solution.py:296
  101.2 3.7 %collective-permute-start.9 = (f32[16,512]{1,0:T(8,128)S(1)}, f32[16,512]{1,0:T(8,128)S(1)}, u32[]{:S(2)}, u32[]{:S(2)}) collective-permute-start(f32[16,512]{1,0:T(8,128)S(1)} %shard_map.128.refs_0_), channel_id=1, source_target_pairs={{0,16},{8,24},{16,0},{24,8},{32,48},{40,56},{48,32},{56,40},{1,17}... | collective-permute-start | bytes 98312 | tf_op jit(solution)/shard_map/ppermute | solution.py:296
  104.9 6.7 %collective-permute-start.10 = (f32[16,512]{1,0:T(8,128)S(1)}, f32[16,512]{1,0:T(8,128)S(1)}, u32[]{:S(2)}, u32[]{:S(2)}) collective-permute-start(f32[16,512]{1,0:T(8,128)S(1)} %shard_map.129.refs_0_), channel_id=1, source_target_pairs={{0,32},{8,40},{16,48},{24,56},{32,0},{40,8},{48,16},{56,24},{1,33}... | collective-permute-start | bytes 98312 | tf_op jit(solution)/shard_map/ppermute | solution.py:296
  112.5 14.4 %collective-permute-start.11 = (f32[2048,128]{1,0:T(8,128)S(1)}, f32[2048,128]{1,0:T(8,128)S(1)}, u32[]{:S(2)}, u32[]{:S(2)}) collective-permute-start(f32[2048,128]{1,0:T(8,128)S(1)} %bitcast.16), channel_id=1, source_target_pairs={{0,1},{1,0},{2,3},{3,2},{4,5},{5,4},{6,7},{7,6},{8,9},{9,8},{10,11... | collective-permute-start | bytes 3145736 | tf_op jit(solution)/shard_map/ppermute | solution.py:291
  118.9 15.0 %all-to-all-start.3 = ((f32[16,16,512]{2,1,0:T(8,128)}), f32[16,16,512]{2,1,0:T(8,128)S(1)}, u32[]{:S(2)}, u32[]{:S(2)}) async-start(f32[16,16,512]{2,1,0:T(8,128)} %shard_map.130), calls=%async_computation.3 | async-start | bytes 1048576 | tf_op jit(solution)/shard_map/all_to_all | solution.py:287
  133.8 2.6 %collective-permute-start.12 = (f32[16,16,512]{2,1,0:T(8,128)S(1)}, f32[16,16,512]{2,1,0:T(8,128)S(1)}, u32[]{:S(2)}, u32[]{:S(2)}) collective-permute-start(f32[16,16,512]{2,1,0:T(8,128)S(1)} %all-to-all-done.3.refs_1_), channel_id=1, source_target_pairs={{0,1},{1,0},{2,3},{3,2},{4,5},{5,4},{6,7},{7,6},{8,9},{9,8},{10,11... | collective-permute-start | bytes 1572872 | tf_op jit(solution)/shard_map/ppermute | solution.py:291

commit v9 on v8

--- a/solution.py
+++ b/solution.py
@@ -132,10 +132,15 @@
 
 
 def prepare_kernel(
-    core_ref, nbr_ref, ew_ref, mine_ref, other_ref, node_ref, init_ref,
-    part_ref, high_ref, low_ref, *, halo_count,
+    core_ref, nbr_ref, ew_ref, mine_ref, other_ref, node_ref, init_ref, weight_ref,
+    part_ref, high_ref, low_ref, whigh_ref, wlow_ref, *, halo_count,
 ):
     rows = node_ref.shape[0]
+    weights = split(weight_ref[...])
+    whigh_ref[...] = weights[0]
+    wlow_ref[...] = weights[1]
+    whigh_ref.push()
+    wlow_ref.push()
     half = mine_ref.shape[0]
     core = core_ref[0]
     nbr = nbr_ref[...].T
@@ -161,10 +166,13 @@
 
 
 def layer_kernel(
-    core_ref, halo_ref, nbr_ref, ew_ref, part_ref, weight_ref, cot_ref,
-    out_ref, keep_ref, give_ref, du_ref, term_ref,
+    core_ref, halo_ref, nbr_ref, ew_ref, part_ref, whigh_ref, wlow_ref, cot_ref,
+    out_ref, keep_ref, give_ref, du_ref,
+    term_ref, work_ref, zhigh_ref, zlow_ref, dhigh_ref, dlow_ref,
 ):
     owners = halo_ref.shape[0] // 8
+    rows = part_ref.shape[0]
+    block, step = 128, 32
     halo = jnp.concatenate(
         [
             jnp.concatenate(
@@ -174,36 +182,56 @@
         ],
         axis=0,
     )
-    place = nbr_ref[...].T[:, :1] - part_ref.shape[0]
+    place = nbr_ref[...].T[:, :1] - rows
     pick = one_hot((place & 1) * owners + (place >> 1), 2 * owners)
+    scale = (1.0 - ALPHA) * ew_ref[...].T[:, :1]
     high, low = split(halo)
-    ew = ew_ref[...].T[:, :1]
-    z = part_ref[...] + ((1.0 - ALPHA) * ew) * (dot(pick, high) + dot(pick, low))
-    zs = split(z)
-    u = (1.0 - BETA) * z + BETA * dot3(zs, split(weight_ref[...]))
-    square = u * u
-    bent = jnp.tanh(GELU_C * (u + GELU_A * (square * u)))
-    embed = (0.5 * u) * (1.0 + bent)
-    slope = 0.5 * (1.0 + bent) + (0.5 * u) * (1.0 - bent * bent) * (
-        GELU_C * (1.0 + (3.0 * GELU_A) * square)
-    )
-    du = cot_ref[...] * slope
-    du_ref[...] = du
+    top = lax.broadcasted_iota(jnp.int32, (step // 16, 2, 8, 128), 2) < 4
+    for start in range(0, rows, block):
+        whole = slice(start, start + block)
+        work_ref[whole, :] = dot(pick[whole], high) + dot(pick[whole], low)
+        for first in range(start, start + block, step):
+            at = slice(first, first + step)
+            z = part_ref[at, :] + scale[at] * work_ref[at, :]
+            zs = split(z)
+            work_ref[at, :] = z
+            zhigh_ref[at, :] = zs[0]
+            zlow_ref[at, :] = zs[1]
+    weights = whigh_ref[...], wlow_ref[...]
+    for start in range(0, rows, block):
+        whole = slice(start, start + block)
+        mixed = dot3((zhigh_ref[whole, :], zlow_ref[whole, :]), weights)
+        work_ref[whole, :] = (1.0 - BETA) * work_ref[whole, :] + BETA * mixed
+        for first in range(start, start + block, step):
+            at = slice(first, first + step)
+            u = work_ref[at, :]
+            square = u * u
+            bent = jnp.tanh(GELU_C * (u + GELU_A * (square * u)))
+            embed = (0.5 * u) * (1.0 + bent)
+            slope = 0.5 * (1.0 + bent) + (0.5 * u) * (1.0 - bent * bent) * (
+                GELU_C * (1.0 + (3.0 * GELU_A) * square)
+            )
+            du = cot_ref[at, :] * slope
+            du_ref[at, :] = du
+            ds = split(du)
+            dhigh_ref[at, :] = ds[0]
+            dlow_ref[at, :] = ds[1]
+            group = slice(first // 16, (first + step) // 16)
+            for pair in range(2):
+                x, y = (
+                    embed[:, l * 128 : (l + 1) * 128].reshape(step // 16, 2, 8, 128)
+                    for l in (2 * pair, 2 * pair + 1)
+                )
+                even = jnp.where(top, x, pltpu.roll(y, 4, 2))
+                odd = jnp.where(top, pltpu.roll(x, 4, 2), y)
+                for h in range(2):
+                    out_ref[group, 2 * h, 8 * pair : 8 * pair + 8, :] = even[:, h]
+                    out_ref[group, 2 * h + 1, 8 * pair : 8 * pair + 8, :] = odd[:, h]
+    out_ref.push()
     du_ref.push()
-    groups = out_ref.shape[0]
-    top = lax.broadcasted_iota(jnp.int32, (groups, 2, 8, 128), 2) < 4
-    for pair in range(2):
-        x, y = (
-            embed[:, l * 128 : (l + 1) * 128].reshape(groups, 2, 8, 128)
-            for l in (2 * pair, 2 * pair + 1)
-        )
-        even = jnp.where(top, x, pltpu.roll(y, 4, 2))
-        odd = jnp.where(top, pltpu.roll(x, 4, 2), y)
-        for h in range(2):
-            out_ref[:, 2 * h, 8 * pair : 8 * pair + 8, :] = even[:, h]
-            out_ref[:, 2 * h + 1, 8 * pair : 8 * pair + 8, :] = odd[:, h]
-    out_ref.push()
-    term_ref[...] = dot3(zs, split(du), 0, 0)
+    term_ref[...] = dot3(
+        (zhigh_ref[...], zlow_ref[...]), (dhigh_ref[...], dlow_ref[...]), 0, 0
+    )
     half = term_ref.shape[0] // 2
     core = core_ref[0]
     keep_ref[...] = term_ref[pl.ds(pl.multiple_of(core * half, half), half), :]
@@ -354,11 +382,12 @@
         flops=10**9,
     )
     halo = exchange(found)
-    part, high, low = call(
+    square = ((width, width), BF16)
+    part, high, low, *weights = call(
         functools.partial(prepare_kernel, halo_count=halo_count),
-        [(full, F32), ((rows, rows), BF16), ((rows, rows), BF16)],
-        (core, nbr, ew, hot_history, swap(hot_history), node_input, initial),
-        spaces="svvhhhhhhh",
+        [(full, F32), ((rows, rows), BF16), ((rows, rows), BF16), square, square],
+        (core, nbr, ew, hot_history, swap(hot_history), node_input, initial, weight),
+        spaces="svvhhhhhhhhhh",
         limit=60,
         flops=6 * 10**9,
     )
@@ -366,9 +395,10 @@
     outgoing, keep, give, du = call(
         layer_kernel,
         [((owners // 4, 4, 16, 128), F32), (half, F32), (half, F32), (full, F32)],
-        (core, halo, nbr, ew, part, weight, cotangent),
-        spaces="svvvhhhhvvh",
-        scratch=[pltpu.VMEM((width, width), F32)],
+        (core, halo, nbr, ew, part, *weights, cotangent),
+        spaces="svvvhhhhhvvh",
+        scratch=[pltpu.VMEM((width, width), F32), pltpu.VMEM(full, F32)]
+        + [pltpu.VMEM(full, BF16)] * 4,
         limit=52,
         flops=3 * 10**9,
     )

time: 138 us -> 139 us (level)
  Pallas kernels: 32.6 us -> 36.3 us
  waiting for transfers between devices: 28.5 us -> 25.1 us
    pallas_call x13, Pallas kernels: 32.6 us -> 36.3 us  [call(): pl.pallas_call(wrapped, out_shape=[jax.ShapeDtypeStruct(*o) for o in outs...]
    all_to_all x3, waiting for transfers between devices: 9.78 us -> 6.35 us  [exchange(): return lax.all_to_all(v, axes, split_axis=0, concat_axis=0, tiled=True)]
  transfers between devices with their start and end apart: 16 -> 16, of which waited for: 11 -> 11; matrix products, arithmetic and copies ran while one was open for 2% -> 2% of each run, Pallas kernels for 19% -> 21%
where the time goes in v9:
time: 139 us; the launch traced here: 138 us
  starting transfers between devices  48.3 us (35%)
  Pallas kernels  36.3 us (26%)
  waiting for transfers between devices  25.1 us (18%)
  blocking collectives  24.4 us (18%)
  local copies, waits for them, and re-layouts  2.85 us (2%)
    pallas_call x13, Pallas kernels, call(): pl.pallas_call(wrapped, out_shape=[jax.ShapeDtypeStruct(*o) for o in outs...  36.3 us
    all_to_all x1, blocking collectives, exchange(): return lax.all_to_all(v, axes, split_axis=0, concat_axis=0, tiled=True)  24.4 us
    all_to_all x3, starting transfers between devices, exchange(): return lax.all_to_all(v, axes, split_axis=0, concat_axis=0, tiled=True)  19.2 us
    ppermute x9, waiting for transfers between devices, move(): return lax.ppermute(v, axis, [(i, i ^ mask) for i in range(count)])  17.1 us
    ppermute x9, starting transfers between devices, move(): return lax.ppermute(v, axis, [(i, i ^ mask) for i in range(count)])  16 us
    ppermute x4, starting transfers between devices, swap(): return lax.ppermute(v, 'rep', [(0, 1), (1, 0)])  13.1 us
    all_to_all x3, waiting for transfers between devices, exchange(): return lax.all_to_all(v, axes, split_axis=0, concat_axis=0, tiled=True)  6.35 us
  transfers between devices with their start and end apart: 16, of which 11 were waited for; matrix products, arithmetic and copies ran while one was open for 2% of the time, Pallas kernels for 21%

profile of v9, /device:TPU:1, one launch (start us, length us, event | category | flops | bytes accessed | tf_op | source)
XLA Modules:
  0.0 138.4 jit_solution(9908315190031605143)
XLA Ops:
  0.6 3.3 %collective-permute-start = (f32[1024,512]{1,0:T(8,128)}, f32[1024,512]{1,0:T(8,128)S(1)}, u32[]{:S(2)}, u32[]{:S(2)}) collective-permute-start(f32[1024,512]{1,0:T(8,128)} %refs_3_.2), channel_id=1, source_target_pairs={{0,1},{1,0},{2,3},{3,2},{4,5},{5,4},{6,7},{7,6},{8,9},{9,8},{10,11... | collective-permute-start | bytes 6291464 | tf_op jit(solution)/shard_map/ppermute | solution.py:319
  4.0 0.8 copy.17
  4.7 24.4 %all_to_all.40 = s32[128,1,2]{2,1,0:T(1,128)} all-to-all(s32[128,1,2]{2,1,0:T(1,128)S(1)} %bitcast.28), channel_id=1, replica_groups=mesh['y'=4,'z'=8,'hist'=4,'rep'=2] {'y','z','hist'}, dimensions={0} | all-to-all | bytes 2048 | tf_op jit(solution)/shard_map/all_to_all | solution.py:315
  29.1 3.9 %shard_map.121 = f32[1024,128]{1,0:T(8,128)} custom-call(s32[128,2]{1,0:T(8,128)} %bitcast.29, f32[1280,512]{1,0:T(8,128)} %refs_3_.3), custom_call_target="tpu_custom_call" | custom-call | flops 1000000000 | bytes 3146752 | tf_op jit(solution)/shard_map/pallas_call | solution.py:106
  33.1 6.4 %all-to-all-start.1 = ((f32[128,8,128]{2,1,0:T(8,128)}), f32[128,8,128]{2,1,0:T(8,128)S(1)}, u32[]{:S(2)}, u32[]{:S(2)}) async-start(f32[128,8,128]{2,1,0:T(8,128)} %bitcast.26), calls=%async_computation.1 | async-start | bytes 1048576 | tf_op jit(solution)/shard_map/all_to_all | solution.py:315
  39.4 0.0 collective-permute-done.refs_4_
  39.5 0.0 copy-start.3
  39.5 1.3 copy-done.3
  40.8 0.0 copy-start
  40.8 0.0 copy-start.1
  40.8 10.9 %shard_map.122 = (f32[512,512]{1,0:T(8,128)}, bf16[512,512]{1,0:T(8,128)(2,1)}, bf16[512,512]{1,0:T(8,128)(2,1)}, bf16[512,512]{1,0:T(8,128)(2,1)}, bf16[512,512]{1,0:T(8,128)(2,1)}) custom-call(s32[1]{0:T(128)} %bitcast.refs_0_, s32[8,512]{1,0:T(8,128)} %bitcast.21, f32[8,512]{1,0:T(8,128)} %bitcast.23, f32[1024,512]{1,0:T(8,128)} %refs_3_.2, ...), custom_call_target="tpu_custom_call" | custom-call | flops 6000000000 | bytes 12615684 | tf_op jit(solution)/shard_map/pallas_call | solution.py:106
  51.7 3.9 %all-to-all-done.1 = f32[128,8,128]{2,1,0:T(8,128)S(1)} async-done(((f32[128,8,128]{2,1,0:T(8,128)}), f32[128,8,128]{2,1,0:T(8,128)S(1)}, u32[]{:S(2)}, u32[]{:S(2)}) %all-to-all-start.1) | async-done | bytes 524320 | tf_op jit(solution)/shard_map/all_to_all | solution.py:315
  55.6 0.0 copy-done
  55.6 0.0 copy-done.1
  55.6 0.0 copy-start.2
  55.6 5.9 %shard_map.123 = (f32[32,4,16,128]{3,2,1,0:T(8,128)}, f32[256,512]{1,0:T(8,128)S(1)}, f32[256,512]{1,0:T(8,128)S(1)}, f32[512,512]{1,0:T(8,128)}) custom-call(s32[1]{0:T(128)} %bitcast.refs_0_, f32[1024,128]{1,0:T(8,128)S(1)} %bitcast.18, s32[8,512]{1,0:T(8,128)S(1)} %bitcast.22, f32[8,512]{1,0:T(8,128)S(1)} %bitcast.24, ...), custom_call_target="tpu_custom_call" | custom-call | flops 3000000000 | bytes 7897092 | tf_op jit(solution)/shard_map/pallas_call | solution.py:106
  61.5 9.2 %all-to-all-start.2 = ((f32[128,16,128]{2,1,0:T(8,128)}), f32[128,16,128]{2,1,0:T(8,128)S(1)}, u32[]{:S(2)}, u32[]{:S(2)}) async-start(f32[128,16,128]{2,1,0:T(8,128)} %bitcast.25), calls=%async_computation.2 | async-start | bytes 2097152 | tf_op jit(solution)/shard_map/all_to_all | solution.py:315
  70.7 2.3 %collective-permute-start.1 = (f32[256,512]{1,0:T(8,128)S(1)}, f32[256,512]{1,0:T(8,128)S(1)}, u32[]{:S(2)}, u32[]{:S(2)}) collective-permute-start(f32[256,512]{1,0:T(8,128)S(1)} %get-tuple-element.40), channel_id=1, source_target_pairs={{0,1},{1,0},{2,3},{3,2},{4,5},{5,4},{6,7},{7,6},{8,9},{9,8},{10,11... | collective-permute-start | bytes 1572872 | tf_op jit(solution)/shard_map/ppermute | solution.py:319
  73.0 0.5 broadcast.3
  73.5 0.0 copy-done.2
  73.5 0.6 reduce.3
  74.2 0.1 reshape.33
  74.3 0.1 copy.18
  74.4 0.1 collective-permute-done.1.refs_2_
  74.5 0.1 shard_map.124
  74.6 0.9 collective-permute-start.2
  75.6 2.4 %collective-permute-start.3 = (f32[64,512]{1,0:T(8,128)S(1)}, f32[64,512]{1,0:T(8,128)S(1)}, u32[]{:S(2)}, u32[]{:S(2)}) collective-permute-start(f32[64,512]{1,0:T(8,128)S(1)} %get-tuple-element.44), channel_id=1, source_target_pairs={{0,4},{2,6},{4,0},{6,2},{1,5},{3,7},{5,1},{7,3},{8,12},{10,14},{12... | collective-permute-start | bytes 393224 | tf_op jit(solution)/shard_map/ppermute | solution.py:324
  78.0 0.6 collective-permute-start.4
  78.6 4.6 %shard_map.125 = f32[512,512]{1,0:T(8,128)} custom-call(f32[512,512]{1,0:T(8,128)} %get-tuple-element.46.refs_0_, f32[512,512]{1,0:T(8,128)} %refs_1_.3, bf16[512,512]{1,0:T(8,128)(2,1)} %get-tuple-element.47.refs_2_, bf16[512,512]{1,0:T(8,128)(2,1)} %get-tuple-element.48.refs_3_), custom_call_target="tpu_custom_call" | custom-call | flops 2000000000 | bytes 5242880 | tf_op jit(solution)/shard_map/pallas_call | solution.py:106
  83.2 0.0 collective-permute-done.2.refs_2_
  83.2 4.8 %collective-permute-done.3.refs_3_ = f32[64,512]{1,0:T(8,128)S(1)} collective-permute-done((f32[64,512]{1,0:T(8,128)S(1)}, f32[64,512]{1,0:T(8,128)S(1)}, u32[]{:S(2)}, u32[]{:S(2)}) %collective-permute-start.3) | collective-permute-done | bytes 131104 | tf_op jit(solution)/shard_map/ppermute | solution.py:324
  88.0 2.1 %collective-permute-done.4.refs_4_ = f32[64,512]{1,0:T(8,128)S(1)} collective-permute-done((f32[64,512]{1,0:T(8,128)S(1)}, f32[64,512]{1,0:T(8,128)S(1)}, u32[]{:S(2)}, u32[]{:S(2)}) %collective-permute-start.4) | collective-permute-done | bytes 131104 | tf_op jit(solution)/shard_map/ppermute | solution.py:324
  90.2 1.3 collective-permute-start.5
  91.5 2.8 %collective-permute-start.6 = (f32[16,512]{1,0:T(8,128)S(1)}, f32[16,512]{1,0:T(8,128)S(1)}, u32[]{:S(2)}, u32[]{:S(2)}) collective-permute-start(f32[16,512]{1,0:T(8,128)S(1)} %get-tuple-element.55), channel_id=1, source_target_pairs={{0,128},{64,192},{128,0},{192,64},{1,129},{65,193},{129,1},{193,65... | collective-permute-start | bytes 98312 | tf_op jit(solution)/shard_map/ppermute | solution.py:324
  94.3 0.0 collective-permute-start.7
  94.3 0.0 collective-permute-done.5.refs_1_
  94.3 2.4 %collective-permute-done.6.refs_2_ = f32[16,512]{1,0:T(8,128)S(1)} collective-permute-done((f32[16,512]{1,0:T(8,128)S(1)}, f32[16,512]{1,0:T(8,128)S(1)}, u32[]{:S(2)}, u32[]{:S(2)}) %collective-permute-start.6) | collective-permute-done | bytes 32800 | tf_op jit(solution)/shard_map/ppermute | solution.py:324
  96.8 2.3 %collective-permute-done.7.refs_3_ = f32[16,512]{1,0:T(8,128)S(1)} collective-permute-done((f32[16,512]{1,0:T(8,128)S(1)}, f32[16,512]{1,0:T(8,128)S(1)}, u32[]{:S(2)}, u32[]{:S(2)}) %collective-permute-start.7) | collective-permute-done | bytes 32800 | tf_op jit(solution)/shard_map/ppermute | solution.py:324
  99.1 1.7 %collective-permute-start.8 = (f32[16,512]{1,0:T(8,128)S(1)}, f32[16,512]{1,0:T(8,128)S(1)}, u32[]{:S(2)}, u32[]{:S(2)}) collective-permute-start(f32[16,512]{1,0:T(8,128)S(1)} %shard_map.127.refs_0_), channel_id=1, source_target_pairs={{0,8},{8,0},{16,24},{24,16},{32,40},{40,32},{48,56},{56,48},{1,9},... | collective-permute-start | bytes 98312 | tf_op jit(solution)/shard_map/ppermute | solution.py:324
  100.8 1.3 collective-permute-done.8.refs_1_
  102.1 2.0 %collective-permute-start.9 = (f32[16,512]{1,0:T(8,128)S(1)}, f32[16,512]{1,0:T(8,128)S(1)}, u32[]{:S(2)}, u32[]{:S(2)}) collective-permute-start(f32[16,512]{1,0:T(8,128)S(1)} %shard_map.128.refs_0_), channel_id=1, source_target_pairs={{0,16},{8,24},{16,0},{24,8},{32,48},{40,56},{48,32},{56,40},{1,17}... | collective-permute-start | bytes 98312 | tf_op jit(solution)/shard_map/ppermute | solution.py:324
  104.1 1.7 %collective-permute-done.9.refs_1_ = f32[16,512]{1,0:T(8,128)S(1)} collective-permute-done((f32[16,512]{1,0:T(8,128)S(1)}, f32[16,512]{1,0:T(8,128)S(1)}, u32[]{:S(2)}, u32[]{:S(2)}) %collective-permute-start.9) | collective-permute-done | bytes 32800 | tf_op jit(solution)/shard_map/ppermute | solution.py:324
  105.8 4.2 %collective-permute-start.10 = (f32[16,512]{1,0:T(8,128)S(1)}, f32[16,512]{1,0:T(8,128)S(1)}, u32[]{:S(2)}, u32[]{:S(2)}) collective-permute-start(f32[16,512]{1,0:T(8,128)S(1)} %shard_map.129.refs_0_), channel_id=1, source_target_pairs={{0,32},{8,40},{16,48},{24,56},{32,0},{40,8},{48,16},{56,24},{1,33}... | collective-permute-start | bytes 98312 | tf_op jit(solution)/shard_map/ppermute | solution.py:324
  110.0 2.5 %collective-permute-done.10.refs_1_ = f32[16,512]{1,0:T(8,128)S(1)} collective-permute-done((f32[16,512]{1,0:T(8,128)S(1)}, f32[16,512]{1,0:T(8,128)S(1)}, u32[]{:S(2)}, u32[]{:S(2)}) %collective-permute-start.10) | collective-permute-done | bytes 32800 | tf_op jit(solution)/shard_map/ppermute | solution.py:324
  112.5 0.9 shard_map.130
  113.3 0.0 all-to-all-done.2
  113.3 6.4 %collective-permute-start.11 = (f32[2048,128]{1,0:T(8,128)S(1)}, f32[2048,128]{1,0:T(8,128)S(1)}, u32[]{:S(2)}, u32[]{:S(2)}) collective-permute-start(f32[2048,128]{1,0:T(8,128)S(1)} %bitcast.16), channel_id=1, source_target_pairs={{0,1},{1,0},{2,3},{3,2},{4,5},{5,4},{6,7},{7,6},{8,9},{9,8},{10,11... | collective-permute-start | bytes 3145736 | tf_op jit(solution)/shard_map/ppermute | solution.py:319
  119.7 3.6 %all-to-all-start.3 = ((f32[16,16,512]{2,1,0:T(8,128)}), f32[16,16,512]{2,1,0:T(8,128)S(1)}, u32[]{:S(2)}, u32[]{:S(2)}) async-start(f32[16,16,512]{2,1,0:T(8,128)} %shard_map.130), calls=%async_computation.3 | async-start | bytes 1048576 | tf_op jit(solution)/shard_map/all_to_all | solution.py:315
  123.3 4.5 %shard_map.131.refs_3_ = f32[1280,512]{1,0:T(8,128)} custom-call(s32[1]{0:T(128)} %bitcast.refs_0_, s32[2,512]{1,0:T(2,128)S(1)} %bitcast.19, f32[2048,128]{1,0:T(8,128)S(1)} %bitcast.17, f32[1280,512]{1,0:T(8,128)} %refs_3_.3), custom_call_target="tpu_custom_call" | custom-call | flops 2000000000 | bytes 6295556 | tf_op jit(solution)/shard_map/pallas_call | solution.py:106
  127.8 0.0 collective-permute-done.11.refs_2_
  127.8 4.4 %shard_map.132 = f32[1280,512]{1,0:T(8,128)} custom-call(s32[1]{0:T(128)S(6)} %sub.3.refs_0_, s32[2,512]{1,0:T(2,128)S(1)} %bitcast.20, f32[2048,128]{1,0:T(8,128)S(1)} %collective-permute-done.11.refs_2_, f32[1280,512]{1,0:T(8,128)} %shard_map.131.refs_3_), custom_call_target="tpu_custom_call" | custom-call | flops 2000000000 | bytes 6295556 | tf_op jit(solution)/shard_map/pallas_call | solution.py:106
  132.2 2.5 %all-to-all-done.3.refs_1_ = f32[16,16,512]{2,1,0:T(8,128)S(1)} async-done(((f32[16,16,512]{2,1,0:T(8,128)}), f32[16,16,512]{2,1,0:T(8,128)S(1)}, u32[]{:S(2)}, u32[]{:S(2)}) %all-to-all-start.3) | async-done | bytes 524320 | tf_op jit(solution)/shard_map/all_to_all | solution.py:315
  134.7 1.1 collective-permute-start.12
  135.8 1.5 %collective-permute-done.12.refs_2_ = f32[16,16,512]{2,1,0:T(8,128)S(1)} collective-permute-done((f32[16,16,512]{2,1,0:T(8,128)S(1)}, f32[16,16,512]{2,1,0:T(8,128)S(1)}, u32[]{:S(2)}, u32[]{:S(2)}) %collective-permute-start.12) | collective-permute-done | bytes 524320 | tf_op jit(solution)/shard_map/ppermute | solution.py:319
  137.3 1.1 shard_map.133
  (5 shorter events, 0.1 us)
Async XLA Ops:
  0.6 38.8 %collective-permute-start = (f32[1024,512]{1,0:T(8,128)}, f32[1024,512]{1,0:T(8,128)S(1)}, u32[]{:S(2)}, u32[]{:S(2)}) collective-permute-start(f32[1024,512]{1,0:T(8,128)} %refs_3_.2), channel_id=1, source_target_pairs={{0,1},{1,0},{2,3},{3,2},{4,5},{5,4},{6,7},{7,6},{8,9},{9,8},{10,11... | collective-permute-start | bytes 6291464 | tf_op jit(solution)/shard_map/ppermute | solution.py:319
  33.1 22.5 %all-to-all-start.1 = ((f32[128,8,128]{2,1,0:T(8,128)}), f32[128,8,128]{2,1,0:T(8,128)S(1)}, u32[]{:S(2)}, u32[]{:S(2)}) async-start(f32[128,8,128]{2,1,0:T(8,128)} %bitcast.26), calls=%async_computation.1 | async-start | bytes 1048576 | tf_op jit(solution)/shard_map/all_to_all | solution.py:315
  39.5 1.3 copy-start.3
  40.8 14.8 %copy-start = (s32[512,8]{0,1:T(8,128)S(1)}, s32[512,8]{0,1:T(8,128)}, u32[]{:S(2)}) copy-start(s32[512,8]{0,1:T(8,128)} %param.15) | copy-start | bytes 49156
  40.8 14.8 %copy-start.1 = (f32[512,8]{0,1:T(8,128)S(1)}, f32[512,8]{0,1:T(8,128)}, u32[]{:S(2)}) copy-start(f32[512,8]{0,1:T(8,128)} %param.14) | copy-start | bytes 49156
  55.6 18.0 %copy-start.2 = (s32[1,1024]{1,0:T(1,128)S(1)}, s32[1,1024]{1,0:T(1,128)}, u32[]{:S(2)}) copy-start(s32[1,1024]{1,0:T(1,128)} %param.19) | copy-start | bytes 12292
  61.5 51.8 %all-to-all-start.2 = ((f32[128,16,128]{2,1,0:T(8,128)}), f32[128,16,128]{2,1,0:T(8,128)S(1)}, u32[]{:S(2)}, u32[]{:S(2)}) async-start(f32[128,16,128]{2,1,0:T(8,128)} %bitcast.25), calls=%async_computation.2 | async-start | bytes 2097152 | tf_op jit(solution)/shard_map/all_to_all | solution.py:315
  70.7 3.8 %collective-permute-start.1 = (f32[256,512]{1,0:T(8,128)S(1)}, f32[256,512]{1,0:T(8,128)S(1)}, u32[]{:S(2)}, u32[]{:S(2)}) collective-permute-start(f32[256,512]{1,0:T(8,128)S(1)} %get-tuple-element.40), channel_id=1, source_target_pairs={{0,1},{1,0},{2,3},{3,2},{4,5},{5,4},{6,7},{7,6},{8,9},{9,8},{10,11... | collective-permute-start | bytes 1572872 | tf_op jit(solution)/shard_map/ppermute | solution.py:319
  74.6 8.6 %collective-permute-start.2 = (f32[64,512]{1,0:T(8,128)S(1)}, f32[64,512]{1,0:T(8,128)S(1)}, u32[]{:S(2)}, u32[]{:S(2)}) collective-permute-start(f32[64,512]{1,0:T(8,128)S(1)} %get-tuple-element.43), channel_id=1, source_target_pairs={{0,2},{2,0},{4,6},{6,4},{1,3},{3,1},{5,7},{7,5},{8,10},{10,8},{12,... | collective-permute-start | bytes 393224 | tf_op jit(solution)/shard_map/ppermute | solution.py:324
  75.6 12.5 %collective-permute-start.3 = (f32[64,512]{1,0:T(8,128)S(1)}, f32[64,512]{1,0:T(8,128)S(1)}, u32[]{:S(2)}, u32[]{:S(2)}) collective-permute-start(f32[64,512]{1,0:T(8,128)S(1)} %get-tuple-element.44), channel_id=1, source_target_pairs={{0,4},{2,6},{4,0},{6,2},{1,5},{3,7},{5,1},{7,3},{8,12},{10,14},{12... | collective-permute-start | bytes 393224 | tf_op jit(solution)/shard_map/ppermute | solution.py:324
  78.0 12.2 %collective-permute-start.4 = (f32[64,512]{1,0:T(8,128)S(1)}, f32[64,512]{1,0:T(8,128)S(1)}, u32[]{:S(2)}, u32[]{:S(2)}) collective-permute-start(f32[64,512]{1,0:T(8,128)S(1)} %get-tuple-element.45), channel_id=1, source_target_pairs={{0,6},{2,4},{4,2},{6,0},{1,7},{3,5},{5,3},{7,1},{8,14},{10,12},{12... | collective-permute-start | bytes 393224 | tf_op jit(solution)/shard_map/ppermute | solution.py:324
  90.2 4.1 %collective-permute-start.5 = (f32[16,512]{1,0:T(8,128)S(1)}, f32[16,512]{1,0:T(8,128)S(1)}, u32[]{:S(2)}, u32[]{:S(2)}) collective-permute-start(f32[16,512]{1,0:T(8,128)S(1)} %get-tuple-element.54), channel_id=1, source_target_pairs={{0,64},{64,0},{128,192},{192,128},{1,65},{65,1},{129,193},{193,129... | collective-permute-start | bytes 98312 | tf_op jit(solution)/shard_map/ppermute | solution.py:324
  91.5 5.3 %collective-permute-start.6 = (f32[16,512]{1,0:T(8,128)S(1)}, f32[16,512]{1,0:T(8,128)S(1)}, u32[]{:S(2)}, u32[]{:S(2)}) collective-permute-start(f32[16,512]{1,0:T(8,128)S(1)} %get-tuple-element.55), channel_id=1, source_target_pairs={{0,128},{64,192},{128,0},{192,64},{1,129},{65,193},{129,1},{193,65... | collective-permute-start | bytes 98312 | tf_op jit(solution)/shard_map/ppermute | solution.py:324
  94.3 4.7 %collective-permute-start.7 = (f32[16,512]{1,0:T(8,128)S(1)}, f32[16,512]{1,0:T(8,128)S(1)}, u32[]{:S(2)}, u32[]{:S(2)}) collective-permute-start(f32[16,512]{1,0:T(8,128)S(1)} %get-tuple-element.56), channel_id=1, source_target_pairs={{0,192},{64,128},{128,64},{192,0},{1,193},{65,129},{129,65},{193,1... | collective-permute-start | bytes 98312 | tf_op jit(solution)/shard_map/ppermute | solution.py:324
  99.1 3.0 %collective-permute-start.8 = (f32[16,512]{1,0:T(8,128)S(1)}, f32[16,512]{1,0:T(8,128)S(1)}, u32[]{:S(2)}, u32[]{:S(2)}) collective-permute-start(f32[16,512]{1,0:T(8,128)S(1)} %shard_map.127.refs_0_), channel_id=1, source_target_pairs={{0,8},{8,0},{16,24},{24,16},{32,40},{40,32},{48,56},{56,48},{1,9},... | collective-permute-start | bytes 98312 | tf_op jit(solution)/shard_map/ppermute | solution.py:324
  102.1 3.7 %collective-permute-start.9 = (f32[16,512]{1,0:T(8,128)S(1)}, f32[16,512]{1,0:T(8,128)S(1)}, u32[]{:S(2)}, u32[]{:S(2)}) collective-permute-start(f32[16,512]{1,0:T(8,128)S(1)} %shard_map.128.refs_0_), channel_id=1, source_target_pairs={{0,16},{8,24},{16,0},{24,8},{32,48},{40,56},{48,32},{56,40},{1,17}... | collective-permute-start | bytes 98312 | tf_op jit(solution)/shard_map/ppermute | solution.py:324
  105.8 6.7 %collective-permute-start.10 = (f32[16,512]{1,0:T(8,128)S(1)}, f32[16,512]{1,0:T(8,128)S(1)}, u32[]{:S(2)}, u32[]{:S(2)}) collective-permute-start(f32[16,512]{1,0:T(8,128)S(1)} %shard_map.129.refs_0_), channel_id=1, source_target_pairs={{0,32},{8,40},{16,48},{24,56},{32,0},{40,8},{48,16},{56,24},{1,33}... | collective-permute-start | bytes 98312 | tf_op jit(solution)/shard_map/ppermute | solution.py:324
  113.3 14.4 %collective-permute-start.11 = (f32[2048,128]{1,0:T(8,128)S(1)}, f32[2048,128]{1,0:T(8,128)S(1)}, u32[]{:S(2)}, u32[]{:S(2)}) collective-permute-start(f32[2048,128]{1,0:T(8,128)S(1)} %bitcast.16), channel_id=1, source_target_pairs={{0,1},{1,0},{2,3},{3,2},{4,5},{5,4},{6,7},{7,6},{8,9},{9,8},{10,11... | collective-permute-start | bytes 3145736 | tf_op jit(solution)/shard_map/ppermute | solution.py:319
  119.7 15.0 %all-to-all-start.3 = ((f32[16,16,512]{2,1,0:T(8,128)}), f32[16,16,512]{2,1,0:T(8,128)S(1)}, u32[]{:S(2)}, u32[]{:S(2)}) async-start(f32[16,16,512]{2,1,0:T(8,128)} %shard_map.130), calls=%async_computation.3 | async-start | bytes 1048576 | tf_op jit(solution)/shard_map/all_to_all | solution.py:315
  134.7 2.6 %collective-permute-start.12 = (f32[16,16,512]{2,1,0:T(8,128)S(1)}, f32[16,16,512]{2,1,0:T(8,128)S(1)}, u32[]{:S(2)}, u32[]{:S(2)}) collective-permute-start(f32[16,16,512]{2,1,0:T(8,128)S(1)} %all-to-all-done.3.refs_1_), channel_id=1, source_target_pairs={{0,1},{1,0},{2,3},{3,2},{4,5},{5,4},{6,7},{7,6},{8,9},{9,8},{10,11... | collective-permute-start | bytes 1572872 | tf_op jit(solution)/shard_map/ppermute | solution.py:319

commit v10 on v9

--- a/solution.py
+++ b/solution.py
@@ -46,29 +46,30 @@
 
 
 class Source:
-    def __init__(self, ref, buffer, sem, rows=None):
-        rows = rows or ref.shape[0]
+    def __init__(self, ref, buffer, sem, chunks=1):
+        rows = ref.shape[0] // chunks
         self.buffer, self.copies, self.shape = buffer, [], ref.shape
-        for i in range(ref.shape[0] // rows):
+        for i in range(chunks):
             at = (pl.ds(i * rows, rows),) + (slice(None),) * (len(ref.shape) - 1)
             copy = pltpu.make_async_copy(ref.at[at], buffer.at[at], sem.at[i])
             copy.start()
             self.copies.append(copy)
 
     def __getitem__(self, index):
-        for copy in self.copies:
-            copy.wait()
-        self.copies = []
+        for i in range(len(self.copies)):
+            self.part(i)
         return self.buffer[index]
 
     def part(self, i):
-        self.copies[i].wait()
+        if self.copies[i] is not None:
+            self.copies[i].wait()
+        self.copies[i] = None
 
 
 class Sink:
-    def __init__(self, ref, buffer, sem, rows=None):
+    def __init__(self, ref, buffer, sem, chunks=1):
         self.ref, self.buffer, self.sem = ref, buffer, sem
-        self.rows, self.copies = rows or ref.shape[0], []
+        self.rows, self.copies = ref.shape[0] // chunks, []
         self.shape = ref.shape
 
     def __setitem__(self, index, value):
@@ -81,20 +82,20 @@
         self.copies.append(copy)
 
 
-def call(kernel, outs, args, spaces=None, scratch=(), limit=8, flops=0, rows=None):
+def call(kernel, outs, args, spaces=None, scratch=(), limit=8, flops=0, chunks=1):
     spaces = spaces or "v" * (len(args) + len(outs))
     shapes = [(a.shape, a.dtype) for a in args] + list(outs)
     where = {"s": SMEM, "v": VMEM, "h": HBM}
     remote = [i for i, space in enumerate(spaces) if space == "h"]
     buffers = [pltpu.VMEM(*shapes[i]) for i in remote]
-    sems = [pltpu.SemaphoreType.DMA((shapes[i][0][0] // rows if rows else 1,)) for i in remote]
+    sems = [pltpu.SemaphoreType.DMA((chunks,)) for _ in remote]
 
     def wrapped(*refs):
         refs, rest = list(refs[: len(shapes)]), refs[len(shapes) :]
         sinks = []
         for n, i in enumerate(remote):
             kind = Source if i < len(args) else Sink
-            refs[i] = kind(refs[i], rest[n], rest[len(remote) + n], rows)
+            refs[i] = kind(refs[i], rest[n], rest[len(remote) + n], chunks)
             if kind is Sink:
                 sinks.append(refs[i])
         kernel(*refs, *rest[2 * len(remote) :])
@@ -116,14 +117,11 @@
 
 def gather_kernel(idx_ref, cold_ref, out_ref):
     owners, per = idx_ref.shape
-    step = cold_ref.shape[0] // len(cold_ref.copies)
-    found = jnp.zeros((per * owners, cold_ref.shape[1]), F32)
-    idx = jnp.concatenate([idx_ref[:, s : s + 1] for s in range(per)], axis=0)
-    picks = [one_hot(idx - block * step, step) for block in range(len(cold_ref.copies))]
-    for block, pick in enumerate(picks):
-        cold_ref.part(block)
-        high, low = split(cold_ref.buffer[block * step : (block + 1) * step, :])
-        found = found + (dot(pick, high) + dot(pick, low))
+    high, low = split(cold_ref[...])
+    pick = jnp.concatenate(
+        [one_hot(idx_ref[:, s : s + 1], cold_ref.shape[0]) for s in range(per)], axis=0
+    )
+    found = dot(pick, high) + dot(pick, low)
     for s in range(per):
         for l in range(4):
             out_ref[pl.ds(s * 4 + l, owners, stride=per * 4), :] = found[
@@ -132,15 +130,10 @@
 
 
 def prepare_kernel(
-    core_ref, nbr_ref, ew_ref, mine_ref, other_ref, node_ref, init_ref, weight_ref,
-    part_ref, high_ref, low_ref, whigh_ref, wlow_ref, *, halo_count,
+    core_ref, nbr_ref, ew_ref, mine_ref, other_ref, node_ref, init_ref,
+    part_ref, high_ref, low_ref, *, halo_count,
 ):
     rows = node_ref.shape[0]
-    weights = split(weight_ref[...])
-    whigh_ref[...] = weights[0]
-    wlow_ref[...] = weights[1]
-    whigh_ref.push()
-    wlow_ref.push()
     half = mine_ref.shape[0]
     core = core_ref[0]
     nbr = nbr_ref[...].T
@@ -166,13 +159,13 @@
 
 
 def layer_kernel(
-    core_ref, halo_ref, nbr_ref, ew_ref, part_ref, whigh_ref, wlow_ref, cot_ref,
+    core_ref, halo_ref, nbr_ref, ew_ref, part_ref, weight_ref, cot_ref,
     out_ref, keep_ref, give_ref, du_ref,
     term_ref, work_ref, zhigh_ref, zlow_ref, dhigh_ref, dlow_ref,
 ):
     owners = halo_ref.shape[0] // 8
     rows = part_ref.shape[0]
-    block, step = 128, 32
+    block, step = rows // 4, 32
     halo = jnp.concatenate(
         [
             jnp.concatenate(
@@ -190,18 +183,20 @@
     for start in range(0, rows, block):
         whole = slice(start, start + block)
         work_ref[whole, :] = dot(pick[whole], high) + dot(pick[whole], low)
+        part_ref.part(start // block)
         for first in range(start, start + block, step):
             at = slice(first, first + step)
-            z = part_ref[at, :] + scale[at] * work_ref[at, :]
+            z = part_ref.buffer[at, :] + scale[at] * work_ref[at, :]
             zs = split(z)
             work_ref[at, :] = z
             zhigh_ref[at, :] = zs[0]
             zlow_ref[at, :] = zs[1]
-    weights = whigh_ref[...], wlow_ref[...]
+    weights = split(weight_ref[...])
     for start in range(0, rows, block):
         whole = slice(start, start + block)
         mixed = dot3((zhigh_ref[whole, :], zlow_ref[whole, :]), weights)
         work_ref[whole, :] = (1.0 - BETA) * work_ref[whole, :] + BETA * mixed
+        cot_ref.part(start // block)
         for first in range(start, start + block, step):
             at = slice(first, first + step)
             u = work_ref[at, :]
@@ -211,7 +206,7 @@
             slope = 0.5 * (1.0 + bent) + (0.5 * u) * (1.0 - bent * bent) * (
                 GELU_C * (1.0 + (3.0 * GELU_A) * square)
             )
-            du = cot_ref[at, :] * slope
+            du = cot_ref.buffer[at, :] * slope
             du_ref[at, :] = du
             ds = split(du)
             dhigh_ref[at, :] = ds[0]
@@ -227,8 +222,8 @@
                 for h in range(2):
                     out_ref[group, 2 * h, 8 * pair : 8 * pair + 8, :] = even[:, h]
                     out_ref[group, 2 * h + 1, 8 * pair : 8 * pair + 8, :] = odd[:, h]
-    out_ref.push()
-    du_ref.push()
+        out_ref.push(start // block)
+        du_ref.push(start // block)
     term_ref[...] = dot3(
         (zhigh_ref[...], zlow_ref[...]), (dhigh_ref[...], dlow_ref[...]), 0, 0
     )
@@ -307,7 +302,7 @@
         scratch=[pltpu.VMEM((rows, width), BF16), pltpu.VMEM((rows, width), BF16)],
         limit=52,
         flops=2 * 10**9,
-        rows=256,
+        chunks=5,
     )[0]
 
 
@@ -376,18 +371,15 @@
         gather_kernel,
         [((halo_count * 4, 128), F32)],
         (wanted, cold_history),
-        spaces="vhv",
-        rows=256,
-        limit=60,
+        limit=16,
         flops=10**9,
     )
     halo = exchange(found)
-    square = ((width, width), BF16)
-    part, high, low, *weights = call(
+    part, high, low = call(
         functools.partial(prepare_kernel, halo_count=halo_count),
-        [(full, F32), ((rows, rows), BF16), ((rows, rows), BF16), square, square],
-        (core, nbr, ew, hot_history, swap(hot_history), node_input, initial, weight),
-        spaces="svvhhhhhhhhhh",
+        [(full, F32), ((rows, rows), BF16), ((rows, rows), BF16)],
+        (core, nbr, ew, hot_history, swap(hot_history), node_input, initial),
+        spaces="svvhhhhhhh",
         limit=60,
         flops=6 * 10**9,
     )
@@ -395,8 +387,9 @@
     outgoing, keep, give, du = call(
         layer_kernel,
         [((owners // 4, 4, 16, 128), F32), (half, F32), (half, F32), (full, F32)],
-        (core, halo, nbr, ew, part, *weights, cotangent),
-        spaces="svvvhhhhhvvh",
+        (core, halo, nbr, ew, part, weight, cotangent),
+        spaces="svvvhhhhvvh",
+        chunks=4,
         scratch=[pltpu.VMEM((width, width), F32), pltpu.VMEM(full, F32)]
         + [pltpu.VMEM(full, BF16)] * 4,
         limit=52,

time: 139 us -> 137 us (0.986)
  Pallas kernels: 36.3 us -> 30.4 us
  waiting for transfers between devices: 25.1 us -> 28.6 us
  local copies, waits for them, and re-layouts: 2.85 us -> 4.63 us
    pallas_call x13, Pallas kernels: 36.3 us -> 30.4 us  [call(): pl.pallas_call(wrapped, out_shape=[jax.ShapeDtypeStruct(*o) for o in outs...]
    all_to_all x3, waiting for transfers between devices: 6.35 us -> 9.97 us  [exchange(): return lax.all_to_all(v, axes, split_axis=0, concat_axis=0, tiled=True)]
    unnamed x11 -> x13, local copies, waits for them, and re-layouts: 2.64 us -> 4.43 us
  transfers between devices with their start and end apart: 16 -> 16, of which waited for: 11 -> 11; matrix products, arithmetic and copies ran while one was open for 2% -> 2% of each run, Pallas kernels for 21% -> 17%
where the time goes in v10:
time: 137 us
  starting transfers between devices  47.6 us (35%)
  Pallas kernels  30.4 us (22%)
  waiting for transfers between devices  28.6 us (21%)
  blocking collectives  24.1 us (18%)
  local copies, waits for them, and re-layouts  4.63 us (3%)
    pallas_call x13, Pallas kernels, call(): pl.pallas_call(wrapped, out_shape=[jax.ShapeDtypeStruct(*o) for o in outs...  30.4 us
    all_to_all x1, blocking collectives, exchange(): return lax.all_to_all(v, axes, split_axis=0, concat_axis=0, tiled=True)  24.1 us
    all_to_all x3, starting transfers between devices, exchange(): return lax.all_to_all(v, axes, split_axis=0, concat_axis=0, tiled=True)  18.5 us
    ppermute x9, waiting for transfers between devices, move(): return lax.ppermute(v, axis, [(i, i ^ mask) for i in range(count)])  17 us
    ppermute x9, starting transfers between devices, move(): return lax.ppermute(v, axis, [(i, i ^ mask) for i in range(count)])  16 us
    ppermute x4, starting transfers between devices, swap(): return lax.ppermute(v, 'rep', [(0, 1), (1, 0)])  13.1 us
    all_to_all x3, waiting for transfers between devices, exchange(): return lax.all_to_all(v, axes, split_axis=0, concat_axis=0, tiled=True)  9.97 us
    unnamed x13, local copies, waits for them, and re-layouts  4.43 us
  transfers between devices with their start and end apart: 16, of which 11 were waited for; matrix products, arithmetic and copies ran while one was open for 2% of the time, Pallas kernels for 17%

profile of v10, /device:TPU:1, one launch (start us, length us, event | category | flops | bytes accessed | tf_op | source)
XLA Modules:
  0.0 136.9 jit_solution(16390443509004158990)
XLA Ops:
  0.6 3.3 %collective-permute-start = (f32[1024,512]{1,0:T(8,128)}, f32[1024,512]{1,0:T(8,128)S(1)}, u32[]{:S(2)}, u32[]{:S(2)}) collective-permute-start(f32[1024,512]{1,0:T(8,128)} %refs_3_.2), channel_id=1, source_target_pairs={{0,1},{1,0},{2,3},{3,2},{4,5},{5,4},{6,7},{7,6},{8,9},{9,8},{10,11... | collective-permute-start | bytes 6291464 | tf_op jit(solution)/shard_map/ppermute | solution.py:314
  4.0 0.8 copy.17
  4.7 24.1 %all_to_all.40 = s32[128,1,2]{2,1,0:T(1,128)S(1)} all-to-all(s32[128,1,2]{2,1,0:T(1,128)S(1)} %bitcast.28), channel_id=1, replica_groups=mesh['y'=4,'z'=8,'hist'=4,'rep'=2] {'y','z','hist'}, dimensions={0} | all-to-all | bytes 2048 | tf_op jit(solution)/shard_map/all_to_all | solution.py:310
  28.9 0.0 copy-start
  28.9 1.7 %copy-done = f32[1280,512]{1,0:T(8,128)S(1)} copy-done((f32[1280,512]{1,0:T(8,128)S(1)}, f32[1280,512]{1,0:T(8,128)}, u32[]{:S(2)}) %copy-start) | copy-done | bytes 2621464
  30.6 1.8 %shard_map.121 = f32[1024,128]{1,0:T(8,128)} custom-call(s32[128,2]{1,0:T(8,128)S(1)} %bitcast.19, f32[1280,512]{1,0:T(8,128)S(1)} %copy-done), custom_call_target="tpu_custom_call" | custom-call | flops 1000000000 | bytes 3146752 | tf_op jit(solution)/shard_map/pallas_call | solution.py:107
  32.4 6.4 %all-to-all-start.1 = ((f32[128,8,128]{2,1,0:T(8,128)}), f32[128,8,128]{2,1,0:T(8,128)S(1)}, u32[]{:S(2)}, u32[]{:S(2)}) async-start(f32[128,8,128]{2,1,0:T(8,128)} %bitcast.3), calls=%async_computation.1 | async-start | bytes 1048576 | tf_op jit(solution)/shard_map/all_to_all | solution.py:310
  38.7 0.0 collective-permute-done.refs_4_
  38.8 0.0 copy-start.4
  38.8 1.3 copy-done.4
  40.1 0.0 copy-start.1
  40.1 0.0 copy-start.2
  40.1 7.5 %shard_map.122 = (f32[512,512]{1,0:T(8,128)}, bf16[512,512]{1,0:T(8,128)(2,1)}, bf16[512,512]{1,0:T(8,128)(2,1)}) custom-call(s32[1]{0:T(128)} %bitcast.refs_0_, s32[8,512]{1,0:T(8,128)} %bitcast.22, f32[8,512]{1,0:T(8,128)} %bitcast.24, f32[1024,512]{1,0:T(8,128)} %refs_3_.2, f32[1024,512]{1,0:T(8,128)} %copy-done.4, f32[512,512]{1,0:T(8,128)} %refs_5_.2, ...), custom_call_target="tpu_custom_call" | custom-call | flops 6000000000 | bytes 9469956 | tf_op jit(solution)/shard_map/pallas_call | solution.py:107
  47.6 7.5 %all-to-all-done.1 = f32[128,8,128]{2,1,0:T(8,128)S(1)} async-done(((f32[128,8,128]{2,1,0:T(8,128)}), f32[128,8,128]{2,1,0:T(8,128)S(1)}, u32[]{:S(2)}, u32[]{:S(2)}) %all-to-all-start.1) | async-done | bytes 524320 | tf_op jit(solution)/shard_map/all_to_all | solution.py:310
  55.1 0.0 copy-done.1
  55.1 0.0 copy-done.2
  55.1 0.0 copy-start.3
  55.1 5.6 %shard_map.123 = (f32[32,4,16,128]{3,2,1,0:T(8,128)}, f32[256,512]{1,0:T(8,128)S(1)}, f32[256,512]{1,0:T(8,128)S(1)}, f32[512,512]{1,0:T(8,128)}) custom-call(s32[1]{0:T(128)} %bitcast.refs_0_, f32[1024,128]{1,0:T(8,128)S(1)} %bitcast.18, s32[8,512]{1,0:T(8,128)S(1)} %bitcast.23, f32[8,512]{1,0:T(8,128)S(1)} %bitcast.25, ...), custom_call_target="tpu_custom_call" | custom-call | flops 3000000000 | bytes 6848516 | tf_op jit(solution)/shard_map/pallas_call | solution.py:107
  60.7 8.5 %all-to-all-start.2 = ((f32[128,16,128]{2,1,0:T(8,128)}), f32[128,16,128]{2,1,0:T(8,128)S(1)}, u32[]{:S(2)}, u32[]{:S(2)}) async-start(f32[128,16,128]{2,1,0:T(8,128)} %bitcast.26), calls=%async_computation.2 | async-start | bytes 2097152 | tf_op jit(solution)/shard_map/all_to_all | solution.py:310
  69.2 2.3 %collective-permute-start.1 = (f32[256,512]{1,0:T(8,128)S(1)}, f32[256,512]{1,0:T(8,128)S(1)}, u32[]{:S(2)}, u32[]{:S(2)}) collective-permute-start(f32[256,512]{1,0:T(8,128)S(1)} %get-tuple-element.36), channel_id=1, source_target_pairs={{0,1},{1,0},{2,3},{3,2},{4,5},{5,4},{6,7},{7,6},{8,9},{9,8},{10,11... | collective-permute-start | bytes 1572872 | tf_op jit(solution)/shard_map/ppermute | solution.py:314
  71.6 0.6 broadcast.3
  72.1 0.0 copy-done.3
  72.1 0.6 reduce.3
  72.8 0.1 reshape.33
  72.9 0.1 copy.18
  73.0 0.1 collective-permute-done.1.refs_2_
  73.1 0.1 shard_map.124
  73.2 0.9 collective-permute-start.2
  74.1 2.4 %collective-permute-start.3 = (f32[64,512]{1,0:T(8,128)S(1)}, f32[64,512]{1,0:T(8,128)S(1)}, u32[]{:S(2)}, u32[]{:S(2)}) collective-permute-start(f32[64,512]{1,0:T(8,128)S(1)} %get-tuple-element.40), channel_id=1, source_target_pairs={{0,4},{2,6},{4,0},{6,2},{1,5},{3,7},{5,1},{7,3},{8,12},{10,14},{12... | collective-permute-start | bytes 393224 | tf_op jit(solution)/shard_map/ppermute | solution.py:319
  76.5 0.6 collective-permute-start.4
  77.1 4.6 %shard_map.125 = f32[512,512]{1,0:T(8,128)} custom-call(f32[512,512]{1,0:T(8,128)} %get-tuple-element.42.refs_0_, f32[512,512]{1,0:T(8,128)} %refs_1_.3, bf16[512,512]{1,0:T(8,128)(2,1)} %get-tuple-element.43.refs_2_, bf16[512,512]{1,0:T(8,128)(2,1)} %get-tuple-element.44.refs_3_), custom_call_target="tpu_custom_call" | custom-call | flops 2000000000 | bytes 5242880 | tf_op jit(solution)/shard_map/pallas_call | solution.py:107
  81.8 0.0 collective-permute-done.2.refs_2_
  81.8 5.5 %collective-permute-done.3.refs_3_ = f32[64,512]{1,0:T(8,128)S(1)} collective-permute-done((f32[64,512]{1,0:T(8,128)S(1)}, f32[64,512]{1,0:T(8,128)S(1)}, u32[]{:S(2)}, u32[]{:S(2)}) %collective-permute-start.3) | collective-permute-done | bytes 131104 | tf_op jit(solution)/shard_map/ppermute | solution.py:319
  87.3 1.4 collective-permute-done.4.refs_4_
  88.7 1.4 collective-permute-start.5
  90.1 2.8 %collective-permute-start.6 = (f32[16,512]{1,0:T(8,128)S(1)}, f32[16,512]{1,0:T(8,128)S(1)}, u32[]{:S(2)}, u32[]{:S(2)}) collective-permute-start(f32[16,512]{1,0:T(8,128)S(1)} %get-tuple-element.51), channel_id=1, source_target_pairs={{0,128},{64,192},{128,0},{192,64},{1,129},{65,193},{129,1},{193,65... | collective-permute-start | bytes 98312 | tf_op jit(solution)/shard_map/ppermute | solution.py:319
  92.9 0.0 collective-permute-start.7
  92.9 0.0 collective-permute-done.5.refs_1_
  92.9 2.9 %collective-permute-done.6.refs_2_ = f32[16,512]{1,0:T(8,128)S(1)} collective-permute-done((f32[16,512]{1,0:T(8,128)S(1)}, f32[16,512]{1,0:T(8,128)S(1)}, u32[]{:S(2)}, u32[]{:S(2)}) %collective-permute-start.6) | collective-permute-done | bytes 32800 | tf_op jit(solution)/shard_map/ppermute | solution.py:319
  95.8 1.9 %collective-permute-done.7.refs_3_ = f32[16,512]{1,0:T(8,128)S(1)} collective-permute-done((f32[16,512]{1,0:T(8,128)S(1)}, f32[16,512]{1,0:T(8,128)S(1)}, u32[]{:S(2)}, u32[]{:S(2)}) %collective-permute-start.7) | collective-permute-done | bytes 32800 | tf_op jit(solution)/shard_map/ppermute | solution.py:319
  97.6 1.6 %collective-permute-start.8 = (f32[16,512]{1,0:T(8,128)S(1)}, f32[16,512]{1,0:T(8,128)S(1)}, u32[]{:S(2)}, u32[]{:S(2)}) collective-permute-start(f32[16,512]{1,0:T(8,128)S(1)} %shard_map.127.refs_0_), channel_id=1, source_target_pairs={{0,8},{8,0},{16,24},{24,16},{32,40},{40,32},{48,56},{56,48},{1,9},... | collective-permute-start | bytes 98312 | tf_op jit(solution)/shard_map/ppermute | solution.py:319
  99.2 1.3 collective-permute-done.8.refs_1_
  100.5 2.1 %collective-permute-start.9 = (f32[16,512]{1,0:T(8,128)S(1)}, f32[16,512]{1,0:T(8,128)S(1)}, u32[]{:S(2)}, u32[]{:S(2)}) collective-permute-start(f32[16,512]{1,0:T(8,128)S(1)} %shard_map.128.refs_0_), channel_id=1, source_target_pairs={{0,16},{8,24},{16,0},{24,8},{32,48},{40,56},{48,32},{56,40},{1,17}... | collective-permute-start | bytes 98312 | tf_op jit(solution)/shard_map/ppermute | solution.py:319
  102.6 1.7 %collective-permute-done.9.refs_1_ = f32[16,512]{1,0:T(8,128)S(1)} collective-permute-done((f32[16,512]{1,0:T(8,128)S(1)}, f32[16,512]{1,0:T(8,128)S(1)}, u32[]{:S(2)}, u32[]{:S(2)}) %collective-permute-start.9) | collective-permute-done | bytes 32800 | tf_op jit(solution)/shard_map/ppermute | solution.py:319
  104.3 4.2 %collective-permute-start.10 = (f32[16,512]{1,0:T(8,128)S(1)}, f32[16,512]{1,0:T(8,128)S(1)}, u32[]{:S(2)}, u32[]{:S(2)}) collective-permute-start(f32[16,512]{1,0:T(8,128)S(1)} %shard_map.129.refs_0_), channel_id=1, source_target_pairs={{0,32},{8,40},{16,48},{24,56},{32,0},{40,8},{48,16},{56,24},{1,33}... | collective-permute-start | bytes 98312 | tf_op jit(solution)/shard_map/ppermute | solution.py:319
  108.5 2.4 %collective-permute-done.10.refs_1_ = f32[16,512]{1,0:T(8,128)S(1)} collective-permute-done((f32[16,512]{1,0:T(8,128)S(1)}, f32[16,512]{1,0:T(8,128)S(1)}, u32[]{:S(2)}, u32[]{:S(2)}) %collective-permute-start.10) | collective-permute-done | bytes 32800 | tf_op jit(solution)/shard_map/ppermute | solution.py:319
  111.0 0.8 shard_map.130
  111.8 0.0 all-to-all-done.2
  111.8 6.4 %collective-permute-start.11 = (f32[2048,128]{1,0:T(8,128)S(1)}, f32[2048,128]{1,0:T(8,128)S(1)}, u32[]{:S(2)}, u32[]{:S(2)}) collective-permute-start(f32[2048,128]{1,0:T(8,128)S(1)} %bitcast.16), channel_id=1, source_target_pairs={{0,1},{1,0},{2,3},{3,2},{4,5},{5,4},{6,7},{7,6},{8,9},{9,8},{10,11... | collective-permute-start | bytes 3145736 | tf_op jit(solution)/shard_map/ppermute | solution.py:314
  118.2 3.6 %all-to-all-start.3 = ((f32[16,16,512]{2,1,0:T(8,128)}), f32[16,16,512]{2,1,0:T(8,128)S(1)}, u32[]{:S(2)}, u32[]{:S(2)}) async-start(f32[16,16,512]{2,1,0:T(8,128)} %shard_map.130), calls=%async_computation.3 | async-start | bytes 1048576 | tf_op jit(solution)/shard_map/all_to_all | solution.py:310
  121.8 4.4 %shard_map.131.refs_3_ = f32[1280,512]{1,0:T(8,128)} custom-call(s32[1]{0:T(128)} %bitcast.refs_0_, s32[2,512]{1,0:T(2,128)S(1)} %bitcast.20, f32[2048,128]{1,0:T(8,128)S(1)} %bitcast.17, f32[1280,512]{1,0:T(8,128)} %refs_3_.3), custom_call_target="tpu_custom_call" | custom-call | flops 2000000000 | bytes 6295556 | tf_op jit(solution)/shard_map/pallas_call | solution.py:107
  126.2 0.0 collective-permute-done.11.refs_2_
  126.3 4.4 %shard_map.132 = f32[1280,512]{1,0:T(8,128)} custom-call(s32[1]{0:T(128)S(6)} %sub.3.refs_0_, s32[2,512]{1,0:T(2,128)S(1)} %bitcast.21, f32[2048,128]{1,0:T(8,128)S(1)} %collective-permute-done.11.refs_2_, f32[1280,512]{1,0:T(8,128)} %shard_map.131.refs_3_), custom_call_target="tpu_custom_call" | custom-call | flops 2000000000 | bytes 6295556 | tf_op jit(solution)/shard_map/pallas_call | solution.py:107
  130.7 2.5 %all-to-all-done.3.refs_1_ = f32[16,16,512]{2,1,0:T(8,128)S(1)} async-done(((f32[16,16,512]{2,1,0:T(8,128)}), f32[16,16,512]{2,1,0:T(8,128)S(1)}, u32[]{:S(2)}, u32[]{:S(2)}) %all-to-all-start.3) | async-done | bytes 524320 | tf_op jit(solution)/shard_map/all_to_all | solution.py:310
  133.2 1.1 collective-permute-start.12
  134.3 1.5 %collective-permute-done.12.refs_2_ = f32[16,16,512]{2,1,0:T(8,128)S(1)} collective-permute-done((f32[16,16,512]{2,1,0:T(8,128)S(1)}, f32[16,16,512]{2,1,0:T(8,128)S(1)}, u32[]{:S(2)}, u32[]{:S(2)}) %collective-permute-start.12) | collective-permute-done | bytes 524320 | tf_op jit(solution)/shard_map/ppermute | solution.py:314
  135.8 1.1 shard_map.133
  (5 shorter events, 0.1 us)
Async XLA Ops:
  0.6 38.1 %collective-permute-start = (f32[1024,512]{1,0:T(8,128)}, f32[1024,512]{1,0:T(8,128)S(1)}, u32[]{:S(2)}, u32[]{:S(2)}) collective-permute-start(f32[1024,512]{1,0:T(8,128)} %refs_3_.2), channel_id=1, source_target_pairs={{0,1},{1,0},{2,3},{3,2},{4,5},{5,4},{6,7},{7,6},{8,9},{9,8},{10,11... | collective-permute-start | bytes 6291464 | tf_op jit(solution)/shard_map/ppermute | solution.py:314
  28.9 1.7 %copy-start = (f32[1280,512]{1,0:T(8,128)S(1)}, f32[1280,512]{1,0:T(8,128)}, u32[]{:S(2)}) copy-start(f32[1280,512]{1,0:T(8,128)} %refs_3_.3) | copy-start | bytes 7864324
  32.4 22.7 %all-to-all-start.1 = ((f32[128,8,128]{2,1,0:T(8,128)}), f32[128,8,128]{2,1,0:T(8,128)S(1)}, u32[]{:S(2)}, u32[]{:S(2)}) async-start(f32[128,8,128]{2,1,0:T(8,128)} %bitcast.3), calls=%async_computation.1 | async-start | bytes 1048576 | tf_op jit(solution)/shard_map/all_to_all | solution.py:310
  38.8 1.3 copy-start.4
  40.1 15.0 %copy-start.1 = (s32[512,8]{0,1:T(8,128)S(1)}, s32[512,8]{0,1:T(8,128)}, u32[]{:S(2)}) copy-start(s32[512,8]{0,1:T(8,128)} %param.15) | copy-start | bytes 49156
  40.1 15.0 %copy-start.2 = (f32[512,8]{0,1:T(8,128)S(1)}, f32[512,8]{0,1:T(8,128)}, u32[]{:S(2)}) copy-start(f32[512,8]{0,1:T(8,128)} %param.14) | copy-start | bytes 49156
  55.1 17.1 %copy-start.3 = (s32[1,1024]{1,0:T(1,128)S(1)}, s32[1,1024]{1,0:T(1,128)}, u32[]{:S(2)}) copy-start(s32[1,1024]{1,0:T(1,128)} %param.19) | copy-start | bytes 12292
  60.7 51.1 %all-to-all-start.2 = ((f32[128,16,128]{2,1,0:T(8,128)}), f32[128,16,128]{2,1,0:T(8,128)S(1)}, u32[]{:S(2)}, u32[]{:S(2)}) async-start(f32[128,16,128]{2,1,0:T(8,128)} %bitcast.26), calls=%async_computation.2 | async-start | bytes 2097152 | tf_op jit(solution)/shard_map/all_to_all | solution.py:310
  69.2 3.9 %collective-permute-start.1 = (f32[256,512]{1,0:T(8,128)S(1)}, f32[256,512]{1,0:T(8,128)S(1)}, u32[]{:S(2)}, u32[]{:S(2)}) collective-permute-start(f32[256,512]{1,0:T(8,128)S(1)} %get-tuple-element.36), channel_id=1, source_target_pairs={{0,1},{1,0},{2,3},{3,2},{4,5},{5,4},{6,7},{7,6},{8,9},{9,8},{10,11... | collective-permute-start | bytes 1572872 | tf_op jit(solution)/shard_map/ppermute | solution.py:314
  73.2 8.6 %collective-permute-start.2 = (f32[64,512]{1,0:T(8,128)S(1)}, f32[64,512]{1,0:T(8,128)S(1)}, u32[]{:S(2)}, u32[]{:S(2)}) collective-permute-start(f32[64,512]{1,0:T(8,128)S(1)} %get-tuple-element.39), channel_id=1, source_target_pairs={{0,2},{2,0},{4,6},{6,4},{1,3},{3,1},{5,7},{7,5},{8,10},{10,8},{12,... | collective-permute-start | bytes 393224 | tf_op jit(solution)/shard_map/ppermute | solution.py:319
  74.1 13.2 %collective-permute-start.3 = (f32[64,512]{1,0:T(8,128)S(1)}, f32[64,512]{1,0:T(8,128)S(1)}, u32[]{:S(2)}, u32[]{:S(2)}) collective-permute-start(f32[64,512]{1,0:T(8,128)S(1)} %get-tuple-element.40), channel_id=1, source_target_pairs={{0,4},{2,6},{4,0},{6,2},{1,5},{3,7},{5,1},{7,3},{8,12},{10,14},{12... | collective-permute-start | bytes 393224 | tf_op jit(solution)/shard_map/ppermute | solution.py:319
  76.5 12.1 %collective-permute-start.4 = (f32[64,512]{1,0:T(8,128)S(1)}, f32[64,512]{1,0:T(8,128)S(1)}, u32[]{:S(2)}, u32[]{:S(2)}) collective-permute-start(f32[64,512]{1,0:T(8,128)S(1)} %get-tuple-element.41), channel_id=1, source_target_pairs={{0,6},{2,4},{4,2},{6,0},{1,7},{3,5},{5,3},{7,1},{8,14},{10,12},{12... | collective-permute-start | bytes 393224 | tf_op jit(solution)/shard_map/ppermute | solution.py:319
  88.7 4.2 %collective-permute-start.5 = (f32[16,512]{1,0:T(8,128)S(1)}, f32[16,512]{1,0:T(8,128)S(1)}, u32[]{:S(2)}, u32[]{:S(2)}) collective-permute-start(f32[16,512]{1,0:T(8,128)S(1)} %get-tuple-element.50), channel_id=1, source_target_pairs={{0,64},{64,0},{128,192},{192,128},{1,65},{65,1},{129,193},{193,129... | collective-permute-start | bytes 98312 | tf_op jit(solution)/shard_map/ppermute | solution.py:319
  90.1 5.7 %collective-permute-start.6 = (f32[16,512]{1,0:T(8,128)S(1)}, f32[16,512]{1,0:T(8,128)S(1)}, u32[]{:S(2)}, u32[]{:S(2)}) collective-permute-start(f32[16,512]{1,0:T(8,128)S(1)} %get-tuple-element.51), channel_id=1, source_target_pairs={{0,128},{64,192},{128,0},{192,64},{1,129},{65,193},{129,1},{193,65... | collective-permute-start | bytes 98312 | tf_op jit(solution)/shard_map/ppermute | solution.py:319
  92.9 4.7 %collective-permute-start.7 = (f32[16,512]{1,0:T(8,128)S(1)}, f32[16,512]{1,0:T(8,128)S(1)}, u32[]{:S(2)}, u32[]{:S(2)}) collective-permute-start(f32[16,512]{1,0:T(8,128)S(1)} %get-tuple-element.52), channel_id=1, source_target_pairs={{0,192},{64,128},{128,64},{192,0},{1,193},{65,129},{129,65},{193,1... | collective-permute-start | bytes 98312 | tf_op jit(solution)/shard_map/ppermute | solution.py:319
  97.6 2.9 %collective-permute-start.8 = (f32[16,512]{1,0:T(8,128)S(1)}, f32[16,512]{1,0:T(8,128)S(1)}, u32[]{:S(2)}, u32[]{:S(2)}) collective-permute-start(f32[16,512]{1,0:T(8,128)S(1)} %shard_map.127.refs_0_), channel_id=1, source_target_pairs={{0,8},{8,0},{16,24},{24,16},{32,40},{40,32},{48,56},{56,48},{1,9},... | collective-permute-start | bytes 98312 | tf_op jit(solution)/shard_map/ppermute | solution.py:319
  100.5 3.7 %collective-permute-start.9 = (f32[16,512]{1,0:T(8,128)S(1)}, f32[16,512]{1,0:T(8,128)S(1)}, u32[]{:S(2)}, u32[]{:S(2)}) collective-permute-start(f32[16,512]{1,0:T(8,128)S(1)} %shard_map.128.refs_0_), channel_id=1, source_target_pairs={{0,16},{8,24},{16,0},{24,8},{32,48},{40,56},{48,32},{56,40},{1,17}... | collective-permute-start | bytes 98312 | tf_op jit(solution)/shard_map/ppermute | solution.py:319
  104.3 6.7 %collective-permute-start.10 = (f32[16,512]{1,0:T(8,128)S(1)}, f32[16,512]{1,0:T(8,128)S(1)}, u32[]{:S(2)}, u32[]{:S(2)}) collective-permute-start(f32[16,512]{1,0:T(8,128)S(1)} %shard_map.129.refs_0_), channel_id=1, source_target_pairs={{0,32},{8,40},{16,48},{24,56},{32,0},{40,8},{48,16},{56,24},{1,33}... | collective-permute-start | bytes 98312 | tf_op jit(solution)/shard_map/ppermute | solution.py:319
  111.8 14.4 %collective-permute-start.11 = (f32[2048,128]{1,0:T(8,128)S(1)}, f32[2048,128]{1,0:T(8,128)S(1)}, u32[]{:S(2)}, u32[]{:S(2)}) collective-permute-start(f32[2048,128]{1,0:T(8,128)S(1)} %bitcast.16), channel_id=1, source_target_pairs={{0,1},{1,0},{2,3},{3,2},{4,5},{5,4},{6,7},{7,6},{8,9},{9,8},{10,11... | collective-permute-start | bytes 3145736 | tf_op jit(solution)/shard_map/ppermute | solution.py:314
  118.2 15.0 %all-to-all-start.3 = ((f32[16,16,512]{2,1,0:T(8,128)}), f32[16,16,512]{2,1,0:T(8,128)S(1)}, u32[]{:S(2)}, u32[]{:S(2)}) async-start(f32[16,16,512]{2,1,0:T(8,128)} %shard_map.130), calls=%async_computation.3 | async-start | bytes 1048576 | tf_op jit(solution)/shard_map/all_to_all | solution.py:310
  133.2 2.6 %collective-permute-start.12 = (f32[16,16,512]{2,1,0:T(8,128)S(1)}, f32[16,16,512]{2,1,0:T(8,128)S(1)}, u32[]{:S(2)}, u32[]{:S(2)}) collective-permute-start(f32[16,16,512]{2,1,0:T(8,128)S(1)} %all-to-all-done.3.refs_1_), channel_id=1, source_target_pairs={{0,1},{1,0},{2,3},{3,2},{4,5},{5,4},{6,7},{7,6},{8,9},{9,8},{10,11... | collective-permute-start | bytes 1572872 | tf_op jit(solution)/shard_map/ppermute | solution.py:314

commit v11 on v10

--- a/solution.py
+++ b/solution.py
@@ -413,14 +413,14 @@
     while 2 * mask < lax.axis_size("z"):
         summed = total(summed, move(summed, "z", mask))
         mask *= 2
+    arrived, summed = together(arrived, summed)
+    arrived_other = swap(arrived)
+    moved = move(summed, "z", mask)
+    history = write_rows(core, dest, arrived, cold_history)
+    moved, history = together(moved, history)
     plane = lax.axis_size(PLANE)
-    (spread,) = call(
-        spread_kernel, [((plane,) + summed.shape, F32)], (summed, move(summed, "z", mask))
-    )
-    arrived, spread = together(arrived, spread)
-    arrived_other = swap(arrived)
+    (spread,) = call(spread_kernel, [((plane,) + summed.shape, F32)], (summed, moved))
     gathered = exchange(spread, PLANE)
-    history = write_rows(core, dest, arrived, cold_history)
     history = write_rows(1 - core, dest, arrived_other, history)
     gathered, history = together(gathered, history)
     all_nodes = rows * lax.axis_size(ALL)

time: 137 us -> 139 us (1.015)
  waiting for transfers between devices: 28.6 us -> 30.2 us
    all_to_all x3, waiting for transfers between devices: 9.97 us -> 14 us  [exchange(): return lax.all_to_all(v, axes, split_axis=0, concat_axis=0, tiled=True)]
    ppermute x9, waiting for transfers between devices: 17 us -> 14.6 us  [move(): return lax.ppermute(v, axis, [(i, i ^ mask) for i in range(count)])]
  transfers between devices with their start and end apart: 16 -> 16, of which waited for: 11 -> 10; matrix products, arithmetic and copies ran while one was open for 2% -> 2% of each run, Pallas kernels for 17% -> 17%
where the time goes in v11:
time: 139 us
  starting transfers between devices  48.1 us (35%)
  Pallas kernels  30.5 us (22%)
  waiting for transfers between devices  30.2 us (22%)
  blocking collectives  24.1 us (17%)
  local copies, waits for them, and re-layouts  4.57 us (3%)
    pallas_call x13, Pallas kernels, call(): pl.pallas_call(wrapped, out_shape=[jax.ShapeDtypeStruct(*o) for o in outs...  30.5 us
    all_to_all x1, blocking collectives, exchange(): return lax.all_to_all(v, axes, split_axis=0, concat_axis=0, tiled=True)  24.1 us
    all_to_all x3, starting transfers between devices, exchange(): return lax.all_to_all(v, axes, split_axis=0, concat_axis=0, tiled=True)  18.5 us
    ppermute x9, starting transfers between devices, move(): return lax.ppermute(v, axis, [(i, i ^ mask) for i in range(count)])  17.2 us
    ppermute x9, waiting for transfers between devices, move(): return lax.ppermute(v, axis, [(i, i ^ mask) for i in range(count)])  14.6 us
    all_to_all x3, waiting for transfers between devices, exchange(): return lax.all_to_all(v, axes, split_axis=0, concat_axis=0, tiled=True)  14 us
    ppermute x4, starting transfers between devices, swap(): return lax.ppermute(v, 'rep', [(0, 1), (1, 0)])  12.4 us
    unnamed x13, local copies, waits for them, and re-layouts  4.37 us
  transfers between devices with their start and end apart: 16, of which 10 were waited for; matrix products, arithmetic and copies ran while one was open for 2% of the time, Pallas kernels for 17%

profile of v11, /device:TPU:1, one launch (start us, length us, event | category | flops | bytes accessed | tf_op | source)
XLA Modules:
  0.0 138.9 jit_solution(295212647654899580)
XLA Ops:
  0.6 3.3 %collective-permute-start = (f32[1024,512]{1,0:T(8,128)}, f32[1024,512]{1,0:T(8,128)S(1)}, u32[]{:S(2)}, u32[]{:S(2)}) collective-permute-start(f32[1024,512]{1,0:T(8,128)} %refs_3_.2), channel_id=1, source_target_pairs={{0,1},{1,0},{2,3},{3,2},{4,5},{5,4},{6,7},{7,6},{8,9},{9,8},{10,11... | collective-permute-start | bytes 6291464 | tf_op jit(solution)/shard_map/ppermute | solution.py:314
  4.0 0.8 copy.17
  4.7 24.1 %all_to_all.40 = s32[128,1,2]{2,1,0:T(1,128)S(1)} all-to-all(s32[128,1,2]{2,1,0:T(1,128)S(1)} %bitcast.28), channel_id=1, replica_groups=mesh['y'=4,'z'=8,'hist'=4,'rep'=2] {'y','z','hist'}, dimensions={0} | all-to-all | bytes 2048 | tf_op jit(solution)/shard_map/all_to_all | solution.py:310
  28.9 0.0 copy-start
  28.9 1.7 %copy-done = f32[1280,512]{1,0:T(8,128)S(1)} copy-done((f32[1280,512]{1,0:T(8,128)S(1)}, f32[1280,512]{1,0:T(8,128)}, u32[]{:S(2)}) %copy-start) | copy-done | bytes 2621464
  30.6 1.8 %shard_map.121 = f32[1024,128]{1,0:T(8,128)} custom-call(s32[128,2]{1,0:T(8,128)S(1)} %bitcast.19, f32[1280,512]{1,0:T(8,128)S(1)} %copy-done), custom_call_target="tpu_custom_call" | custom-call | flops 1000000000 | bytes 3146752 | tf_op jit(solution)/shard_map/pallas_call | solution.py:107
  32.4 6.4 %all-to-all-start.1 = ((f32[128,8,128]{2,1,0:T(8,128)}), f32[128,8,128]{2,1,0:T(8,128)S(1)}, u32[]{:S(2)}, u32[]{:S(2)}) async-start(f32[128,8,128]{2,1,0:T(8,128)} %bitcast.3), calls=%async_computation.1 | async-start | bytes 1048576 | tf_op jit(solution)/shard_map/all_to_all | solution.py:310
  38.8 0.0 collective-permute-done.refs_4_
  38.8 0.0 copy-start.4
  38.8 1.3 copy-done.4
  40.1 0.0 copy-start.1
  40.1 0.0 copy-start.2
  40.1 7.5 %shard_map.122 = (f32[512,512]{1,0:T(8,128)}, bf16[512,512]{1,0:T(8,128)(2,1)}, bf16[512,512]{1,0:T(8,128)(2,1)}) custom-call(s32[1]{0:T(128)} %bitcast.refs_0_, s32[8,512]{1,0:T(8,128)} %bitcast.22, f32[8,512]{1,0:T(8,128)} %bitcast.24, f32[1024,512]{1,0:T(8,128)} %refs_3_.2, f32[1024,512]{1,0:T(8,128)} %copy-done.4, f32[512,512]{1,0:T(8,128)} %refs_5_.2, ...), custom_call_target="tpu_custom_call" | custom-call | flops 6000000000 | bytes 9469956 | tf_op jit(solution)/shard_map/pallas_call | solution.py:107
  47.6 7.5 %all-to-all-done.1 = f32[128,8,128]{2,1,0:T(8,128)S(1)} async-done(((f32[128,8,128]{2,1,0:T(8,128)}), f32[128,8,128]{2,1,0:T(8,128)S(1)}, u32[]{:S(2)}, u32[]{:S(2)}) %all-to-all-start.1) | async-done | bytes 524320 | tf_op jit(solution)/shard_map/all_to_all | solution.py:310
  55.1 0.0 copy-done.1
  55.1 0.0 copy-done.2
  55.1 0.0 copy-start.3
  55.1 5.6 %shard_map.123 = (f32[32,4,16,128]{3,2,1,0:T(8,128)}, f32[256,512]{1,0:T(8,128)S(1)}, f32[256,512]{1,0:T(8,128)S(1)}, f32[512,512]{1,0:T(8,128)}) custom-call(s32[1]{0:T(128)} %bitcast.refs_0_, f32[1024,128]{1,0:T(8,128)S(1)} %bitcast.18, s32[8,512]{1,0:T(8,128)S(1)} %bitcast.23, f32[8,512]{1,0:T(8,128)S(1)} %bitcast.25, ...), custom_call_target="tpu_custom_call" | custom-call | flops 3000000000 | bytes 6848516 | tf_op jit(solution)/shard_map/pallas_call | solution.py:107
  60.7 8.5 %all-to-all-start.2 = ((f32[128,16,128]{2,1,0:T(8,128)}), f32[128,16,128]{2,1,0:T(8,128)S(1)}, u32[]{:S(2)}, u32[]{:S(2)}) async-start(f32[128,16,128]{2,1,0:T(8,128)} %bitcast.26), calls=%async_computation.2 | async-start | bytes 2097152 | tf_op jit(solution)/shard_map/all_to_all | solution.py:310
  69.3 2.3 %collective-permute-start.1 = (f32[256,512]{1,0:T(8,128)S(1)}, f32[256,512]{1,0:T(8,128)S(1)}, u32[]{:S(2)}, u32[]{:S(2)}) collective-permute-start(f32[256,512]{1,0:T(8,128)S(1)} %get-tuple-element.38), channel_id=1, source_target_pairs={{0,1},{1,0},{2,3},{3,2},{4,5},{5,4},{6,7},{7,6},{8,9},{9,8},{10,11... | collective-permute-start | bytes 1572872 | tf_op jit(solution)/shard_map/ppermute | solution.py:314
  71.6 0.5 broadcast.3
  72.1 0.0 copy-done.3
  72.1 0.7 reduce.3
  72.8 0.1 reshape.33
  72.9 0.1 copy.18
  73.0 0.1 collective-permute-done.1.refs_2_
  73.1 0.1 shard_map.124
  73.2 0.9 collective-permute-start.2
  74.2 2.4 %collective-permute-start.3 = (f32[64,512]{1,0:T(8,128)S(1)}, f32[64,512]{1,0:T(8,128)S(1)}, u32[]{:S(2)}, u32[]{:S(2)}) collective-permute-start(f32[64,512]{1,0:T(8,128)S(1)} %get-tuple-element.42), channel_id=1, source_target_pairs={{0,4},{2,6},{4,0},{6,2},{1,5},{3,7},{5,1},{7,3},{8,12},{10,14},{12... | collective-permute-start | bytes 393224 | tf_op jit(solution)/shard_map/ppermute | solution.py:319
  76.5 0.6 collective-permute-start.4
  77.2 4.6 %shard_map.125 = f32[512,512]{1,0:T(8,128)} custom-call(f32[512,512]{1,0:T(8,128)} %get-tuple-element.44.refs_0_, f32[512,512]{1,0:T(8,128)} %refs_1_.3, bf16[512,512]{1,0:T(8,128)(2,1)} %get-tuple-element.45.refs_2_, bf16[512,512]{1,0:T(8,128)(2,1)} %get-tuple-element.46.refs_3_), custom_call_target="tpu_custom_call" | custom-call | flops 2000000000 | bytes 5242880 | tf_op jit(solution)/shard_map/pallas_call | solution.py:107
  81.8 0.0 collective-permute-done.2.refs_2_
  81.8 5.5 %collective-permute-done.3.refs_3_ = f32[64,512]{1,0:T(8,128)S(1)} collective-permute-done((f32[64,512]{1,0:T(8,128)S(1)}, f32[64,512]{1,0:T(8,128)S(1)}, u32[]{:S(2)}, u32[]{:S(2)}) %collective-permute-start.3) | collective-permute-done | bytes 131104 | tf_op jit(solution)/shard_map/ppermute | solution.py:319
  87.3 1.3 collective-permute-done.4.refs_4_
  88.7 1.4 collective-permute-start.5
  90.1 2.8 %collective-permute-start.6 = (f32[16,512]{1,0:T(8,128)S(1)}, f32[16,512]{1,0:T(8,128)S(1)}, u32[]{:S(2)}, u32[]{:S(2)}) collective-permute-start(f32[16,512]{1,0:T(8,128)S(1)} %get-tuple-element.53), channel_id=1, source_target_pairs={{0,128},{64,192},{128,0},{192,64},{1,129},{65,193},{129,1},{193,65... | collective-permute-start | bytes 98312 | tf_op jit(solution)/shard_map/ppermute | solution.py:319
  92.9 0.0 collective-permute-start.7
  92.9 0.0 collective-permute-done.5.refs_1_
  92.9 2.9 %collective-permute-done.6.refs_2_ = f32[16,512]{1,0:T(8,128)S(1)} collective-permute-done((f32[16,512]{1,0:T(8,128)S(1)}, f32[16,512]{1,0:T(8,128)S(1)}, u32[]{:S(2)}, u32[]{:S(2)}) %collective-permute-start.6) | collective-permute-done | bytes 32800 | tf_op jit(solution)/shard_map/ppermute | solution.py:319
  95.8 1.9 %collective-permute-done.7.refs_3_ = f32[16,512]{1,0:T(8,128)S(1)} collective-permute-done((f32[16,512]{1,0:T(8,128)S(1)}, f32[16,512]{1,0:T(8,128)S(1)}, u32[]{:S(2)}, u32[]{:S(2)}) %collective-permute-start.7) | collective-permute-done | bytes 32800 | tf_op jit(solution)/shard_map/ppermute | solution.py:319
  97.6 1.6 %collective-permute-start.8 = (f32[16,512]{1,0:T(8,128)S(1)}, f32[16,512]{1,0:T(8,128)S(1)}, u32[]{:S(2)}, u32[]{:S(2)}) collective-permute-start(f32[16,512]{1,0:T(8,128)S(1)} %shard_map.127.refs_0_), channel_id=1, source_target_pairs={{0,8},{8,0},{16,24},{24,16},{32,40},{40,32},{48,56},{56,48},{1,9},... | collective-permute-start | bytes 98312 | tf_op jit(solution)/shard_map/ppermute | solution.py:319
  99.2 1.3 collective-permute-done.8.refs_1_
  100.5 2.1 %collective-permute-start.9 = (f32[16,512]{1,0:T(8,128)S(1)}, f32[16,512]{1,0:T(8,128)S(1)}, u32[]{:S(2)}, u32[]{:S(2)}) collective-permute-start(f32[16,512]{1,0:T(8,128)S(1)} %shard_map.128.refs_0_), channel_id=1, source_target_pairs={{0,16},{8,24},{16,0},{24,8},{32,48},{40,56},{48,32},{56,40},{1,17}... | collective-permute-start | bytes 98312 | tf_op jit(solution)/shard_map/ppermute | solution.py:319
  102.6 1.7 %collective-permute-done.9.refs_1_ = f32[16,512]{1,0:T(8,128)S(1)} collective-permute-done((f32[16,512]{1,0:T(8,128)S(1)}, f32[16,512]{1,0:T(8,128)S(1)}, u32[]{:S(2)}, u32[]{:S(2)}) %collective-permute-start.9) | collective-permute-done | bytes 32800 | tf_op jit(solution)/shard_map/ppermute | solution.py:319
  104.3 0.0 all-to-all-done.2
  104.3 5.3 %collective-permute-start.11 = (f32[2048,128]{1,0:T(8,128)S(1)}, f32[2048,128]{1,0:T(8,128)S(1)}, u32[]{:S(2)}, u32[]{:S(2)}) collective-permute-start(f32[2048,128]{1,0:T(8,128)S(1)} %bitcast.16), channel_id=1, source_target_pairs={{0,1},{1,0},{2,3},{3,2},{4,5},{5,4},{6,7},{7,6},{8,9},{9,8},{10,11... | collective-permute-start | bytes 3145736 | tf_op jit(solution)/shard_map/ppermute | solution.py:314
  109.5 5.4 %collective-permute-start.10 = (f32[16,512]{1,0:T(8,128)S(1)}, f32[16,512]{1,0:T(8,128)S(1)}, u32[]{:S(2)}, u32[]{:S(2)}) collective-permute-start(f32[16,512]{1,0:T(8,128)S(1)} %shard_map.129.refs_0_), channel_id=1, source_target_pairs={{0,32},{8,40},{16,48},{24,56},{32,0},{40,8},{48,16},{56,24},{1,33}... | collective-permute-start | bytes 98312 | tf_op jit(solution)/shard_map/ppermute | solution.py:319
  115.0 4.4 %shard_map.130.refs_3_ = f32[1280,512]{1,0:T(8,128)} custom-call(s32[1]{0:T(128)} %bitcast.refs_0_, s32[2,512]{1,0:T(2,128)S(1)} %bitcast.20, f32[2048,128]{1,0:T(8,128)S(1)} %bitcast.17, f32[1280,512]{1,0:T(8,128)} %refs_3_.3), custom_call_target="tpu_custom_call" | custom-call | flops 2000000000 | bytes 6295556 | tf_op jit(solution)/shard_map/pallas_call | solution.py:107
  119.4 0.0 collective-permute-done.10.refs_1_
  119.4 0.8 shard_map.131
  120.3 3.6 %all-to-all-start.3 = ((f32[16,16,512]{2,1,0:T(8,128)}), f32[16,16,512]{2,1,0:T(8,128)S(1)}, u32[]{:S(2)}, u32[]{:S(2)}) async-start(f32[16,16,512]{2,1,0:T(8,128)} %shard_map.131), calls=%async_computation.3 | async-start | bytes 1048576 | tf_op jit(solution)/shard_map/all_to_all | solution.py:310
  123.9 0.0 collective-permute-done.11.refs_2_
  123.9 4.5 %shard_map.132 = f32[1280,512]{1,0:T(8,128)} custom-call(s32[1]{0:T(128)S(6)} %sub.3.refs_0_, s32[2,512]{1,0:T(2,128)S(1)} %bitcast.21, f32[2048,128]{1,0:T(8,128)S(1)} %collective-permute-done.11.refs_2_, f32[1280,512]{1,0:T(8,128)} %shard_map.130.refs_3_), custom_call_target="tpu_custom_call" | custom-call | flops 2000000000 | bytes 6295556 | tf_op jit(solution)/shard_map/pallas_call | solution.py:107
  128.3 6.5 %all-to-all-done.3.refs_1_ = f32[16,16,512]{2,1,0:T(8,128)S(1)} async-done(((f32[16,16,512]{2,1,0:T(8,128)}), f32[16,16,512]{2,1,0:T(8,128)S(1)}, u32[]{:S(2)}, u32[]{:S(2)}) %all-to-all-start.3) | async-done | bytes 524320 | tf_op jit(solution)/shard_map/all_to_all | solution.py:310
  134.8 1.5 %collective-permute-start.12 = (f32[16,16,512]{2,1,0:T(8,128)S(1)}, f32[16,16,512]{2,1,0:T(8,128)S(1)}, u32[]{:S(2)}, u32[]{:S(2)}) collective-permute-start(f32[16,16,512]{2,1,0:T(8,128)S(1)} %all-to-all-done.3.refs_1_), channel_id=1, source_target_pairs={{0,1},{1,0},{2,3},{3,2},{4,5},{5,4},{6,7},{7,6},{8,9},{9,8},{10,11... | collective-permute-start | bytes 1572872 | tf_op jit(solution)/shard_map/ppermute | solution.py:314
  136.3 1.5 %collective-permute-done.12.refs_2_ = f32[16,16,512]{2,1,0:T(8,128)S(1)} collective-permute-done((f32[16,16,512]{2,1,0:T(8,128)S(1)}, f32[16,16,512]{2,1,0:T(8,128)S(1)}, u32[]{:S(2)}, u32[]{:S(2)}) %collective-permute-start.12) | collective-permute-done | bytes 524320 | tf_op jit(solution)/shard_map/ppermute | solution.py:314
  137.8 1.1 shard_map.133
  (5 shorter events, 0.1 us)
Async XLA Ops:
  0.6 38.1 %collective-permute-start = (f32[1024,512]{1,0:T(8,128)}, f32[1024,512]{1,0:T(8,128)S(1)}, u32[]{:S(2)}, u32[]{:S(2)}) collective-permute-start(f32[1024,512]{1,0:T(8,128)} %refs_3_.2), channel_id=1, source_target_pairs={{0,1},{1,0},{2,3},{3,2},{4,5},{5,4},{6,7},{7,6},{8,9},{9,8},{10,11... | collective-permute-start | bytes 6291464 | tf_op jit(solution)/shard_map/ppermute | solution.py:314
  28.9 1.7 %copy-start = (f32[1280,512]{1,0:T(8,128)S(1)}, f32[1280,512]{1,0:T(8,128)}, u32[]{:S(2)}) copy-start(f32[1280,512]{1,0:T(8,128)} %refs_3_.3) | copy-start | bytes 7864324
  32.4 22.7 %all-to-all-start.1 = ((f32[128,8,128]{2,1,0:T(8,128)}), f32[128,8,128]{2,1,0:T(8,128)S(1)}, u32[]{:S(2)}, u32[]{:S(2)}) async-start(f32[128,8,128]{2,1,0:T(8,128)} %bitcast.3), calls=%async_computation.1 | async-start | bytes 1048576 | tf_op jit(solution)/shard_map/all_to_all | solution.py:310
  38.8 1.3 copy-start.4
  40.1 15.0 %copy-start.1 = (s32[512,8]{0,1:T(8,128)S(1)}, s32[512,8]{0,1:T(8,128)}, u32[]{:S(2)}) copy-start(s32[512,8]{0,1:T(8,128)} %param.15) | copy-start | bytes 49156
  40.1 15.0 %copy-start.2 = (f32[512,8]{0,1:T(8,128)S(1)}, f32[512,8]{0,1:T(8,128)}, u32[]{:S(2)}) copy-start(f32[512,8]{0,1:T(8,128)} %param.14) | copy-start | bytes 49156
  55.1 17.0 %copy-start.3 = (s32[1,1024]{1,0:T(1,128)S(1)}, s32[1,1024]{1,0:T(1,128)}, u32[]{:S(2)}) copy-start(s32[1,1024]{1,0:T(1,128)} %param.19) | copy-start | bytes 12292
  60.7 43.6 %all-to-all-start.2 = ((f32[128,16,128]{2,1,0:T(8,128)}), f32[128,16,128]{2,1,0:T(8,128)S(1)}, u32[]{:S(2)}, u32[]{:S(2)}) async-start(f32[128,16,128]{2,1,0:T(8,128)} %bitcast.26), calls=%async_computation.2 | async-start | bytes 2097152 | tf_op jit(solution)/shard_map/all_to_all | solution.py:310
  69.3 3.9 %collective-permute-start.1 = (f32[256,512]{1,0:T(8,128)S(1)}, f32[256,512]{1,0:T(8,128)S(1)}, u32[]{:S(2)}, u32[]{:S(2)}) collective-permute-start(f32[256,512]{1,0:T(8,128)S(1)} %get-tuple-element.38), channel_id=1, source_target_pairs={{0,1},{1,0},{2,3},{3,2},{4,5},{5,4},{6,7},{7,6},{8,9},{9,8},{10,11... | collective-permute-start | bytes 1572872 | tf_op jit(solution)/shard_map/ppermute | solution.py:314
  73.2 8.6 %collective-permute-start.2 = (f32[64,512]{1,0:T(8,128)S(1)}, f32[64,512]{1,0:T(8,128)S(1)}, u32[]{:S(2)}, u32[]{:S(2)}) collective-permute-start(f32[64,512]{1,0:T(8,128)S(1)} %get-tuple-element.41), channel_id=1, source_target_pairs={{0,2},{2,0},{4,6},{6,4},{1,3},{3,1},{5,7},{7,5},{8,10},{10,8},{12,... | collective-permute-start | bytes 393224 | tf_op jit(solution)/shard_map/ppermute | solution.py:319
  74.2 13.2 %collective-permute-start.3 = (f32[64,512]{1,0:T(8,128)S(1)}, f32[64,512]{1,0:T(8,128)S(1)}, u32[]{:S(2)}, u32[]{:S(2)}) collective-permute-start(f32[64,512]{1,0:T(8,128)S(1)} %get-tuple-element.42), channel_id=1, source_target_pairs={{0,4},{2,6},{4,0},{6,2},{1,5},{3,7},{5,1},{7,3},{8,12},{10,14},{12... | collective-permute-start | bytes 393224 | tf_op jit(solution)/shard_map/ppermute | solution.py:319
  76.5 12.1 %collective-permute-start.4 = (f32[64,512]{1,0:T(8,128)S(1)}, f32[64,512]{1,0:T(8,128)S(1)}, u32[]{:S(2)}, u32[]{:S(2)}) collective-permute-start(f32[64,512]{1,0:T(8,128)S(1)} %get-tuple-element.43), channel_id=1, source_target_pairs={{0,6},{2,4},{4,2},{6,0},{1,7},{3,5},{5,3},{7,1},{8,14},{10,12},{12... | collective-permute-start | bytes 393224 | tf_op jit(solution)/shard_map/ppermute | solution.py:319
  88.7 4.2 %collective-permute-start.5 = (f32[16,512]{1,0:T(8,128)S(1)}, f32[16,512]{1,0:T(8,128)S(1)}, u32[]{:S(2)}, u32[]{:S(2)}) collective-permute-start(f32[16,512]{1,0:T(8,128)S(1)} %get-tuple-element.52), channel_id=1, source_target_pairs={{0,64},{64,0},{128,192},{192,128},{1,65},{65,1},{129,193},{193,129... | collective-permute-start | bytes 98312 | tf_op jit(solution)/shard_map/ppermute | solution.py:319
  90.1 5.7 %collective-permute-start.6 = (f32[16,512]{1,0:T(8,128)S(1)}, f32[16,512]{1,0:T(8,128)S(1)}, u32[]{:S(2)}, u32[]{:S(2)}) collective-permute-start(f32[16,512]{1,0:T(8,128)S(1)} %get-tuple-element.53), channel_id=1, source_target_pairs={{0,128},{64,192},{128,0},{192,64},{1,129},{65,193},{129,1},{193,65... | collective-permute-start | bytes 98312 | tf_op jit(solution)/shard_map/ppermute | solution.py:319
  92.9 4.7 %collective-permute-start.7 = (f32[16,512]{1,0:T(8,128)S(1)}, f32[16,512]{1,0:T(8,128)S(1)}, u32[]{:S(2)}, u32[]{:S(2)}) collective-permute-start(f32[16,512]{1,0:T(8,128)S(1)} %get-tuple-element.54), channel_id=1, source_target_pairs={{0,192},{64,128},{128,64},{192,0},{1,193},{65,129},{129,65},{193,1... | collective-permute-start | bytes 98312 | tf_op jit(solution)/shard_map/ppermute | solution.py:319
  97.6 2.9 %collective-permute-start.8 = (f32[16,512]{1,0:T(8,128)S(1)}, f32[16,512]{1,0:T(8,128)S(1)}, u32[]{:S(2)}, u32[]{:S(2)}) collective-permute-start(f32[16,512]{1,0:T(8,128)S(1)} %shard_map.127.refs_0_), channel_id=1, source_target_pairs={{0,8},{8,0},{16,24},{24,16},{32,40},{40,32},{48,56},{56,48},{1,9},... | collective-permute-start | bytes 98312 | tf_op jit(solution)/shard_map/ppermute | solution.py:319
  100.5 3.7 %collective-permute-start.9 = (f32[16,512]{1,0:T(8,128)S(1)}, f32[16,512]{1,0:T(8,128)S(1)}, u32[]{:S(2)}, u32[]{:S(2)}) collective-permute-start(f32[16,512]{1,0:T(8,128)S(1)} %shard_map.128.refs_0_), channel_id=1, source_target_pairs={{0,16},{8,24},{16,0},{24,8},{32,48},{40,56},{48,32},{56,40},{1,17}... | collective-permute-start | bytes 98312 | tf_op jit(solution)/shard_map/ppermute | solution.py:319
  104.3 19.6 %collective-permute-start.11 = (f32[2048,128]{1,0:T(8,128)S(1)}, f32[2048,128]{1,0:T(8,128)S(1)}, u32[]{:S(2)}, u32[]{:S(2)}) collective-permute-start(f32[2048,128]{1,0:T(8,128)S(1)} %bitcast.16), channel_id=1, source_target_pairs={{0,1},{1,0},{2,3},{3,2},{4,5},{5,4},{6,7},{7,6},{8,9},{9,8},{10,11... | collective-permute-start | bytes 3145736 | tf_op jit(solution)/shard_map/ppermute | solution.py:314
  109.5 9.9 %collective-permute-start.10 = (f32[16,512]{1,0:T(8,128)S(1)}, f32[16,512]{1,0:T(8,128)S(1)}, u32[]{:S(2)}, u32[]{:S(2)}) collective-permute-start(f32[16,512]{1,0:T(8,128)S(1)} %shard_map.129.refs_0_), channel_id=1, source_target_pairs={{0,32},{8,40},{16,48},{24,56},{32,0},{40,8},{48,16},{56,24},{1,33}... | collective-permute-start | bytes 98312 | tf_op jit(solution)/shard_map/ppermute | solution.py:319
  120.3 14.5 %all-to-all-start.3 = ((f32[16,16,512]{2,1,0:T(8,128)}), f32[16,16,512]{2,1,0:T(8,128)S(1)}, u32[]{:S(2)}, u32[]{:S(2)}) async-start(f32[16,16,512]{2,1,0:T(8,128)} %shard_map.131), calls=%async_computation.3 | async-start | bytes 1048576 | tf_op jit(solution)/shard_map/all_to_all | solution.py:310
  134.8 3.0 %collective-permute-start.12 = (f32[16,16,512]{2,1,0:T(8,128)S(1)}, f32[16,16,512]{2,1,0:T(8,128)S(1)}, u32[]{:S(2)}, u32[]{:S(2)}) collective-permute-start(f32[16,16,512]{2,1,0:T(8,128)S(1)} %all-to-all-done.3.refs_1_), channel_id=1, source_target_pairs={{0,1},{1,0},{2,3},{3,2},{4,5},{5,4},{6,7},{7,6},{8,9},{9,8},{10,11... | collective-permute-start | bytes 1572872 | tf_op jit(solution)/shard_map/ppermute | solution.py:314

commit v12 on v10

--- a/solution.py
+++ b/solution.py
@@ -409,10 +409,10 @@
     pieces = trade(scatter(at_y, *pieces), "y")
     arrived = exchange(outgoing.reshape(owners * 16, 128))
     summed = total(*pieces)
-    mask = 1
-    while 2 * mask < lax.axis_size("z"):
+    mask = lax.axis_size("z") // 2
+    while mask > 1:
         summed = total(summed, move(summed, "z", mask))
-        mask *= 2
+        mask //= 2
     plane = lax.axis_size(PLANE)
     (spread,) = call(
         spread_kernel, [((plane,) + summed.shape, F32)], (summed, move(summed, "z", mask))

time: 137 us -> 138 us (level)
  no operation moved by 1% of the time
where the time goes in v12:
time: 138 us; the launch traced here: 137 us
  starting transfers between devices  47.2 us (34%)
  Pallas kernels  30.4 us (22%)
  waiting for transfers between devices  29.2 us (21%)
  blocking collectives  24.1 us (17%)
  local copies, waits for them, and re-layouts  4.63 us (3%)
    pallas_call x13, Pallas kernels, call(): pl.pallas_call(wrapped, out_shape=[jax.ShapeDtypeStruct(*o) for o in outs...  30.4 us
    all_to_all x1, blocking collectives, exchange(): return lax.all_to_all(v, axes, split_axis=0, concat_axis=0, tiled=True)  24.1 us
    all_to_all x3, starting transfers between devices, exchange(): return lax.all_to_all(v, axes, split_axis=0, concat_axis=0, tiled=True)  18.5 us
    ppermute x9, waiting for transfers between devices, move(): return lax.ppermute(v, axis, [(i, i ^ mask) for i in range(count)])  17.6 us
    ppermute x9, starting transfers between devices, move(): return lax.ppermute(v, axis, [(i, i ^ mask) for i in range(count)])  15.8 us
    ppermute x4, starting transfers between devices, swap(): return lax.ppermute(v, 'rep', [(0, 1), (1, 0)])  13 us
    all_to_all x3, waiting for transfers between devices, exchange(): return lax.all_to_all(v, axes, split_axis=0, concat_axis=0, tiled=True)  9.97 us
    unnamed x13, local copies, waits for them, and re-layouts  4.43 us
  transfers between devices with their start and end apart: 16, of which 11 were waited for; matrix products, arithmetic and copies ran while one was open for 2% of the time, Pallas kernels for 17%

profile of v12, /device:TPU:1, one launch (start us, length us, event | category | flops | bytes accessed | tf_op | source)
XLA Modules:
  0.0 137.0 jit_solution(15868372377840311667)
XLA Ops:
  0.6 3.3 %collective-permute-start = (f32[1024,512]{1,0:T(8,128)}, f32[1024,512]{1,0:T(8,128)S(1)}, u32[]{:S(2)}, u32[]{:S(2)}) collective-permute-start(f32[1024,512]{1,0:T(8,128)} %refs_3_.2), channel_id=1, source_target_pairs={{0,1},{1,0},{2,3},{3,2},{4,5},{5,4},{6,7},{7,6},{8,9},{9,8},{10,11... | collective-permute-start | bytes 6291464 | tf_op jit(solution)/shard_map/ppermute | solution.py:314
  4.0 0.8 copy.17
  4.7 24.1 %all_to_all.40 = s32[128,1,2]{2,1,0:T(1,128)S(1)} all-to-all(s32[128,1,2]{2,1,0:T(1,128)S(1)} %bitcast.28), channel_id=1, replica_groups=mesh['y'=4,'z'=8,'hist'=4,'rep'=2] {'y','z','hist'}, dimensions={0} | all-to-all | bytes 2048 | tf_op jit(solution)/shard_map/all_to_all | solution.py:310
  28.9 0.0 copy-start
  28.9 1.7 %copy-done = f32[1280,512]{1,0:T(8,128)S(1)} copy-done((f32[1280,512]{1,0:T(8,128)S(1)}, f32[1280,512]{1,0:T(8,128)}, u32[]{:S(2)}) %copy-start) | copy-done | bytes 2621464
  30.6 1.8 %shard_map.121 = f32[1024,128]{1,0:T(8,128)} custom-call(s32[128,2]{1,0:T(8,128)S(1)} %bitcast.19, f32[1280,512]{1,0:T(8,128)S(1)} %copy-done), custom_call_target="tpu_custom_call" | custom-call | flops 1000000000 | bytes 3146752 | tf_op jit(solution)/shard_map/pallas_call | solution.py:107
  32.4 6.4 %all-to-all-start.1 = ((f32[128,8,128]{2,1,0:T(8,128)}), f32[128,8,128]{2,1,0:T(8,128)S(1)}, u32[]{:S(2)}, u32[]{:S(2)}) async-start(f32[128,8,128]{2,1,0:T(8,128)} %bitcast.3), calls=%async_computation.1 | async-start | bytes 1048576 | tf_op jit(solution)/shard_map/all_to_all | solution.py:310
  38.7 0.0 collective-permute-done.refs_4_
  38.8 0.0 copy-start.4
  38.8 1.3 copy-done.4
  40.1 0.0 copy-start.1
  40.1 0.0 copy-start.2
  40.1 7.5 %shard_map.122 = (f32[512,512]{1,0:T(8,128)}, bf16[512,512]{1,0:T(8,128)(2,1)}, bf16[512,512]{1,0:T(8,128)(2,1)}) custom-call(s32[1]{0:T(128)} %bitcast.refs_0_, s32[8,512]{1,0:T(8,128)} %bitcast.22, f32[8,512]{1,0:T(8,128)} %bitcast.24, f32[1024,512]{1,0:T(8,128)} %refs_3_.2, f32[1024,512]{1,0:T(8,128)} %copy-done.4, f32[512,512]{1,0:T(8,128)} %refs_5_.2, ...), custom_call_target="tpu_custom_call" | custom-call | flops 6000000000 | bytes 9469956 | tf_op jit(solution)/shard_map/pallas_call | solution.py:107
  47.6 7.5 %all-to-all-done.1 = f32[128,8,128]{2,1,0:T(8,128)S(1)} async-done(((f32[128,8,128]{2,1,0:T(8,128)}), f32[128,8,128]{2,1,0:T(8,128)S(1)}, u32[]{:S(2)}, u32[]{:S(2)}) %all-to-all-start.1) | async-done | bytes 524320 | tf_op jit(solution)/shard_map/all_to_all | solution.py:310
  55.1 0.0 copy-done.1
  55.1 0.0 copy-done.2
  55.1 0.0 copy-start.3
  55.1 5.6 %shard_map.123 = (f32[32,4,16,128]{3,2,1,0:T(8,128)}, f32[256,512]{1,0:T(8,128)S(1)}, f32[256,512]{1,0:T(8,128)S(1)}, f32[512,512]{1,0:T(8,128)}) custom-call(s32[1]{0:T(128)} %bitcast.refs_0_, f32[1024,128]{1,0:T(8,128)S(1)} %bitcast.18, s32[8,512]{1,0:T(8,128)S(1)} %bitcast.23, f32[8,512]{1,0:T(8,128)S(1)} %bitcast.25, ...), custom_call_target="tpu_custom_call" | custom-call | flops 3000000000 | bytes 6848516 | tf_op jit(solution)/shard_map/pallas_call | solution.py:107
  60.7 8.5 %all-to-all-start.2 = ((f32[128,16,128]{2,1,0:T(8,128)}), f32[128,16,128]{2,1,0:T(8,128)S(1)}, u32[]{:S(2)}, u32[]{:S(2)}) async-start(f32[128,16,128]{2,1,0:T(8,128)} %bitcast.26), calls=%async_computation.2 | async-start | bytes 2097152 | tf_op jit(solution)/shard_map/all_to_all | solution.py:310
  69.2 2.3 %collective-permute-start.1 = (f32[256,512]{1,0:T(8,128)S(1)}, f32[256,512]{1,0:T(8,128)S(1)}, u32[]{:S(2)}, u32[]{:S(2)}) collective-permute-start(f32[256,512]{1,0:T(8,128)S(1)} %get-tuple-element.36), channel_id=1, source_target_pairs={{0,1},{1,0},{2,3},{3,2},{4,5},{5,4},{6,7},{7,6},{8,9},{9,8},{10,11... | collective-permute-start | bytes 1572872 | tf_op jit(solution)/shard_map/ppermute | solution.py:314
  71.6 0.6 broadcast.3
  72.1 0.0 copy-done.3
  72.1 0.6 reduce.3
  72.8 0.1 reshape.33
  72.9 0.1 copy.18
  73.0 0.1 collective-permute-done.1.refs_2_
  73.1 0.1 shard_map.124
  73.2 0.9 collective-permute-start.2
  74.1 2.4 %collective-permute-start.3 = (f32[64,512]{1,0:T(8,128)S(1)}, f32[64,512]{1,0:T(8,128)S(1)}, u32[]{:S(2)}, u32[]{:S(2)}) collective-permute-start(f32[64,512]{1,0:T(8,128)S(1)} %get-tuple-element.40), channel_id=1, source_target_pairs={{0,4},{2,6},{4,0},{6,2},{1,5},{3,7},{5,1},{7,3},{8,12},{10,14},{12... | collective-permute-start | bytes 393224 | tf_op jit(solution)/shard_map/ppermute | solution.py:319
  76.5 0.6 collective-permute-start.4
  77.1 4.6 %shard_map.125 = f32[512,512]{1,0:T(8,128)} custom-call(f32[512,512]{1,0:T(8,128)} %get-tuple-element.42.refs_0_, f32[512,512]{1,0:T(8,128)} %refs_1_.3, bf16[512,512]{1,0:T(8,128)(2,1)} %get-tuple-element.43.refs_2_, bf16[512,512]{1,0:T(8,128)(2,1)} %get-tuple-element.44.refs_3_), custom_call_target="tpu_custom_call" | custom-call | flops 2000000000 | bytes 5242880 | tf_op jit(solution)/shard_map/pallas_call | solution.py:107
  81.8 0.0 collective-permute-done.2.refs_2_
  81.8 5.5 %collective-permute-done.3.refs_3_ = f32[64,512]{1,0:T(8,128)S(1)} collective-permute-done((f32[64,512]{1,0:T(8,128)S(1)}, f32[64,512]{1,0:T(8,128)S(1)}, u32[]{:S(2)}, u32[]{:S(2)}) %collective-permute-start.3) | collective-permute-done | bytes 131104 | tf_op jit(solution)/shard_map/ppermute | solution.py:319
  87.3 1.4 collective-permute-done.4.refs_4_
  88.7 1.4 collective-permute-start.5
  90.1 2.8 %collective-permute-start.6 = (f32[16,512]{1,0:T(8,128)S(1)}, f32[16,512]{1,0:T(8,128)S(1)}, u32[]{:S(2)}, u32[]{:S(2)}) collective-permute-start(f32[16,512]{1,0:T(8,128)S(1)} %get-tuple-element.51), channel_id=1, source_target_pairs={{0,128},{64,192},{128,0},{192,64},{1,129},{65,193},{129,1},{193,65... | collective-permute-start | bytes 98312 | tf_op jit(solution)/shard_map/ppermute | solution.py:319
  92.9 0.0 collective-permute-start.7
  92.9 0.0 collective-permute-done.5.refs_1_
  92.9 2.9 %collective-permute-done.6.refs_2_ = f32[16,512]{1,0:T(8,128)S(1)} collective-permute-done((f32[16,512]{1,0:T(8,128)S(1)}, f32[16,512]{1,0:T(8,128)S(1)}, u32[]{:S(2)}, u32[]{:S(2)}) %collective-permute-start.6) | collective-permute-done | bytes 32800 | tf_op jit(solution)/shard_map/ppermute | solution.py:319
  95.8 1.9 %collective-permute-done.7.refs_3_ = f32[16,512]{1,0:T(8,128)S(1)} collective-permute-done((f32[16,512]{1,0:T(8,128)S(1)}, f32[16,512]{1,0:T(8,128)S(1)}, u32[]{:S(2)}, u32[]{:S(2)}) %collective-permute-start.7) | collective-permute-done | bytes 32800 | tf_op jit(solution)/shard_map/ppermute | solution.py:319
  97.6 4.1 %collective-permute-start.8 = (f32[16,512]{1,0:T(8,128)S(1)}, f32[16,512]{1,0:T(8,128)S(1)}, u32[]{:S(2)}, u32[]{:S(2)}) collective-permute-start(f32[16,512]{1,0:T(8,128)S(1)} %shard_map.127.refs_0_), channel_id=1, source_target_pairs={{0,32},{8,40},{16,48},{24,56},{32,0},{40,8},{48,16},{56,24},{1,33}... | collective-permute-start | bytes 98312 | tf_op jit(solution)/shard_map/ppermute | solution.py:319
  101.8 2.7 %collective-permute-done.8.refs_1_ = f32[16,512]{1,0:T(8,128)S(1)} collective-permute-done((f32[16,512]{1,0:T(8,128)S(1)}, f32[16,512]{1,0:T(8,128)S(1)}, u32[]{:S(2)}, u32[]{:S(2)}) %collective-permute-start.8) | collective-permute-done | bytes 32800 | tf_op jit(solution)/shard_map/ppermute | solution.py:319
  104.4 2.4 %collective-permute-start.9 = (f32[16,512]{1,0:T(8,128)S(1)}, f32[16,512]{1,0:T(8,128)S(1)}, u32[]{:S(2)}, u32[]{:S(2)}) collective-permute-start(f32[16,512]{1,0:T(8,128)S(1)} %shard_map.128.refs_0_), channel_id=1, source_target_pairs={{0,16},{8,24},{16,0},{24,8},{32,48},{40,56},{48,32},{56,40},{1,17}... | collective-permute-start | bytes 98312 | tf_op jit(solution)/shard_map/ppermute | solution.py:319
  106.8 1.7 %collective-permute-done.9.refs_1_ = f32[16,512]{1,0:T(8,128)S(1)} collective-permute-done((f32[16,512]{1,0:T(8,128)S(1)}, f32[16,512]{1,0:T(8,128)S(1)}, u32[]{:S(2)}, u32[]{:S(2)}) %collective-permute-start.9) | collective-permute-done | bytes 32800 | tf_op jit(solution)/shard_map/ppermute | solution.py:319
  108.5 1.1 collective-permute-start.10
  109.6 1.7 %collective-permute-done.10.refs_1_ = f32[16,512]{1,0:T(8,128)S(1)} collective-permute-done((f32[16,512]{1,0:T(8,128)S(1)}, f32[16,512]{1,0:T(8,128)S(1)}, u32[]{:S(2)}, u32[]{:S(2)}) %collective-permute-start.10) | collective-permute-done | bytes 32800 | tf_op jit(solution)/shard_map/ppermute | solution.py:319
  111.3 0.8 shard_map.130
  112.1 0.0 all-to-all-done.2
  112.1 6.2 %collective-permute-start.11 = (f32[2048,128]{1,0:T(8,128)S(1)}, f32[2048,128]{1,0:T(8,128)S(1)}, u32[]{:S(2)}, u32[]{:S(2)}) collective-permute-start(f32[2048,128]{1,0:T(8,128)S(1)} %bitcast.16), channel_id=1, source_target_pairs={{0,1},{1,0},{2,3},{3,2},{4,5},{5,4},{6,7},{7,6},{8,9},{9,8},{10,11... | collective-permute-start | bytes 3145736 | tf_op jit(solution)/shard_map/ppermute | solution.py:314
  118.4 3.6 %all-to-all-start.3 = ((f32[16,16,512]{2,1,0:T(8,128)}), f32[16,16,512]{2,1,0:T(8,128)S(1)}, u32[]{:S(2)}, u32[]{:S(2)}) async-start(f32[16,16,512]{2,1,0:T(8,128)} %shard_map.130), calls=%async_computation.3 | async-start | bytes 1048576 | tf_op jit(solution)/shard_map/all_to_all | solution.py:310
  121.9 4.4 %shard_map.131.refs_3_ = f32[1280,512]{1,0:T(8,128)} custom-call(s32[1]{0:T(128)} %bitcast.refs_0_, s32[2,512]{1,0:T(2,128)S(1)} %bitcast.20, f32[2048,128]{1,0:T(8,128)S(1)} %bitcast.17, f32[1280,512]{1,0:T(8,128)} %refs_3_.3), custom_call_target="tpu_custom_call" | custom-call | flops 2000000000 | bytes 6295556 | tf_op jit(solution)/shard_map/pallas_call | solution.py:107
  126.4 0.0 collective-permute-done.11.refs_2_
  126.4 4.4 %shard_map.132 = f32[1280,512]{1,0:T(8,128)} custom-call(s32[1]{0:T(128)S(6)} %sub.3.refs_0_, s32[2,512]{1,0:T(2,128)S(1)} %bitcast.21, f32[2048,128]{1,0:T(8,128)S(1)} %collective-permute-done.11.refs_2_, f32[1280,512]{1,0:T(8,128)} %shard_map.131.refs_3_), custom_call_target="tpu_custom_call" | custom-call | flops 2000000000 | bytes 6295556 | tf_op jit(solution)/shard_map/pallas_call | solution.py:107
  130.8 2.5 %all-to-all-done.3.refs_1_ = f32[16,16,512]{2,1,0:T(8,128)S(1)} async-done(((f32[16,16,512]{2,1,0:T(8,128)}), f32[16,16,512]{2,1,0:T(8,128)S(1)}, u32[]{:S(2)}, u32[]{:S(2)}) %all-to-all-start.3) | async-done | bytes 524320 | tf_op jit(solution)/shard_map/all_to_all | solution.py:310
  133.3 1.1 collective-permute-start.12
  134.4 1.5 %collective-permute-done.12.refs_2_ = f32[16,16,512]{2,1,0:T(8,128)S(1)} collective-permute-done((f32[16,16,512]{2,1,0:T(8,128)S(1)}, f32[16,16,512]{2,1,0:T(8,128)S(1)}, u32[]{:S(2)}, u32[]{:S(2)}) %collective-permute-start.12) | collective-permute-done | bytes 524320 | tf_op jit(solution)/shard_map/ppermute | solution.py:314
  135.9 1.1 shard_map.133
  (5 shorter events, 0.1 us)
Async XLA Ops:
  0.6 38.1 %collective-permute-start = (f32[1024,512]{1,0:T(8,128)}, f32[1024,512]{1,0:T(8,128)S(1)}, u32[]{:S(2)}, u32[]{:S(2)}) collective-permute-start(f32[1024,512]{1,0:T(8,128)} %refs_3_.2), channel_id=1, source_target_pairs={{0,1},{1,0},{2,3},{3,2},{4,5},{5,4},{6,7},{7,6},{8,9},{9,8},{10,11... | collective-permute-start | bytes 6291464 | tf_op jit(solution)/shard_map/ppermute | solution.py:314
  28.9 1.7 %copy-start = (f32[1280,512]{1,0:T(8,128)S(1)}, f32[1280,512]{1,0:T(8,128)}, u32[]{:S(2)}) copy-start(f32[1280,512]{1,0:T(8,128)} %refs_3_.3) | copy-start | bytes 7864324
  32.4 22.7 %all-to-all-start.1 = ((f32[128,8,128]{2,1,0:T(8,128)}), f32[128,8,128]{2,1,0:T(8,128)S(1)}, u32[]{:S(2)}, u32[]{:S(2)}) async-start(f32[128,8,128]{2,1,0:T(8,128)} %bitcast.3), calls=%async_computation.1 | async-start | bytes 1048576 | tf_op jit(solution)/shard_map/all_to_all | solution.py:310
  38.8 1.3 copy-start.4
  40.1 15.0 %copy-start.1 = (s32[512,8]{0,1:T(8,128)S(1)}, s32[512,8]{0,1:T(8,128)}, u32[]{:S(2)}) copy-start(s32[512,8]{0,1:T(8,128)} %param.15) | copy-start | bytes 49156
  40.1 15.0 %copy-start.2 = (f32[512,8]{0,1:T(8,128)S(1)}, f32[512,8]{0,1:T(8,128)}, u32[]{:S(2)}) copy-start(f32[512,8]{0,1:T(8,128)} %param.14) | copy-start | bytes 49156
  55.1 17.1 %copy-start.3 = (s32[1,1024]{1,0:T(1,128)S(1)}, s32[1,1024]{1,0:T(1,128)}, u32[]{:S(2)}) copy-start(s32[1,1024]{1,0:T(1,128)} %param.19) | copy-start | bytes 12292
  60.7 51.4 %all-to-all-start.2 = ((f32[128,16,128]{2,1,0:T(8,128)}), f32[128,16,128]{2,1,0:T(8,128)S(1)}, u32[]{:S(2)}, u32[]{:S(2)}) async-start(f32[128,16,128]{2,1,0:T(8,128)} %bitcast.26), calls=%async_computation.2 | async-start | bytes 2097152 | tf_op jit(solution)/shard_map/all_to_all | solution.py:310
  69.2 3.9 %collective-permute-start.1 = (f32[256,512]{1,0:T(8,128)S(1)}, f32[256,512]{1,0:T(8,128)S(1)}, u32[]{:S(2)}, u32[]{:S(2)}) collective-permute-start(f32[256,512]{1,0:T(8,128)S(1)} %get-tuple-element.36), channel_id=1, source_target_pairs={{0,1},{1,0},{2,3},{3,2},{4,5},{5,4},{6,7},{7,6},{8,9},{9,8},{10,11... | collective-permute-start | bytes 1572872 | tf_op jit(solution)/shard_map/ppermute | solution.py:314
  73.2 8.6 %collective-permute-start.2 = (f32[64,512]{1,0:T(8,128)S(1)}, f32[64,512]{1,0:T(8,128)S(1)}, u32[]{:S(2)}, u32[]{:S(2)}) collective-permute-start(f32[64,512]{1,0:T(8,128)S(1)} %get-tuple-element.39), channel_id=1, source_target_pairs={{0,2},{2,0},{4,6},{6,4},{1,3},{3,1},{5,7},{7,5},{8,10},{10,8},{12,... | collective-permute-start | bytes 393224 | tf_op jit(solution)/shard_map/ppermute | solution.py:319
  74.1 13.2 %collective-permute-start.3 = (f32[64,512]{1,0:T(8,128)S(1)}, f32[64,512]{1,0:T(8,128)S(1)}, u32[]{:S(2)}, u32[]{:S(2)}) collective-permute-start(f32[64,512]{1,0:T(8,128)S(1)} %get-tuple-element.40), channel_id=1, source_target_pairs={{0,4},{2,6},{4,0},{6,2},{1,5},{3,7},{5,1},{7,3},{8,12},{10,14},{12... | collective-permute-start | bytes 393224 | tf_op jit(solution)/shard_map/ppermute | solution.py:319
  76.5 12.1 %collective-permute-start.4 = (f32[64,512]{1,0:T(8,128)S(1)}, f32[64,512]{1,0:T(8,128)S(1)}, u32[]{:S(2)}, u32[]{:S(2)}) collective-permute-start(f32[64,512]{1,0:T(8,128)S(1)} %get-tuple-element.41), channel_id=1, source_target_pairs={{0,6},{2,4},{4,2},{6,0},{1,7},{3,5},{5,3},{7,1},{8,14},{10,12},{12... | collective-permute-start | bytes 393224 | tf_op jit(solution)/shard_map/ppermute | solution.py:319
  88.7 4.2 %collective-permute-start.5 = (f32[16,512]{1,0:T(8,128)S(1)}, f32[16,512]{1,0:T(8,128)S(1)}, u32[]{:S(2)}, u32[]{:S(2)}) collective-permute-start(f32[16,512]{1,0:T(8,128)S(1)} %get-tuple-element.50), channel_id=1, source_target_pairs={{0,64},{64,0},{128,192},{192,128},{1,65},{65,1},{129,193},{193,129... | collective-permute-start | bytes 98312 | tf_op jit(solution)/shard_map/ppermute | solution.py:319
  90.1 5.7 %collective-permute-start.6 = (f32[16,512]{1,0:T(8,128)S(1)}, f32[16,512]{1,0:T(8,128)S(1)}, u32[]{:S(2)}, u32[]{:S(2)}) collective-permute-start(f32[16,512]{1,0:T(8,128)S(1)} %get-tuple-element.51), channel_id=1, source_target_pairs={{0,128},{64,192},{128,0},{192,64},{1,129},{65,193},{129,1},{193,65... | collective-permute-start | bytes 98312 | tf_op jit(solution)/shard_map/ppermute | solution.py:319
  92.9 4.7 %collective-permute-start.7 = (f32[16,512]{1,0:T(8,128)S(1)}, f32[16,512]{1,0:T(8,128)S(1)}, u32[]{:S(2)}, u32[]{:S(2)}) collective-permute-start(f32[16,512]{1,0:T(8,128)S(1)} %get-tuple-element.52), channel_id=1, source_target_pairs={{0,192},{64,128},{128,64},{192,0},{1,193},{65,129},{129,65},{193,1... | collective-permute-start | bytes 98312 | tf_op jit(solution)/shard_map/ppermute | solution.py:319
  97.6 6.8 %collective-permute-start.8 = (f32[16,512]{1,0:T(8,128)S(1)}, f32[16,512]{1,0:T(8,128)S(1)}, u32[]{:S(2)}, u32[]{:S(2)}) collective-permute-start(f32[16,512]{1,0:T(8,128)S(1)} %shard_map.127.refs_0_), channel_id=1, source_target_pairs={{0,32},{8,40},{16,48},{24,56},{32,0},{40,8},{48,16},{56,24},{1,33}... | collective-permute-start | bytes 98312 | tf_op jit(solution)/shard_map/ppermute | solution.py:319
  104.4 4.1 %collective-permute-start.9 = (f32[16,512]{1,0:T(8,128)S(1)}, f32[16,512]{1,0:T(8,128)S(1)}, u32[]{:S(2)}, u32[]{:S(2)}) collective-permute-start(f32[16,512]{1,0:T(8,128)S(1)} %shard_map.128.refs_0_), channel_id=1, source_target_pairs={{0,16},{8,24},{16,0},{24,8},{32,48},{40,56},{48,32},{56,40},{1,17}... | collective-permute-start | bytes 98312 | tf_op jit(solution)/shard_map/ppermute | solution.py:319
  108.5 2.8 %collective-permute-start.10 = (f32[16,512]{1,0:T(8,128)S(1)}, f32[16,512]{1,0:T(8,128)S(1)}, u32[]{:S(2)}, u32[]{:S(2)}) collective-permute-start(f32[16,512]{1,0:T(8,128)S(1)} %shard_map.129.refs_0_), channel_id=1, source_target_pairs={{0,8},{8,0},{16,24},{24,16},{32,40},{40,32},{48,56},{56,48},{1,9},... | collective-permute-start | bytes 98312 | tf_op jit(solution)/shard_map/ppermute | solution.py:319
  112.1 14.3 %collective-permute-start.11 = (f32[2048,128]{1,0:T(8,128)S(1)}, f32[2048,128]{1,0:T(8,128)S(1)}, u32[]{:S(2)}, u32[]{:S(2)}) collective-permute-start(f32[2048,128]{1,0:T(8,128)S(1)} %bitcast.16), channel_id=1, source_target_pairs={{0,1},{1,0},{2,3},{3,2},{4,5},{5,4},{6,7},{7,6},{8,9},{9,8},{10,11... | collective-permute-start | bytes 3145736 | tf_op jit(solution)/shard_map/ppermute | solution.py:314
  118.4 15.0 %all-to-all-start.3 = ((f32[16,16,512]{2,1,0:T(8,128)}), f32[16,16,512]{2,1,0:T(8,128)S(1)}, u32[]{:S(2)}, u32[]{:S(2)}) async-start(f32[16,16,512]{2,1,0:T(8,128)} %shard_map.130), calls=%async_computation.3 | async-start | bytes 1048576 | tf_op jit(solution)/shard_map/all_to_all | solution.py:310
  133.3 2.6 %collective-permute-start.12 = (f32[16,16,512]{2,1,0:T(8,128)S(1)}, f32[16,16,512]{2,1,0:T(8,128)S(1)}, u32[]{:S(2)}, u32[]{:S(2)}) collective-permute-start(f32[16,16,512]{2,1,0:T(8,128)S(1)} %all-to-all-done.3.refs_1_), channel_id=1, source_target_pairs={{0,1},{1,0},{2,3},{3,2},{4,5},{5,4},{6,7},{7,6},{8,9},{9,8},{10,11... | collective-permute-start | bytes 1572872 | tf_op jit(solution)/shard_map/ppermute | solution.py:314

commit v13 on v10

--- a/solution.py
+++ b/solution.py
@@ -270,18 +270,25 @@
     out_ref.push()
 
 
-def history_kernel(which_ref, dest_ref, recv_ref, base_ref, out_ref, high_ref, low_ref):
-    owners = recv_ref.shape[0] // 16
-    for s in range(4):
-        for l in range(4):
-            high, low = split(recv_ref[pl.ds(4 * l + s, owners, stride=16), :])
-            at = slice(s * owners, (s + 1) * owners)
-            high_ref[at, l * 128 : (l + 1) * 128] = high
-            low_ref[at, l * 128 : (l + 1) * 128] = low
-    dest = dest_ref[pl.ds(which_ref[0], 1), :]
+def history_kernel(
+    core_ref, dest_ref, mine_ref, other_ref, base_ref, out_ref, high_ref, low_ref
+):
+    owners = mine_ref.shape[0] // 16
+    rows = 4 * owners
+    for r, ref in enumerate((mine_ref, other_ref)):
+        for s in range(4):
+            for l in range(4):
+                high, low = split(ref[pl.ds(4 * l + s, owners, stride=16), :])
+                at = slice(r * rows + s * owners, r * rows + (s + 1) * owners)
+                high_ref[at, l * 128 : (l + 1) * 128] = high
+                low_ref[at, l * 128 : (l + 1) * 128] = low
+    core = core_ref[0]
+    dest = jnp.concatenate(
+        [dest_ref[pl.ds(core, 1), :], dest_ref[pl.ds(1 - core, 1), :]], axis=1
+    )
     step = out_ref.rows
     for block in range(out_ref.shape[0] // step):
-        ids = lax.broadcasted_iota(jnp.int32, (step, dest.shape[1]), 0) + block * step
+        ids = lax.broadcasted_iota(jnp.int32, (step, 2 * rows), 0) + block * step
         hit = jnp.where(ids == dest, 1.0, 0.0)
         count = jnp.sum(hit, axis=1, keepdims=True)
         place = hit.astype(BF16)
@@ -292,16 +299,16 @@
         out_ref.push(block)
 
 
-def write_rows(which, dest, recv, base):
-    rows, width = dest.shape[1], base.shape[1]
+def write_rows(core, dest, mine, other, base):
+    rows, width = 2 * dest.shape[1], base.shape[1]
     return call(
         history_kernel,
         [(base.shape, F32)],
-        (which, dest, recv, base),
-        spaces="svvhh",
+        (core, dest, mine, other, base),
+        spaces="svvvhh",
         scratch=[pltpu.VMEM((rows, width), BF16), pltpu.VMEM((rows, width), BF16)],
         limit=52,
-        flops=2 * 10**9,
+        flops=4 * 10**9,
         chunks=5,
     )[0]
 
@@ -420,8 +427,7 @@
     arrived, spread = together(arrived, spread)
     arrived_other = swap(arrived)
     gathered = exchange(spread, PLANE)
-    history = write_rows(core, dest, arrived, cold_history)
-    history = write_rows(1 - core, dest, arrived_other, history)
+    history = write_rows(core, dest, arrived, arrived_other, cold_history)
     gathered, history = together(gathered, history)
     all_nodes = rows * lax.axis_size(ALL)
     (grad_weight,) = call(

time: 137 us -> 137 us (level)
  Pallas kernels: 30.4 us -> 28.1 us
  waiting for transfers between devices: 28.6 us -> 30 us
    pallas_call x13 -> x12, Pallas kernels: 30.4 us -> 28.1 us  [call(): pl.pallas_call(wrapped, out_shape=[jax.ShapeDtypeStruct(*o) for o in outs...]
    unnamed x13 -> x15, local copies, waits for them, and re-layouts: 4.43 us -> 5.36 us
  transfers between devices with their start and end apart: 16 -> 16, of which waited for: 11 -> 11; matrix products, arithmetic and copies ran while one was open for 2% -> 2% of each run, Pallas kernels for 17% -> 16%
where the time goes in v13:
time: 137 us
  starting transfers between devices  47.6 us (35%)
  waiting for transfers between devices  30 us (22%)
  Pallas kernels  28.1 us (21%)
  blocking collectives  24.1 us (18%)
  local copies, waits for them, and re-layouts  5.56 us (4%)
    pallas_call x12, Pallas kernels, call(): pl.pallas_call(wrapped, out_shape=[jax.ShapeDtypeStruct(*o) for o in outs...  28.1 us
    all_to_all x1, blocking collectives, exchange(): return lax.all_to_all(v, axes, split_axis=0, concat_axis=0, tiled=True)  24.1 us
    all_to_all x3, starting transfers between devices, exchange(): return lax.all_to_all(v, axes, split_axis=0, concat_axis=0, tiled=True)  18.5 us
    ppermute x9, waiting for transfers between devices, move(): return lax.ppermute(v, axis, [(i, i ^ mask) for i in range(count)])  17 us
    ppermute x9, starting transfers between devices, move(): return lax.ppermute(v, axis, [(i, i ^ mask) for i in range(count)])  16 us
    ppermute x4, starting transfers between devices, swap(): return lax.ppermute(v, 'rep', [(0, 1), (1, 0)])  13.1 us
    all_to_all x3, waiting for transfers between devices, exchange(): return lax.all_to_all(v, axes, split_axis=0, concat_axis=0, tiled=True)  11.3 us
    unnamed x15, local copies, waits for them, and re-layouts  5.36 us
  transfers between devices with their start and end apart: 16, of which 11 were waited for; matrix products, arithmetic and copies ran while one was open for 2% of the time, Pallas kernels for 16%

profile of v13, /device:TPU:1, one launch (start us, length us, event | category | flops | bytes accessed | tf_op | source)
XLA Modules:
  0.0 136.9 jit_solution(5847296871162179414)
XLA Ops:
  0.6 3.3 %collective-permute-start = (f32[1024,512]{1,0:T(8,128)}, f32[1024,512]{1,0:T(8,128)S(1)}, u32[]{:S(2)}, u32[]{:S(2)}) collective-permute-start(f32[1024,512]{1,0:T(8,128)} %refs_3_.1), channel_id=1, source_target_pairs={{0,1},{1,0},{2,3},{3,2},{4,5},{5,4},{6,7},{7,6},{8,9},{9,8},{10,11... | collective-permute-start | bytes 6291464 | tf_op jit(solution)/shard_map/ppermute | solution.py:321
  4.0 0.8 copy.17
  4.7 24.1 %all_to_all.40 = s32[128,1,2]{2,1,0:T(1,128)S(1)} all-to-all(s32[128,1,2]{2,1,0:T(1,128)S(1)} %bitcast.27), channel_id=1, replica_groups=mesh['y'=4,'z'=8,'hist'=4,'rep'=2] {'y','z','hist'}, dimensions={0} | all-to-all | bytes 2048 | tf_op jit(solution)/shard_map/all_to_all | solution.py:317
  28.9 0.0 copy-start
  28.9 1.7 %copy-done = f32[1280,512]{1,0:T(8,128)S(1)} copy-done((f32[1280,512]{1,0:T(8,128)S(1)}, f32[1280,512]{1,0:T(8,128)}, u32[]{:S(2)}) %copy-start) | copy-done | bytes 2621464
  30.6 1.8 %shard_map.121 = f32[1024,128]{1,0:T(8,128)} custom-call(s32[128,2]{1,0:T(8,128)S(1)} %bitcast.19, f32[1280,512]{1,0:T(8,128)S(1)} %copy-done), custom_call_target="tpu_custom_call" | custom-call | flops 1000000000 | bytes 3146752 | tf_op jit(solution)/shard_map/pallas_call | solution.py:107
  32.4 6.4 %all-to-all-start.1 = ((f32[128,8,128]{2,1,0:T(8,128)}), f32[128,8,128]{2,1,0:T(8,128)S(1)}, u32[]{:S(2)}, u32[]{:S(2)}) async-start(f32[128,8,128]{2,1,0:T(8,128)} %bitcast.3), calls=%async_computation.1 | async-start | bytes 1048576 | tf_op jit(solution)/shard_map/all_to_all | solution.py:317
  38.7 0.0 collective-permute-done.refs_4_
  38.8 0.0 copy-start.4
  38.8 1.3 copy-done.4
  40.1 0.0 copy-start.1
  40.1 0.0 copy-start.2
  40.1 7.5 %shard_map.122 = (f32[512,512]{1,0:T(8,128)}, bf16[512,512]{1,0:T(8,128)(2,1)}, bf16[512,512]{1,0:T(8,128)(2,1)}) custom-call(s32[1]{0:T(128)} %bitcast.refs_0_, s32[8,512]{1,0:T(8,128)} %bitcast.21, f32[8,512]{1,0:T(8,128)} %bitcast.23, f32[1024,512]{1,0:T(8,128)} %refs_3_.1, f32[1024,512]{1,0:T(8,128)} %copy-done.4, f32[512,512]{1,0:T(8,128)} %refs_5_.2, ...), custom_call_target="tpu_custom_call" | custom-call | flops 6000000000 | bytes 9469956 | tf_op jit(solution)/shard_map/pallas_call | solution.py:107
  47.6 7.5 %all-to-all-done.1 = f32[128,8,128]{2,1,0:T(8,128)S(1)} async-done(((f32[128,8,128]{2,1,0:T(8,128)}), f32[128,8,128]{2,1,0:T(8,128)S(1)}, u32[]{:S(2)}, u32[]{:S(2)}) %all-to-all-start.1) | async-done | bytes 524320 | tf_op jit(solution)/shard_map/all_to_all | solution.py:317
  55.1 0.0 copy-done.1
  55.1 0.0 copy-done.2
  55.1 0.0 copy-start.3
  55.1 5.6 %shard_map.123 = (f32[32,4,16,128]{3,2,1,0:T(8,128)}, f32[256,512]{1,0:T(8,128)S(1)}, f32[256,512]{1,0:T(8,128)S(1)}, f32[512,512]{1,0:T(8,128)}) custom-call(s32[1]{0:T(128)} %bitcast.refs_0_, f32[1024,128]{1,0:T(8,128)S(1)} %bitcast.18, s32[8,512]{1,0:T(8,128)S(1)} %bitcast.22, f32[8,512]{1,0:T(8,128)S(1)} %bitcast.24, ...), custom_call_target="tpu_custom_call" | custom-call | flops 3000000000 | bytes 6848516 | tf_op jit(solution)/shard_map/pallas_call | solution.py:107
  60.7 8.5 %all-to-all-start.2 = ((f32[128,16,128]{2,1,0:T(8,128)}), f32[128,16,128]{2,1,0:T(8,128)S(1)}, u32[]{:S(2)}, u32[]{:S(2)}) async-start(f32[128,16,128]{2,1,0:T(8,128)} %bitcast.25), calls=%async_computation.2 | async-start | bytes 2097152 | tf_op jit(solution)/shard_map/all_to_all | solution.py:317
  69.2 2.3 %collective-permute-start.1 = (f32[256,512]{1,0:T(8,128)S(1)}, f32[256,512]{1,0:T(8,128)S(1)}, u32[]{:S(2)}, u32[]{:S(2)}) collective-permute-start(f32[256,512]{1,0:T(8,128)S(1)} %get-tuple-element.36), channel_id=1, source_target_pairs={{0,1},{1,0},{2,3},{3,2},{4,5},{5,4},{6,7},{7,6},{8,9},{9,8},{10,11... | collective-permute-start | bytes 1572872 | tf_op jit(solution)/shard_map/ppermute | solution.py:321
  71.6 0.5 broadcast.3
  72.1 0.0 copy-done.3
  72.1 0.7 reduce.3
  72.8 0.1 reshape.33
  72.9 0.1 copy.18
  73.0 0.1 collective-permute-done.1.refs_2_
  73.1 0.1 shard_map.124
  73.2 0.9 collective-permute-start.2
  74.1 2.4 %collective-permute-start.3 = (f32[64,512]{1,0:T(8,128)S(1)}, f32[64,512]{1,0:T(8,128)S(1)}, u32[]{:S(2)}, u32[]{:S(2)}) collective-permute-start(f32[64,512]{1,0:T(8,128)S(1)} %get-tuple-element.40), channel_id=1, source_target_pairs={{0,4},{2,6},{4,0},{6,2},{1,5},{3,7},{5,1},{7,3},{8,12},{10,14},{12... | collective-permute-start | bytes 393224 | tf_op jit(solution)/shard_map/ppermute | solution.py:326
  76.5 0.6 collective-permute-start.4
  77.1 4.6 %shard_map.125 = f32[512,512]{1,0:T(8,128)} custom-call(f32[512,512]{1,0:T(8,128)} %get-tuple-element.42.refs_0_, f32[512,512]{1,0:T(8,128)} %refs_1_.3, bf16[512,512]{1,0:T(8,128)(2,1)} %get-tuple-element.43.refs_2_, bf16[512,512]{1,0:T(8,128)(2,1)} %get-tuple-element.44.refs_3_), custom_call_target="tpu_custom_call" | custom-call | flops 2000000000 | bytes 5242880 | tf_op jit(solution)/shard_map/pallas_call | solution.py:107
  81.8 0.0 collective-permute-done.2.refs_2_
  81.8 5.5 %collective-permute-done.3.refs_3_ = f32[64,512]{1,0:T(8,128)S(1)} collective-permute-done((f32[64,512]{1,0:T(8,128)S(1)}, f32[64,512]{1,0:T(8,128)S(1)}, u32[]{:S(2)}, u32[]{:S(2)}) %collective-permute-start.3) | collective-permute-done | bytes 131104 | tf_op jit(solution)/shard_map/ppermute | solution.py:326
  87.3 1.4 collective-permute-done.4.refs_4_
  88.7 1.4 collective-permute-start.5
  90.1 2.8 %collective-permute-start.6 = (f32[16,512]{1,0:T(8,128)S(1)}, f32[16,512]{1,0:T(8,128)S(1)}, u32[]{:S(2)}, u32[]{:S(2)}) collective-permute-start(f32[16,512]{1,0:T(8,128)S(1)} %get-tuple-element.51), channel_id=1, source_target_pairs={{0,128},{64,192},{128,0},{192,64},{1,129},{65,193},{129,1},{193,65... | collective-permute-start | bytes 98312 | tf_op jit(solution)/shard_map/ppermute | solution.py:326
  92.9 0.0 collective-permute-start.7
  92.9 0.0 collective-permute-done.5.refs_1_
  92.9 2.9 %collective-permute-done.6.refs_2_ = f32[16,512]{1,0:T(8,128)S(1)} collective-permute-done((f32[16,512]{1,0:T(8,128)S(1)}, f32[16,512]{1,0:T(8,128)S(1)}, u32[]{:S(2)}, u32[]{:S(2)}) %collective-permute-start.6) | collective-permute-done | bytes 32800 | tf_op jit(solution)/shard_map/ppermute | solution.py:326
  95.8 1.9 %collective-permute-done.7.refs_3_ = f32[16,512]{1,0:T(8,128)S(1)} collective-permute-done((f32[16,512]{1,0:T(8,128)S(1)}, f32[16,512]{1,0:T(8,128)S(1)}, u32[]{:S(2)}, u32[]{:S(2)}) %collective-permute-start.7) | collective-permute-done | bytes 32800 | tf_op jit(solution)/shard_map/ppermute | solution.py:326
  97.6 1.6 %collective-permute-start.8 = (f32[16,512]{1,0:T(8,128)S(1)}, f32[16,512]{1,0:T(8,128)S(1)}, u32[]{:S(2)}, u32[]{:S(2)}) collective-permute-start(f32[16,512]{1,0:T(8,128)S(1)} %shard_map.127.refs_0_), channel_id=1, source_target_pairs={{0,8},{8,0},{16,24},{24,16},{32,40},{40,32},{48,56},{56,48},{1,9},... | collective-permute-start | bytes 98312 | tf_op jit(solution)/shard_map/ppermute | solution.py:326
  99.2 1.3 collective-permute-done.8.refs_1_
  100.5 2.1 %collective-permute-start.9 = (f32[16,512]{1,0:T(8,128)S(1)}, f32[16,512]{1,0:T(8,128)S(1)}, u32[]{:S(2)}, u32[]{:S(2)}) collective-permute-start(f32[16,512]{1,0:T(8,128)S(1)} %shard_map.128.refs_0_), channel_id=1, source_target_pairs={{0,16},{8,24},{16,0},{24,8},{32,48},{40,56},{48,32},{56,40},{1,17}... | collective-permute-start | bytes 98312 | tf_op jit(solution)/shard_map/ppermute | solution.py:326
  102.6 1.7 %collective-permute-done.9.refs_1_ = f32[16,512]{1,0:T(8,128)S(1)} collective-permute-done((f32[16,512]{1,0:T(8,128)S(1)}, f32[16,512]{1,0:T(8,128)S(1)}, u32[]{:S(2)}, u32[]{:S(2)}) %collective-permute-start.9) | collective-permute-done | bytes 32800 | tf_op jit(solution)/shard_map/ppermute | solution.py:326
  104.3 4.2 %collective-permute-start.10 = (f32[16,512]{1,0:T(8,128)S(1)}, f32[16,512]{1,0:T(8,128)S(1)}, u32[]{:S(2)}, u32[]{:S(2)}) collective-permute-start(f32[16,512]{1,0:T(8,128)S(1)} %shard_map.129.refs_0_), channel_id=1, source_target_pairs={{0,32},{8,40},{16,48},{24,56},{32,0},{40,8},{48,16},{56,24},{1,33}... | collective-permute-start | bytes 98312 | tf_op jit(solution)/shard_map/ppermute | solution.py:326
  108.5 2.4 %collective-permute-done.10.refs_1_ = f32[16,512]{1,0:T(8,128)S(1)} collective-permute-done((f32[16,512]{1,0:T(8,128)S(1)}, f32[16,512]{1,0:T(8,128)S(1)}, u32[]{:S(2)}, u32[]{:S(2)}) %collective-permute-start.10) | collective-permute-done | bytes 32800 | tf_op jit(solution)/shard_map/ppermute | solution.py:326
  111.0 0.9 shard_map.130
  111.8 0.0 all-to-all-done.2
  111.8 6.4 %collective-permute-start.11 = (f32[2048,128]{1,0:T(8,128)S(1)}, f32[2048,128]{1,0:T(8,128)S(1)}, u32[]{:S(2)}, u32[]{:S(2)}) collective-permute-start(f32[2048,128]{1,0:T(8,128)S(1)} %bitcast.16), channel_id=1, source_target_pairs={{0,1},{1,0},{2,3},{3,2},{4,5},{5,4},{6,7},{7,6},{8,9},{9,8},{10,11... | collective-permute-start | bytes 3145736 | tf_op jit(solution)/shard_map/ppermute | solution.py:321
  118.2 3.6 %all-to-all-start.3 = ((f32[16,16,512]{2,1,0:T(8,128)}), f32[16,16,512]{2,1,0:T(8,128)S(1)}, u32[]{:S(2)}, u32[]{:S(2)}) async-start(f32[16,16,512]{2,1,0:T(8,128)} %shard_map.130), calls=%async_computation.3 | async-start | bytes 1048576 | tf_op jit(solution)/shard_map/all_to_all | solution.py:317
  121.8 0.0 collective-permute-done.11.refs_3_
  121.8 0.0 copy-start.5
  121.8 1.0 copy-done.5
  122.8 6.6 %shard_map.131 = f32[1280,512]{1,0:T(8,128)} custom-call(s32[1]{0:T(128)} %bitcast.refs_0_, s32[2,512]{1,0:T(2,128)S(1)} %bitcast.20, f32[2048,128]{1,0:T(8,128)S(1)} %bitcast.17, f32[2048,128]{1,0:T(8,128)} %copy-done.5, f32[1280,512]{1,0:T(8,128)} %refs_4_.1), custom_call_target="tpu_custom_call" | custom-call | flops 4000000000 | bytes 7344132 | tf_op jit(solution)/shard_map/pallas_call | solution.py:107
  129.4 3.8 %all-to-all-done.3.refs_1_ = f32[16,16,512]{2,1,0:T(8,128)S(1)} async-done(((f32[16,16,512]{2,1,0:T(8,128)}), f32[16,16,512]{2,1,0:T(8,128)S(1)}, u32[]{:S(2)}, u32[]{:S(2)}) %all-to-all-start.3) | async-done | bytes 524320 | tf_op jit(solution)/shard_map/all_to_all | solution.py:317
  133.2 1.1 collective-permute-start.12
  134.3 1.5 %collective-permute-done.12.refs_2_ = f32[16,16,512]{2,1,0:T(8,128)S(1)} collective-permute-done((f32[16,16,512]{2,1,0:T(8,128)S(1)}, f32[16,16,512]{2,1,0:T(8,128)S(1)}, u32[]{:S(2)}, u32[]{:S(2)}) %collective-permute-start.12) | collective-permute-done | bytes 524320 | tf_op jit(solution)/shard_map/ppermute | solution.py:321
  135.8 1.1 shard_map.132
  (5 shorter events, 0.1 us)
Async XLA Ops:
  0.6 38.1 %collective-permute-start = (f32[1024,512]{1,0:T(8,128)}, f32[1024,512]{1,0:T(8,128)S(1)}, u32[]{:S(2)}, u32[]{:S(2)}) collective-permute-start(f32[1024,512]{1,0:T(8,128)} %refs_3_.1), channel_id=1, source_target_pairs={{0,1},{1,0},{2,3},{3,2},{4,5},{5,4},{6,7},{7,6},{8,9},{9,8},{10,11... | collective-permute-start | bytes 6291464 | tf_op jit(solution)/shard_map/ppermute | solution.py:321
  28.9 1.7 %copy-start = (f32[1280,512]{1,0:T(8,128)S(1)}, f32[1280,512]{1,0:T(8,128)}, u32[]{:S(2)}) copy-start(f32[1280,512]{1,0:T(8,128)} %refs_4_.1) | copy-start | bytes 7864324
  32.4 22.7 %all-to-all-start.1 = ((f32[128,8,128]{2,1,0:T(8,128)}), f32[128,8,128]{2,1,0:T(8,128)S(1)}, u32[]{:S(2)}, u32[]{:S(2)}) async-start(f32[128,8,128]{2,1,0:T(8,128)} %bitcast.3), calls=%async_computation.1 | async-start | bytes 1048576 | tf_op jit(solution)/shard_map/all_to_all | solution.py:317
  38.8 1.3 copy-start.4
  40.1 15.0 %copy-start.1 = (s32[512,8]{0,1:T(8,128)S(1)}, s32[512,8]{0,1:T(8,128)}, u32[]{:S(2)}) copy-start(s32[512,8]{0,1:T(8,128)} %param.15) | copy-start | bytes 49156
  40.1 15.0 %copy-start.2 = (f32[512,8]{0,1:T(8,128)S(1)}, f32[512,8]{0,1:T(8,128)}, u32[]{:S(2)}) copy-start(f32[512,8]{0,1:T(8,128)} %param.14) | copy-start | bytes 49156
  55.1 17.0 %copy-start.3 = (s32[1,1024]{1,0:T(1,128)S(1)}, s32[1,1024]{1,0:T(1,128)}, u32[]{:S(2)}) copy-start(s32[1,1024]{1,0:T(1,128)} %param.19) | copy-start | bytes 12292
  60.7 51.1 %all-to-all-start.2 = ((f32[128,16,128]{2,1,0:T(8,128)}), f32[128,16,128]{2,1,0:T(8,128)S(1)}, u32[]{:S(2)}, u32[]{:S(2)}) async-start(f32[128,16,128]{2,1,0:T(8,128)} %bitcast.25), calls=%async_computation.2 | async-start | bytes 2097152 | tf_op jit(solution)/shard_map/all_to_all | solution.py:317
  69.2 3.9 %collective-permute-start.1 = (f32[256,512]{1,0:T(8,128)S(1)}, f32[256,512]{1,0:T(8,128)S(1)}, u32[]{:S(2)}, u32[]{:S(2)}) collective-permute-start(f32[256,512]{1,0:T(8,128)S(1)} %get-tuple-element.36), channel_id=1, source_target_pairs={{0,1},{1,0},{2,3},{3,2},{4,5},{5,4},{6,7},{7,6},{8,9},{9,8},{10,11... | collective-permute-start | bytes 1572872 | tf_op jit(solution)/shard_map/ppermute | solution.py:321
  73.2 8.6 %collective-permute-start.2 = (f32[64,512]{1,0:T(8,128)S(1)}, f32[64,512]{1,0:T(8,128)S(1)}, u32[]{:S(2)}, u32[]{:S(2)}) collective-permute-start(f32[64,512]{1,0:T(8,128)S(1)} %get-tuple-element.39), channel_id=1, source_target_pairs={{0,2},{2,0},{4,6},{6,4},{1,3},{3,1},{5,7},{7,5},{8,10},{10,8},{12,... | collective-permute-start | bytes 393224 | tf_op jit(solution)/shard_map/ppermute | solution.py:326
  74.1 13.2 %collective-permute-start.3 = (f32[64,512]{1,0:T(8,128)S(1)}, f32[64,512]{1,0:T(8,128)S(1)}, u32[]{:S(2)}, u32[]{:S(2)}) collective-permute-start(f32[64,512]{1,0:T(8,128)S(1)} %get-tuple-element.40), channel_id=1, source_target_pairs={{0,4},{2,6},{4,0},{6,2},{1,5},{3,7},{5,1},{7,3},{8,12},{10,14},{12... | collective-permute-start | bytes 393224 | tf_op jit(solution)/shard_map/ppermute | solution.py:326
  76.5 12.1 %collective-permute-start.4 = (f32[64,512]{1,0:T(8,128)S(1)}, f32[64,512]{1,0:T(8,128)S(1)}, u32[]{:S(2)}, u32[]{:S(2)}) collective-permute-start(f32[64,512]{1,0:T(8,128)S(1)} %get-tuple-element.41), channel_id=1, source_target_pairs={{0,6},{2,4},{4,2},{6,0},{1,7},{3,5},{5,3},{7,1},{8,14},{10,12},{12... | collective-permute-start | bytes 393224 | tf_op jit(solution)/shard_map/ppermute | solution.py:326
  88.7 4.2 %collective-permute-start.5 = (f32[16,512]{1,0:T(8,128)S(1)}, f32[16,512]{1,0:T(8,128)S(1)}, u32[]{:S(2)}, u32[]{:S(2)}) collective-permute-start(f32[16,512]{1,0:T(8,128)S(1)} %get-tuple-element.50), channel_id=1, source_target_pairs={{0,64},{64,0},{128,192},{192,128},{1,65},{65,1},{129,193},{193,129... | collective-permute-start | bytes 98312 | tf_op jit(solution)/shard_map/ppermute | solution.py:326
  90.1 5.7 %collective-permute-start.6 = (f32[16,512]{1,0:T(8,128)S(1)}, f32[16,512]{1,0:T(8,128)S(1)}, u32[]{:S(2)}, u32[]{:S(2)}) collective-permute-start(f32[16,512]{1,0:T(8,128)S(1)} %get-tuple-element.51), channel_id=1, source_target_pairs={{0,128},{64,192},{128,0},{192,64},{1,129},{65,193},{129,1},{193,65... | collective-permute-start | bytes 98312 | tf_op jit(solution)/shard_map/ppermute | solution.py:326
  92.9 4.7 %collective-permute-start.7 = (f32[16,512]{1,0:T(8,128)S(1)}, f32[16,512]{1,0:T(8,128)S(1)}, u32[]{:S(2)}, u32[]{:S(2)}) collective-permute-start(f32[16,512]{1,0:T(8,128)S(1)} %get-tuple-element.52), channel_id=1, source_target_pairs={{0,192},{64,128},{128,64},{192,0},{1,193},{65,129},{129,65},{193,1... | collective-permute-start | bytes 98312 | tf_op jit(solution)/shard_map/ppermute | solution.py:326
  97.6 2.9 %collective-permute-start.8 = (f32[16,512]{1,0:T(8,128)S(1)}, f32[16,512]{1,0:T(8,128)S(1)}, u32[]{:S(2)}, u32[]{:S(2)}) collective-permute-start(f32[16,512]{1,0:T(8,128)S(1)} %shard_map.127.refs_0_), channel_id=1, source_target_pairs={{0,8},{8,0},{16,24},{24,16},{32,40},{40,32},{48,56},{56,48},{1,9},... | collective-permute-start | bytes 98312 | tf_op jit(solution)/shard_map/ppermute | solution.py:326
  100.5 3.7 %collective-permute-start.9 = (f32[16,512]{1,0:T(8,128)S(1)}, f32[16,512]{1,0:T(8,128)S(1)}, u32[]{:S(2)}, u32[]{:S(2)}) collective-permute-start(f32[16,512]{1,0:T(8,128)S(1)} %shard_map.128.refs_0_), channel_id=1, source_target_pairs={{0,16},{8,24},{16,0},{24,8},{32,48},{40,56},{48,32},{56,40},{1,17}... | collective-permute-start | bytes 98312 | tf_op jit(solution)/shard_map/ppermute | solution.py:326
  104.3 6.7 %collective-permute-start.10 = (f32[16,512]{1,0:T(8,128)S(1)}, f32[16,512]{1,0:T(8,128)S(1)}, u32[]{:S(2)}, u32[]{:S(2)}) collective-permute-start(f32[16,512]{1,0:T(8,128)S(1)} %shard_map.129.refs_0_), channel_id=1, source_target_pairs={{0,32},{8,40},{16,48},{24,56},{32,0},{40,8},{48,16},{56,24},{1,33}... | collective-permute-start | bytes 98312 | tf_op jit(solution)/shard_map/ppermute | solution.py:326
  111.8 10.0 %collective-permute-start.11 = (f32[2048,128]{1,0:T(8,128)S(1)}, f32[2048,128]{1,0:T(8,128)S(1)}, u32[]{:S(2)}, u32[]{:S(2)}) collective-permute-start(f32[2048,128]{1,0:T(8,128)S(1)} %bitcast.16), channel_id=1, source_target_pairs={{0,1},{1,0},{2,3},{3,2},{4,5},{5,4},{6,7},{7,6},{8,9},{9,8},{10,11... | collective-permute-start | bytes 3145736 | tf_op jit(solution)/shard_map/ppermute | solution.py:321
  118.2 15.0 %all-to-all-start.3 = ((f32[16,16,512]{2,1,0:T(8,128)}), f32[16,16,512]{2,1,0:T(8,128)S(1)}, u32[]{:S(2)}, u32[]{:S(2)}) async-start(f32[16,16,512]{2,1,0:T(8,128)} %shard_map.130), calls=%async_computation.3 | async-start | bytes 1048576 | tf_op jit(solution)/shard_map/all_to_all | solution.py:317
  121.8 1.0 copy-start.5
  133.2 2.6 %collective-permute-start.12 = (f32[16,16,512]{2,1,0:T(8,128)S(1)}, f32[16,16,512]{2,1,0:T(8,128)S(1)}, u32[]{:S(2)}, u32[]{:S(2)}) collective-permute-start(f32[16,16,512]{2,1,0:T(8,128)S(1)} %all-to-all-done.3.refs_1_), channel_id=1, source_target_pairs={{0,1},{1,0},{2,3},{3,2},{4,5},{5,4},{6,7},{7,6},{8,9},{9,8},{10,11... | collective-permute-start | bytes 1572872 | tf_op jit(solution)/shard_map/ppermute | solution.py:321
